TPU v7x, 32 devices: a whole 2x2x4 slice. The times are simulated.
32 devices in a mesh: dp: 4 (over z), fsdp: 8 (over y, x, core).
Axes of the slice: x: 2, y: 2, z: 4, core: 2. Of those that a mesh axis runs over, the one named last changes fastest.
Arguments:
- tokens: bfloat16 [128, 64, 768], P(('dp', 'fsdp')), may hold values from -6 to 6
- memory: bfloat16 [128, 228, 768], P(('dp', 'fsdp')), may hold values from -6 to 6
- lengths: int32 [128], P(('dp', 'fsdp')), may hold values from 1 to 64, 5120 in all
- cotangent: bfloat16 [128, 64, 768], P(('dp', 'fsdp')), may hold values from -6 to 6
- self_qkv: bfloat16 [768, 2304], P(('dp', 'fsdp')), may hold values from -0.21875 to 0.21875
- self_out: bfloat16 [768, 768], P(('dp', 'fsdp')), may hold values from -0.5 to 0.5
- cross_q: bfloat16 [768, 768], P(('dp', 'fsdp')), may hold values from -0.21875 to 0.21875
- cross_kv: bfloat16 [768, 1536], P(('dp', 'fsdp')), may hold values from -0.21875 to 0.21875
- cross_out: bfloat16 [768, 768], P(('dp', 'fsdp')), may hold values from -0.875 to 0.875
- mlp_in: bfloat16 [768, 3072], P(('dp', 'fsdp')), may hold values from -0.21875 to 0.21875
- mlp_out: bfloat16 [3072, 768], P(('dp', 'fsdp')), may hold values from -0.15625 to 0.15625
- norm_gains: bfloat16 [3, 768], P(None, ('dp', 'fsdp')), may hold values from 0.099609375 to 1.8984375
- norm_biases: bfloat16 [3, 768], P(None, ('dp', 'fsdp')), may hold values from -1.5 to 1.5
Outputs:
- output: bfloat16 [128, 64, 768], P(('dp', 'fsdp'))
- grad_tokens: bfloat16 [128, 64, 768], P(('dp', 'fsdp'))
- grad_memory: bfloat16 [128, 228, 768], P(('dp', 'fsdp'))
- grad_self_qkv: float32 [768, 2304], P(('dp', 'fsdp'))
- grad_self_out: float32 [768, 768], P(('dp', 'fsdp'))
- grad_cross_q: float32 [768, 768], P(('dp', 'fsdp'))
- grad_cross_kv: float32 [768, 1536], P(('dp', 'fsdp'))
- grad_cross_out: float32 [768, 768], P(('dp', 'fsdp'))
- grad_mlp_in: float32 [768, 3072], P(('dp', 'fsdp'))
- grad_mlp_out: float32 [3072, 768], P(('dp', 'fsdp'))
- grad_gains: float32 [3, 768], P(None, ('dp', 'fsdp'))
- grad_biases: float32 [3, 768], P(None, ('dp', 'fsdp'))
Inputs may be any that keep to these rules, and one draw needn't show every extreme that they name: `lengths`: slots of a suffix at or beyond its length are padding; some suffix has length 64.
All inputs are finite; a program needn't handle non-finite values. No bound on the sum of `lengths` on one device may be relied on, other than what follows from the above.
Results may differ from a plain program's by a relative error of at most 0.02.
Values may be sent and summed in bfloat16 or wider, within the bound.
No kernel may reach another device: no remote copies, remote signals or barrier semaphores. Data moves between devices by JAX's collectives and lax.ppermute only.
A program may use at most 192 MiB of HBM per device.

v0:
```python
import jax
import jax.numpy as jnp
from jax import lax
from jax.sharding import PartitionSpec as P

HEADS = 12


epsilon = 1e-06
big_negative = -1e30


def norm_rows(values, gain, bias):
    mean = jnp.mean(values, -1, keepdims=True)
    centered = values - mean
    spread = jnp.mean(centered * centered, -1, keepdims=True)
    return centered * lax.rsqrt(spread + epsilon) * gain + bias


def norm_back(values, gain, bias, grad):
    _, pull = jax.vjp(norm_rows, values, gain, bias)
    return pull(grad)


def project(values, weight):
    return jnp.einsum("bld,de->ble", values, weight, preferred_element_type=jnp.float32)


def project_back(grad, weight):
    return jnp.einsum("ble,de->bld", grad, weight, preferred_element_type=jnp.float32)


def weight_grad(values, grad):
    return jnp.einsum("bld,ble->de", values, grad, preferred_element_type=jnp.float32)


def heads_of(values):
    return values.reshape(values.shape[0], values.shape[1], HEADS, values.shape[2] // HEADS)


def term_of(products, vectors, count):
    parts = [
        weight_grad(lax.slice_in_dim(values, 0, count, axis=2), grad) for values, grad in products
    ]
    parts = parts + [lax.slice_in_dim(vec, 0, count, axis=0)[:, None] for vec in vectors]
    return jnp.concatenate(parts, 1)


def split_columns(block, widths):
    pieces = []
    offset = 0
    for width in widths:
        pieces.append(block[:, offset : offset + width])
        offset = offset + width
    return pieces


def attention(query, keys, values, valid, scale):
    scores = jnp.einsum("bqhe,bkhe->bhqk", query, keys, preferred_element_type=jnp.float32) * scale
    scores = jnp.where(valid[:, None], scores, big_negative)
    peak = jnp.max(scores, -1, keepdims=True)
    total = jnp.sum(jnp.exp(scores - peak), -1, keepdims=True)
    probs = jnp.exp(scores - peak - jnp.log(total))
    probs_low = probs.astype(jnp.bfloat16)
    mixed = jnp.einsum("bhqk,bkhe->bqhe", probs_low, values, preferred_element_type=jnp.float32)
    mixed = mixed.reshape(mixed.shape[0], mixed.shape[1], -1).astype(jnp.bfloat16)
    return (probs, probs_low, mixed)


def attention_back(grad_mixed, query, keys, values, probs, probs_low, scale):
    grad_heads = heads_of(grad_mixed)
    dprobs = jnp.einsum("bqhe,bkhe->bhqk", grad_heads, values, preferred_element_type=jnp.float32)
    delta = jnp.sum(probs * dprobs, -1, keepdims=True)
    dscores = (probs * (dprobs - delta)).astype(jnp.bfloat16)
    dquery = (
        jnp.einsum("bhqk,bkhe->bqhe", dscores, keys, preferred_element_type=jnp.float32) * scale
    )
    dkeys = (
        jnp.einsum("bhqk,bqhe->bkhe", dscores, query, preferred_element_type=jnp.float32) * scale
    )
    dvalues = jnp.einsum(
        "bhqk,bqhe->bkhe", probs_low, grad_heads, preferred_element_type=jnp.float32
    )
    flat = lambda v: v.reshape(v.shape[0], v.shape[1], -1)
    return (flat(dquery), flat(dkeys), flat(dvalues))


def run_forward(tokens32, memory, valid, weights):
    self_qkv, self_out, cross_q, cross_kv, cross_out, mlp_in, mlp_out, norm_gains, norm_biases = (
        weights
    )
    gains = norm_gains.astype(jnp.float32)
    biases = norm_biases.astype(jnp.float32)
    width = tokens32.shape[-1]
    scale = (width // HEADS) ** (-0.5)
    first = norm_rows(tokens32, gains[0], biases[0]).astype(jnp.bfloat16)
    packed = project(first, self_qkv).astype(jnp.bfloat16)
    query = heads_of(packed[..., :width])
    keys = heads_of(packed[..., width : 2 * width])
    values = heads_of(packed[..., 2 * width :])
    probs, probs_low, mixed = attention(query, keys, values, valid, scale)
    resid_one = tokens32 + project(mixed, self_out)
    second = norm_rows(resid_one, gains[1], biases[1]).astype(jnp.bfloat16)
    cross_query = heads_of(project(second, cross_q).astype(jnp.bfloat16))
    cross_packed = project(memory, cross_kv).astype(jnp.bfloat16)
    cross_keys = heads_of(cross_packed[..., :width])
    cross_values = heads_of(cross_packed[..., width:])
    full = jnp.ones((tokens32.shape[0], tokens32.shape[1], memory.shape[1]), bool)
    cross_probs, cross_low, cross_mixed = attention(
        cross_query, cross_keys, cross_values, full, scale
    )
    resid_two = resid_one + project(cross_mixed, cross_out)
    third = norm_rows(resid_two, gains[2], biases[2]).astype(jnp.bfloat16)
    inner = project(third, mlp_in)
    hidden = jax.nn.gelu(inner, approximate=False).astype(jnp.bfloat16)
    output = resid_two + project(hidden, mlp_out)
    saved = dict(
        first=first,
        query=query,
        keys=keys,
        values=values,
        probs=probs,
        probs_low=probs_low,
        mixed=mixed,
        resid_one=resid_one,
        second=second,
        cross_query=cross_query,
        cross_keys=cross_keys,
        cross_values=cross_values,
        cross_probs=cross_probs,
        cross_low=cross_low,
        cross_mixed=cross_mixed,
        resid_two=resid_two,
        third=third,
        inner=inner,
        hidden=hidden,
        gains=gains,
        biases=biases,
        scale=scale,
    )
    return (output, saved)


def per_device(
    tokens,
    memory,
    lengths,
    cotangent,
    self_qkv,
    self_out,
    cross_q,
    cross_kv,
    cross_out,
    mlp_in,
    mlp_out,
    norm_gains,
    norm_biases,
):
    gathered = (
        lax.all_gather(self_qkv, ("dp", "fsdp"), axis=0, tiled=True),
        lax.all_gather(self_out, ("dp", "fsdp"), axis=0, tiled=True),
        lax.all_gather(cross_q, ("dp", "fsdp"), axis=0, tiled=True),
        lax.all_gather(cross_kv, ("dp", "fsdp"), axis=0, tiled=True),
        lax.all_gather(cross_out, ("dp", "fsdp"), axis=0, tiled=True),
        lax.all_gather(mlp_in, ("dp", "fsdp"), axis=0, tiled=True),
        lax.all_gather(mlp_out, ("dp", "fsdp"), axis=0, tiled=True),
        lax.all_gather(norm_gains, ("dp", "fsdp"), axis=1, tiled=True),
        lax.all_gather(norm_biases, ("dp", "fsdp"), axis=1, tiled=True),
    )
    tokens32 = tokens.astype(jnp.float32)
    places = jnp.arange(tokens.shape[1], dtype=jnp.int32)
    live = places[None, :] < lengths[:, None]
    valid = (places[:, None] >= places[None, :])[None] & live[:, None, :]
    output, _ = run_forward(tokens32, memory, valid, gathered)
    again = (
        lax.all_gather(self_qkv, ("dp", "fsdp"), axis=0, tiled=True),
        lax.all_gather(self_out, ("dp", "fsdp"), axis=0, tiled=True),
        lax.all_gather(cross_q, ("dp", "fsdp"), axis=0, tiled=True),
        lax.all_gather(cross_kv, ("dp", "fsdp"), axis=0, tiled=True),
        lax.all_gather(cross_out, ("dp", "fsdp"), axis=0, tiled=True),
        lax.all_gather(mlp_in, ("dp", "fsdp"), axis=0, tiled=True),
        lax.all_gather(mlp_out, ("dp", "fsdp"), axis=0, tiled=True),
        lax.all_gather(norm_gains, ("dp", "fsdp"), axis=1, tiled=True),
        lax.all_gather(norm_biases, ("dp", "fsdp"), axis=1, tiled=True),
    )
    _, saved = run_forward(tokens32, memory, valid, again)
    w_qkv, w_out, w_cq, w_ckv, w_cout, w_in, w_mlpout, _, _ = again
    gains = saved["gains"]
    biases = saved["biases"]
    scale = saved["scale"]
    width = tokens.shape[-1]
    hidden_width = w_in.shape[1]
    model_rows = self_qkv.shape[0]
    hidden_rows = mlp_out.shape[0]
    grad_out = cotangent.astype(jnp.float32) * live[..., None].astype(jnp.float32)
    grad_three = grad_out.astype(jnp.bfloat16)
    grad_hidden = project_back(grad_three, w_mlpout)
    _, gelu_pull = jax.vjp(lambda v: jax.nn.gelu(v, approximate=False), saved["inner"])
    grad_inner = gelu_pull(grad_hidden)[0].astype(jnp.bfloat16)
    grad_third = project_back(grad_inner, w_in)
    back_two, gain_three, bias_three = norm_back(
        saved["resid_two"], gains[2], biases[2], grad_third
    )
    grad_resid_two = grad_out + back_two
    grad_two = grad_resid_two.astype(jnp.bfloat16)
    grad_cross_mixed = project_back(grad_two, w_cout).astype(jnp.bfloat16)
    dcq, dck, dcv = attention_back(
        grad_cross_mixed,
        saved["cross_query"],
        saved["cross_keys"],
        saved["cross_values"],
        saved["cross_probs"],
        saved["cross_low"],
        scale,
    )
    dcq = dcq.astype(jnp.bfloat16)
    dckv = jnp.concatenate([dck, dcv], -1).astype(jnp.bfloat16)
    grad_memory = project_back(dckv, w_ckv).astype(jnp.bfloat16)
    grad_second = project_back(dcq, w_cq)
    back_one, gain_two, bias_two = norm_back(saved["resid_one"], gains[1], biases[1], grad_second)
    grad_resid_one = grad_resid_two + back_one
    grad_one = grad_resid_one.astype(jnp.bfloat16)
    grad_mixed = project_back(grad_one, w_out).astype(jnp.bfloat16)
    dsq, dsk, dsv = attention_back(
        grad_mixed,
        saved["query"],
        saved["keys"],
        saved["values"],
        saved["probs"],
        saved["probs_low"],
        scale,
    )
    dpacked = jnp.concatenate([dsq, dsk, dsv], -1).astype(jnp.bfloat16)
    grad_first = project_back(dpacked, w_qkv)
    back_zero, gain_one, bias_one = norm_back(tokens32, gains[0], biases[0], grad_first)
    grad_tokens = (grad_resid_one + back_zero).astype(jnp.bfloat16)
    block_rows = lax.psum_scatter(
        term_of(
            [
                (saved["first"], dpacked),
                (saved["mixed"], grad_one),
                (saved["second"], dcq),
                (memory, dckv),
                (saved["cross_mixed"], grad_two),
                (saved["third"], grad_inner),
            ],
            [gain_one, gain_two, gain_three, bias_one, bias_two, bias_three],
            lax.axis_size(("dp", "fsdp")) * model_rows,
        ),
        ("dp", "fsdp"),
        scatter_dimension=0,
        tiled=True,
    )
    sum_mlpout = lax.psum_scatter(
        term_of([(saved["hidden"], grad_three)], [], lax.axis_size(("dp", "fsdp")) * hidden_rows),
        ("dp", "fsdp"),
        scatter_dimension=0,
        tiled=True,
    )
    pieces = split_columns(
        block_rows, [3 * width, width, width, 2 * width, width, hidden_width, 1, 1, 1, 1, 1, 1]
    )
    sum_qkv, sum_out, sum_cq, sum_ckv, sum_cout, sum_in = pieces[:6]
    sum_gains = jnp.concatenate(pieces[6:9], 1).T
    sum_biases = jnp.concatenate(pieces[9:12], 1).T
    return (
        output.astype(jnp.bfloat16),
        grad_tokens,
        grad_memory,
        sum_qkv,
        sum_out,
        sum_cq,
        sum_ckv,
        sum_cout,
        sum_in,
        sum_mlpout,
        sum_gains,
        sum_biases,
    )


def solution(mesh):
    in_specs = (
        P(("dp", "fsdp"), None, None),
        P(("dp", "fsdp"), None, None),
        P(("dp", "fsdp")),
        P(("dp", "fsdp"), None, None),
        P(("dp", "fsdp"), None),
        P(("dp", "fsdp"), None),
        P(("dp", "fsdp"), None),
        P(("dp", "fsdp"), None),
        P(("dp", "fsdp"), None),
        P(("dp", "fsdp"), None),
        P(("dp", "fsdp"), None),
        P(None, ("dp", "fsdp")),
        P(None, ("dp", "fsdp")),
    )
    out_specs = (
        P(("dp", "fsdp"), None, None),
        P(("dp", "fsdp"), None, None),
        P(("dp", "fsdp"), None, None),
        P(("dp", "fsdp"), None),
        P(("dp", "fsdp"), None),
        P(("dp", "fsdp"), None),
        P(("dp", "fsdp"), None),
        P(("dp", "fsdp"), None),
        P(("dp", "fsdp"), None),
        P(("dp", "fsdp"), None),
        P(None, ("dp", "fsdp")),
        P(None, ("dp", "fsdp")),
    )
    return jax.shard_map(
        per_device, mesh=mesh, in_specs=in_specs, out_specs=out_specs, check_vma=False
    )
```

profile of v0, /device:TPU:0, one launch (start us, length us, event | category | flops | bytes accessed | tf_op | source)
XLA Modules:
  0.0 1158.9 jit_solution(5236115626375896291)
XLA Ops:
  11.9 43.5 %all-gather.1 = bf16[32,24,3]{1,2,0:T(4,128)(2,1)S(1)} all-gather(bf16[1,24,3]{1,2,0:T(4,128)(2,1)} %bitcast.170), channel_id=1, replica_groups=mesh['dp'=4,'fsdp'=8] {'dp','fsdp'}, dimensions={0}, use_global_device_ids=true | all-gather | bytes 4752 | tf_op jit(solution)/shard_map/all_gather | solution.py:168
  55.7 36.9 %all-gather = bf16[32,24,3]{1,2,0:T(4,128)(2,1)S(1)} all-gather(bf16[1,24,3]{1,2,0:T(4,128)(2,1)} %bitcast.171), channel_id=1, replica_groups=mesh['dp'=4,'fsdp'=8] {'dp','fsdp'}, dimensions={0}, use_global_device_ids=true | all-gather | bytes 4752 | tf_op jit(solution)/shard_map/all_gather | solution.py:167
  98.0 4.5 convolution_convert_fusion.1
  105.2 27.6 %all-gather.10.cloned.1.call-done = bf16[768,2304]{1,0:T(8,128)(2,1)} async-done(((bf16[24,2304]{1,0:T(8,128)(2,1)}), bf16[768,2304]{1,0:T(8,128)(2,1)}) %all-gather.10.cloned.1.call-update) | async-done | bytes 3538960 | tf_op jit(solution)/shard_map/all_gather | solution.py:160
  132.8 3.2 convolution_convert_fusion
  138.7 2.4 copy.227
  142.3 3.1 fusion.33
  145.4 3.6 convolution_convert_fusion.4
  149.0 39.6 %all-gather.12.cloned.1.call-done = bf16[768,768]{1,0:T(8,128)(2,1)} async-done(((bf16[24,768]{1,0:T(8,128)(2,1)}), bf16[768,768]{1,0:T(8,128)(2,1)}) %all-gather.12.cloned.1.call-update) | async-done | bytes 1179664 | tf_op jit(solution)/shard_map/all_gather | solution.py:161
  188.6 2.1 fusion.128
  191.0 53.4 %all-gather.16.cloned.1.call-done = bf16[768,768]{1,0:T(8,128)(2,1)} async-done(((bf16[24,768]{1,0:T(8,128)(2,1)}), bf16[768,768]{1,0:T(8,128)(2,1)}) %all-gather.16.cloned.1.call-update) | async-done | bytes 1179664 | tf_op jit(solution)/shard_map/all_gather | solution.py:162
  244.4 2.6 convolution_convert_fusion.8
  248.3 2.5 multiply_subtract_fusion
  250.8 5.6 convolution_convert_fusion.5
  256.5 43.6 %all-gather.18.cloned.1.call-done = bf16[768,768]{1,0:T(8,128)(2,1)} async-done(((bf16[24,768]{1,0:T(8,128)(2,1)}), bf16[768,768]{1,0:T(8,128)(2,1)}) %all-gather.18.cloned.1.call-update) | async-done | bytes 1179664 | tf_op jit(solution)/shard_map/all_gather | solution.py:164
  300.1 2.1 fusion.129
  304.3 61.2 %all-gather.20.cloned.1.call-done = bf16[768,3072]{1,0:T(8,128)(2,1)} async-done(((bf16[24,3072]{1,0:T(8,128)(2,1)}), bf16[768,3072]{1,0:T(8,128)(2,1)}) %all-gather.20.cloned.1.call-update) | async-done | bytes 4718608 | tf_op jit(solution)/shard_map/all_gather | solution.py:165
  365.4 4.7 fusion.75
  371.8 8.4 multiply_convert_fusion.2
  380.2 50.6 %all-gather.22.cloned.1.call-done = bf16[3072,768]{1,0:T(8,128)(2,1)} async-done(((bf16[96,768]{1,0:T(8,128)(2,1)}), bf16[3072,768]{1,0:T(8,128)(2,1)}) %all-gather.22.cloned.1.call-update) | async-done | bytes 4718608 | tf_op jit(solution)/shard_map/all_gather | solution.py:166
  430.8 6.3 add_convert_fusion
  437.2 5.1 multiply_reduce_fusion.3
  446.6 2.2 copy.230
  448.7 2.4 fusion.130
  451.3 9.2 multiply_reduce_fusion
  463.8 2.0 convert_element_type.150
  465.8 2.6 fusion.121
  471.5 3.7 convolution_convert_fusion.3
  476.8 3.2 multiply_reduce_fusion.2
  484.1 5.7 convolution_convert_fusion.2
  489.8 2.9 multiply_convert_fusion
  492.8 1.9 convolution_bitcast_fusion.6
  494.7 2.1 convolution_bitcast_fusion.5
  496.9 2.0 convolution_bitcast_fusion.4
  498.9 5.3 convolution_bitcast_fusion.1
  508.7 5.3 convolution_bitcast_fusion.2
  514.0 2.6 fusion.122
  516.6 2.7 copy.193
  521.0 7.1 convolution_bitcast_fusion.3
  528.1 6.0 copy.199
  534.2 2.3 fusion.68
  544.7 32.0 %concatenate.17 = f32[768,9222]{1,0:T(8,128)} concatenate(f32[768,2304]{1,0:T(8,128)} %convolution_bitcast_fusion.2, f32[768,768]{1,0:T(8,128)S(1)} %copy-done.4, f32[768,768]{1,0:T(8,128)} %convolution_bitcast_fusion.5, f32[768,1536]{1,0:T(8,128)} %copy.199, f32[768,768]{1,0:T(8,128)} %convolution_bitcast_fusion.4, f32[768,3072]{1,0:T(8,128)} %convolution_bitcast_fusion.1, ...), dimensions={1} | concatenate | bytes 56659968 | tf_op jit(solution)/shard_map/concatenate | solution.py:46
  578.2 6.0 convolution_bitcast_fusion
  584.3 4.9 fusion.34
  591.9 4.6 fusion.50
  596.5 413.5 %all-reduce.3.cloned.1.call-done = f32[768,9222]{1,0:T(8,128)} async-done(((f32[768,9222]{1,0:T(8,128)}), f32[768,9222]{1,0:T(8,128)}) %all-reduce.3.cloned.1.call-update) | async-done | bytes 28330000
  1013.8 1.8 dynamic-slice.6
  1019.0 133.1 %reduce-scatter.2.cloned.1.call-done = f32[96,768]{1,0:T(8,128)} async-done(((f32[3072,768]{1,0:T(8,128)}), f32[96,768]{1,0:T(8,128)}) %reduce-scatter.2.cloned.1.call-update) | async-done | bytes 294928 | tf_op jit(solution)/shard_map/reduce_scatter | solution.py:254
  (218 shorter events, 64.4 us)
Async XLA Ops:
  7.2 90.8 %all-gather.14.cloned.1.call-start = ((), (), s32[]{:S(2)}) async-start(), calls=%async_computation.3 | async-start | bytes 2433024 | tf_op jit(solution)/shard_map/all_gather | solution.py:163
  7.9 124.9 %all-gather.10.cloned.1.call-start = ((), (), s32[]{:S(2)}) async-start(), calls=%async_computation.1 | async-start | bytes 3649536 | tf_op jit(solution)/shard_map/all_gather | solution.py:160
  8.7 179.9 %all-gather.12.cloned.1.call-start = ((), (), s32[]{:S(2)}) async-start(), calls=%async_computation.2 | async-start | bytes 1216512 | tf_op jit(solution)/shard_map/all_gather | solution.py:161
  9.4 235.0 %all-gather.16.cloned.1.call-start = ((), (), s32[]{:S(2)}) async-start(), calls=%async_computation.4 | async-start | bytes 1216512 | tf_op jit(solution)/shard_map/all_gather | solution.py:162
  10.0 290.1 %all-gather.18.cloned.1.call-start = ((), (), s32[]{:S(2)}) async-start(), calls=%async_computation.5 | async-start | bytes 1216512 | tf_op jit(solution)/shard_map/all_gather | solution.py:164
  10.6 354.9 %all-gather.20.cloned.1.call-start = ((), (), s32[]{:S(2)}) async-start(), calls=%async_computation.6 | async-start | bytes 4866048 | tf_op jit(solution)/shard_map/all_gather | solution.py:165
  11.1 419.7 %all-gather.22.cloned.1.call-start = ((), (), s32[]{:S(2)}) async-start(), calls=%async_computation.7 | async-start | bytes 4866048 | tf_op jit(solution)/shard_map/all_gather | solution.py:166
  11.9 998.1 %all-reduce.3.cloned.1.call-start = ((), (), s32[]{:S(2)}) async-start(), calls=%async_computation.9 | async-start | bytes 57409536
  96.0 6.5 copy-start.48
  97.3 35.5 %copy-start.43 = (f32[4,64]{1,0:T(4,128)}, f32[4,64]{1,0:T(4,128)S(1)}, u32[]{:S(2)}) copy-start(f32[4,64]{1,0:T(4,128)S(1)} %fusion.108) | copy-start | bytes 3076
  102.7 30.2 %copy-start.3 = (bf16[4,64,768]{2,1,0:T(8,128)(2,1)S(1)}, bf16[4,64,768]{2,1,0:T(8,128)(2,1)}, u32[]{:S(2)}) copy-start(bf16[4,64,768]{2,1,0:T(8,128)(2,1)} %param.13) | copy-start | bytes 1179652
  136.0 6.3 copy-start.34
  138.7 10.3 copy-start.16
  191.0 53.4 %copy-start.50 = (f32[4,64]{1,0:T(4,128)}, f32[4,64]{1,0:T(4,128)S(1)}, u32[]{:S(2)}) copy-start(f32[4,64]{1,0:T(4,128)S(1)} %multiply_reduce_fusion.8) | copy-start | bytes 3076
  191.0 53.4 %copy-start.38 = (f32[4,64]{1,0:T(4,128)}, f32[4,64]{1,0:T(4,128)S(1)}, u32[]{:S(2)}) copy-start(f32[4,64]{1,0:T(4,128)S(1)} %fusion.109) | copy-start | bytes 3076
  248.3 8.1 copy-start.10
  302.2 134.9 %copy-start.7 = (f32[4,64,768]{2,1,0:T(8,128)}, f32[4,64,768]{2,1,0:T(8,128)S(1)}, u32[]{:S(2)}) copy-start(f32[4,64,768]{2,1,0:T(8,128)S(1)} %get-tuple-element.98) | copy-start | bytes 2359300
  430.8 6.3 copy-start.46
  430.8 6.3 copy-start.54
  430.8 6.3 copy-start.56
  437.1 5.2 copy-start.64
  437.2 5.2 copy-start.53
  437.2 6.8 copy-start.25
  437.2 6.8 copy-start.35
  443.9 7.2 copy-start.5
  462.2 6.1 copy-start.51
  462.2 6.2 copy-start.39
  463.8 5.6 copy-start.6
  463.8 5.6 copy-start.26
  463.8 5.6 copy-start.36
  463.8 5.6 copy-start.42
  469.8 5.4 copy-start.17
  482.6 7.2 copy-start.1
  489.8 4.9 copy-start.29
  489.8 4.9 copy-start.40
  489.8 4.9 copy-start.62
  494.7 4.2 copy-start.8
  494.7 4.2 copy-start.47
  494.7 4.1 copy-start.55
  498.9 5.3 copy-start.32
  504.4 4.3 copy-start.44
  504.4 4.3 copy-start.60
  508.7 5.3 copy-start.33
  508.7 5.3 copy-start.63
  534.2 9.6 copy-start.59
  534.2 10.5 copy-start.4
  576.8 575.4 %reduce-scatter.2.cloned.1.call-start = ((), (), s32[]{:S(2)}) async-start(), calls=%async_computation.8 | async-start | bytes 9732096 | tf_op jit(solution)/shard_map/reduce_scatter | solution.py:254
  584.2 6.6 copy-start.58
  (27 other events, 62.0 us)
Sparse Core Ops, SparseCore 0:
  10.9 59.9 all-gather.13
  73.8 58.9 all-gather.9
  135.7 52.8 all-gather.11
  191.4 52.9 all-gather.15
  247.1 52.9 all-gather.17
  302.9 62.5 all-gather.19
  368.3 62.4 all-gather.21
  576.9 433.0 all-reduce.2
  1016.4 135.6 reduce-scatter.1
where the time goes:
time: 1160 us
  waiting for transfers between devices  827 us (71%)
  matrix products  111 us (10%)
  local copies, waits for them, and re-layouts  91.4 us (8%)
  blocking collectives  80.4 us (7%)
  other arithmetic  33.7 us (3%)
  between operations  14.8 us (1%)
    unnamed x10, waiting for transfers between devices  418 us
    reduce_scatter x1, waiting for transfers between devices, per_device(): lax.psum_scatter(term_of([(saved['hidden'], grad_three)], [], lax.axis_si...  133 us
    all_gather x1, waiting for transfers between devices, per_device(): lax.all_gather(mlp_in, ('dp', 'fsdp'), axis=0, tiled=True)  61.2 us
    all_gather x1, waiting for transfers between devices, per_device(): lax.all_gather(cross_q, ('dp', 'fsdp'), axis=0, tiled=True)  53.4 us
    all_gather x1, waiting for transfers between devices, per_device(): lax.all_gather(mlp_out, ('dp', 'fsdp'), axis=0, tiled=True)  50.6 us
    all_gather x1, waiting for transfers between devices, per_device(): lax.all_gather(cross_out, ('dp', 'fsdp'), axis=0, tiled=True)  43.6 us
    all_gather x1, blocking collectives, per_device(): lax.all_gather(norm_biases, ('dp', 'fsdp'), axis=1, tiled=True)  43.5 us
    all_gather x1, waiting for transfers between devices, per_device(): lax.all_gather(self_out, ('dp', 'fsdp'), axis=0, tiled=True)  39.6 us
  transfers between devices with their start and end apart: 9, of which 8 were waited for; matrix products, arithmetic and copies ran while one was open for 7% of the time, Pallas kernels for 0%

commit v1 on v0

v1 whole, which is shorter than its diff:
```python
import jax
import jax.numpy as jnp
import numpy as np
from jax import lax
from jax.experimental import pallas as pl
from jax.experimental.pallas import tpu as pltpu
from jax.sharding import PartitionSpec as P

AXES = ("dp", "fsdp")
HEADS = 12
HALF = HEADS // 2
HEAD = 64
D = 768
DH = D // 2
LEN = 64
EPS = 1e-06
NEG = -1e30
SCALE = HEAD ** (-0.5)
F32 = jnp.float32
BF = jnp.bfloat16
VMEM_LIMIT = 48 << 20

VM = pl.BlockSpec(memory_space=pltpu.VMEM)
SM = pl.BlockSpec(memory_space=pltpu.SMEM)
ANY = pl.BlockSpec(memory_space=pl.ANY)


def sds(shape, dtype):
    return jax.ShapeDtypeStruct(shape, dtype)


def kernel_call(body, ins, in_specs, outs, out_specs=None, scratch=(), flops=0):
    nbytes = sum(int(np.prod(a.shape)) * a.dtype.itemsize for a in list(ins) + list(outs))
    return pl.pallas_call(
        body,
        out_shape=list(outs),
        in_specs=list(in_specs),
        out_specs=[VM] * len(outs) if out_specs is None else list(out_specs),
        scratch_shapes=list(scratch),
        compiler_params=pltpu.CompilerParams(vmem_limit_bytes=VMEM_LIMIT),
        cost_estimate=pl.CostEstimate(flops=flops, bytes_accessed=nbytes, transcendentals=0),
    )(*ins)


def nn(a, b):
    return lax.dot_general(a, b, (((1,), (0,)), ((), ())), preferred_element_type=F32)


def nt(a, b):
    return lax.dot_general(a, b, (((1,), (1,)), ((), ())), preferred_element_type=F32)


def tn(a, b):
    return lax.dot_general(a, b, (((0,), (0,)), ((), ())), preferred_element_type=F32)


def normalise(v):
    mean = jnp.mean(v, -1, keepdims=True)
    cen = v - mean
    inv = lax.rsqrt(jnp.mean(cen * cen, -1, keepdims=True) + EPS)
    return cen * inv, inv


def norm_back(v, gain, dy):
    xhat, inv = normalise(v)
    dxh = dy * gain
    m1 = jnp.mean(dxh, -1, keepdims=True)
    m2 = jnp.mean(dxh * xhat, -1, keepdims=True)
    dx = inv * (dxh - m1 - xhat * m2)
    return dx, jnp.sum(dy * xhat, 0, keepdims=True), jnp.sum(dy, 0, keepdims=True)


def head_of_lane(rows):
    return lax.shift_right_logical(lax.broadcasted_iota(jnp.int32, (rows, DH), 1), 6)


def spread(q):
    head = head_of_lane(1)
    parts = [q * (head == h).astype(F32).astype(q.dtype) for h in range(HALF)]
    return jnp.concatenate(parts, 0)


def fold(o):
    head = head_of_lane(LEN)
    total = jnp.where(head == 0, o[:LEN], 0.0)
    for h in range(1, HALF):
        total = jnp.where(head == h, o[h * LEN : (h + 1) * LEN], total)
    return total


def attend(q, k, v, allowed):
    st = nt(k, spread(q)) * SCALE
    st = jnp.where(allowed, st, NEG)
    e = jnp.exp(st - jnp.max(st, 0, keepdims=True))
    p = (e * (1.0 / jnp.sum(e, 0, keepdims=True))).astype(BF)
    return p, fold(tn(p, v)).astype(BF)


def attend_back(g, q, k, v, p):
    gs, qs = spread(g), spread(q)
    dp = nt(v, gs)
    pf = p.astype(F32)
    t = pf * dp
    ds = (t - pf * jnp.sum(t, 0, keepdims=True)).astype(BF)
    dq = (fold(tn(ds, k)) * SCALE).astype(BF)
    dk = (nn(ds, qs) * SCALE).astype(BF)
    dv = nn(p, gs).astype(BF)
    return dq, dk, dv


def seq_rows(s):
    return pl.ds(pl.multiple_of(s * LEN, LEN), LEN)


def half_lanes(c):
    return pl.ds(pl.multiple_of(c * DH, DH), DH)


def loop(n, body, unroll=1):
    def step(i, carry):
        body(i)
        return carry

    lax.fori_loop(0, n, step, 0, unroll=unroll)


def assemble_kernel(cols, blk, offs_ref, *refs):
    n = len(cols)
    pieces, outs, sems = refs[:4], refs[4 : 4 + n], refs[4 + n]
    copies = []
    for q in range(4):
        for r in range(4):
            for o, (lo, hi, which) in enumerate(cols):
                row = pl.multiple_of(offs_ref[which, q * 4 + r] * blk, 16)
                copies.append(
                    pltpu.make_async_copy(
                        pieces[q].at[pl.ds(r * blk, blk), pl.ds(lo, hi - lo)],
                        outs[o].at[pl.ds(row, blk), :],
                        sems.at[(q * 4 + r) * n + o],
                    )
                )
    for cp in copies:
        cp.start()
    for cp in copies:
        cp.wait()


def assemble(pieces, offs, cols):
    blk = pieces[0].shape[0] // 4
    body = lambda *refs: assemble_kernel(cols, blk, *refs)
    outs = [sds((16 * blk, hi - lo), BF) for lo, hi, _ in cols]
    return kernel_call(
        body,
        [offs, *pieces],
        [SM] + [ANY] * 4,
        outs,
        [ANY] * len(outs),
        [pltpu.SemaphoreType.DMA((16 * len(cols),))],
    )


def send_out(dw, offs_ref, outs, sems, blk):
    copies = []
    for q in range(4):
        for r in range(4):
            row = pl.multiple_of(offs_ref[0, q * 4 + r] * blk, 16)
            copies.append(
                pltpu.make_async_copy(
                    dw.at[pl.ds(row, blk), :],
                    outs[q].at[pl.ds(r * blk, blk), :],
                    sems.at[q * 4 + r],
                )
            )
    for cp in copies:
        cp.start()
    for cp in copies:
        cp.wait()


def self_kernel(lens, core, tok, gcol, wqkv, wkeep, wrecv, first, packed, probs, mixed, partial, vec):
    c = core[0]
    vec[...] = jnp.transpose(gcol[...].astype(F32))[:8]
    gain, bias = vec[0:1], vec[3:4]

    def norm(s):
        xhat, _ = normalise(tok[seq_rows(s), :].astype(F32))
        first[seq_rows(s), :] = (xhat * gain + bias).astype(BF)

    loop(8, norm)

    def proj(b):
        rows = pl.ds(pl.multiple_of(b * 256, 256), 256)
        packed[rows, :] = nn(first[rows, :], wqkv[...]).astype(BF)

    loop(2, proj)
    key = lax.broadcasted_iota(jnp.int32, (LEN, DH), 0)
    query = lax.broadcasted_iota(jnp.int32, (LEN, DH), 1) & (LEN - 1)

    def att(s):
        allowed = (key <= query) & (key < lens[s])
        rows = seq_rows(s)
        p, m = attend(packed[rows, 0:DH], packed[rows, DH : 2 * DH], packed[rows, 2 * DH :], allowed)
        probs[s] = p
        mixed[rows, :] = m

    loop(8, att, 2)
    partial[:, half_lanes(c)] = nn(mixed[...], wkeep[...]).astype(BF)
    partial[:, half_lanes(1 - c)] = nn(mixed[...], wrecv[...]).astype(BF)


def kv_kernel(mem, wckv, kv):
    def step(b):
        rows = pl.ds(pl.multiple_of(b * 480, 480), 480)
        kv[rows, :] = nn(mem[rows, :], wckv[...]).astype(BF)

    loop(mem.shape[0] // 480, step)


def swapped(s):
    return pl.ds(pl.multiple_of(((s + 4) & 7) * LEN, LEN), LEN)


def cross_kernel(mem_len, core, tok, part, recv, vec, wcq, wkeep, wrecv, kv, resid, second, cq, probs, mixed, partial):
    c = core[0]
    gain, bias = vec[1:2], vec[4:5]

    def norm(s):
        rows = seq_rows(s)
        both = part[rows, :].astype(F32) + recv[swapped(s), :].astype(F32)
        v = tok[rows, :].astype(F32) + both
        resid[rows, :] = v
        xhat, _ = normalise(v)
        second[rows, :] = (xhat * gain + bias).astype(BF)

    loop(8, norm)
    cq[...] = nn(second[...], wcq[...]).astype(BF)
    pad = probs.shape[1]
    allowed = lax.broadcasted_iota(jnp.int32, (pad, DH), 0) < mem_len

    def att(s):
        rows = seq_rows(s)
        keys = pl.ds(pl.multiple_of(s * pad, 16), pad)
        p, m = attend(cq[rows, :], kv[keys, 0:DH], kv[keys, DH:], allowed)
        probs[s] = p
        mixed[rows, :] = m

    loop(8, att, 2)
    partial[:, half_lanes(c)] = nn(mixed[...], wkeep[...]).astype(BF)
    partial[:, half_lanes(1 - c)] = nn(mixed[...], wrecv[...]).astype(BF)


def inner_kernel(resid, part, recv, vec, win, resid_two, third, hidden, slope):
    gain, bias = vec[2:3], vec[5:6]

    def norm(s):
        rows = seq_rows(s)
        both = part[rows, :].astype(F32) + recv[swapped(s), :].astype(F32)
        v = resid[rows, :] + both
        resid_two[rows, :] = v
        xhat, _ = normalise(v)
        third[rows, :] = (xhat * gain + bias).astype(BF)

    loop(8, norm)
    width = win.shape[1]

    def step(b):
        rows = pl.ds(pl.multiple_of(b * 128, 128), 128)
        x = nn(third[rows, :], win[...])
        cdf = 0.5 + 0.5 * lax.erf(x * (0.5**0.5))
        hidden[rows, :] = (x * cdf).astype(BF)
        density = jnp.exp(x * x * -0.5) * ((2.0 * np.pi) ** -0.5)
        slope[rows, :] = (cdf + x * density).astype(BF)

    loop(4, step)


def mlp_kernel(hidden, slope, g, wout, win, partial, ginner, gthird):
    def step(b):
        rows = pl.ds(pl.multiple_of(b * 256, 256), 256)
        partial[rows, :] = nn(hidden[rows, :], wout[...]).astype(BF)
        gh = nt(g[rows, :], wout[...])
        ginner[rows, :] = (gh * slope[rows, :].astype(F32)).astype(BF)
        gthird[rows, :] = nt(ginner[rows, :], win[...]).astype(BF)

    loop(2, step)


def dmlpout_kernel(offs, hidden, g, *refs):
    outs, dw, sems = refs[:4], refs[4], refs[5]
    for b in range(0, dw.shape[0], 512):
        dw[b : b + 512, :] = tn(hidden[:, b : b + 512], g[...]).astype(BF)
    send_out(dw, offs, outs, sems, dw.shape[0] // 16)


def dmlpin_kernel(offs, third, ginner, *refs):
    outs, dw, sems = refs[:4], refs[4], refs[5]
    for b in range(0, dw.shape[0], 256):
        dw[b : b + 256, :] = tn(third[:, b : b + 256], ginner[...]).astype(BF)
    send_out(dw, offs, outs, sems, dw.shape[0] // 16)


def cross_back_kernel(
    core, resid, part, recv, g, vec, wcq, wkeep, wrecv, kv, cq, probs, gresid, gtwo, dcq, dkv, gsecond, dvec, gm
):
    c = core[0]
    gain = vec[2:3]
    dvec[...] = jnp.zeros_like(dvec)

    def norm(s):
        rows = seq_rows(s)
        dy = part[rows, :].astype(F32) + recv[swapped(s), :].astype(F32)
        dx, dg, db = norm_back(resid[rows, :], gain, dy)
        total = g[rows, :].astype(F32) + dx
        gresid[rows, :] = total
        gtwo[rows, :] = total.astype(BF)

        @pl.when(s < 4)
        def _():
            dvec[0:1, :] += dg
            dvec[1:2, :] += db

    loop(8, norm)
    gm[...] = (nt(gtwo[:, half_lanes(c)], wkeep[...]) + nt(gtwo[:, half_lanes(1 - c)], wrecv[...])).astype(BF)
    pad = probs.shape[1]

    def att(s):
        rows = seq_rows(s)
        keys = pl.ds(pl.multiple_of(s * pad, 16), pad)
        dq, dk, dv = attend_back(gm[rows, :], cq[rows, :], kv[keys, 0:DH], kv[keys, DH:], probs[s])
        dcq[rows, :] = dq
        dkv[keys, 0:DH] = dk
        dkv[keys, DH:] = dv

    loop(8, att, 2)
    gsecond[...] = nt(dcq[...], wcq[...]).astype(BF)


def out_grad(dw, lo, c, mine, other, g):
    cols = half_lanes(c)
    dw[half_lanes(c), lo : lo + DH] = tn(mine[...], g[:, cols]).astype(BF)
    rest = tn(other[256:, :], g[:256, cols]) + tn(other[:256, :], g[256:, cols])
    dw[half_lanes(1 - c), lo : lo + DH] = rest.astype(BF)


def dcross_kernel(offs, core, mixed, mixed_other, gtwo, second, dcq, mem, dkv, wckv, *refs):
    outs, gmem, dw, sems = refs[:4], refs[4], refs[5], refs[6]
    out_grad(dw, 0, core[0], mixed, mixed_other, gtwo)
    dw[:, DH : 2 * DH] = tn(second[...], dcq[...]).astype(BF)
    for b in range(0, D, 256):
        dw[b : b + 256, 2 * DH :] = tn(mem[:, b : b + 256], dkv[...]).astype(BF)

    def step(b):
        rows = pl.ds(pl.multiple_of(b * 480, 480), 480)
        gmem[rows, :] = nt(dkv[rows, :], wckv[...]).astype(BF)

    loop(mem.shape[0] // 480, step)
    send_out(dw, offs, outs, sems, D // 16)


def self_back_kernel(
    core, resid, part, recv, gresid_two, vec, wqkv, wkeep, wrecv, packed, probs, gresid, gone, dpacked, gfirst, dvec, gm
):
    c = core[0]
    gain = vec[1:2]
    dvec[...] = jnp.zeros_like(dvec)

    def norm(s):
        rows = seq_rows(s)
        dy = part[rows, :].astype(F32) + recv[swapped(s), :].astype(F32)
        dx, dg, db = norm_back(resid[rows, :], gain, dy)
        total = gresid_two[rows, :] + dx
        gresid[rows, :] = total
        gone[rows, :] = total.astype(BF)

        @pl.when(s < 4)
        def _():
            dvec[0:1, :] += dg
            dvec[1:2, :] += db

    loop(8, norm)
    gm[...] = (nt(gone[:, half_lanes(c)], wkeep[...]) + nt(gone[:, half_lanes(1 - c)], wrecv[...])).astype(BF)

    def att(s):
        rows = seq_rows(s)
        dq, dk, dv = attend_back(
            gm[rows, :], packed[rows, 0:DH], packed[rows, DH : 2 * DH], packed[rows, 2 * DH :], probs[s]
        )
        dpacked[rows, 0:DH] = dq
        dpacked[rows, DH : 2 * DH] = dk
        dpacked[rows, 2 * DH :] = dv

    loop(8, att, 2)
    gfirst[...] = nt(dpacked[...], wqkv[...]).astype(BF)


def dself_kernel(offs, core, mixed, mixed_other, gone, first, dpacked, *refs):
    outs, dw, sems = refs[:4], refs[4], refs[5]
    out_grad(dw, 0, core[0], mixed, mixed_other, gone)
    for b in range(0, D, 256):
        dw[b : b + 256, DH:] = tn(first[:, b : b + 256], dpacked[...]).astype(BF)
    send_out(dw, offs, outs, sems, D // 16)


def tokens_back_kernel(tok, part, recv, gresid, vec, gtok, dvec):
    gain = vec[0:1]
    dvec[...] = jnp.zeros_like(dvec)

    def norm(s):
        rows = seq_rows(s)
        dy = part[rows, :].astype(F32) + recv[rows, :].astype(F32)
        dx, dg, db = norm_back(tok[rows, :].astype(F32), gain, dy)
        gtok[rows, :] = (gresid[rows, :] + dx).astype(BF)
        dvec[0:1, :] += dg
        dvec[1:2, :] += db

    loop(4, norm)


class Moves:
    def __init__(self, mesh):
        self.nz, self.nf = mesh.shape["dp"], mesh.shape["fsdp"]
        self.n = self.nz * self.nf
        self.doubling = self.nz == 4 and self.nf == 8

    def permute(self, x, target):
        pairs = [(d, target(d // self.nf, (d % self.nf) // 2, d % 2)) for d in range(self.n)]
        return lax.ppermute(x, AXES, [(a, (z * self.nf) + 2 * yx + c) for a, (z, yx, c) in pairs])

    def sibling(self, x):
        return self.permute(x, lambda z, yx, c: (z, yx, 1 - c))

    def near_z(self, x):
        return self.permute(x, lambda z, yx, c: (z ^ 1, yx, c))

    def far_z(self, x):
        return self.permute(x, lambda z, yx, c: (z ^ 2, yx, c))

    def side_a(self, x):
        return self.permute(x, lambda z, yx, c: (z, yx ^ (1 + c), c))

    def side_b(self, x):
        return self.permute(x, lambda z, yx, c: (z, yx ^ (2 - c), c))

    def gather(self, piece):
        two = jnp.concatenate([piece, self.near_z(piece)], 0)
        four = jnp.concatenate([two, self.far_z(two)], 0)
        a = self.side_a(four)
        b = self.side_b(four)
        return [four, a, b, self.side_b(a)]

    def scatter(self, parts):
        own, a, b, ab = parts
        blk = own.shape[0] // 4
        got_ab = self.side_a(ab)
        got_a = self.side_a(a)
        got_b = self.side_b(b + got_ab)
        total = own.astype(F32) + got_a.astype(F32) + got_b.astype(F32)
        got = self.far_z(total[2 * blk :].astype(BF))
        total = total[: 2 * blk] + got.astype(F32)
        got = self.near_z(total[blk:].astype(BF))
        return total[:blk] + got.astype(F32)


def per_device(moves, tokens, memory, lengths, cotangent, self_qkv, self_out, cross_q, cross_kv, cross_out, mlp_in, mlp_out, norm_gains, norm_biases):
    seqs, mem_len = memory.shape[0], memory.shape[1]
    rows = seqs * LEN
    place = lax.axis_index(AXES)
    c = place % 2
    chip = place // 2
    core = jnp.reshape(c, (1,)).astype(jnp.int32)
    wr, hr = self_qkv.shape[0], mlp_out.shape[0]
    ff = mlp_in.shape[1]
    fh = ff // 2

    pad = -(-mem_len // 16) * 16
    live = jnp.arange(LEN, dtype=jnp.int32)[None, :] < lengths[:, None]
    g_own = jnp.where(live[..., None], cotangent, jnp.zeros_like(cotangent)).reshape(rows, D)
    tok_own = tokens.reshape(rows, D)
    mem_own = jnp.pad(memory, ((0, 0), (0, pad - mem_len), (0, 0))).reshape(seqs * pad, D)

    def pair_up(x):
        return jnp.concatenate([x, moves.sibling(x)], 0)

    def col_half(w, groups, which):
        w = w.reshape(w.shape[0], groups, 2, w.shape[1] // (2 * groups))
        return lax.dynamic_index_in_dim(w, which, 2, keepdims=False).reshape(w.shape[0], -1)

    vectors = jnp.concatenate([norm_gains, norm_biases], 0).T
    vectors = jnp.pad(vectors, ((0, 0), (0, 128 - vectors.shape[1])))

    def halves(which):
        one = jnp.concatenate([col_half(self_qkv, 3, which), col_half(self_out, 1, which), vectors], 1)
        two = jnp.concatenate(
            [col_half(cross_out, 1, which), col_half(cross_q, 1, which), col_half(cross_kv, 2, which)], 1
        )
        three = col_half(mlp_in, ff // (2 * hr), which)
        return one, two, three

    if moves.doubling:
        keep, send = halves(c), halves(1 - c)

        def chip_rows(mine, other):
            got = moves.sibling(other)
            return jnp.where(c == 0, jnp.concatenate([mine, got], 0), jnp.concatenate([got, mine], 0))

        bits = jnp.arange(4, dtype=jnp.int32)
        plane = jnp.stack([jnp.int32(0), 1 + c, 2 - c, jnp.int32(3)]).astype(jnp.int32)
        z, yx = chip // 4, chip % 4
        chips = ((z ^ bits)[None, :] * 4 + (yx ^ plane)[:, None]).reshape(16).astype(jnp.int32)
        gathered = [moves.gather(chip_rows(m, o)) for m, o in zip(keep, send)]
        gathered.append(moves.gather(mlp_out))
    else:
        chips = jnp.arange(16, dtype=jnp.int32)
        whole = lambda w: lax.all_gather(w, AXES, axis=0, tiled=True)
        split = lambda w: [w[i * w.shape[0] // 4 : (i + 1) * w.shape[0] // 4] for i in range(4)]
        rowed = whole(mlp_out).reshape(moves.n // 2, 2, hr, D)
        gathered = [split(whole(w)) for w in halves(c)]
        gathered.append(split(lax.dynamic_index_in_dim(rowed, c, 1, keepdims=False).reshape(fh, D)))
    turned = ((chips // 8) ^ c) * 8 + chips % 8
    offs = jnp.stack([chips, turned]).astype(jnp.int32)

    tok = pair_up(tok_own)
    lens = pair_up(lengths)
    g = pair_up(g_own)
    mem = pair_up(mem_own)

    w_qkv, w_out, g_col = assemble(gathered[0], offs, [(0, 3 * DH, 0), (3 * DH, 4 * DH, 1), (4 * DH, 4 * DH + 128, 0)])
    out_keep, out_recv = w_out[:DH], moves.sibling(w_out[DH:])
    w_cout, w_cq, w_ckv = assemble(gathered[1], offs, [(0, DH, 1), (DH, 2 * DH, 0), (2 * DH, 4 * DH, 0)])
    cout_keep, cout_recv = w_cout[:DH], moves.sibling(w_cout[DH:])
    (w_in,) = assemble(gathered[2], offs, [(0, fh, 0)])
    (w_mlpout,) = assemble(gathered[3], offs, [(0, D, 0)])

    r2 = 2 * rows
    s2 = 2 * seqs
    flops = lambda m, k, n: 2 * m * k * n
    first, packed, probs, mixed, part, vec = kernel_call(
        self_kernel,
        [lens, core, tok, g_col, w_qkv, out_keep, out_recv],
        [SM, SM] + [VM] * 5,
        [
            sds((r2, D), BF),
            sds((r2, 3 * DH), BF),
            sds((s2, LEN, DH), BF),
            sds((r2, DH), BF),
            sds((r2, D), BF),
            sds((8, D), F32),
        ],
        flops=flops(r2, D, 4 * DH),
    )
    recv = moves.sibling(part)
    mixed_other = moves.sibling(mixed)
    (kv,) = kernel_call(kv_kernel, [mem, w_ckv], [VM, VM], [sds(mem.shape, BF)], flops=flops(mem.shape[0], D, D))
    resid_one, second, cq, cprobs, cmixed, part = kernel_call(
        lambda *refs: cross_kernel(mem_len, *refs),
        [core, tok, part, recv, vec, w_cq, cout_keep, cout_recv, kv],
        [SM] + [VM] * 8,
        [
            sds((r2, D), F32),
            sds((r2, D), BF),
            sds((r2, DH), BF),
            sds((s2, pad, DH), BF),
            sds((r2, DH), BF),
            sds((r2, D), BF),
        ],
        flops=flops(r2, D, 3 * DH),
    )
    recv = moves.sibling(part)
    cmixed_other = moves.sibling(cmixed)
    resid_two, third, hidden, slope = kernel_call(
        inner_kernel,
        [resid_one, part, recv, vec, w_in],
        [VM] * 5,
        [sds((r2, D), F32), sds((r2, D), BF), sds((r2, fh), BF), sds((r2, fh), BF)],
        flops=flops(r2, D, fh),
    )

    def grads(body, ins, specs, nrows, ncols, extra=(), cost=0):
        blk = nrows // 16
        return kernel_call(
            body,
            [offs, *ins],
            [SM, *specs],
            [sds((4 * blk, ncols), BF)] * 4 + list(extra),
            [ANY] * 4 + [VM] * len(extra),
            [pltpu.VMEM((nrows, ncols), BF), pltpu.SemaphoreType.DMA((16,))],
            flops=cost,
        )

    d_mlpout = grads(dmlpout_kernel, [hidden, g], [VM] * 2, fh, D, cost=flops(r2, D, fh))
    part, ginner, gthird = kernel_call(
        mlp_kernel,
        [hidden, slope, g, w_mlpout, w_in],
        [VM] * 5,
        [sds((r2, D), BF), sds((r2, fh), BF), sds((r2, D), BF)],
        flops=3 * flops(r2, D, fh),
    )
    recv = moves.sibling(gthird)
    got = moves.sibling(part[rows:])
    output = (resid_two[:rows] + (part[:rows].astype(F32) + got.astype(F32))).astype(BF)
    d_mlpin = grads(dmlpin_kernel, [third, ginner], [VM] * 2, D, fh, cost=flops(r2, D, fh))
    gresid_two, gtwo, dcq, dkv, gsecond, dvec_two = kernel_call(
        cross_back_kernel,
        [core, resid_two, gthird, recv, g, vec, w_cq, cout_keep, cout_recv, kv, cq, cprobs],
        [SM] + [VM] * 11,
        [
            sds((r2, D), F32),
            sds((r2, D), BF),
            sds((r2, DH), BF),
            sds(kv.shape, BF),
            sds((r2, D), BF),
            sds((8, D), F32),
        ],
        scratch=[pltpu.VMEM((r2, DH), BF)],
        flops=flops(r2, D, 3 * DH),
    )
    recv = moves.sibling(gsecond)
    *d_cross, gmem = grads(
        dcross_kernel,
        [core, cmixed, cmixed_other, gtwo, second, dcq, mem, dkv, w_ckv],
        [SM] + [VM] * 8,
        D,
        4 * DH,
        [sds(mem.shape, BF)],
        cost=2 * flops(mem.shape[0], D, D),
    )
    half = seqs * pad
    got = moves.sibling(gmem[half:])
    grad_memory = (gmem[:half].astype(F32) + got.astype(F32)).astype(BF)
    grad_memory = grad_memory.reshape(seqs, pad, D)[:, :mem_len]
    gresid_one, gone, dpacked, gfirst, dvec_one = kernel_call(
        self_back_kernel,
        [core, resid_one, gsecond, recv, gresid_two, vec, w_qkv, out_keep, out_recv, packed, probs],
        [SM] + [VM] * 10,
        [
            sds((r2, D), F32),
            sds((r2, D), BF),
            sds((r2, 3 * DH), BF),
            sds((r2, D), BF),
            sds((8, D), F32),
        ],
        scratch=[pltpu.VMEM((r2, DH), BF)],
        flops=flops(r2, D, 4 * DH),
    )
    recv = moves.sibling(gfirst[rows:])
    d_self = grads(
        dself_kernel,
        [core, mixed, mixed_other, gone, first, dpacked],
        [SM] + [VM] * 5,
        D,
        4 * DH,
        cost=flops(r2, D, 4 * DH),
    )
    grad_tokens, dvec_zero = kernel_call(
        tokens_back_kernel,
        [tok_own, gfirst[:rows], recv, gresid_one[:rows], vec],
        [VM] * 5,
        [sds((rows, D), BF), sds((8, D), F32)],
    )
    dvec = jnp.concatenate(
        [dvec_zero[0:1], dvec_one[0:1], dvec_two[0:1], dvec_zero[1:2], dvec_one[1:2], dvec_two[1:2]], 0
    )

    if moves.doubling:
        sum_mlpout = moves.scatter(d_mlpout)

        def own_rows(parts):
            total = moves.scatter(parts)
            mine = lax.dynamic_slice_in_dim(total, c * wr, wr, 0)
            got = moves.sibling(lax.dynamic_slice_in_dim(total, (1 - c) * wr, wr, 0))
            return jnp.where(c == 0, mine, got), jnp.where(c == 0, got, mine)

        in_halves, cross_halves, self_halves = own_rows(d_mlpin), own_rows(d_cross), own_rows(d_self)
        for step in (moves.sibling, moves.near_z, moves.far_z, moves.side_a, moves.side_b):
            dvec = dvec + step(dvec)
    else:

        def placed(parts):
            term = jnp.concatenate(parts, 0).astype(F32)
            both = jnp.stack([jnp.where(c == 0, term, 0.0), jnp.where(c == 1, term, 0.0)], 1)
            total = lax.psum_scatter(both, AXES, scatter_dimension=0, tiled=True)
            return total[:, 0], total[:, 1]

        in_halves, cross_halves, self_halves = placed(d_mlpin), placed(d_cross), placed(d_self)
        term = jnp.concatenate(d_mlpout, 0).astype(F32).reshape(moves.n // 2, 1, hr, D)
        both = jnp.concatenate([jnp.where(c == 0, term, 0.0), jnp.where(c == 1, term, 0.0)], 1)
        sum_mlpout = lax.psum_scatter(both.reshape(ff, D), AXES, scatter_dimension=0, tiled=True)
        dvec = lax.psum(dvec, AXES)

    def join(pair, lo, hi, groups):
        parts = [p[:, lo:hi].reshape(wr, groups, 1, (hi - lo) // groups) for p in pair]
        return jnp.concatenate(parts, 2).reshape(wr, 2 * (hi - lo))

    own_vec = lax.dynamic_slice_in_dim(dvec, place * wr, wr, 1)
    return (
        output.reshape(tokens.shape),
        grad_tokens.reshape(tokens.shape),
        grad_memory,
        join(self_halves, DH, 4 * DH, 3),
        join(self_halves, 0, DH, 1),
        join(cross_halves, DH, 2 * DH, 1),
        join(cross_halves, 2 * DH, 4 * DH, 2),
        join(cross_halves, 0, DH, 1),
        join(in_halves, 0, fh, ff // (2 * hr)),
        sum_mlpout,
        own_vec[:3],
        own_vec[3:],
    )


def solution(mesh):
    batch = P(AXES, None, None)
    rows = P(AXES, None)
    cols = P(None, AXES)
    moves = Moves(mesh)
    in_specs = (batch, batch, P(AXES), batch) + (rows,) * 7 + (cols,) * 2
    out_specs = (batch,) * 3 + (rows,) * 7 + (cols,) * 2
    return jax.shard_map(
        lambda *args: per_device(moves, *args),
        mesh=mesh,
        in_specs=in_specs,
        out_specs=out_specs,
        check_vma=False,
    )
```

time: 1160 us -> 382 us (0.33)
  waiting for transfers between devices: 827 us -> 143 us
  Pallas kernels: 0 us -> 113 us
  matrix products: 111 us -> 0 us
  blocking collectives: 80.4 us -> 0 us
  local copies, waits for them, and re-layouts: 91.4 us -> 39.7 us
  starting transfers between devices: 0.34 us -> 49.8 us
  between operations: 14.8 us -> 2.48 us
    unnamed x10 -> x0, waiting for transfers between devices: 418 us -> none
    all_gather x7 -> x0, waiting for transfers between devices: 276 us -> none  [the longest x1 61.2 us: per_device(): lax.all_gather(mlp_in, ('dp', 'fsdp'), axis=0, tiled=True)]
    ppermute x0 -> x66, waiting for transfers between devices: none -> 143 us  [permute(): lax.ppermute(x, AXES, [(a, z * self.nf + 2 * yx + c) for a, (z, yx, c) in...]
    reduce_scatter x1 -> x0, waiting for transfers between devices: 133 us -> none  [per_device(): lax.psum_scatter(term_of([(saved['hidden'], grad_three)], [], lax.axis_si...]
    pallas_call x0 -> x16, Pallas kernels: none -> 113 us  [kernel_call(): pl.pallas_call(body, out_shape=list(outs), in_specs=list(in_specs), out_s...]
    dot_general x31 -> x0, matrix products: 106 us -> none  [the longest x7 29.6 us: weight_grad(): jnp.einsum('bld,ble->de', values, grad, preferred_element_type=jnp.float32)]
    all_gather x2 -> x0, blocking collectives: 80.4 us -> none  [the longest x1 43.5 us: per_device(): lax.all_gather(norm_biases, ('dp', 'fsdp'), axis=1, tiled=True)]
    ppermute x0 -> x66, starting transfers between devices: none -> 49.8 us  [permute(): lax.ppermute(x, AXES, [(a, z * self.nf + 2 * yx + c) for a, (z, yx, c) in...]
  transfers between devices with their start and end apart: 9 -> 66, of which waited for: 8 -> 25; matrix products, arithmetic and copies ran while one was open for 7% -> 14% of each run, Pallas kernels for 0% -> 26%
where the time goes in v1:
time: 382 us; the launch traced here: 376 us
  waiting for transfers between devices  143 us (37%)
  Pallas kernels  113 us (30%)
  starting transfers between devices  49.8 us (13%)
  local copies, waits for them, and re-layouts  39.7 us (10%)
  other arithmetic  27.5 us (7%)
    ppermute x66, waiting for transfers between devices, permute(): lax.ppermute(x, AXES, [(a, z * self.nf + 2 * yx + c) for a, (z, yx, c) in...  143 us
    pallas_call x16, Pallas kernels, kernel_call(): pl.pallas_call(body, out_shape=list(outs), in_specs=list(in_specs), out_s...  113 us
    ppermute x66, starting transfers between devices, permute(): lax.ppermute(x, AXES, [(a, z * self.nf + 2 * yx + c) for a, (z, yx, c) in...  49.8 us
    unnamed x125, local copies, waits for them, and re-layouts  17.1 us
  transfers between devices with their start and end apart: 66, of which 25 were waited for; matrix products, arithmetic and copies ran while one was open for 14% of the time, Pallas kernels for 26%

profile of v1, /device:TPU:0, one launch (start us, length us, event | category | flops | bytes accessed | tf_op | source)
XLA Modules:
  0.0 376.1 jit_solution(16314130499670940319)
XLA Ops:
  7.6 3.0 collective-permute-start.26
  11.1 7.0 %collective-permute-done.3 = bf16[48,1664]{1,0:T(8,128)(2,1)S(1)} collective-permute-done((bf16[48,1664]{1,0:T(8,128)(2,1)S(1)}, bf16[48,1664]{1,0:T(8,128)(2,1)S(1)}, u32[]{:S(2)}, u32[]{:S(2)}) %collective-permute-start.3) | collective-permute-done | bytes 159776 | tf_op jit(solution)/shard_map/ppermute | solution.py:427
  18.2 2.8 collective-permute-start.4
  21.9 13.1 %collective-permute-done.4 = bf16[96,1664]{1,0:T(8,128)(2,1)S(1)} collective-permute-done((bf16[96,1664]{1,0:T(8,128)(2,1)S(1)}, bf16[96,1664]{1,0:T(8,128)(2,1)S(1)}, u32[]{:S(2)}, u32[]{:S(2)}) %collective-permute-start.4) | collective-permute-done | bytes 319520 | tf_op jit(solution)/shard_map/ppermute | solution.py:427
  43.2 2.7 collective-permute-done.11
  45.9 2.8 collective-permute-start.12
  51.8 9.6 %collective-permute-done.12 = bf16[96,1536]{1,0:T(8,128)(2,1)S(1)} collective-permute-done((bf16[96,1536]{1,0:T(8,128)(2,1)S(1)}, bf16[96,1536]{1,0:T(8,128)(2,1)S(1)}, u32[]{:S(2)}, u32[]{:S(2)}) %collective-permute-start.12) | collective-permute-done | bytes 294944 | tf_op jit(solution)/shard_map/ppermute | solution.py:427
  61.4 2.4 collective-permute-start.13
  65.5 3.1 collective-permute-done.7.refs_4_
  69.6 2.0 shard_map.220
  71.8 2.1 collective-permute-start.21
  73.9 15.8 %collective-permute-done.27 = bf16[192,768]{1,0:T(8,128)(2,1)S(1)} collective-permute-done((bf16[192,768]{1,0:T(8,128)(2,1)S(1)}, bf16[192,768]{1,0:T(8,128)(2,1)S(1)}, u32[]{:S(2)}, u32[]{:S(2)}) %collective-permute-start.27) | collective-permute-done | bytes 294944 | tf_op jit(solution)/shard_map/ppermute | solution.py:427
  89.7 2.0 collective-permute-start.15
  92.9 9.0 %shard_map.221 = (bf16[512,768]{1,0:T(8,128)(2,1)S(1)}, bf16[512,1152]{1,0:T(8,128)(2,1)S(1)}, bf16[8,64,384]{2,1,0:T(8,128)(2,1)S(1)}, bf16[512,384]{1,0:T(8,12...) custom-call(s32[8]{0:T(128)S(1)} %pad_add_fusion.1.lens, s32[1]{0:T(128)} %bitcast.core.refs_0_, ...), custom_call_target="tpu_custom_call" | custom-call | flops 1207959552 | bytes 6905892 | tf_op jit(solution)/shard_map/pallas_call | solution.py:34
  103.3 1.9 collective-permute-start.28
  105.9 1.8 collective-permute-start.22
  109.7 3.4 pad_maximum_fusion.mem
  113.1 4.8 %shard_map.223.refs_8_.kv = bf16[1920,768]{1,0:T(8,128)(2,1)S(1)} custom-call(bf16[1920,768]{1,0:T(8,128)(2,1)} %pad_maximum_fusion.mem, bf16[768,768]{1,0:T(8,128)(2,1)S(1)} %get-tuple-element.74.wckv), custom_call_target="tpu_custom_call" | custom-call | flops 2264924160 | bytes 7077888 | tf_op jit(solution)/shard_map/pallas_call | solution.py:34
  119.6 11.1 %shard_map.224 = (f32[512,768]{1,0:T(8,128)}, bf16[512,768]{1,0:T(8,128)(2,1)S(1)}, bf16[512,384]{1,0:T(8,128)(2,1)S(1)}, bf16[8,240,384]{2,1,0:T(8,128)(2,1)}, ...) custom-call(s32[1]{0:T(128)} %bitcast.core.refs_0_, bf16[512,768]{1,0:T(8,128)(2,1)S(1)} %pad_maximum_fusion.1.tok.refs_1_, ...), custom_call_target="tpu_custom_call" | custom-call | flops 905969664 | bytes 11919364 | tf_op jit(solution)/shard_map/pallas_call | solution.py:34
  135.8 5.8 %collective-permute-done.29.refs_3_ = bf16[384,768]{1,0:T(8,128)(2,1)S(1)} collective-permute-done((bf16[384,768]{1,0:T(8,128)(2,1)S(1)}, bf16[384,768]{1,0:T(8,128)(2,1)S(1)}, u32[]{:S(2)}, u32[]{:S(2)}) %collective-permute-start.29) | collective-permute-done | bytes 589856 | tf_op jit(solution)/shard_map/ppermute | solution.py:427
  141.6 6.3 %collective-permute-done.30.refs_4_ = bf16[384,768]{1,0:T(8,128)(2,1)S(1)} collective-permute-done((bf16[384,768]{1,0:T(8,128)(2,1)S(1)}, bf16[384,768]{1,0:T(8,128)(2,1)S(1)}, u32[]{:S(2)}, u32[]{:S(2)}) %collective-permute-start.30) | collective-permute-done | bytes 589856 | tf_op jit(solution)/shard_map/ppermute | solution.py:427
  147.9 4.3 %shard_map.227.wout = bf16[1536,768]{1,0:T(8,128)(2,1)S(1)} custom-call(s32[2,16]{1,0:T(2,128)S(1)} %pad_add_fusion.refs_0_.offs, bf16[384,768]{1,0:T(8,128)(2,1)S(1)} %constant_dynamic-update-slice_fusion.refs_1_, bf16[384,768]{1,0:T(8,128)(2,1)S(1)} %collective-permute-done.28.refs_2_, bf16[384,768]{1,0:T(8,128)(2,1)S(1)} %collective-permute-done.29.refs_3_, ...), custom_call_target="tpu_custom_call" | custom-call | bytes 4718720 | tf_op jit(solution)/shard_map/pallas_call | solution.py:34
  154.2 6.3 %collective-permute-done.24.refs_4_ = bf16[192,1536]{1,0:T(8,128)(2,1)S(1)} collective-permute-done((bf16[192,1536]{1,0:T(8,128)(2,1)S(1)}, bf16[192,1536]{1,0:T(8,128)(2,1)S(1)}, u32[]{:S(2)}, u32[]{:S(2)}) %collective-permute-start.24) | collective-permute-done | bytes 589856 | tf_op jit(solution)/shard_map/ppermute | solution.py:427
  160.5 4.3 %shard_map.225.win = bf16[768,1536]{1,0:T(8,128)(2,1)S(1)} custom-call(s32[2,16]{1,0:T(2,128)S(1)} %pad_add_fusion.refs_0_.offs, bf16[192,1536]{1,0:T(8,128)(2,1)S(1)} %pad_maximum_fusion.5.refs_1_, bf16[192,1536]{1,0:T(8,128)(2,1)S(1)} %collective-permute-done.22.refs_2_, bf16[192,1536]{1,0:T(8,128)(2,1)S(1)} %collective-permute-done.23.refs_3_, ...), custom_call_target="tpu_custom_call" | custom-call | bytes 4718720 | tf_op jit(solution)/shard_map/pallas_call | solution.py:34
  166.3 7.4 %shard_map.226 = (f32[512,768]{1,0:T(8,128)S(1)}, bf16[512,768]{1,0:T(8,128)(2,1)S(1)}, bf16[512,1536]{1,0:T(8,128)(2,1)S(1)}, bf16[512,1536]{1,0:T(8,128)(2,1)}) custom-call(f32[512,768]{1,0:T(8,128)} %get-tuple-element.75.resid, bf16[512,768]{1,0:T(8,128)(2,1)S(1)} %get-tuple-element.76.part, bf16[512,768]{1,0:T(8,128)(2,1)S(1)} %collective-permute-done.18.recv, ...), custom_call_target="tpu_custom_call" | custom-call | flops 1207959552 | bytes 11034624 | tf_op jit(solution)/shard_map/pallas_call | solution.py:34
  173.7 8.6 %shard_map.228 = (bf16[512,768]{1,0:T(8,128)(2,1)}, bf16[512,1536]{1,0:T(8,128)(2,1)S(1)}, bf16[512,768]{1,0:T(8,128)(2,1)}) custom-call(bf16[512,1536]{1,0:T(8,128)(2,1)S(1)} %get-tuple-element.78.hidden, bf16[512,1536]{1,0:T(8,128)(2,1)} %get-tuple-element.79.slope, bf16[512,768]{1,0:T(8,128)(2,1)S(1)} %pad_maximum_fusion.2.g, ...), custom_call_target="tpu_custom_call" | custom-call | flops 3623878656 | bytes 11796480 | tf_op jit(solution)/shard_map/pallas_call | solution.py:34
  184.6 5.5 %shard_map.234 = (bf16[192,1536]{1,0:T(8,128)(2,1)S(1)}, bf16[192,1536]{1,0:T(8,128)(2,1)S(1)}, bf16[192,1536]{1,0:T(8,128)(2,1)S(1)}, bf16[192,1536]{1,0:T(8,128)(2,1)}) custom-call(s32[2,16]{1,0:T(2,128)S(1)} %pad_add_fusion.refs_0_.offs, bf16[512,768]{1,0:T(8,128)(2,1)S(1)} %get-tuple-element.109.third, bf16[512,1536]{1,0:T(8,128)(2,1)S(1)} %get-tuple-element.110.ginner), custom_call_target="tpu_custom_call" | custom-call | flops 1207959552 | bytes 4718720 | tf_op jit(solution)/shard_map/pallas_call | solution.py:34
  192.0 5.3 %shard_map.235 = (bf16[384,768]{1,0:T(8,128)(2,1)S(1)}, bf16[384,768]{1,0:T(8,128)(2,1)S(1)}, bf16[384,768]{1,0:T(8,128)(2,1)S(1)}, bf16[384,768]{1,0:T(8,128)(2,1)}) custom-call(s32[2,16]{1,0:T(2,128)S(1)} %pad_add_fusion.refs_0_.offs, bf16[512,1536]{1,0:T(8,128)(2,1)S(1)} %get-tuple-element.78.hidden, bf16[512,768]{1,0:T(8,128)(2,1)S(1)} %pad_maximum_fusion.2.g), custom_call_target="tpu_custom_call" | custom-call | flops 1207959552 | bytes 4718720 | tf_op jit(solution)/shard_map/pallas_call | solution.py:34
  199.8 1.8 collective-permute-start.57
  202.1 2.1 add_convert_fusion.1
  205.7 4.3 %collective-permute-done.57 = bf16[384,768]{1,0:T(8,128)(2,1)} collective-permute-done((bf16[384,768]{1,0:T(8,128)(2,1)}, bf16[384,768]{1,0:T(8,128)(2,1)}, u32[]{:S(2)}, u32[]{:S(2)}) %collective-permute-start.57) | collective-permute-done | bytes 589856 | tf_op jit(solution)/shard_map/ppermute | solution.py:427
  210.0 1.8 collective-permute-start.56
  213.5 14.8 %shard_map.229 = (f32[512,768]{1,0:T(8,128)}, bf16[512,768]{1,0:T(8,128)(2,1)S(1)}, bf16[512,384]{1,0:T(8,128)(2,1)S(1)}, bf16[1920,768]{1,0:T(8,128)(2,1)}, bf1...) custom-call(s32[1]{0:T(128)} %bitcast.core.refs_0_, f32[512,768]{1,0:T(8,128)} %copy-done.2, ...), custom_call_target="tpu_custom_call" | custom-call | flops 905969664 | bytes 16465924 | tf_op jit(solution)/shard_map/pallas_call | solution.py:34
  229.9 15.3 %shard_map.232 = (bf16[192,1536]{1,0:T(8,128)(2,1)S(1)}, bf16[192,1536]{1,0:T(8,128)(2,1)S(1)}, bf16[192,1536]{1,0:T(8,128)(2,1)S(1)}, bf16[192,1536]{1,0:T(8,128)(2,1)S(1)}, bf16[1920,768]{1,0:T(8,128)(2,1)}) custom-call(s32[2,16]{1,0:T(2,128)S(1)} %pad_add_fusion.refs_0_.offs, s32[1]{0:T(128)} %bitcast.core.refs_0_, ...), custom_call_target="tpu_custom_call" | custom-call | flops 4529848320 | bytes 15138948 | tf_op jit(solution)/shard_map/pallas_call | solution.py:34
  245.1 2.7 slice.160
  249.5 8.3 %collective-permute-done.45 = bf16[192,1536]{1,0:T(8,128)(2,1)S(1)} collective-permute-done((bf16[192,1536]{1,0:T(8,128)(2,1)S(1)}, bf16[192,1536]{1,0:T(8,128)(2,1)S(1)}, u32[]{:S(2)}, u32[]{:S(2)}) %collective-permute-start.45) | collective-permute-done | bytes 589856 | tf_op jit(solution)/shard_map/ppermute | solution.py:427
  259.0 5.5 %collective-permute-done.53 = bf16[96,1536]{1,0:T(8,128)(2,1)S(1)} collective-permute-done((bf16[96,1536]{1,0:T(8,128)(2,1)S(1)}, bf16[96,1536]{1,0:T(8,128)(2,1)S(1)}, u32[]{:S(2)}, u32[]{:S(2)}) %collective-permute-start.53) | collective-permute-done | bytes 294944 | tf_op jit(solution)/shard_map/ppermute | solution.py:427
  264.6 15.3 %collective-permute-done.59 = bf16[192,768]{1,0:T(8,128)(2,1)S(1)} collective-permute-done((bf16[192,768]{1,0:T(8,128)(2,1)S(1)}, bf16[192,768]{1,0:T(8,128)(2,1)S(1)}, u32[]{:S(2)}, u32[]{:S(2)}) %collective-permute-start.59) | collective-permute-done | bytes 294944 | tf_op jit(solution)/shard_map/ppermute | solution.py:427
  282.1 11.6 %shard_map.230 = (f32[512,768]{1,0:T(8,128)}, bf16[512,768]{1,0:T(8,128)(2,1)S(1)}, bf16[512,1152]{1,0:T(8,128)(2,1)S(1)}, bf16[512,768]{1,0:T(8,128)(2,1)S(1)}, f32[8,768]{1,0:T(8,128)S(1)}) custom-call(s32[1]{0:T(128)} %bitcast.core.refs_0_, f32[512,768]{1,0:T(8,128)} %get-tuple-element.75.resid, bf16[512,768]{1,0:T(8,128)(2,1)S(1)} %get-tuple-element.84.part, ...), custom_call_target="tpu_custom_call" | custom-call | flops 1207959552 | bytes 13025284 | tf_op jit(solution)/shard_map/pallas_call | solution.py:34
  295.1 2.1 collective-permute-start.60
  297.2 5.6 %shard_map.233 = (bf16[192,1536]{1,0:T(8,128)(2,1)S(1)}, bf16[192,1536]{1,0:T(8,128)(2,1)S(1)}, bf16[192,1536]{1,0:T(8,128)(2,1)S(1)}, bf16[192,1536]{1,0:T(8,128)(2,1)S(1)}) custom-call(s32[2,16]{1,0:T(2,128)S(1)} %pad_add_fusion.refs_0_.offs, s32[1]{0:T(128)} %bitcast.core.refs_0_, bf16[512,384]{1,0:T(8,128)(2,1)S(1)} %copy-done.37, ...), custom_call_target="tpu_custom_call" | custom-call | flops 1207959552 | bytes 5898372 | tf_op jit(solution)/shard_map/pallas_call | solution.py:34
  304.6 2.0 shard_map.231
  310.7 2.0 collective-permute-done.62
  323.6 2.2 reshape.375
  334.6 8.4 %collective-permute-done.47 = bf16[96,1536]{1,0:T(8,128)(2,1)S(1)} collective-permute-done((bf16[96,1536]{1,0:T(8,128)(2,1)S(1)}, bf16[96,1536]{1,0:T(8,128)(2,1)S(1)}, u32[]{:S(2)}, u32[]{:S(2)}) %collective-permute-start.47) | collective-permute-done | bytes 294944 | tf_op jit(solution)/shard_map/ppermute | solution.py:427
  343.1 1.8 add_convert_fusion
  349.9 15.3 %collective-permute-done.41 = bf16[96,1536]{1,0:T(8,128)(2,1)S(1)} collective-permute-done((bf16[96,1536]{1,0:T(8,128)(2,1)S(1)}, bf16[96,1536]{1,0:T(8,128)(2,1)S(1)}, u32[]{:S(2)}, u32[]{:S(2)}) %collective-permute-start.41) | collective-permute-done | bytes 294944 | tf_op jit(solution)/shard_map/ppermute | solution.py:427
  365.6 5.6 %collective-permute-done.42 = bf16[48,1536]{1,0:T(8,128)(2,1)S(1)} collective-permute-done((bf16[48,1536]{1,0:T(8,128)(2,1)S(1)}, bf16[48,1536]{1,0:T(8,128)(2,1)S(1)}, u32[]{:S(2)}, u32[]{:S(2)}) %collective-permute-start.42) | collective-permute-done | bytes 147488 | tf_op jit(solution)/shard_map/ppermute | solution.py:427
  (344 shorter events, 91.1 us)
Async XLA Ops:
  0.7 71.1 %collective-permute-start = (bf16[256,768]{1,0:T(8,128)(2,1)}, bf16[256,768]{1,0:T(8,128)(2,1)}, u32[]{:S(2)}, u32[]{:S(2)}) collective-permute-start(bf16[256,768]{1,0:T(8,128)(2,1)} %bitcast.60), channel_id=1, source_target_pairs={{0,1},{1,0},{2,3},{3,2},{4,5},{5,4},{6,7},{7,6},{8,9},{9,8},{10,11... | collective-permute-start | bytes 1179656 | tf_op jit(solution)/shard_map/ppermute | solution.py:427
  1.2 41.8 %collective-permute-start.1 = (s32[4]{0:T(128)}, s32[4]{0:T(128)S(1)}, u32[]{:S(2)}, u32[]{:S(2)}) collective-permute-start(s32[4]{0:T(128)} %param.15), channel_id=1, source_target_pairs={{0,1},{1,0},{2,3},{3,2},{4,5},{5,4},{6,7},{7,6},{8,9},{9,8},{10,11... | collective-permute-start | bytes 56 | tf_op jit(solution)/shard_map/ppermute | solution.py:427
  7.5 32.2 %collective-permute-start.10 = (bf16[24,1536]{1,0:T(8,128)(2,1)}, bf16[24,1536]{1,0:T(8,128)(2,1)}, u32[]{:S(2)}, u32[]{:S(2)}) collective-permute-start(bf16[24,1536]{1,0:T(8,128)(2,1)} %pad_maximum_fusion.14), channel_id=1, source_target_pairs={{0,1},{1,0},{2,3},{3,2},{4,5},{5,4},{6,7},{7,6},{8,9},{9,8},{10,11... | collective-permute-start | bytes 221192 | tf_op jit(solution)/shard_map/ppermute | solution.py:427
  7.6 43.1 %collective-permute-start.26 = (bf16[96,768]{1,0:T(8,128)(2,1)S(1)}, bf16[96,768]{1,0:T(8,128)(2,1)}, u32[]{:S(2)}, u32[]{:S(2)}) collective-permute-start(bf16[96,768]{1,0:T(8,128)(2,1)S(1)} %copy-done.45), channel_id=1, source_target_pairs={{0,8},{1,9},{2,10},{3,11},{4,12},{5,13},{6,14},{7,15},{8,0},{9,1},... | collective-permute-start | bytes 442376 | tf_op jit(solution)/shard_map/ppermute | solution.py:427
  18.2 16.8 %collective-permute-start.4 = (bf16[96,1664]{1,0:T(8,128)(2,1)S(1)}, bf16[96,1664]{1,0:T(8,128)(2,1)S(1)}, u32[]{:S(2)}, u32[]{:S(2)}) collective-permute-start(bf16[96,1664]{1,0:T(8,128)(2,1)S(1)} %pad_maximum_fusion.7), channel_id=1, source_target_pairs={{0,16},{1,17},{2,18},{3,19},{4,20},{5,21},{6,22},{7,23},{8,24},{9,... | collective-permute-start | bytes 958472 | tf_op jit(solution)/shard_map/ppermute | solution.py:427
  35.0 14.5 %collective-permute-start.5 = (bf16[192,1664]{1,0:T(8,128)(2,1)S(1)}, bf16[192,1664]{1,0:T(8,128)(2,1)S(1)}, u32[]{:S(2)}, u32[]{:S(2)}) collective-permute-start(bf16[192,1664]{1,0:T(8,128)(2,1)S(1)} %pad_maximum_fusion.3.refs_1_), channel_id=1, source_target_pairs={{0,2},{1,5},{2,0},{3,7},{4,6},{5,1},{6,4},{7,3},{8,10},{9,13},{10,... | collective-permute-start | bytes 1916936 | tf_op jit(solution)/shard_map/ppermute | solution.py:427
  45.9 15.4 %collective-permute-start.12 = (bf16[96,1536]{1,0:T(8,128)(2,1)S(1)}, bf16[96,1536]{1,0:T(8,128)(2,1)S(1)}, u32[]{:S(2)}, u32[]{:S(2)}) collective-permute-start(bf16[96,1536]{1,0:T(8,128)(2,1)S(1)} %pad_maximum_fusion.8), channel_id=1, source_target_pairs={{0,16},{1,17},{2,18},{3,19},{4,20},{5,21},{6,22},{7,23},{8,24},{9,... | collective-permute-start | bytes 884744 | tf_op jit(solution)/shard_map/ppermute | solution.py:427
  48.7 16.1 %collective-permute-start.6 = (bf16[192,1664]{1,0:T(8,128)(2,1)S(1)}, bf16[192,1664]{1,0:T(8,128)(2,1)S(1)}, u32[]{:S(2)}, u32[]{:S(2)}) collective-permute-start(bf16[192,1664]{1,0:T(8,128)(2,1)S(1)} %pad_maximum_fusion.3.refs_1_), channel_id=1, source_target_pairs={{0,4},{1,3},{2,6},{3,1},{4,0},{5,7},{6,2},{7,5},{8,12},{9,11},{10,... | collective-permute-start | bytes 1916936 | tf_op jit(solution)/shard_map/ppermute | solution.py:427
  49.6 19.1 %collective-permute-start.7 = (bf16[192,1664]{1,0:T(8,128)(2,1)S(1)}, bf16[192,1664]{1,0:T(8,128)(2,1)S(1)}, u32[]{:S(2)}, u32[]{:S(2)}) collective-permute-start(bf16[192,1664]{1,0:T(8,128)(2,1)S(1)} %collective-permute-done.5.refs_2_), channel_id=1, source_target_pairs={{0,4},{1,3},{2,6},{3,1},{4,0},{5,7},{6,2},{7,5},{8,12},{9,11},{10,... | collective-permute-start | bytes 1916936 | tf_op jit(solution)/shard_map/ppermute | solution.py:427
  50.8 58.8 %collective-permute-start.17 = (bf16[960,768]{1,0:T(8,128)(2,1)}, bf16[960,768]{1,0:T(8,128)(2,1)S(1)}, u32[]{:S(2)}, u32[]{:S(2)}) collective-permute-start(bf16[960,768]{1,0:T(8,128)(2,1)} %bitcast.11), channel_id=1, source_target_pairs={{0,1},{1,0},{2,3},{3,2},{4,5},{5,4},{6,7},{7,6},{8,9},{9,8},{10,11... | collective-permute-start | bytes 4423688 | tf_op jit(solution)/shard_map/ppermute | solution.py:427
  61.4 28.3 %collective-permute-start.13 = (bf16[192,1536]{1,0:T(8,128)(2,1)S(1)}, bf16[192,1536]{1,0:T(8,128)(2,1)S(1)}, u32[]{:S(2)}, u32[]{:S(2)}) collective-permute-start(bf16[192,1536]{1,0:T(8,128)(2,1)S(1)} %pad_maximum_fusion.4.refs_1_), channel_id=1, source_target_pairs={{0,2},{1,5},{2,0},{3,7},{4,6},{5,1},{6,4},{7,3},{8,10},{9,13},{10,... | collective-permute-start | bytes 1769480 | tf_op jit(solution)/shard_map/ppermute | solution.py:427
  68.7 21.0 %collective-permute-start.27 = (bf16[192,768]{1,0:T(8,128)(2,1)S(1)}, bf16[192,768]{1,0:T(8,128)(2,1)S(1)}, u32[]{:S(2)}, u32[]{:S(2)}) collective-permute-start(bf16[192,768]{1,0:T(8,128)(2,1)S(1)} %pad_maximum_fusion.10), channel_id=1, source_target_pairs={{0,16},{1,17},{2,18},{3,19},{4,20},{5,21},{6,22},{7,23},{8,24},{9,... | collective-permute-start | bytes 884744 | tf_op jit(solution)/shard_map/ppermute | solution.py:427
  71.7 21.1 %collective-permute-start.8 = (bf16[384,384]{1,0:T(8,128)(2,1)S(1)}, bf16[384,384]{1,0:T(8,128)(2,1)S(1)}, u32[]{:S(2)}, u32[]{:S(2)}) collective-permute-start(bf16[384,384]{1,0:T(8,128)(2,1)S(1)} %get-tuple-element.132), channel_id=1, source_target_pairs={{0,1},{1,0},{2,3},{3,2},{4,5},{5,4},{6,7},{7,6},{8,9},{9,8},{10,11... | collective-permute-start | bytes 884744 | tf_op jit(solution)/shard_map/ppermute | solution.py:427
  71.8 30.9 %collective-permute-start.21 = (bf16[96,1536]{1,0:T(8,128)(2,1)S(1)}, bf16[96,1536]{1,0:T(8,128)(2,1)S(1)}, u32[]{:S(2)}, u32[]{:S(2)}) collective-permute-start(bf16[96,1536]{1,0:T(8,128)(2,1)S(1)} %pad_maximum_fusion.9), channel_id=1, source_target_pairs={{0,16},{1,17},{2,18},{3,19},{4,20},{5,21},{6,22},{7,23},{8,24},{9,... | collective-permute-start | bytes 884744 | tf_op jit(solution)/shard_map/ppermute | solution.py:427
  89.7 13.6 %collective-permute-start.14 = (bf16[192,1536]{1,0:T(8,128)(2,1)S(1)}, bf16[192,1536]{1,0:T(8,128)(2,1)S(1)}, u32[]{:S(2)}, u32[]{:S(2)}) collective-permute-start(bf16[192,1536]{1,0:T(8,128)(2,1)S(1)} %pad_maximum_fusion.4.refs_1_), channel_id=1, source_target_pairs={{0,4},{1,3},{2,6},{3,1},{4,0},{5,7},{6,2},{7,5},{8,12},{9,11},{10,... | collective-permute-start | bytes 1769480 | tf_op jit(solution)/shard_map/ppermute | solution.py:427
  89.7 16.2 %collective-permute-start.15 = (bf16[192,1536]{1,0:T(8,128)(2,1)S(1)}, bf16[192,1536]{1,0:T(8,128)(2,1)S(1)}, u32[]{:S(2)}, u32[]{:S(2)}) collective-permute-start(bf16[192,1536]{1,0:T(8,128)(2,1)S(1)} %collective-permute-done.13.refs_2_), channel_id=1, source_target_pairs={{0,4},{1,3},{2,6},{3,1},{4,0},{5,7},{6,2},{7,5},{8,12},{9,11},{10,... | collective-permute-start | bytes 1769480 | tf_op jit(solution)/shard_map/ppermute | solution.py:427
  92.8 40.9 %collective-permute-start.25 = (bf16[256,768]{1,0:T(8,128)(2,1)S(1)}, bf16[256,768]{1,0:T(8,128)(2,1)S(1)}, u32[]{:S(2)}, u32[]{:S(2)}) collective-permute-start(bf16[256,768]{1,0:T(8,128)(2,1)S(1)} %bitcast.64), channel_id=1, source_target_pairs={{0,1},{1,0},{2,3},{3,2},{4,5},{5,4},{6,7},{7,6},{8,9},{9,8},{10,11... | collective-permute-start | bytes 1179656 | tf_op jit(solution)/shard_map/ppermute | solution.py:427
  102.7 16.8 %collective-permute-start.9 = (bf16[512,768]{1,0:T(8,128)(2,1)S(1)}, bf16[512,768]{1,0:T(8,128)(2,1)S(1)}, u32[]{:S(2)}, u32[]{:S(2)}) collective-permute-start(bf16[512,768]{1,0:T(8,128)(2,1)S(1)} %get-tuple-element.70.refs_2_), channel_id=1, source_target_pairs={{0,1},{1,0},{2,3},{3,2},{4,5},{5,4},{6,7},{7,6},{8,9},{9,8},{10,11... | collective-permute-start | bytes 2359304 | tf_op jit(solution)/shard_map/ppermute | solution.py:427
  103.3 28.8 %collective-permute-start.28 = (bf16[384,768]{1,0:T(8,128)(2,1)S(1)}, bf16[384,768]{1,0:T(8,128)(2,1)S(1)}, u32[]{:S(2)}, u32[]{:S(2)}) collective-permute-start(bf16[384,768]{1,0:T(8,128)(2,1)S(1)} %constant_dynamic-update-slice_fusion.refs_1_), channel_id=1, source_target_pairs={{0,2},{1,5},{2,0},{3,7},{4,6},{5,1},{6,4},{7,3},{8,10},{9,13},{10,... | collective-permute-start | bytes 1769480 | tf_op jit(solution)/shard_map/ppermute | solution.py:427
  105.9 28.3 %collective-permute-start.22 = (bf16[192,1536]{1,0:T(8,128)(2,1)S(1)}, bf16[192,1536]{1,0:T(8,128)(2,1)S(1)}, u32[]{:S(2)}, u32[]{:S(2)}) collective-permute-start(bf16[192,1536]{1,0:T(8,128)(2,1)S(1)} %pad_maximum_fusion.5.refs_1_), channel_id=1, source_target_pairs={{0,2},{1,5},{2,0},{3,7},{4,6},{5,1},{6,4},{7,3},{8,10},{9,13},{10,... | collective-permute-start | bytes 1769480 | tf_op jit(solution)/shard_map/ppermute | solution.py:427
  109.6 10.0 %collective-permute-start.16 = (bf16[384,384]{1,0:T(8,128)(2,1)S(1)}, bf16[384,384]{1,0:T(8,128)(2,1)S(1)}, u32[]{:S(2)}, u32[]{:S(2)}) collective-permute-start(bf16[384,384]{1,0:T(8,128)(2,1)S(1)} %get-tuple-element.130), channel_id=1, source_target_pairs={{0,1},{1,0},{2,3},{3,2},{4,5},{5,4},{6,7},{7,6},{8,9},{9,8},{10,11... | collective-permute-start | bytes 884744 | tf_op jit(solution)/shard_map/ppermute | solution.py:427
  131.5 34.8 %collective-permute-start.18 = (bf16[512,768]{1,0:T(8,128)(2,1)S(1)}, bf16[512,768]{1,0:T(8,128)(2,1)S(1)}, u32[]{:S(2)}, u32[]{:S(2)}) collective-permute-start(bf16[512,768]{1,0:T(8,128)(2,1)S(1)} %get-tuple-element.76.part), channel_id=1, source_target_pairs={{0,1},{1,0},{2,3},{3,2},{4,5},{5,4},{6,7},{7,6},{8,9},{9,8},{10,11... | collective-permute-start | bytes 2359304 | tf_op jit(solution)/shard_map/ppermute | solution.py:427
  132.2 15.7 %collective-permute-start.30 = (bf16[384,768]{1,0:T(8,128)(2,1)S(1)}, bf16[384,768]{1,0:T(8,128)(2,1)S(1)}, u32[]{:S(2)}, u32[]{:S(2)}) collective-permute-start(bf16[384,768]{1,0:T(8,128)(2,1)S(1)} %collective-permute-done.28.refs_2_), channel_id=1, source_target_pairs={{0,4},{1,3},{2,6},{3,1},{4,0},{5,7},{6,2},{7,5},{8,12},{9,11},{10,... | collective-permute-start | bytes 1769480 | tf_op jit(solution)/shard_map/ppermute | solution.py:427
  133.7 20.5 %collective-permute-start.23 = (bf16[192,1536]{1,0:T(8,128)(2,1)S(1)}, bf16[192,1536]{1,0:T(8,128)(2,1)S(1)}, u32[]{:S(2)}, u32[]{:S(2)}) collective-permute-start(bf16[192,1536]{1,0:T(8,128)(2,1)S(1)} %pad_maximum_fusion.5.refs_1_), channel_id=1, source_target_pairs={{0,4},{1,3},{2,6},{3,1},{4,0},{5,7},{6,2},{7,5},{8,12},{9,11},{10,... | collective-permute-start | bytes 1769480 | tf_op jit(solution)/shard_map/ppermute | solution.py:427
  134.2 26.3 %collective-permute-start.24 = (bf16[192,1536]{1,0:T(8,128)(2,1)S(1)}, bf16[192,1536]{1,0:T(8,128)(2,1)S(1)}, u32[]{:S(2)}, u32[]{:S(2)}) collective-permute-start(bf16[192,1536]{1,0:T(8,128)(2,1)S(1)} %collective-permute-done.22.refs_2_), channel_id=1, source_target_pairs={{0,4},{1,3},{2,6},{3,1},{4,0},{5,7},{6,2},{7,5},{8,12},{9,11},{10,... | collective-permute-start | bytes 1769480 | tf_op jit(solution)/shard_map/ppermute | solution.py:427
  184.0 17.5 %collective-permute-start.31 = (bf16[256,768]{1,0:T(8,128)(2,1)}, bf16[256,768]{1,0:T(8,128)(2,1)}, u32[]{:S(2)}, u32[]{:S(2)}) collective-permute-start(bf16[256,768]{1,0:T(8,128)(2,1)} %slice.155), channel_id=1, source_target_pairs={{0,1},{1,0},{2,3},{3,2},{4,5},{5,4},{6,7},{7,6},{8,9},{9,8},{10,11... | collective-permute-start | bytes 1179656 | tf_op jit(solution)/shard_map/ppermute | solution.py:427
  184.0 28.9 %collective-permute-start.32 = (bf16[512,768]{1,0:T(8,128)(2,1)}, bf16[512,768]{1,0:T(8,128)(2,1)}, u32[]{:S(2)}, u32[]{:S(2)}) collective-permute-start(bf16[512,768]{1,0:T(8,128)(2,1)} %get-tuple-element.81.part), channel_id=1, source_target_pairs={{0,1},{1,0},{2,3},{3,2},{4,5},{5,4},{6,7},{7,6},{8,9},{9,8},{10,11... | collective-permute-start | bytes 2359304 | tf_op jit(solution)/shard_map/ppermute | solution.py:427
  191.8 12.4 %collective-permute-start.51 = (bf16[192,1536]{1,0:T(8,128)(2,1)}, bf16[192,1536]{1,0:T(8,128)(2,1)}, u32[]{:S(2)}, u32[]{:S(2)}) collective-permute-start(bf16[192,1536]{1,0:T(8,128)(2,1)} %get-tuple-element.114), channel_id=1, source_target_pairs={{0,2},{1,5},{2,0},{3,7},{4,6},{5,1},{6,4},{7,3},{8,10},{9,13},{10,... | collective-permute-start | bytes 1769480 | tf_op jit(solution)/shard_map/ppermute | solution.py:427
  199.8 10.2 %collective-permute-start.57 = (bf16[384,768]{1,0:T(8,128)(2,1)}, bf16[384,768]{1,0:T(8,128)(2,1)}, u32[]{:S(2)}, u32[]{:S(2)}) collective-permute-start(bf16[384,768]{1,0:T(8,128)(2,1)} %get-tuple-element.118), channel_id=1, source_target_pairs={{0,2},{1,5},{2,0},{3,7},{4,6},{5,1},{6,4},{7,3},{8,10},{9,13},{10,... | collective-permute-start | bytes 1769480 | tf_op jit(solution)/shard_map/ppermute | solution.py:427
  201.6 26.7 %collective-permute-start.35 = (bf16[512,384]{1,0:T(8,128)(2,1)}, bf16[512,384]{1,0:T(8,128)(2,1)}, u32[]{:S(2)}, u32[]{:S(2)}) collective-permute-start(bf16[512,384]{1,0:T(8,128)(2,1)} %get-tuple-element.91.mixed), channel_id=1, source_target_pairs={{0,1},{1,0},{2,3},{3,2},{4,5},{5,4},{6,7},{7,6},{8,9},{9,8},{10,11... | collective-permute-start | bytes 1179656 | tf_op jit(solution)/shard_map/ppermute | solution.py:427
  201.6 93.5 %collective-permute-start.37 = (bf16[512,384]{1,0:T(8,128)(2,1)}, bf16[512,384]{1,0:T(8,128)(2,1)S(1)}, u32[]{:S(2)}, u32[]{:S(2)}) collective-permute-start(bf16[512,384]{1,0:T(8,128)(2,1)} %copy-done.36), channel_id=1, source_target_pairs={{0,1},{1,0},{2,3},{3,2},{4,5},{5,4},{6,7},{7,6},{8,9},{9,8},{10,11... | collective-permute-start | bytes 1179656 | tf_op jit(solution)/shard_map/ppermute | solution.py:427
  204.2 43.7 %collective-permute-start.50 = (bf16[192,1536]{1,0:T(8,128)(2,1)S(1)}, bf16[192,1536]{1,0:T(8,128)(2,1)S(1)}, u32[]{:S(2)}, u32[]{:S(2)}) collective-permute-start(bf16[192,1536]{1,0:T(8,128)(2,1)S(1)} %copy-done.35), channel_id=1, source_target_pairs={{0,2},{1,5},{2,0},{3,7},{4,6},{5,1},{6,4},{7,3},{8,10},{9,13},{10,... | collective-permute-start | bytes 1769480 | tf_op jit(solution)/shard_map/ppermute | solution.py:427
  210.0 38.5 %collective-permute-start.56 = (bf16[384,768]{1,0:T(8,128)(2,1)S(1)}, bf16[384,768]{1,0:T(8,128)(2,1)S(1)}, u32[]{:S(2)}, u32[]{:S(2)}) collective-permute-start(bf16[384,768]{1,0:T(8,128)(2,1)S(1)} %copy-done.33), channel_id=1, source_target_pairs={{0,2},{1,5},{2,0},{3,7},{4,6},{5,1},{6,4},{7,3},{8,10},{9,13},{10,... | collective-permute-start | bytes 1769480 | tf_op jit(solution)/shard_map/ppermute | solution.py:427
  213.0 34.9 %collective-permute-start.52 = (bf16[192,1536]{1,0:T(8,128)(2,1)S(1)}, bf16[192,1536]{1,0:T(8,128)(2,1)S(1)}, u32[]{:S(2)}, u32[]{:S(2)}) collective-permute-start(bf16[192,1536]{1,0:T(8,128)(2,1)S(1)} %add.224), channel_id=1, source_target_pairs={{0,4},{1,3},{2,6},{3,1},{4,0},{5,7},{6,2},{7,5},{8,12},{9,11},{10,... | collective-permute-start | bytes 1769480 | tf_op jit(solution)/shard_map/ppermute | solution.py:427
  228.3 20.7 %collective-permute-start.58 = (bf16[384,768]{1,0:T(8,128)(2,1)S(1)}, bf16[384,768]{1,0:T(8,128)(2,1)S(1)}, u32[]{:S(2)}, u32[]{:S(2)}) collective-permute-start(bf16[384,768]{1,0:T(8,128)(2,1)S(1)} %add.229), channel_id=1, source_target_pairs={{0,4},{1,3},{2,6},{3,1},{4,0},{5,7},{6,2},{7,5},{8,12},{9,11},{10,... | collective-permute-start | bytes 1769480 | tf_op jit(solution)/shard_map/ppermute | solution.py:427
  247.9 34.1 %collective-permute-start.33 = (bf16[512,768]{1,0:T(8,128)(2,1)S(1)}, bf16[512,768]{1,0:T(8,128)(2,1)S(1)}, u32[]{:S(2)}, u32[]{:S(2)}) collective-permute-start(bf16[512,768]{1,0:T(8,128)(2,1)S(1)} %get-tuple-element.84.part), channel_id=1, source_target_pairs={{0,1},{1,0},{2,3},{3,2},{4,5},{5,4},{6,7},{7,6},{8,9},{9,8},{10,11... | collective-permute-start | bytes 2359304 | tf_op jit(solution)/shard_map/ppermute | solution.py:427
  248.5 94.6 %collective-permute-start.36 = (bf16[960,768]{1,0:T(8,128)(2,1)}, bf16[960,768]{1,0:T(8,128)(2,1)}, u32[]{:S(2)}, u32[]{:S(2)}) collective-permute-start(bf16[960,768]{1,0:T(8,128)(2,1)} %slice.160), channel_id=1, source_target_pairs={{0,1},{1,0},{2,3},{3,2},{4,5},{5,4},{6,7},{7,6},{8,9},{9,8},{10,11... | collective-permute-start | bytes 4423688 | tf_op jit(solution)/shard_map/ppermute | solution.py:427
  249.0 15.5 %collective-permute-start.53 = (bf16[96,1536]{1,0:T(8,128)(2,1)S(1)}, bf16[96,1536]{1,0:T(8,128)(2,1)S(1)}, u32[]{:S(2)}, u32[]{:S(2)}) collective-permute-start(bf16[96,1536]{1,0:T(8,128)(2,1)S(1)} %slice.249), channel_id=1, source_target_pairs={{0,16},{1,17},{2,18},{3,19},{4,20},{5,21},{6,22},{7,23},{8,24},{9,... | collective-permute-start | bytes 884744 | tf_op jit(solution)/shard_map/ppermute | solution.py:427
  257.8 69.8 %collective-permute-start.44 = (bf16[192,1536]{1,0:T(8,128)(2,1)S(1)}, bf16[192,1536]{1,0:T(8,128)(2,1)}, u32[]{:S(2)}, u32[]{:S(2)}) collective-permute-start(bf16[192,1536]{1,0:T(8,128)(2,1)S(1)} %get-tuple-element.106), channel_id=1, source_target_pairs={{0,2},{1,5},{2,0},{3,7},{4,6},{5,1},{6,4},{7,3},{8,10},{9,13},{10,... | collective-permute-start | bytes 1769480 | tf_op jit(solution)/shard_map/ppermute | solution.py:427
  264.5 15.4 %collective-permute-start.59 = (bf16[192,768]{1,0:T(8,128)(2,1)S(1)}, bf16[192,768]{1,0:T(8,128)(2,1)S(1)}, u32[]{:S(2)}, u32[]{:S(2)}) collective-permute-start(bf16[192,768]{1,0:T(8,128)(2,1)S(1)} %slice.248), channel_id=1, source_target_pairs={{0,16},{1,17},{2,18},{3,19},{4,20},{5,21},{6,22},{7,23},{8,24},{9,... | collective-permute-start | bytes 884744 | tf_op jit(solution)/shard_map/ppermute | solution.py:427
  279.9 48.4 %collective-permute-start.46 = (bf16[192,1536]{1,0:T(8,128)(2,1)}, bf16[192,1536]{1,0:T(8,128)(2,1)}, u32[]{:S(2)}, u32[]{:S(2)}) collective-permute-start(bf16[192,1536]{1,0:T(8,128)(2,1)} %add.219), channel_id=1, source_target_pairs={{0,4},{1,3},{2,6},{3,1},{4,0},{5,7},{6,2},{7,5},{8,12},{9,11},{10,... | collective-permute-start | bytes 1769480 | tf_op jit(solution)/shard_map/ppermute | solution.py:427
  282.0 20.8 %collective-permute-start.54 = (bf16[48,1536]{1,0:T(8,128)(2,1)S(1)}, bf16[48,1536]{1,0:T(8,128)(2,1)S(1)}, u32[]{:S(2)}, u32[]{:S(2)}) collective-permute-start(bf16[48,1536]{1,0:T(8,128)(2,1)S(1)} %slice.253), channel_id=1, source_target_pairs={{0,8},{1,9},{2,10},{3,11},{4,12},{5,13},{6,14},{7,15},{8,0},{9,1},... | collective-permute-start | bytes 442376 | tf_op jit(solution)/shard_map/ppermute | solution.py:427
  295.1 13.7 %collective-permute-start.60 = (bf16[96,768]{1,0:T(8,128)(2,1)}, bf16[96,768]{1,0:T(8,128)(2,1)}, u32[]{:S(2)}, u32[]{:S(2)}) collective-permute-start(bf16[96,768]{1,0:T(8,128)(2,1)} %slice.252), channel_id=1, source_target_pairs={{0,8},{1,9},{2,10},{3,11},{4,12},{5,13},{6,14},{7,15},{8,0},{9,1},... | collective-permute-start | bytes 442376 | tf_op jit(solution)/shard_map/ppermute | solution.py:427
  312.7 19.8 %collective-permute-start.39 = (bf16[192,1536]{1,0:T(8,128)(2,1)}, bf16[192,1536]{1,0:T(8,128)(2,1)}, u32[]{:S(2)}, u32[]{:S(2)}) collective-permute-start(bf16[192,1536]{1,0:T(8,128)(2,1)} %copy-done.31), channel_id=1, source_target_pairs={{0,2},{1,5},{2,0},{3,7},{4,6},{5,1},{6,4},{7,3},{8,10},{9,13},{10,... | collective-permute-start | bytes 1769480 | tf_op jit(solution)/shard_map/ppermute | solution.py:427
  325.8 22.7 %collective-permute-start.38 = (bf16[192,1536]{1,0:T(8,128)(2,1)S(1)}, bf16[192,1536]{1,0:T(8,128)(2,1)S(1)}, u32[]{:S(2)}, u32[]{:S(2)}) collective-permute-start(bf16[192,1536]{1,0:T(8,128)(2,1)S(1)} %copy-done.30), channel_id=1, source_target_pairs={{0,2},{1,5},{2,0},{3,7},{4,6},{5,1},{6,4},{7,3},{8,10},{9,13},{10,... | collective-permute-start | bytes 1769480 | tf_op jit(solution)/shard_map/ppermute | solution.py:427
  329.8 13.1 %collective-permute-start.47 = (bf16[96,1536]{1,0:T(8,128)(2,1)S(1)}, bf16[96,1536]{1,0:T(8,128)(2,1)S(1)}, u32[]{:S(2)}, u32[]{:S(2)}) collective-permute-start(bf16[96,1536]{1,0:T(8,128)(2,1)S(1)} %slice.250), channel_id=1, source_target_pairs={{0,16},{1,17},{2,18},{3,19},{4,20},{5,21},{6,22},{7,23},{8,24},{9,... | collective-permute-start | bytes 884744 | tf_op jit(solution)/shard_map/ppermute | solution.py:427
  333.8 14.7 %collective-permute-start.40 = (bf16[192,1536]{1,0:T(8,128)(2,1)S(1)}, bf16[192,1536]{1,0:T(8,128)(2,1)S(1)}, u32[]{:S(2)}, u32[]{:S(2)}) collective-permute-start(bf16[192,1536]{1,0:T(8,128)(2,1)S(1)} %add.212), channel_id=1, source_target_pairs={{0,4},{1,3},{2,6},{3,1},{4,0},{5,7},{6,2},{7,5},{8,12},{9,11},{10,... | collective-permute-start | bytes 1769480 | tf_op jit(solution)/shard_map/ppermute | solution.py:427
  348.8 16.4 %collective-permute-start.41 = (bf16[96,1536]{1,0:T(8,128)(2,1)S(1)}, bf16[96,1536]{1,0:T(8,128)(2,1)S(1)}, u32[]{:S(2)}, u32[]{:S(2)}) collective-permute-start(bf16[96,1536]{1,0:T(8,128)(2,1)S(1)} %slice.251), channel_id=1, source_target_pairs={{0,16},{1,17},{2,18},{3,19},{4,20},{5,21},{6,22},{7,23},{8,24},{9,... | collective-permute-start | bytes 884744 | tf_op jit(solution)/shard_map/ppermute | solution.py:427
  (72 other events, 595.8 us)

commit v2 on v1

v2 whole, which is shorter than its diff:
```python
import jax
import jax.numpy as jnp
import numpy as np
from jax import lax
from jax.experimental import pallas as pl
from jax.experimental.pallas import tpu as pltpu
from jax.sharding import PartitionSpec as P

AXES = ("dp", "fsdp")
HEADS = 12
HALF = HEADS // 2
HEAD = 64
D = 768
DH = D // 2
LEN = 64
EPS = 1e-06
NEG = -1e30
SCALE = HEAD ** (-0.5)
F32 = jnp.float32
BF = jnp.bfloat16
VMEM_LIMIT = 48 << 20

VM = pl.BlockSpec(memory_space=pltpu.VMEM)
SM = pl.BlockSpec(memory_space=pltpu.SMEM)
ANY = pl.BlockSpec(memory_space=pl.ANY)


def sds(shape, dtype):
    return jax.ShapeDtypeStruct(shape, dtype)


def kernel_call(body, ins, in_specs, outs, out_specs=None, scratch=(), flops=0, after=()):
    n, skip = len(ins), len(after)
    run = body if not after else (lambda *refs: body(*refs[:n], *refs[n + skip :]))
    nbytes = sum(int(np.prod(a.shape)) * a.dtype.itemsize for a in list(ins) + list(outs))
    return pl.pallas_call(
        run,
        out_shape=list(outs),
        in_specs=list(in_specs) + [ANY] * skip,
        out_specs=[VM] * len(outs) if out_specs is None else list(out_specs),
        scratch_shapes=list(scratch),
        compiler_params=pltpu.CompilerParams(vmem_limit_bytes=VMEM_LIMIT),
        cost_estimate=pl.CostEstimate(flops=16 * flops + 16 * 10**9, bytes_accessed=nbytes, transcendentals=0),
    )(*ins, *after)


def tie(x, *earlier):
    return pl.pallas_call(
        lambda *refs: None,
        out_shape=sds(x.shape, x.dtype),
        in_specs=[ANY] * (1 + len(earlier)),
        out_specs=ANY,
        input_output_aliases={0: 0},
        cost_estimate=pl.CostEstimate(flops=0, bytes_accessed=0, transcendentals=0),
    )(x, *earlier)


def nn(a, b):
    return lax.dot_general(a, b, (((1,), (0,)), ((), ())), preferred_element_type=F32)


def nt(a, b):
    return lax.dot_general(a, b, (((1,), (1,)), ((), ())), preferred_element_type=F32)


def tn(a, b):
    return lax.dot_general(a, b, (((0,), (0,)), ((), ())), preferred_element_type=F32)


def normalise(v):
    mean = jnp.mean(v, -1, keepdims=True)
    cen = v - mean
    inv = lax.rsqrt(jnp.mean(cen * cen, -1, keepdims=True) + EPS)
    return cen * inv, inv


def norm_back(v, gain, dy):
    xhat, inv = normalise(v)
    dxh = dy * gain
    m1 = jnp.mean(dxh, -1, keepdims=True)
    m2 = jnp.mean(dxh * xhat, -1, keepdims=True)
    dx = inv * (dxh - m1 - xhat * m2)
    return dx, jnp.sum(dy * xhat, 0, keepdims=True), jnp.sum(dy, 0, keepdims=True)


def head_of_lane(rows):
    return lax.shift_right_logical(lax.broadcasted_iota(jnp.int32, (rows, DH), 1), 6)


def spread(q):
    head = head_of_lane(1)
    parts = [q * (head == h).astype(F32).astype(q.dtype) for h in range(HALF)]
    return jnp.concatenate(parts, 0)


def fold(o):
    head = head_of_lane(LEN)
    total = jnp.where(head == 0, o[:LEN], 0.0)
    for h in range(1, HALF):
        total = jnp.where(head == h, o[h * LEN : (h + 1) * LEN], total)
    return total


def attend(q, k, v, allowed):
    st = nt(k, spread(q)) * SCALE
    st = jnp.where(allowed, st, NEG)
    e = jnp.exp(st - jnp.max(st, 0, keepdims=True))
    p = (e * (1.0 / jnp.sum(e, 0, keepdims=True))).astype(BF)
    return p, fold(tn(p, v)).astype(BF)


def attend_back(g, q, k, v, p):
    gs, qs = spread(g), spread(q)
    dp = nt(v, gs)
    pf = p.astype(F32)
    t = pf * dp
    ds = (t - pf * jnp.sum(t, 0, keepdims=True)).astype(BF)
    dq = (fold(tn(ds, k)) * SCALE).astype(BF)
    dk = (nn(ds, qs) * SCALE).astype(BF)
    dv = nn(p, gs).astype(BF)
    return dq, dk, dv


def seq_rows(s):
    return pl.ds(pl.multiple_of(s * LEN, LEN), LEN)


def half_lanes(c):
    return pl.ds(pl.multiple_of(c * DH, DH), DH)


def loop(n, body, unroll=1):
    def step(i, carry):
        body(i)
        return carry

    lax.fori_loop(0, n, step, 0, unroll=unroll)


def assemble_kernel(cols, blk, offs_ref, *refs):
    n = len(cols)
    n_out = 1 + max(c[2] for c in cols)
    pieces, outs, sems = refs[:4], refs[4 : 4 + n_out], refs[4 + n_out]
    copies = []
    for q in range(4):
        for r in range(4):
            for i, (lo, hi, o, which, step, shift) in enumerate(cols):
                row = pl.multiple_of(offs_ref[which, q * 4 + r] * step + shift, 16)
                copies.append(
                    pltpu.make_async_copy(
                        pieces[q].at[pl.ds(r * blk, blk), pl.ds(lo, hi - lo)],
                        outs[o].at[pl.ds(row, blk), :],
                        sems.at[(q * 4 + r) * n + i],
                    )
                )
    for cp in copies:
        cp.start()
    for cp in copies:
        cp.wait()


def assemble(pieces, offs, cols, shapes):
    blk = pieces[0].shape[0] // 4
    body = lambda *refs: assemble_kernel(cols, blk, *refs)
    return kernel_call(
        body,
        [offs, *pieces],
        [SM] + [ANY] * 4,
        [sds(shape, BF) for shape in shapes],
        [ANY] * len(shapes),
        [pltpu.SemaphoreType.DMA((16 * len(cols),))],
    )


def send_out(dw, offs_ref, outs, sems):
    own, to_b, to_a = outs
    blk = dw.shape[0] // 16
    copies = []
    for q, (dst, base) in enumerate(((own, 0), (to_a, 0), (to_b, 0), (to_a, 4))):
        for r in range(4):
            row = pl.multiple_of(offs_ref[0, q * 4 + r] * blk, 16)
            copies.append(
                pltpu.make_async_copy(
                    dw.at[pl.ds(row, blk), :],
                    dst.at[pl.ds((base + r) * blk, blk), :],
                    sems.at[q * 4 + r],
                )
            )
    for cp in copies:
        cp.start()
    for cp in copies:
        cp.wait()


def pack_kernel(core, qkv, out, cq, ckv, cout, win, gains, biases, keep, send, vecs):
    c = core[0]
    vecs[...] = jnp.zeros_like(vecs)
    vecs[0:3, 0:24] = gains[...].astype(F32)
    vecs[3:6, 0:24] = biases[...].astype(F32)
    rows = keep.shape[0]
    wide = jnp.transpose(vecs[...])[:rows].astype(BF)
    for dst, which in ((keep, c), (send, 1 - c)):
        at = 0
        for w, groups in ((qkv, 3), (None, 0), (out, 1), (cout, 1), (cq, 1), (ckv, 2)):
            if w is None:
                dst[:, at : at + 128] = wide
                at += 128
            for k in range(groups):
                lanes = pl.ds(pl.multiple_of(k * D + which * DH, 128), DH)
                dst[:, at : at + DH] = w[:, lanes]
                at += DH
    hr = 96
    for k in range(win.shape[1] // (2 * hr)):
        first = win[:, 2 * k * hr : (2 * k + 1) * hr]
        second = win[:, (2 * k + 1) * hr : (2 * k + 2) * hr]
        keep[:, at + k * hr : at + (k + 1) * hr] = jnp.where(c == 0, first, second)
        send[:, at + k * hr : at + (k + 1) * hr] = jnp.where(c == 0, second, first)


def prepare_kernel(own, other, tok, g, mem, lens, xhat):
    rows = tok.shape[0] // 2
    nmem = mem.shape[0] // 2
    for b, src in ((0, own), (1, other)):
        tok[b * rows : (b + 1) * rows, :] = src[0:rows, :]
        g[b * rows : (b + 1) * rows, :] = src[rows : 2 * rows, :]
        mem[b * nmem : (b + 1) * nmem, :] = src[2 * rows : 2 * rows + nmem, :]
        lens[4 * b : 4 * b + 4, :] = src[2 * rows + nmem :, :].astype(F32)[:4]

    def norm(s):
        xhat[seq_rows(s), :] = normalise(tok[seq_rows(s), :].astype(F32))[0]

    loop(8, norm)


def self_kernel(lens, xhat, gcol, wqkv, first, packed, probs, mixed, vec):
    vec[...] = jnp.transpose(gcol[...].astype(F32))[:8]
    gain, bias = vec[0:1], vec[3:4]

    def norm(s):
        first[seq_rows(s), :] = (xhat[seq_rows(s), :] * gain + bias).astype(BF)

    loop(8, norm)

    def proj(b):
        rows = pl.ds(pl.multiple_of(b * 256, 256), 256)
        packed[rows, :] = nn(first[rows, :], wqkv[...]).astype(BF)

    loop(2, proj)
    key = lax.broadcasted_iota(jnp.int32, (LEN, DH), 0)
    query = lax.broadcasted_iota(jnp.int32, (LEN, DH), 1) & (LEN - 1)

    def att(s):
        allowed = (key <= query) & (key.astype(F32) < lens[pl.ds(s, 1), 0:DH])
        rows = seq_rows(s)
        p, m = attend(packed[rows, 0:DH], packed[rows, DH : 2 * DH], packed[rows, 2 * DH :], allowed)
        probs[s] = p
        mixed[rows, :] = m

    loop(8, att, 2)


def out_kernel(core, mixed, wkeep, wrecv, comb):
    c = core[0]
    comb[:, half_lanes(c)] = nn(mixed[...], wkeep[...]).astype(BF)
    comb[:, half_lanes(1 - c)] = nn(mixed[...], wrecv[...]).astype(BF)
    comb[:, D:] = mixed[...]


def kv_kernel(mem, wckv, kv):
    def step(b):
        rows = pl.ds(pl.multiple_of(b * 480, 480), 480)
        kv[rows, :] = nn(mem[rows, :], wckv[...]).astype(BF)

    loop(mem.shape[0] // 480, step)


def swapped(s):
    return pl.ds(pl.multiple_of(((s + 4) & 7) * LEN, LEN), LEN)


def cross_kernel(mem_len, core, tok, part, recv, vec, wcq, wkeep, wrecv, kv, resid, second, cq, probs, comb):
    c = core[0]
    gain, bias = vec[1:2], vec[4:5]

    def norm(s):
        rows = seq_rows(s)
        both = part[rows, 0:D].astype(F32) + recv[swapped(s), 0:D].astype(F32)
        v = tok[rows, :].astype(F32) + both
        resid[rows, :] = v
        xhat, _ = normalise(v)
        second[rows, :] = (xhat * gain + bias).astype(BF)

    loop(8, norm)
    cq[...] = nn(second[...], wcq[...]).astype(BF)
    pad = probs.shape[1]
    allowed = lax.broadcasted_iota(jnp.int32, (pad, DH), 0) < mem_len

    def att(s):
        rows = seq_rows(s)
        keys = pl.ds(pl.multiple_of(s * pad, 16), pad)
        p, m = attend(cq[rows, :], kv[keys, 0:DH], kv[keys, DH:], allowed)
        probs[s] = p
        comb[rows, D:] = m

    loop(8, att, 2)
    comb[:, half_lanes(c)] = nn(comb[:, D:], wkeep[...]).astype(BF)
    comb[:, half_lanes(1 - c)] = nn(comb[:, D:], wrecv[...]).astype(BF)


def inner_kernel(resid, part, recv, vec, win, resid_two, third, hidden, slope):
    gain, bias = vec[2:3], vec[5:6]

    def norm(s):
        rows = seq_rows(s)
        both = part[rows, 0:D].astype(F32) + recv[swapped(s), 0:D].astype(F32)
        v = resid[rows, :] + both
        resid_two[rows, :] = v
        xhat, _ = normalise(v)
        third[rows, :] = (xhat * gain + bias).astype(BF)

    loop(8, norm)
    width = win.shape[1]

    def step(b):
        rows = pl.ds(pl.multiple_of(b * 128, 128), 128)
        x = nn(third[rows, :], win[...])
        cdf = 0.5 + 0.5 * lax.erf(x * (0.5**0.5))
        hidden[rows, :] = (x * cdf).astype(BF)
        density = jnp.exp(x * x * -0.5) * ((2.0 * np.pi) ** -0.5)
        slope[rows, :] = (cdf + x * density).astype(BF)

    loop(4, step)


def mlp_kernel(hidden, slope, g, wout, win, own, comb, ginner):
    half = own.shape[0]

    def back(b):
        rows = pl.ds(pl.multiple_of(b * 256, 256), 256)
        gh = nt(g[rows, :], wout[...])
        ginner[rows, :] = (gh * slope[rows, :].astype(F32)).astype(BF)
        comb[rows, :] = nt(ginner[rows, :], win[...]).astype(BF)

    loop(2, back)
    own[...] = nn(hidden[0:half, :], wout[...]).astype(BF)
    comb[2 * half :, :] = nn(hidden[half:, :], wout[...]).astype(BF)


def dmlpout_kernel(offs, hidden, g, *refs):
    outs, dw, sems = refs[:3], refs[3], refs[4]
    blk = dw.shape[0] // 16
    for b in range(4):
        part = tn(hidden[:, b * 8 * blk : (b + 1) * 8 * blk], g[...]).astype(BF)
        for k in range(8):
            row = (4 * b + k // 2) * blk
            dw[row : row + blk, (k % 2) * D : (k % 2 + 1) * D] = part[k * blk : (k + 1) * blk]
    send_out(dw, offs, outs, sems)


def dmlpin_kernel(offs, third, ginner, *refs):
    outs, dw, sems = refs[:3], refs[3], refs[4]
    for b in range(0, dw.shape[0], 256):
        dw[b : b + 256, :] = tn(third[:, b : b + 256], ginner[...]).astype(BF)
    send_out(dw, offs, outs, sems)


def cross_back_kernel(
    core, resid, part, recv, own, g, vec, wcq, wkeep, wrecv, kv, cq, probs, output, gresid, gtwo, dcq, dkv, gsecond, dvec, gm
):
    c = core[0]
    gain = vec[2:3]
    dvec[...] = jnp.zeros_like(dvec)

    def norm(s):
        rows = seq_rows(s)
        dy = part[rows, :].astype(F32) + recv[swapped(s), :].astype(F32)
        dx, dg, db = norm_back(resid[rows, :], gain, dy)
        total = g[rows, :].astype(F32) + dx
        gresid[rows, :] = total
        gtwo[rows, :] = total.astype(BF)

        @pl.when(s < 4)
        def _():
            dvec[0:1, :] += dg
            dvec[1:2, :] += db
            extra = own[rows, :].astype(F32) + recv[pl.ds(pl.multiple_of(512 + s * LEN, LEN), LEN), :].astype(F32)
            output[rows, :] = (resid[rows, :] + extra).astype(BF)

    loop(8, norm)
    gm[...] = (nt(gtwo[:, half_lanes(c)], wkeep[...]) + nt(gtwo[:, half_lanes(1 - c)], wrecv[...])).astype(BF)
    pad = probs.shape[1]

    def att(s):
        rows = seq_rows(s)
        keys = pl.ds(pl.multiple_of(s * pad, 16), pad)
        dq, dk, dv = attend_back(gm[rows, :], cq[rows, :], kv[keys, 0:DH], kv[keys, DH:], probs[s])
        dcq[rows, :] = dq
        dkv[keys, 0:DH] = dk
        dkv[keys, DH:] = dv

    loop(8, att, 2)
    gsecond[...] = nt(dcq[...], wcq[...]).astype(BF)


def out_grad(dw, lo, c, mine, other, g):
    cols = half_lanes(c)
    dw[half_lanes(c), lo : lo + DH] = tn(mine[:, D:], g[:, cols]).astype(BF)
    rest = tn(other[256:, D:], g[:256, cols]) + tn(other[:256, D:], g[256:, cols])
    dw[half_lanes(1 - c), lo : lo + DH] = rest.astype(BF)


def dcross_kernel(offs, core, mixed, mixed_other, gtwo, second, dcq, mem, dkv, wckv, *refs):
    outs, gmem, dw, sems = refs[:3], refs[3:5], refs[5], refs[6]
    out_grad(dw, 0, core[0], mixed, mixed_other, gtwo)
    dw[:, DH : 2 * DH] = tn(second[...], dcq[...]).astype(BF)
    for b in range(0, D, 256):
        dw[b : b + 256, 2 * DH :] = tn(mem[:, b : b + 256], dkv[...]).astype(BF)

    half = mem.shape[0] // 2
    for b in range(0, half, 480):
        gmem[0][b : b + 480, :] = nt(dkv[b : b + 480, :], wckv[...]).astype(BF)
        gmem[1][b : b + 480, :] = nt(dkv[half + b : half + b + 480, :], wckv[...]).astype(BF)
    send_out(dw, offs, outs, sems)


def self_back_kernel(
    core, xhat, resid, part, recv, gresid_two, vec, wqkv, wkeep, wrecv, packed, probs, gresid, gone, dpacked, gfirst_own, gfirst_other, dvec, gm
):
    c = core[0]
    gain = vec[1:2]
    dvec[...] = jnp.zeros_like(dvec)

    def norm(s):
        rows = seq_rows(s)
        dy = part[rows, :].astype(F32) + recv[swapped(s), :].astype(F32)
        dx, dg, db = norm_back(resid[rows, :], gain, dy)
        total = gresid_two[rows, :] + dx
        gresid[rows, :] = total
        gone[rows, :] = total.astype(BF)

        @pl.when(s < 4)
        def _():
            dvec[0:1, :] += dg
            dvec[1:2, :] += db

    loop(8, norm)
    gm[...] = (nt(gone[:, half_lanes(c)], wkeep[...]) + nt(gone[:, half_lanes(1 - c)], wrecv[...])).astype(BF)

    def att(s):
        rows = seq_rows(s)
        dq, dk, dv = attend_back(
            gm[rows, :], packed[rows, 0:DH], packed[rows, DH : 2 * DH], packed[rows, 2 * DH :], probs[s]
        )
        dpacked[rows, 0:DH] = dq
        dpacked[rows, DH : 2 * DH] = dk
        dpacked[rows, 2 * DH :] = dv

    loop(8, att, 2)
    half = gfirst_own.shape[0]
    for b, dst in ((0, gfirst_own), (half, gfirst_other)):
        term = nt(dpacked[b : b + half, :], wqkv[...])
        dst[...] = term.astype(BF)
        dvec[2:3, :] += jnp.sum(term * xhat[b : b + half, :], 0, keepdims=True)
        dvec[3:4, :] += jnp.sum(term, 0, keepdims=True)


def dself_kernel(offs, core, mixed, mixed_other, gone, first, dpacked, dvec_two, dvec_one, *refs):
    outs, dw, vecs, sems = refs[:3], refs[3], refs[4], refs[5]
    out_grad(dw, 0, core[0], mixed, mixed_other, gone)
    for b in range(0, D, 256):
        dw[b : b + 256, DH : 4 * DH] = tn(first[:, b : b + 256], dpacked[...]).astype(BF)
    vecs[...] = jnp.zeros_like(vecs)
    for i, (v, row) in enumerate(((dvec_one, 2), (dvec_one, 0), (dvec_two, 0), (dvec_one, 3), (dvec_one, 1), (dvec_two, 1))):
        vecs[i : i + 1, :] = v[row : row + 1, :]
    dw[:, 4 * DH :] = jnp.transpose(vecs[...]).astype(BF)
    send_out(dw, offs, outs, sems)


def tokens_back_kernel(tok, part, recv, gresid, vec, gmem, gmem_recv, gtok, gmemory):
    gmemory[...] = (gmem[...].astype(F32) + gmem_recv[...].astype(F32)).astype(BF)
    gain = vec[0:1]

    def norm(s):
        rows = seq_rows(s)
        dy = part[rows, :].astype(F32) + recv[rows, :].astype(F32)
        dx, _, _ = norm_back(tok[rows, :].astype(F32), gain, dy)
        gtok[rows, :] = (gresid[rows, :] + dx).astype(BF)

    loop(4, norm)


def join_kernel(core, mine, got, *outs):
    c = core[0]
    at = 0
    for out in outs[: 2 if mine.shape[1] > 4 * DH else 3]:
        for k in range(out.shape[1] // D):
            out[:, pl.ds(pl.multiple_of(k * D + c * DH, 128), DH)] = mine[:, at : at + DH]
            out[:, pl.ds(pl.multiple_of(k * D + (1 - c) * DH, 128), DH)] = got[:, at : at + DH]
            at += DH
    if mine.shape[1] > at:
        gains, biases, wide = outs[2:]
        rows = mine.shape[0]
        wide[...] = jnp.zeros_like(wide)
        wide[0:rows, :] = mine[:, at:] + got[:, at:]
        turned = jnp.transpose(wide[...])
        gains[...] = turned[0:3, 0:rows]
        biases[...] = turned[3:6, 0:rows]


class Moves:
    def __init__(self, mesh):
        self.nz, self.nf = mesh.shape["dp"], mesh.shape["fsdp"]
        self.n = self.nz * self.nf
        self.doubling = self.nz == 4 and self.nf == 8

    def permute(self, x, target):
        pairs = [(d, target(d // self.nf, (d % self.nf) // 2, d % 2)) for d in range(self.n)]
        return lax.ppermute(x, AXES, [(a, (z * self.nf) + 2 * yx + c) for a, (z, yx, c) in pairs])

    def sibling(self, x):
        return self.permute(x, lambda z, yx, c: (z, yx, 1 - c))

    def near_z(self, x):
        return self.permute(x, lambda z, yx, c: (z ^ 1, yx, c))

    def far_z(self, x):
        return self.permute(x, lambda z, yx, c: (z ^ 2, yx, c))

    def side_a(self, x):
        return self.permute(x, lambda z, yx, c: (z, yx ^ (1 + c), c))

    def side_b(self, x):
        return self.permute(x, lambda z, yx, c: (z, yx ^ (2 - c), c))

    def opposite_z(self, x):
        return self.permute(x, lambda z, yx, c: (z ^ 3, yx, c))


def per_device(moves, tokens, memory, lengths, cotangent, self_qkv, self_out, cross_q, cross_kv, cross_out, mlp_in, mlp_out, norm_gains, norm_biases):
    seqs, mem_len = memory.shape[0], memory.shape[1]
    rows = seqs * LEN
    place = lax.axis_index(AXES)
    c = place % 2
    chip = place // 2
    core = jnp.reshape(c, (1,)).astype(jnp.int32)
    wr, hr = self_qkv.shape[0], mlp_out.shape[0]
    ff = mlp_in.shape[1]
    fh = ff // 2
    r2, s2 = 2 * rows, 2 * seqs
    wb = D // 16
    flops = lambda m, k, n: 2 * m * k * n

    pad = -(-mem_len // 16) * 16
    live = jnp.arange(LEN, dtype=jnp.int32)[None, :] < lengths[:, None]
    g_own = jnp.where(live[..., None], cotangent, jnp.zeros_like(cotangent)).reshape(rows, D)
    tok_own = tokens.reshape(rows, D)
    mem_own = jnp.pad(memory, ((0, 0), (0, pad - mem_len), (0, 0))).reshape(seqs * pad, D)
    len_own = jnp.broadcast_to(jnp.pad(lengths, (0, 16 - seqs)).astype(BF)[:, None], (16, D))

    def prepare(own, other):
        return kernel_call(
            prepare_kernel,
            [own, other],
            [VM] * 2,
            [sds((r2, D), BF)] * 2 + [sds((s2 * pad, D), BF), sds((8, D), F32), sds((r2, D), F32)],
        )

    def self_attention(pieces, chips, prepared):
        w_qkv, g_col = assemble(
            pieces,
            chips[None],
            [(0, 3 * DH, 0, 0, wb, 0), (3 * DH, 3 * DH + 128, 1, 0, wb, 0)],
            [(D, 3 * DH), (D, 128)],
        )
        return w_qkv, *kernel_call(
            self_kernel,
            [prepared[3], prepared[4], g_col, w_qkv],
            [VM] * 4,
            [sds((r2, D), BF), sds((r2, 3 * DH), BF), sds((s2, LEN, DH), BF), sds((r2, DH), BF), sds((8, D), F32)],
            flops=flops(r2, D, 3 * DH),
        )

    if moves.doubling:
        keep, send = kernel_call(
            pack_kernel,
            [core, self_qkv, self_out, cross_q, cross_kv, cross_out, mlp_in, norm_gains, norm_biases],
            [SM] + [VM] * 8,
            [sds((wr, 12 * DH + 128), BF)] * 2,
            scratch=[pltpu.VMEM((128, 128), F32)],
        )
        got = moves.sibling(send)
        own = jnp.concatenate([tok_own, g_own, mem_own, len_own], 0)
        other = moves.sibling(own)

        def chip_rows(lo, hi):
            a, b = keep[:, lo:hi], got[:, lo:hi]
            return jnp.where(c == 0, jnp.concatenate([a, b], 0), jnp.concatenate([b, a], 0))

        bits = jnp.arange(4, dtype=jnp.int32)
        plane = jnp.stack([jnp.int32(0), 1 + c, 2 - c, jnp.int32(3)]).astype(jnp.int32)
        z, yx = chip // 4, chip % 4
        chips = ((z ^ bits)[None, :] * 4 + (yx ^ plane)[:, None]).reshape(16).astype(jnp.int32)
        one = chip_rows(0, 3 * DH + 128)
        one = jnp.concatenate([one, moves.near_z(one), moves.far_z(one), moves.opposite_z(one)], 0)
        prepared = prepare(own, other)
        one = tie(one, prepared[0])
        rest = jnp.concatenate([chip_rows(3 * DH + 128, 12 * DH + 128), mlp_out[: 2 * wr], mlp_out[2 * wr :]], 1)
        rest = tie(rest, one)
        rest = jnp.concatenate([rest, moves.near_z(rest)], 0)
        a, b = moves.side_a(one), moves.side_b(one)
        gathered = [[one, a, b, moves.side_b(a)]]
        kernels_done = self_attention(gathered[0], chips, prepared)

        def far_part(lo, hi, earlier):
            two = tie(rest[:, lo:hi], earlier)
            far = moves.far_z(two)
            return far, jnp.concatenate([two, far], 0)

        far, four = far_part(0, 5 * DH, a)
        four = tie(four, gathered[0][3])
        a, b = moves.side_a(four), moves.side_b(four)
        gathered.append([four, a, b, moves.side_b(a)])
        far, four = far_part(5 * DH, 9 * DH, far)
        four = tie(four, b, kernels_done[1])
        a, b = moves.side_a(four), moves.side_b(four)
        gathered.append([four, a, b, moves.side_b(a)])
        far, four_last = far_part(9 * DH, 13 * DH, far)
        b_before = b
    else:
        own = jnp.concatenate([tok_own, g_own, mem_own, len_own], 0)
        other = moves.sibling(own)
        chips = jnp.arange(16, dtype=jnp.int32)
        whole = lambda w: lax.all_gather(w, AXES, axis=0, tiled=True)
        split = lambda w: [w[i * w.shape[0] // 4 : (i + 1) * w.shape[0] // 4] for i in range(4)]

        def col_half(w, groups):
            w = w.reshape(w.shape[0], groups, 2, w.shape[1] // (2 * groups))
            return lax.dynamic_index_in_dim(w, c, 2, keepdims=False).reshape(w.shape[0], -1)

        vectors = jnp.pad(jnp.concatenate([norm_gains, norm_biases], 0).T, ((0, 0), (0, 122)))
        one = jnp.concatenate([col_half(self_qkv, 3), vectors], 1)
        two = jnp.concatenate([col_half(w, w.shape[1] // D) for w in (self_out, cross_out, cross_q, cross_kv)], 1)
        rowed = whole(mlp_out).reshape(moves.n // 2, 2, hr, D)
        gathered = [split(whole(w)) for w in (one, two, col_half(mlp_in, ff // (2 * hr)))]
        rowed = lax.dynamic_index_in_dim(rowed, c, 1, keepdims=False).reshape(16, 2, fh // 32, D)
        gathered.append(split(rowed.transpose(0, 2, 1, 3).reshape(D, 2 * D)))
        prepared = prepare(own, other)
        kernels_done = self_attention(gathered[0], chips, prepared)
    turned = ((chips // 8) ^ c) * 16 + chips % 8
    offs = jnp.stack([chips, turned, turned + 8]).astype(jnp.int32)

    tok, g, mem, lens, xhat = prepared
    w_qkv, first, packed, probs, mixed, vec = kernels_done
    w_outs, w_cq, w_ckv = assemble(
        gathered[1],
        offs,
        [
            (0, DH, 0, 1, wb, 0),
            (DH, 2 * DH, 0, 2, wb, 0),
            (2 * DH, 3 * DH, 1, 0, wb, 0),
            (3 * DH, 5 * DH, 2, 0, wb, 0),
        ],
        [(2 * D, DH), (D, DH), (D, 2 * DH)],
    )
    outs_recv = moves.sibling(w_outs[D:])
    out_keep, out_recv, cout_keep, cout_recv = w_outs[:DH], outs_recv[:DH], w_outs[DH:D], outs_recv[DH:]

    (comb,) = kernel_call(
        out_kernel,
        [core, mixed, out_keep, out_recv],
        [SM] + [VM] * 3,
        [sds((r2, 3 * DH), BF)],
        flops=flops(r2, DH, D),
    )
    recv = moves.sibling(comb)
    self_mixed = (comb, recv)
    (kv,) = kernel_call(kv_kernel, [mem, w_ckv], [VM, VM], [sds(mem.shape, BF)], flops=flops(mem.shape[0], D, D))
    if moves.doubling:
        four = tie(four_last, b_before, kv, recv)
        a, b = moves.side_a(four), moves.side_b(four)
        gathered.append([four, a, b, moves.side_b(a)])
    resid_one, second, cq, cprobs, comb = kernel_call(
        lambda *refs: cross_kernel(mem_len, *refs),
        [core, tok, comb, recv, vec, w_cq, cout_keep, cout_recv, kv],
        [SM] + [VM] * 8,
        [
            sds((r2, D), F32),
            sds((r2, D), BF),
            sds((r2, DH), BF),
            sds((s2, pad, DH), BF),
            sds((r2, 3 * DH), BF),
        ],
        flops=flops(r2, D, 3 * DH),
    )
    recv = moves.sibling(comb)
    cross_mixed = (comb, recv)
    (w_in,) = assemble(gathered[2], offs, [(0, fh, 0, 0, wb, 0)], [(D, fh)])
    resid_two, third, hidden, slope = kernel_call(
        inner_kernel,
        [resid_one, comb, recv, vec, w_in],
        [VM] * 5,
        [sds((r2, D), F32), sds((r2, D), BF), sds((r2, fh), BF), sds((r2, fh), BF)],
        flops=flops(r2, D, fh),
        after=gathered[3][1:3],
    )

    def grads(body, ins, specs, ncols, extra=(), scratch=(), cost=0, after=()):
        return kernel_call(
            body,
            [offs, *ins],
            [SM, *specs],
            [sds((4 * wb, ncols), BF)] * 2 + [sds((8 * wb, ncols), BF)] + list(extra),
            [ANY] * 3 + [VM] * len(extra),
            [pltpu.VMEM((D, ncols), BF), *scratch, pltpu.SemaphoreType.DMA((16,))],
            flops=cost,
            after=after,
        )

    def step_a(parts):
        return moves.side_a(parts[2]) if moves.doubling else None

    def step_b(parts, got):
        half = 4 * wb
        return moves.side_b(parts[1] + got[half:]) if moves.doubling else None

    def plane_sum(parts, got_a, got_b):
        return parts[0].astype(F32) + got_a[: 4 * wb].astype(F32) + got_b.astype(F32) if moves.doubling else None

    def step_far(total):
        return moves.far_z(total[2 * wb :].astype(BF)) if moves.doubling else None

    def step_near(total, got):
        if not moves.doubling:
            return None
        total = total[: 2 * wb] + got.astype(F32)
        return total[:wb] + moves.near_z(total[wb:].astype(BF)).astype(F32)

    def there(*arrays):
        return [x for x in arrays if x is not None]

    d_mlpout = grads(dmlpout_kernel, [hidden, g], [VM] * 2, 2 * D, cost=flops(r2, D, fh), after=gathered[3][3:])
    a_one = step_a(d_mlpout)
    (w_mlpout,) = assemble(gathered[3], offs, [(0, D, 0, 0, 2 * wb, 0), (D, 2 * D, 0, 0, 2 * wb, wb)], [(fh, D)])
    part, comb, ginner = kernel_call(
        mlp_kernel,
        [hidden, slope, g, w_mlpout, w_in],
        [VM] * 5,
        [sds((rows, D), BF), sds((3 * rows, D), BF), sds((r2, fh), BF)],
        flops=3 * flops(r2, D, fh),
    )
    recv = moves.sibling(comb)
    d_mlpin = grads(dmlpin_kernel, [third, ginner], [VM] * 2, fh, cost=flops(r2, D, fh))
    a_two = step_a(d_mlpin)
    b_one = step_b(d_mlpout, a_one)
    output, gresid_two, gtwo, dcq, dkv, gsecond, dvec_two = kernel_call(
        cross_back_kernel,
        [core, resid_two, comb, recv, part, g, vec, w_cq, cout_keep, cout_recv, kv, cq, cprobs],
        [SM] + [VM] * 12,
        [
            sds((rows, D), BF),
            sds((r2, D), F32),
            sds((r2, D), BF),
            sds((r2, DH), BF),
            sds(kv.shape, BF),
            sds((r2, D), BF),
            sds((8, D), F32),
        ],
        scratch=[pltpu.VMEM((r2, DH), BF)],
        flops=flops(r2, D, 3 * DH),
        after=there(a_one),
    )
    recv = moves.sibling(gsecond)
    sum_one = plane_sum(d_mlpout, a_one, b_one)
    far_one = step_far(sum_one)
    b_two = step_b(d_mlpin, a_two)
    *d_cross, gmem, gmem_other = grads(
        dcross_kernel,
        [core, *cross_mixed, gtwo, second, dcq, mem, dkv, w_ckv],
        [SM] + [VM] * 8,
        4 * DH,
        [sds((seqs * pad, D), BF)] * 2,
        cost=2 * flops(mem.shape[0], D, D),
        after=there(a_two, b_one),
    )
    a_three = step_a(d_cross)
    sum_two = plane_sum(d_mlpin, a_two, b_two)
    far_two = step_far(sum_two)
    own_one = step_near(sum_one, far_one)
    gmem_recv = moves.sibling(gmem_other)
    gresid_one, gone, dpacked, gfirst, gfirst_other, dvec_one = kernel_call(
        self_back_kernel,
        [core, xhat, resid_one, gsecond, recv, gresid_two, vec, w_qkv, out_keep, out_recv, packed, probs],
        [SM] + [VM] * 11,
        [
            sds((r2, D), F32),
            sds((r2, D), BF),
            sds((r2, 3 * DH), BF),
            sds((rows, D), BF),
            sds((rows, D), BF),
            sds((8, D), F32),
        ],
        scratch=[pltpu.VMEM((r2, DH), BF)],
        flops=flops(r2, D, 4 * DH),
        after=there(far_one, b_two),
    )
    recv = moves.sibling(gfirst_other)
    b_three = step_b(d_cross, a_three)
    own_two = step_near(sum_two, far_two)
    d_self = grads(
        dself_kernel,
        [core, *self_mixed, gone, first, dpacked, dvec_two, dvec_one],
        [SM] + [VM] * 7,
        4 * DH + 128,
        scratch=[pltpu.VMEM((128, D), F32)],
        cost=flops(r2, D, 4 * DH),
        after=there(a_three, own_one, far_two),
    )
    a_four = step_a(d_self)
    sum_three = plane_sum(d_cross, a_three, b_three)
    far_three = step_far(sum_three)
    grad_tokens, grad_memory = kernel_call(
        tokens_back_kernel,
        [tok_own, gfirst, recv, gresid_one[:rows], vec, gmem, gmem_recv],
        [VM] * 7,
        [sds((rows, D), BF), sds(gmem.shape, BF)],
        after=there(b_three, own_two),
    )
    grad_memory = grad_memory.reshape(seqs, pad, D)[:, :mem_len]
    if moves.doubling:

        def own_rows(total):
            mine = lax.dynamic_slice_in_dim(total, c * wr, wr, 0)
            return mine, moves.sibling(lax.dynamic_slice_in_dim(total, (1 - c) * wr, wr, 0))

        def join(pair, *shapes, scratch=()):
            return kernel_call(
                join_kernel, [core, *pair], [SM, VM, VM], [sds(shape, F32) for shape in shapes], scratch=scratch
            )

        three = step_near(sum_three, far_three)
        sum_four = plane_sum(d_self, a_four, step_b(d_self, a_four))
        low = sum_four.astype(BF)
        four = sum_four[:wb] + moves.near_z(low[wb : 2 * wb]).astype(F32)
        four = four + moves.far_z(low[2 * wb : 3 * wb]).astype(F32) + moves.opposite_z(low[3 * wb :]).astype(F32)
        sum_mlpout = jnp.concatenate([own_one[:, :D], own_one[:, D:]], 0)
        mine, got = own_rows(own_two)
        pair = (jnp.where(c == 0, mine, got), jnp.where(c == 0, got, mine))
        parts = [p.reshape(wr, ff // (2 * hr), 1, hr) for p in pair]
        grad_in = jnp.concatenate(parts, 2).reshape(wr, ff)
        grad_cout, grad_cq, grad_ckv = join(own_rows(three), (wr, D), (wr, D), (wr, 2 * D))
        grad_out, grad_qkv, own_gains, own_biases = join(
            own_rows(four), (wr, D), (wr, 3 * D), (3, wr), (3, wr), scratch=[pltpu.VMEM((128, 128), F32)]
        )
    else:

        def placed(parts):
            own, to_b, to_a = parts
            term = jnp.concatenate([own, to_a[: 4 * wb], to_b, to_a[4 * wb :]], 0).astype(F32)
            both = jnp.stack([jnp.where(c == 0, term, 0.0), jnp.where(c == 1, term, 0.0)], 1)
            return lax.psum_scatter(both, AXES, scatter_dimension=0, tiled=True)

        def joined(total, lo, hi, groups):
            return total[:, :, lo:hi].reshape(wr, 2, groups, -1).transpose(0, 2, 1, 3).reshape(wr, -1)

        total = placed(d_cross)
        grad_cout, grad_cq, grad_ckv = (
            joined(total, 0, DH, 1),
            joined(total, DH, 2 * DH, 1),
            joined(total, 2 * DH, 4 * DH, 2),
        )
        total = placed(d_self)
        grad_out, grad_qkv = joined(total, 0, DH, 1), joined(total, DH, 4 * DH, 3)
        vectors = jnp.sum(total[:, :, 4 * DH : 4 * DH + 6], 1).T
        own_gains, own_biases = vectors[:3], vectors[3:]
        grad_in = joined(placed(d_mlpin), 0, fh, ff // (2 * hr))
        own, to_b, to_a = d_mlpout
        term = jnp.concatenate([own, to_a[: 4 * wb], to_b, to_a[4 * wb :]], 0).astype(F32)
        term = term.reshape(16, wb, 2, D).transpose(0, 2, 1, 3).reshape(moves.n // 2, 1, hr, D)
        both = jnp.concatenate([jnp.where(c == 0, term, 0.0), jnp.where(c == 1, term, 0.0)], 1)
        sum_mlpout = lax.psum_scatter(both.reshape(ff, D), AXES, scatter_dimension=0, tiled=True)

    return (
        output.reshape(tokens.shape),
        grad_tokens.reshape(tokens.shape),
        grad_memory,
        grad_qkv,
        grad_out,
        grad_cq,
        grad_ckv,
        grad_cout,
        grad_in,
        sum_mlpout,
        own_gains,
        own_biases,
    )


def solution(mesh):
    batch = P(AXES, None, None)
    rows = P(AXES, None)
    cols = P(None, AXES)
    moves = Moves(mesh)
    in_specs = (batch, batch, P(AXES), batch) + (rows,) * 7 + (cols,) * 2
    out_specs = (batch,) * 3 + (rows,) * 7 + (cols,) * 2
    return jax.shard_map(
        lambda *args: per_device(moves, *args),
        mesh=mesh,
        in_specs=in_specs,
        out_specs=out_specs,
        check_vma=False,
    )
```

time: 382 us -> 322 us (0.84); the launches traced: 376 us -> 321 us
  waiting for transfers between devices: 143 us -> 90.2 us
  local copies, waits for them, and re-layouts: 39.7 us -> 46.8 us
  starting transfers between devices: 49.8 us -> 42.9 us
  other arithmetic: 27.5 us -> 22.3 us
  Pallas kernels: 113 us -> 117 us
    ppermute x66 -> x48, waiting for transfers between devices: 143 us -> 90.2 us  [permute(): lax.ppermute(x, AXES, [(a, z * self.nf + 2 * yx + c) for a, (z, yx, c) in...]
    unnamed x125 -> x166, local copies, waits for them, and re-layouts: 17.1 us -> 35.9 us
    add x22 -> x15, other arithmetic: 12.5 us -> 4.76 us  [the longest x3 1.71 us: plane_sum(): parts[0].astype(F32) + got_a[:4 * wb].astype(F32) + got_b.astype(F32)]
    ppermute x66 -> x48, starting transfers between devices: 49.8 us -> 42.9 us  [permute(): lax.ppermute(x, AXES, [(a, z * self.nf + 2 * yx + c) for a, (z, yx, c) in...]
    concatenate x20 -> x11, other arithmetic: 8.22 us -> 13.8 us  [the longest x3 5.63 us: far_part(): return (far, jnp.concatenate([two, far], 0))]
    reshape x21 -> x3, local copies, waits for them, and re-layouts: 9.98 us -> 5.61 us  [the longest x2 3.38 us: per_device(): parts = [p.reshape(wr, ff // (2 * hr), 1, hr) for p in pair]]
    pallas_call x16 -> x29, Pallas kernels: 113 us -> 117 us  [the longest x21 117 us: kernel_call(): pl.pallas_call(run, out_shape=list(outs), in_specs=list(in_specs) + [ANY]...]
  transfers between devices with their start and end apart: 66 -> 48, of which waited for: 25 -> 19; matrix products, arithmetic and copies ran while one was open for 14% -> 9% of each run, Pallas kernels for 26% -> 32%
where the time goes in v2:
time: 322 us; the launch traced here: 321 us
  Pallas kernels  117 us (36%)
  waiting for transfers between devices  90.2 us (28%)
  local copies, waits for them, and re-layouts  46.8 us (15%)
  starting transfers between devices  42.9 us (13%)
  other arithmetic  22.3 us (7%)
    pallas_call x21, Pallas kernels, kernel_call(): pl.pallas_call(run, out_shape=list(outs), in_specs=list(in_specs) + [ANY]...  117 us
    ppermute x48, waiting for transfers between devices, permute(): lax.ppermute(x, AXES, [(a, z * self.nf + 2 * yx + c) for a, (z, yx, c) in...  90.2 us
    ppermute x48, starting transfers between devices, permute(): lax.ppermute(x, AXES, [(a, z * self.nf + 2 * yx + c) for a, (z, yx, c) in...  42.9 us
    unnamed x166, local copies, waits for them, and re-layouts  35.9 us
  transfers between devices with their start and end apart: 48, of which 19 were waited for; matrix products, arithmetic and copies ran while one was open for 9% of the time, Pallas kernels for 32%

profile of v2, /device:TPU:0, one launch (start us, length us, event | category | flops | bytes accessed | tf_op | source)
XLA Modules:
  0.0 320.9 jit_solution(17854716638960140961)
XLA Ops:
  4.8 2.1 maximum_maximum_fusion.own
  8.6 3.2 %collective-permute-done.1 = bf16[24,4736]{1,0:T(8,128)(2,1)S(1)} collective-permute-done((bf16[24,4736]{1,0:T(8,128)(2,1)S(1)}, bf16[24,4736]{1,0:T(8,128)(2,1)S(1)}, u32[]{:S(2)}, u32[]{:S(2)}) %collective-permute-start.1) | collective-permute-done | bytes 227360 | tf_op jit(solution)/shard_map/ppermute | solution.py:518
  11.9 5.0 %collective-permute-start.4 = (bf16[48,1280]{1,0:T(8,128)(2,1)S(1)}, bf16[48,1280]{1,0:T(8,128)(2,1)S(1)}, u32[]{:S(2)}, u32[]{:S(2)}) collective-permute-start(bf16[48,1280]{1,0:T(8,128)(2,1)S(1)} %maximum_select_fusion.1), channel_id=1, source_target_pairs={{0,24},{1,25},{2,26},{3,27},{4,28},{5,29},{6,30},{7,31},{8,16},{9,... | collective-permute-start | bytes 368648 | tf_op jit(solution)/shard_map/ppermute | solution.py:518
  18.5 2.6 collective-permute-done.4
  21.1 6.5 %collective-permute-done.3 = bf16[48,1280]{1,0:T(8,128)(2,1)S(1)} collective-permute-done((bf16[48,1280]{1,0:T(8,128)(2,1)S(1)}, bf16[48,1280]{1,0:T(8,128)(2,1)S(1)}, u32[]{:S(2)}, u32[]{:S(2)}) %collective-permute-start.3) | collective-permute-done | bytes 122912 | tf_op jit(solution)/shard_map/ppermute | solution.py:518
  28.4 4.9 %shard_map.220 = (bf16[512,768]{1,0:T(8,128)(2,1)S(1)}, bf16[512,768]{1,0:T(8,128)(2,1)S(1)}, bf16[1920,768]{1,0:T(8,128)(2,1)}, f32[8,768]{1,0:T(8,128)S(1)}, f32[512,768]{1,0:T(8,128)S(1)}) custom-call(bf16[1488,768]{1,0:T(8,128)(2,1)S(1)} %maximum_maximum_fusion.own, bf16[1488,768]{1,0:T(8,128)(2,1)} %collective-permute-done.other), custom_call_target="tpu_custom_call" | custom-call | flops 16000000000 | bytes 10690560 | tf_op jit(solution)/shard_map/pallas_call | solution.py:36
  39.1 9.6 %collective-permute-done.8 = bf16[48,4992]{1,0:T(8,128)(2,1)S(1)} collective-permute-done((bf16[48,4992]{1,0:T(8,128)(2,1)}, bf16[48,4992]{1,0:T(8,128)(2,1)S(1)}, u32[]{:S(2)}, u32[]{:S(2)}) %collective-permute-start.8) | collective-permute-done | bytes 479264 | tf_op jit(solution)/shard_map/ppermute | solution.py:518
  48.7 1.7 fusion.refs_0_
  55.5 13.6 %collective-permute-done.9.refs_1_ = bf16[96,1920]{1,0:T(8,128)(2,1)S(1)} collective-permute-done((bf16[96,1920]{1,0:T(8,128)(2,1)}, bf16[96,1920]{1,0:T(8,128)(2,1)S(1)}, u32[]{:S(2)}, u32[]{:S(2)}) %collective-permute-start.9) | collective-permute-done | bytes 368672 | tf_op jit(solution)/shard_map/ppermute | solution.py:518
  69.8 1.9 pad_maximum_fusion.refs_0_
  76.6 2.2 shard_map.223
  80.0 11.8 %collective-permute-done.10.refs_2_ = bf16[192,1920]{1,0:T(8,128)(2,1)S(1)} collective-permute-done((bf16[192,1920]{1,0:T(8,128)(2,1)}, bf16[192,1920]{1,0:T(8,128)(2,1)S(1)}, u32[]{:S(2)}, u32[]{:S(2)}) %collective-permute-start.10) | collective-permute-done | bytes 737312 | tf_op jit(solution)/shard_map/ppermute | solution.py:518
  92.9 6.9 %shard_map.224 = (bf16[512,768]{1,0:T(8,128)(2,1)S(1)}, bf16[512,1152]{1,0:T(8,128)(2,1)S(1)}, bf16[8,64,384]{2,1,0:T(8,128)(2,1)S(1)}, bf16[512,384]{1,0:T(8,128)(2,1)S(1)}, f32[8,768]{1,0:T(8,128)S(1)}) custom-call(f32[8,768]{1,0:T(8,128)S(1)} %get-tuple-element.78.lens, f32[512,768]{1,0:T(8,128)S(1)} %copy-done.47, ...), custom_call_target="tpu_custom_call" | custom-call | flops 30495514624 | bytes 6340608 | tf_op jit(solution)/shard_map/pallas_call | solution.py:36
  103.3 2.6 collective-permute-start.20
  106.0 1.9 pad_maximum_fusion.1.refs_0_
  113.4 2.2 shard_map.228
  117.8 1.8 pad_maximum_fusion.2.refs_0_
  121.8 1.9 fusion.10
  125.1 4.8 %shard_map.230.refs_8_.refs_2_.refs_10_ = bf16[1920,768]{1,0:T(8,128)(2,1)S(1)} custom-call(bf16[1920,768]{1,0:T(8,128)(2,1)} %get-tuple-element.88.mem.refs_7_, bf16[768,768]{1,0:T(8,128)(2,1)S(1)} %copy-done.50), custom_call_target="tpu_custom_call" | custom-call | flops 52238786560 | bytes 7077888 | tf_op jit(solution)/shard_map/pallas_call | solution.py:36
  138.8 11.5 %shard_map.231 = (f32[512,768]{1,0:T(8,128)}, bf16[512,768]{1,0:T(8,128)(2,1)S(1)}, bf16[512,384]{1,0:T(8,128)(2,1)S(1)}, bf16[8,240,384]{2,1,0:T(8,128)(2,1)}, bf16[512,1152]{1,0:T(8,128)(2,1)S(1)}) custom-call(s32[1]{0:T(128)} %bitcast.core.refs_0_.refs_1_, bf16[512,768]{1,0:T(8,128)(2,1)S(1)} %copy-done.8, bf16[512,1152]{1,0:T(8,128)(2,1)S(1)} %copy-done.28, ...), custom_call_target="tpu_custom_call" | custom-call | flops 30495514624 | bytes 12705796 | tf_op jit(solution)/shard_map/pallas_call | solution.py:36
  150.4 3.5 %shard_map.234.refs_4_.win = bf16[768,1536]{1,0:T(8,128)(2,1)S(1)} custom-call(s32[3,16]{1,0:T(4,128)S(1)} %pad_add_fusion.refs_0_.offs, bf16[192,1536]{1,0:T(8,128)(2,1)S(1)} %copy-done.4, bf16[192,1536]{1,0:T(8,128)(2,1)} %collective-permute-done.17.refs_2_, bf16[192,1536]{1,0:T(8,128)(2,1)S(1)} %copy-done.14, ...), custom_call_target="tpu_custom_call" | custom-call | flops 16000000000 | bytes 4718784 | tf_op jit(solution)/shard_map/pallas_call | solution.py:36
  155.9 8.4 %shard_map.237 = (f32[512,768]{1,0:T(8,128)S(1)}, bf16[512,768]{1,0:T(8,128)(2,1)S(1)}, bf16[512,1536]{1,0:T(8,128)(2,1)}, bf16[512,1536]{1,0:T(8,128)(2,1)}) custom-call(f32[512,768]{1,0:T(8,128)} %get-tuple-element.90.refs_0_.refs_2_, bf16[512,1152]{1,0:T(8,128)(2,1)S(1)} %get-tuple-element.91.refs_1_.refs_2_, ...), custom_call_target="tpu_custom_call" | custom-call | flops 35327352832 | bytes 11821056 | tf_op jit(solution)/shard_map/pallas_call | solution.py:36
  165.3 1.6 shard_map.238.wout
  168.3 7.3 %shard_map.239 = (bf16[256,768]{1,0:T(8,128)(2,1)S(1)}, bf16[768,768]{1,0:T(8,128)(2,1)S(1)}, bf16[512,1536]{1,0:T(8,128)(2,1)S(1)}) custom-call(bf16[512,1536]{1,0:T(8,128)(2,1)S(1)} %copy-done.59, bf16[512,1536]{1,0:T(8,128)(2,1)} %get-tuple-element.95.slope, bf16[512,768]{1,0:T(8,128)(2,1)S(1)} %copy-done.52, bf16[1536,768]{1,0:T(8,128)(2,1)} %copy-done.44, ...), custom_call_target="tpu_custom_call" | custom-call | flops 73982058496 | bytes 11796480 | tf_op jit(solution)/shard_map/pallas_call | solution.py:36
  176.1 5.2 %shard_map.240 = (bf16[192,1536]{1,0:T(8,128)(2,1)S(1)}, bf16[192,1536]{1,0:T(8,128)(2,1)S(1)}, bf16[384,1536]{1,0:T(8,128)(2,1)S(1)}) custom-call(s32[3,16]{1,0:T(4,128)S(1)} %pad_add_fusion.refs_0_.offs, bf16[512,1536]{1,0:T(8,128)(2,1)S(1)} %copy-done.59, bf16[512,768]{1,0:T(8,128)(2,1)S(1)} %copy-done.52, ...), custom_call_target="tpu_custom_call" | custom-call | flops 35327352832 | bytes 4718784 | tf_op jit(solution)/shard_map/pallas_call | solution.py:36
  182.6 5.2 %shard_map.242 = (bf16[192,1536]{1,0:T(8,128)(2,1)S(1)}, bf16[192,1536]{1,0:T(8,128)(2,1)S(1)}, bf16[384,1536]{1,0:T(8,128)(2,1)S(1)}) custom-call(s32[3,16]{1,0:T(4,128)S(1)} %pad_add_fusion.refs_0_.offs, bf16[512,768]{1,0:T(8,128)(2,1)S(1)} %get-tuple-element.109.third, bf16[512,1536]{1,0:T(8,128)(2,1)S(1)} %get-tuple-element.110.ginner), custom_call_target="tpu_custom_call" | custom-call | flops 35327352832 | bytes 4718784 | tf_op jit(solution)/shard_map/pallas_call | solution.py:36
  188.7 8.8 %collective-permute-done.25.refs_13_ = bf16[384,1536]{1,0:T(8,128)(2,1)S(1)} collective-permute-done((bf16[384,1536]{1,0:T(8,128)(2,1)S(1)}, bf16[384,1536]{1,0:T(8,128)(2,1)S(1)}, u32[]{:S(2)}, u32[]{:S(2)}) %collective-permute-start.25) | collective-permute-done | bytes 1179680 | tf_op jit(solution)/shard_map/ppermute | solution.py:518
  199.2 14.6 %shard_map.241 = (bf16[256,768]{1,0:T(8,128)(2,1)}, f32[512,768]{1,0:T(8,128)}, bf16[512,768]{1,0:T(8,128)(2,1)S(1)}, bf16[512,384]{1,0:T(8,128)(2,1)S(1)}, bf16...) custom-call(s32[1]{0:T(128)} %bitcast.core.refs_0_.refs_1_, f32[512,768]{1,0:T(8,128)} %copy-done.56, ...), custom_call_target="tpu_custom_call" | custom-call | flops 30495514624 | bytes 18038788 | tf_op jit(solution)/shard_map/pallas_call | solution.py:36
  213.9 2.6 collective-permute-done.29.refs_10_
  218.9 14.0 %shard_map.244 = (bf16[192,1536]{1,0:T(8,128)(2,1)S(1)}, bf16[192,1536]{1,0:T(8,128)(2,1)S(1)}, bf16[384,1536]{1,0:T(8,128)(2,1)S(1)}, bf16[960,768]{1,0:T(8,128)(2,1)}, bf16[960,768]{1,0:T(8,128)(2,1)}) custom-call(s32[3,16]{1,0:T(4,128)S(1)} %pad_add_fusion.refs_0_.offs, s32[1]{0:T(128)} %bitcast.core.refs_0_.refs_1_, bf16[512,1152]{1,0:T(8,128)(2,1)S(1)} %copy-done.31, ...), custom_call_target="tpu_custom_call" | custom-call | flops 88477573120 | bytes 16711876 | tf_op jit(solution)/shard_map/pallas_call | solution.py:36
  234.5 2.0 collective-permute-start.35
  236.6 11.9 %shard_map.243 = (f32[512,768]{1,0:T(8,128)}, bf16[512,768]{1,0:T(8,128)(2,1)S(1)}, bf16[512,1152]{1,0:T(8,128)(2,1)}, bf16[256,768]{1,0:T(8,128)(2,1)S(1)}, bf1...) custom-call(s32[1]{0:T(128)} %bitcast.core.refs_0_.refs_1_, f32[512,768]{1,0:T(8,128)} %copy-done.46, ...), custom_call_target="tpu_custom_call" | custom-call | flops 35327352832 | bytes 14598148 | tf_op jit(solution)/shard_map/pallas_call | solution.py:36
  248.6 2.2 collective-permute-done.35.refs_11_
  251.2 2.1 collective-permute-start.37
  253.3 4.3 %collective-permute-done.36 = bf16[48,1536]{1,0:T(8,128)(2,1)S(1)} collective-permute-done((bf16[48,1536]{1,0:T(8,128)(2,1)S(1)}, bf16[48,1536]{1,0:T(8,128)(2,1)S(1)}, u32[]{:S(2)}, u32[]{:S(2)}) %collective-permute-start.36) | collective-permute-done | bytes 147488 | tf_op jit(solution)/shard_map/ppermute | solution.py:518
  261.5 5.8 %shard_map.246 = (bf16[192,1664]{1,0:T(8,128)(2,1)S(1)}, bf16[192,1664]{1,0:T(8,128)(2,1)S(1)}, bf16[384,1664]{1,0:T(8,128)(2,1)}) custom-call(s32[3,16]{1,0:T(4,128)S(1)} %pad_add_fusion.refs_0_.offs, s32[1]{0:T(128)} %bitcast.core.refs_0_.refs_1_, bf16[512,1152]{1,0:T(8,128)(2,1)S(1)} %copy-done.29, bf16[512,1152]{1,0:T(8,128)(2,1)S(1)} %copy-done.6, ...), custom_call_target="tpu_custom_call" | custom-call | flops 35327352832 | bytes 7717060 | tf_op jit(solution)/shard_map/pallas_call | solution.py:36
  267.3 1.7 collective-permute-start.38
  273.7 1.7 collective-permute-start.44
  276.1 1.7 reshape.236
  277.8 1.7 reshape.235
  281.6 2.2 reshape.237
  283.8 3.9 %collective-permute-done.44 = bf16[96,1536]{1,0:T(8,128)(2,1)} collective-permute-done((bf16[96,1536]{1,0:T(8,128)(2,1)}, bf16[96,1536]{1,0:T(8,128)(2,1)}, u32[]{:S(2)}, u32[]{:S(2)}) %collective-permute-start.44) | collective-permute-done | bytes 294944 | tf_op jit(solution)/shard_map/ppermute | solution.py:518
  291.0 3.8 %shard_map.245 = (bf16[256,768]{1,0:T(8,128)(2,1)}, bf16[960,768]{1,0:T(8,128)(2,1)S(1)}) custom-call(bf16[256,768]{1,0:T(8,128)(2,1)S(1)} %bitcast.11, bf16[256,768]{1,0:T(8,128)(2,1)S(1)} %copy-done.58, bf16[256,768]{1,0:T(8,128)(2,1)} %collective-permute-done.31.refs_2_, f32[256,768]{1,0:T(8,128)S(1)} %slice.150.refs_3_, ...), custom_call_target="tpu_custom_call" | custom-call | flops 16000000000 | bytes 6807552 | tf_op jit(solution)/shard_map/pallas_call | solution.py:36
  294.9 1.6 copy.36
  296.5 4.3 %collective-permute-done.39 = bf16[192,1664]{1,0:T(8,128)(2,1)S(1)} collective-permute-done((bf16[192,1664]{1,0:T(8,128)(2,1)S(1)}, bf16[192,1664]{1,0:T(8,128)(2,1)S(1)}, u32[]{:S(2)}, u32[]{:S(2)}) %collective-permute-start.39) | collective-permute-done | bytes 639008 | tf_op jit(solution)/shard_map/ppermute | solution.py:518
  302.2 2.6 collective-permute-start.42
  306.8 4.4 %collective-permute-done.42 = bf16[48,1664]{1,0:T(8,128)(2,1)S(1)} collective-permute-done((bf16[48,1664]{1,0:T(8,128)(2,1)S(1)}, bf16[48,1664]{1,0:T(8,128)(2,1)S(1)}, u32[]{:S(2)}, u32[]{:S(2)}) %collective-permute-start.42) | collective-permute-done | bytes 159776 | tf_op jit(solution)/shard_map/ppermute | solution.py:518
  311.1 7.5 %collective-permute-done.41 = bf16[48,1664]{1,0:T(8,128)(2,1)S(1)} collective-permute-done((bf16[48,1664]{1,0:T(8,128)(2,1)S(1)}, bf16[48,1664]{1,0:T(8,128)(2,1)S(1)}, u32[]{:S(2)}, u32[]{:S(2)}) %collective-permute-start.41) | collective-permute-done | bytes 159776 | tf_op jit(solution)/shard_map/ppermute | solution.py:518
  (306 shorter events, 83.6 us)
Async XLA Ops:
  7.0 21.5 %collective-permute-start = (bf16[1488,768]{1,0:T(8,128)(2,1)S(1)}, bf16[1488,768]{1,0:T(8,128)(2,1)}, u32[]{:S(2)}, u32[]{:S(2)}) collective-permute-start(bf16[1488,768]{1,0:T(8,128)(2,1)S(1)} %maximum_maximum_fusion.own), channel_id=1, source_target_pairs={{0,1},{1,0},{2,3},{3,2},{4,5},{5,4},{6,7},{7,6},{8,9},{9,8},{10,11... | collective-permute-start | bytes 6856712 | tf_op jit(solution)/shard_map/ppermute | solution.py:518
  8.5 3.4 %collective-permute-start.1 = (bf16[24,4736]{1,0:T(8,128)(2,1)S(1)}, bf16[24,4736]{1,0:T(8,128)(2,1)S(1)}, u32[]{:S(2)}, u32[]{:S(2)}) collective-permute-start(bf16[24,4736]{1,0:T(8,128)(2,1)S(1)} %get-tuple-element.81), channel_id=1, source_target_pairs={{0,1},{1,0},{2,3},{3,2},{4,5},{5,4},{6,7},{7,6},{8,9},{9,8},{10,11... | collective-permute-start | bytes 681992 | tf_op jit(solution)/shard_map/ppermute | solution.py:518
  11.9 9.2 %collective-permute-start.4 = (bf16[48,1280]{1,0:T(8,128)(2,1)S(1)}, bf16[48,1280]{1,0:T(8,128)(2,1)S(1)}, u32[]{:S(2)}, u32[]{:S(2)}) collective-permute-start(bf16[48,1280]{1,0:T(8,128)(2,1)S(1)} %maximum_select_fusion.1), channel_id=1, source_target_pairs={{0,24},{1,25},{2,26},{3,27},{4,28},{5,29},{6,30},{7,31},{8,16},{9,... | collective-permute-start | bytes 368648 | tf_op jit(solution)/shard_map/ppermute | solution.py:518
  16.9 10.7 %collective-permute-start.3 = (bf16[48,1280]{1,0:T(8,128)(2,1)S(1)}, bf16[48,1280]{1,0:T(8,128)(2,1)S(1)}, u32[]{:S(2)}, u32[]{:S(2)}) collective-permute-start(bf16[48,1280]{1,0:T(8,128)(2,1)S(1)} %maximum_select_fusion.1), channel_id=1, source_target_pairs={{0,16},{1,17},{2,18},{3,19},{4,20},{5,21},{6,22},{7,23},{8,24},{9,... | collective-permute-start | bytes 368648 | tf_op jit(solution)/shard_map/ppermute | solution.py:518
  16.9 10.7 %collective-permute-start.2 = (bf16[48,1280]{1,0:T(8,128)(2,1)S(1)}, bf16[48,1280]{1,0:T(8,128)(2,1)S(1)}, u32[]{:S(2)}, u32[]{:S(2)}) collective-permute-start(bf16[48,1280]{1,0:T(8,128)(2,1)S(1)} %maximum_select_fusion.1), channel_id=1, source_target_pairs={{0,8},{1,9},{2,10},{3,11},{4,12},{5,13},{6,14},{7,15},{8,0},{9,1},... | collective-permute-start | bytes 368648 | tf_op jit(solution)/shard_map/ppermute | solution.py:518
  36.3 12.4 %collective-permute-start.8 = (bf16[48,4992]{1,0:T(8,128)(2,1)}, bf16[48,4992]{1,0:T(8,128)(2,1)S(1)}, u32[]{:S(2)}, u32[]{:S(2)}) collective-permute-start(bf16[48,4992]{1,0:T(8,128)(2,1)} %shard_map.225), channel_id=1, source_target_pairs={{0,8},{1,9},{2,10},{3,11},{4,12},{5,13},{6,14},{7,15},{8,0},{9,1},... | collective-permute-start | bytes 1437704 | tf_op jit(solution)/shard_map/ppermute | solution.py:518
  37.3 13.1 %collective-permute-start.5 = (bf16[192,1280]{1,0:T(8,128)(2,1)S(1)}, bf16[192,1280]{1,0:T(8,128)(2,1)S(1)}, u32[]{:S(2)}, u32[]{:S(2)}) collective-permute-start(bf16[192,1280]{1,0:T(8,128)(2,1)S(1)} %copy-done), channel_id=1, source_target_pairs={{0,2},{1,5},{2,0},{3,7},{4,6},{5,1},{6,4},{7,3},{8,10},{9,13},{10,... | collective-permute-start | bytes 1474568 | tf_op jit(solution)/shard_map/ppermute | solution.py:518
  51.2 17.9 %collective-permute-start.9 = (bf16[96,1920]{1,0:T(8,128)(2,1)}, bf16[96,1920]{1,0:T(8,128)(2,1)S(1)}, u32[]{:S(2)}, u32[]{:S(2)}) collective-permute-start(bf16[96,1920]{1,0:T(8,128)(2,1)} %shard_map.226), channel_id=1, source_target_pairs={{0,16},{1,17},{2,18},{3,19},{4,20},{5,21},{6,22},{7,23},{8,24},{9,... | collective-permute-start | bytes 1105928 | tf_op jit(solution)/shard_map/ppermute | solution.py:518
  52.5 23.0 %collective-permute-start.6 = (bf16[192,1280]{1,0:T(8,128)(2,1)S(1)}, bf16[192,1280]{1,0:T(8,128)(2,1)}, u32[]{:S(2)}, u32[]{:S(2)}) collective-permute-start(bf16[192,1280]{1,0:T(8,128)(2,1)S(1)} %copy-done), channel_id=1, source_target_pairs={{0,4},{1,3},{2,6},{3,1},{4,0},{5,7},{6,2},{7,5},{8,12},{9,11},{10,... | collective-permute-start | bytes 1474568 | tf_op jit(solution)/shard_map/ppermute | solution.py:518
  54.1 17.6 %collective-permute-start.7 = (bf16[192,1280]{1,0:T(8,128)(2,1)}, bf16[192,1280]{1,0:T(8,128)(2,1)S(1)}, u32[]{:S(2)}, u32[]{:S(2)}) collective-permute-start(bf16[192,1280]{1,0:T(8,128)(2,1)} %copy-done.15), channel_id=1, source_target_pairs={{0,4},{1,3},{2,6},{3,1},{4,0},{5,7},{6,2},{7,5},{8,12},{9,11},{10,... | collective-permute-start | bytes 1474568 | tf_op jit(solution)/shard_map/ppermute | solution.py:518
  69.8 33.5 %collective-permute-start.16 = (bf16[96,1536]{1,0:T(8,128)(2,1)}, bf16[96,1536]{1,0:T(8,128)(2,1)}, u32[]{:S(2)}, u32[]{:S(2)}) collective-permute-start(bf16[96,1536]{1,0:T(8,128)(2,1)} %shard_map.232), channel_id=1, source_target_pairs={{0,16},{1,17},{2,18},{3,19},{4,20},{5,21},{6,22},{7,23},{8,24},{9,... | collective-permute-start | bytes 884744 | tf_op jit(solution)/shard_map/ppermute | solution.py:518
  72.5 19.3 %collective-permute-start.10 = (bf16[192,1920]{1,0:T(8,128)(2,1)}, bf16[192,1920]{1,0:T(8,128)(2,1)S(1)}, u32[]{:S(2)}, u32[]{:S(2)}) collective-permute-start(bf16[192,1920]{1,0:T(8,128)(2,1)} %shard_map.227.refs_1_), channel_id=1, source_target_pairs={{0,2},{1,5},{2,0},{3,7},{4,6},{5,1},{6,4},{7,3},{8,10},{9,13},{10,... | collective-permute-start | bytes 2211848 | tf_op jit(solution)/shard_map/ppermute | solution.py:518
  74.0 33.8 %collective-permute-start.11 = (bf16[192,1920]{1,0:T(8,128)(2,1)}, bf16[192,1920]{1,0:T(8,128)(2,1)S(1)}, u32[]{:S(2)}, u32[]{:S(2)}) collective-permute-start(bf16[192,1920]{1,0:T(8,128)(2,1)} %shard_map.227.refs_1_), channel_id=1, source_target_pairs={{0,4},{1,3},{2,6},{3,1},{4,0},{5,7},{6,2},{7,5},{8,12},{9,11},{10,... | collective-permute-start | bytes 2211848 | tf_op jit(solution)/shard_map/ppermute | solution.py:518
  91.8 18.4 %collective-permute-start.12 = (bf16[192,1920]{1,0:T(8,128)(2,1)S(1)}, bf16[192,1920]{1,0:T(8,128)(2,1)S(1)}, u32[]{:S(2)}, u32[]{:S(2)}) collective-permute-start(bf16[192,1920]{1,0:T(8,128)(2,1)S(1)} %collective-permute-done.10.refs_2_), channel_id=1, source_target_pairs={{0,4},{1,3},{2,6},{3,1},{4,0},{5,7},{6,2},{7,5},{8,12},{9,11},{10,... | collective-permute-start | bytes 2211848 | tf_op jit(solution)/shard_map/ppermute | solution.py:518
  103.3 14.5 %collective-permute-start.20 = (bf16[96,1536]{1,0:T(8,128)(2,1)}, bf16[96,1536]{1,0:T(8,128)(2,1)}, u32[]{:S(2)}, u32[]{:S(2)}) collective-permute-start(bf16[96,1536]{1,0:T(8,128)(2,1)} %shard_map.235), channel_id=1, source_target_pairs={{0,16},{1,17},{2,18},{3,19},{4,20},{5,21},{6,22},{7,23},{8,24},{9,... | collective-permute-start | bytes 884744 | tf_op jit(solution)/shard_map/ppermute | solution.py:518
  108.7 12.4 %collective-permute-start.17 = (bf16[192,1536]{1,0:T(8,128)(2,1)}, bf16[192,1536]{1,0:T(8,128)(2,1)}, u32[]{:S(2)}, u32[]{:S(2)}) collective-permute-start(bf16[192,1536]{1,0:T(8,128)(2,1)} %shard_map.233.refs_1_), channel_id=1, source_target_pairs={{0,2},{1,5},{2,0},{3,7},{4,6},{5,1},{6,4},{7,3},{8,10},{9,13},{10,... | collective-permute-start | bytes 1769480 | tf_op jit(solution)/shard_map/ppermute | solution.py:518
  117.5 4.2 %collective-permute-start.13 = (bf16[768,384]{1,0:T(8,128)(2,1)}, bf16[768,384]{1,0:T(8,128)(2,1)}, u32[]{:S(2)}, u32[]{:S(2)}) collective-permute-start(bf16[768,384]{1,0:T(8,128)(2,1)} %slice.140), channel_id=1, source_target_pairs={{0,1},{1,0},{2,3},{3,2},{4,5},{5,4},{6,7},{7,6},{8,9},{9,8},{10,11... | collective-permute-start | bytes 1769480 | tf_op jit(solution)/shard_map/ppermute | solution.py:518
  119.6 11.9 %collective-permute-start.18 = (bf16[192,1536]{1,0:T(8,128)(2,1)S(1)}, bf16[192,1536]{1,0:T(8,128)(2,1)S(1)}, u32[]{:S(2)}, u32[]{:S(2)}) collective-permute-start(bf16[192,1536]{1,0:T(8,128)(2,1)S(1)} %copy-done.4), channel_id=1, source_target_pairs={{0,4},{1,3},{2,6},{3,1},{4,0},{5,7},{6,2},{7,5},{8,12},{9,11},{10,... | collective-permute-start | bytes 1769480 | tf_op jit(solution)/shard_map/ppermute | solution.py:518
  121.2 29.2 %collective-permute-start.19 = (bf16[192,1536]{1,0:T(8,128)(2,1)}, bf16[192,1536]{1,0:T(8,128)(2,1)}, u32[]{:S(2)}, u32[]{:S(2)}) collective-permute-start(bf16[192,1536]{1,0:T(8,128)(2,1)} %collective-permute-done.17.refs_2_), channel_id=1, source_target_pairs={{0,4},{1,3},{2,6},{3,1},{4,0},{5,7},{6,2},{7,5},{8,12},{9,11},{10,... | collective-permute-start | bytes 1769480 | tf_op jit(solution)/shard_map/ppermute | solution.py:518
  124.4 7.1 %collective-permute-start.14 = (bf16[512,1152]{1,0:T(8,128)(2,1)S(1)}, bf16[512,1152]{1,0:T(8,128)(2,1)S(1)}, u32[]{:S(2)}, u32[]{:S(2)}) collective-permute-start(bf16[512,1152]{1,0:T(8,128)(2,1)S(1)} %shard_map.229.refs_2_), channel_id=1, source_target_pairs={{0,1},{1,0},{2,3},{3,2},{4,5},{5,4},{6,7},{7,6},{8,9},{9,8},{10,11... | collective-permute-start | bytes 3538952 | tf_op jit(solution)/shard_map/ppermute | solution.py:518
  133.5 21.9 %collective-permute-start.21 = (bf16[192,1536]{1,0:T(8,128)(2,1)}, bf16[192,1536]{1,0:T(8,128)(2,1)S(1)}, u32[]{:S(2)}, u32[]{:S(2)}) collective-permute-start(bf16[192,1536]{1,0:T(8,128)(2,1)} %shard_map.236.refs_1_), channel_id=1, source_target_pairs={{0,2},{1,5},{2,0},{3,7},{4,6},{5,1},{6,4},{7,3},{8,10},{9,13},{10,... | collective-permute-start | bytes 1769480 | tf_op jit(solution)/shard_map/ppermute | solution.py:518
  134.0 21.9 %collective-permute-start.22 = (bf16[192,1536]{1,0:T(8,128)(2,1)}, bf16[192,1536]{1,0:T(8,128)(2,1)S(1)}, u32[]{:S(2)}, u32[]{:S(2)}) collective-permute-start(bf16[192,1536]{1,0:T(8,128)(2,1)} %shard_map.236.refs_1_), channel_id=1, source_target_pairs={{0,4},{1,3},{2,6},{3,1},{4,0},{5,7},{6,2},{7,5},{8,12},{9,11},{10,... | collective-permute-start | bytes 1769480 | tf_op jit(solution)/shard_map/ppermute | solution.py:518
  150.3 5.6 %collective-permute-start.15 = (bf16[512,1152]{1,0:T(8,128)(2,1)S(1)}, bf16[512,1152]{1,0:T(8,128)(2,1)S(1)}, u32[]{:S(2)}, u32[]{:S(2)}) collective-permute-start(bf16[512,1152]{1,0:T(8,128)(2,1)S(1)} %get-tuple-element.91.refs_1_.refs_2_), channel_id=1, source_target_pairs={{0,1},{1,0},{2,3},{3,2},{4,5},{5,4},{6,7},{7,6},{8,9},{9,8},{10,11... | collective-permute-start | bytes 3538952 | tf_op jit(solution)/shard_map/ppermute | solution.py:518
  155.4 9.9 %collective-permute-start.23 = (bf16[192,1536]{1,0:T(8,128)(2,1)S(1)}, bf16[192,1536]{1,0:T(8,128)(2,1)S(1)}, u32[]{:S(2)}, u32[]{:S(2)}) collective-permute-start(bf16[192,1536]{1,0:T(8,128)(2,1)S(1)} %collective-permute-done.21.refs_5_.refs_2_), channel_id=1, source_target_pairs={{0,4},{1,3},{2,6},{3,1},{4,0},{5,7},{6,2},{7,5},{8,12},{9,11},{10,... | collective-permute-start | bytes 1769480 | tf_op jit(solution)/shard_map/ppermute | solution.py:518
  175.7 22.5 %collective-permute-start.24 = (bf16[768,768]{1,0:T(8,128)(2,1)S(1)}, bf16[768,768]{1,0:T(8,128)(2,1)S(1)}, u32[]{:S(2)}, u32[]{:S(2)}) collective-permute-start(bf16[768,768]{1,0:T(8,128)(2,1)S(1)} %get-tuple-element.97.refs_2_), channel_id=1, source_target_pairs={{0,1},{1,0},{2,3},{3,2},{4,5},{5,4},{6,7},{7,6},{8,9},{9,8},{10,11... | collective-permute-start | bytes 3538952 | tf_op jit(solution)/shard_map/ppermute | solution.py:518
  181.3 16.3 %collective-permute-start.25 = (bf16[384,1536]{1,0:T(8,128)(2,1)S(1)}, bf16[384,1536]{1,0:T(8,128)(2,1)S(1)}, u32[]{:S(2)}, u32[]{:S(2)}) collective-permute-start(bf16[384,1536]{1,0:T(8,128)(2,1)S(1)} %get-tuple-element.101), channel_id=1, source_target_pairs={{0,2},{1,5},{2,0},{3,7},{4,6},{5,1},{6,4},{7,3},{8,10},{9,13},{10,... | collective-permute-start | bytes 3538952 | tf_op jit(solution)/shard_map/ppermute | solution.py:518
  187.9 28.7 %collective-permute-start.29 = (bf16[384,1536]{1,0:T(8,128)(2,1)S(1)}, bf16[384,1536]{1,0:T(8,128)(2,1)S(1)}, u32[]{:S(2)}, u32[]{:S(2)}) collective-permute-start(bf16[384,1536]{1,0:T(8,128)(2,1)S(1)} %get-tuple-element.112), channel_id=1, source_target_pairs={{0,2},{1,5},{2,0},{3,7},{4,6},{5,1},{6,4},{7,3},{8,10},{9,13},{10,... | collective-permute-start | bytes 3538952 | tf_op jit(solution)/shard_map/ppermute | solution.py:518
  197.6 19.5 %collective-permute-start.27 = (bf16[192,1536]{1,0:T(8,128)(2,1)S(1)}, bf16[192,1536]{1,0:T(8,128)(2,1)S(1)}, u32[]{:S(2)}, u32[]{:S(2)}) collective-permute-start(bf16[192,1536]{1,0:T(8,128)(2,1)S(1)} %slice_add_fusion.6), channel_id=1, source_target_pairs={{0,4},{1,3},{2,6},{3,1},{4,0},{5,7},{6,2},{7,5},{8,12},{9,11},{10,... | collective-permute-start | bytes 1769480 | tf_op jit(solution)/shard_map/ppermute | solution.py:518
  213.8 22.8 %collective-permute-start.26 = (bf16[512,768]{1,0:T(8,128)(2,1)S(1)}, bf16[512,768]{1,0:T(8,128)(2,1)S(1)}, u32[]{:S(2)}, u32[]{:S(2)}) collective-permute-start(bf16[512,768]{1,0:T(8,128)(2,1)S(1)} %get-tuple-element.103.refs_3_), channel_id=1, source_target_pairs={{0,1},{1,0},{2,3},{3,2},{4,5},{5,4},{6,7},{7,6},{8,9},{9,8},{10,11... | collective-permute-start | bytes 2359304 | tf_op jit(solution)/shard_map/ppermute | solution.py:518
  216.6 17.6 %collective-permute-start.30 = (bf16[192,1536]{1,0:T(8,128)(2,1)S(1)}, bf16[192,1536]{1,0:T(8,128)(2,1)S(1)}, u32[]{:S(2)}, u32[]{:S(2)}) collective-permute-start(bf16[192,1536]{1,0:T(8,128)(2,1)S(1)} %slice_add_fusion.5), channel_id=1, source_target_pairs={{0,4},{1,3},{2,6},{3,1},{4,0},{5,7},{6,2},{7,5},{8,12},{9,11},{10,... | collective-permute-start | bytes 1769480 | tf_op jit(solution)/shard_map/ppermute | solution.py:518
  217.8 18.8 %collective-permute-start.28 = (bf16[96,1536]{1,0:T(8,128)(2,1)S(1)}, bf16[96,1536]{1,0:T(8,128)(2,1)S(1)}, u32[]{:S(2)}, u32[]{:S(2)}) collective-permute-start(bf16[96,1536]{1,0:T(8,128)(2,1)S(1)} %slice.248), channel_id=1, source_target_pairs={{0,16},{1,17},{2,18},{3,19},{4,20},{5,21},{6,22},{7,23},{8,24},{9,... | collective-permute-start | bytes 884744 | tf_op jit(solution)/shard_map/ppermute | solution.py:518
  232.9 58.1 %collective-permute-start.32 = (bf16[960,768]{1,0:T(8,128)(2,1)}, bf16[960,768]{1,0:T(8,128)(2,1)}, u32[]{:S(2)}, u32[]{:S(2)}) collective-permute-start(bf16[960,768]{1,0:T(8,128)(2,1)} %get-tuple-element.121), channel_id=1, source_target_pairs={{0,1},{1,0},{2,3},{3,2},{4,5},{5,4},{6,7},{7,6},{8,9},{9,8},{10,11... | collective-permute-start | bytes 4423688 | tf_op jit(solution)/shard_map/ppermute | solution.py:518
  233.0 27.0 %collective-permute-start.33 = (bf16[384,1536]{1,0:T(8,128)(2,1)S(1)}, bf16[384,1536]{1,0:T(8,128)(2,1)S(1)}, u32[]{:S(2)}, u32[]{:S(2)}) collective-permute-start(bf16[384,1536]{1,0:T(8,128)(2,1)S(1)} %get-tuple-element.123), channel_id=1, source_target_pairs={{0,2},{1,5},{2,0},{3,7},{4,6},{5,1},{6,4},{7,3},{8,10},{9,13},{10,... | collective-permute-start | bytes 3538952 | tf_op jit(solution)/shard_map/ppermute | solution.py:518
  234.5 16.3 %collective-permute-start.35 = (bf16[96,1536]{1,0:T(8,128)(2,1)S(1)}, bf16[96,1536]{1,0:T(8,128)(2,1)S(1)}, u32[]{:S(2)}, u32[]{:S(2)}) collective-permute-start(bf16[96,1536]{1,0:T(8,128)(2,1)S(1)} %slice.247), channel_id=1, source_target_pairs={{0,16},{1,17},{2,18},{3,19},{4,20},{5,21},{6,22},{7,23},{8,24},{9,... | collective-permute-start | bytes 884744 | tf_op jit(solution)/shard_map/ppermute | solution.py:518
  248.5 42.5 %collective-permute-start.31 = (bf16[256,768]{1,0:T(8,128)(2,1)S(1)}, bf16[256,768]{1,0:T(8,128)(2,1)}, u32[]{:S(2)}, u32[]{:S(2)}) collective-permute-start(bf16[256,768]{1,0:T(8,128)(2,1)S(1)} %get-tuple-element.114), channel_id=1, source_target_pairs={{0,1},{1,0},{2,3},{3,2},{4,5},{5,4},{6,7},{7,6},{8,9},{9,8},{10,11... | collective-permute-start | bytes 1179656 | tf_op jit(solution)/shard_map/ppermute | solution.py:518
  250.9 6.6 %collective-permute-start.36 = (bf16[48,1536]{1,0:T(8,128)(2,1)S(1)}, bf16[48,1536]{1,0:T(8,128)(2,1)S(1)}, u32[]{:S(2)}, u32[]{:S(2)}) collective-permute-start(bf16[48,1536]{1,0:T(8,128)(2,1)S(1)} %slice.251), channel_id=1, source_target_pairs={{0,8},{1,9},{2,10},{3,11},{4,12},{5,13},{6,14},{7,15},{8,0},{9,1},... | collective-permute-start | bytes 442376 | tf_op jit(solution)/shard_map/ppermute | solution.py:518
  251.2 8.0 %collective-permute-start.37 = (bf16[48,1536]{1,0:T(8,128)(2,1)S(1)}, bf16[48,1536]{1,0:T(8,128)(2,1)S(1)}, u32[]{:S(2)}, u32[]{:S(2)}) collective-permute-start(bf16[48,1536]{1,0:T(8,128)(2,1)S(1)} %slice.250), channel_id=1, source_target_pairs={{0,8},{1,9},{2,10},{3,11},{4,12},{5,13},{6,14},{7,15},{8,0},{9,1},... | collective-permute-start | bytes 442376 | tf_op jit(solution)/shard_map/ppermute | solution.py:518
  257.6 17.8 %collective-permute-start.47 = (f32[24,1536]{1,0:T(8,128)S(1)}, f32[24,1536]{1,0:T(8,128)S(1)}, u32[]{:S(2)}, u32[]{:S(2)}) collective-permute-start(f32[24,1536]{1,0:T(8,128)S(1)} %constant_dynamic-slice_fusion), channel_id=1, source_target_pairs={{0,1},{1,0},{2,3},{3,2},{4,5},{5,4},{6,7},{7,6},{8,9},{9,8},{10,11... | collective-permute-start | bytes 442376 | tf_op jit(solution)/shard_map/ppermute | solution.py:518
  260.1 10.6 %collective-permute-start.34 = (bf16[192,1536]{1,0:T(8,128)(2,1)S(1)}, bf16[192,1536]{1,0:T(8,128)(2,1)S(1)}, u32[]{:S(2)}, u32[]{:S(2)}) collective-permute-start(bf16[192,1536]{1,0:T(8,128)(2,1)S(1)} %slice_add_fusion.4), channel_id=1, source_target_pairs={{0,4},{1,3},{2,6},{3,1},{4,0},{5,7},{6,2},{7,5},{8,12},{9,11},{10,... | collective-permute-start | bytes 1769480 | tf_op jit(solution)/shard_map/ppermute | solution.py:518
  267.3 21.8 %collective-permute-start.38 = (bf16[384,1664]{1,0:T(8,128)(2,1)}, bf16[384,1664]{1,0:T(8,128)(2,1)}, u32[]{:S(2)}, u32[]{:S(2)}) collective-permute-start(bf16[384,1664]{1,0:T(8,128)(2,1)} %get-tuple-element.132), channel_id=1, source_target_pairs={{0,2},{1,5},{2,0},{3,7},{4,6},{5,1},{6,4},{7,3},{8,10},{9,13},{10,... | collective-permute-start | bytes 3833864 | tf_op jit(solution)/shard_map/ppermute | solution.py:518
  273.7 14.0 %collective-permute-start.44 = (bf16[96,1536]{1,0:T(8,128)(2,1)}, bf16[96,1536]{1,0:T(8,128)(2,1)}, u32[]{:S(2)}, u32[]{:S(2)}) collective-permute-start(bf16[96,1536]{1,0:T(8,128)(2,1)} %slice.246), channel_id=1, source_target_pairs={{0,16},{1,17},{2,18},{3,19},{4,20},{5,21},{6,22},{7,23},{8,24},{9,... | collective-permute-start | bytes 884744 | tf_op jit(solution)/shard_map/ppermute | solution.py:518
  289.0 7.5 %collective-permute-start.45 = (bf16[48,1536]{1,0:T(8,128)(2,1)S(1)}, bf16[48,1536]{1,0:T(8,128)(2,1)S(1)}, u32[]{:S(2)}, u32[]{:S(2)}) collective-permute-start(bf16[48,1536]{1,0:T(8,128)(2,1)S(1)} %slice.249), channel_id=1, source_target_pairs={{0,8},{1,9},{2,10},{3,11},{4,12},{5,13},{6,14},{7,15},{8,0},{9,1},... | collective-permute-start | bytes 442376 | tf_op jit(solution)/shard_map/ppermute | solution.py:518
  290.4 10.5 %collective-permute-start.39 = (bf16[192,1664]{1,0:T(8,128)(2,1)S(1)}, bf16[192,1664]{1,0:T(8,128)(2,1)S(1)}, u32[]{:S(2)}, u32[]{:S(2)}) collective-permute-start(bf16[192,1664]{1,0:T(8,128)(2,1)S(1)} %slice_add_fusion), channel_id=1, source_target_pairs={{0,4},{1,3},{2,6},{3,1},{4,0},{5,7},{6,2},{7,5},{8,12},{9,11},{10,... | collective-permute-start | bytes 1916936 | tf_op jit(solution)/shard_map/ppermute | solution.py:518
  302.2 8.9 %collective-permute-start.42 = (bf16[48,1664]{1,0:T(8,128)(2,1)S(1)}, bf16[48,1664]{1,0:T(8,128)(2,1)S(1)}, u32[]{:S(2)}, u32[]{:S(2)}) collective-permute-start(bf16[48,1664]{1,0:T(8,128)(2,1)S(1)} %get-tuple-element.151), channel_id=1, source_target_pairs={{0,24},{1,25},{2,26},{3,27},{4,28},{5,29},{6,30},{7,31},{8,16},{9,... | collective-permute-start | bytes 479240 | tf_op jit(solution)/shard_map/ppermute | solution.py:518
  304.8 13.8 %collective-permute-start.41 = (bf16[48,1664]{1,0:T(8,128)(2,1)S(1)}, bf16[48,1664]{1,0:T(8,128)(2,1)S(1)}, u32[]{:S(2)}, u32[]{:S(2)}) collective-permute-start(bf16[48,1664]{1,0:T(8,128)(2,1)S(1)} %get-tuple-element.152), channel_id=1, source_target_pairs={{0,16},{1,17},{2,18},{3,19},{4,20},{5,21},{6,22},{7,23},{8,24},{9,... | collective-permute-start | bytes 479240 | tf_op jit(solution)/shard_map/ppermute | solution.py:518
  305.6 13.0 %collective-permute-start.40 = (bf16[48,1664]{1,0:T(8,128)(2,1)S(1)}, bf16[48,1664]{1,0:T(8,128)(2,1)S(1)}, u32[]{:S(2)}, u32[]{:S(2)}) collective-permute-start(bf16[48,1664]{1,0:T(8,128)(2,1)S(1)} %get-tuple-element.150), channel_id=1, source_target_pairs={{0,8},{1,9},{2,10},{3,11},{4,12},{5,13},{6,14},{7,15},{8,0},{9,1},... | collective-permute-start | bytes 479240 | tf_op jit(solution)/shard_map/ppermute | solution.py:518
  306.7 12.1 %collective-permute-start.46 = (f32[24,1536]{1,0:T(8,128)S(1)}, f32[24,1536]{1,0:T(8,128)S(1)}, u32[]{:S(2)}, u32[]{:S(2)}) collective-permute-start(f32[24,1536]{1,0:T(8,128)S(1)} %get-tuple-element.161), channel_id=1, source_target_pairs={{0,1},{1,0},{2,3},{3,2},{4,5},{5,4},{6,7},{7,6},{8,9},{9,8},{10,11... | collective-permute-start | bytes 442376 | tf_op jit(solution)/shard_map/ppermute | solution.py:518
  318.7 1.5 collective-permute-start.43
  (82 other events, 283.9 us)

commit v3 on v2

v3 whole, which is shorter than its diff:
```python
import jax
import jax.numpy as jnp
import numpy as np
from jax import lax
from jax.experimental import pallas as pl
from jax.experimental.pallas import tpu as pltpu
from jax.sharding import PartitionSpec as P

AXES = ("dp", "fsdp")
HEADS = 12
HALF = HEADS // 2
HEAD = 64
D = 768
DH = D // 2
LEN = 64
EPS = 1e-06
NEG = -1e30
SCALE = HEAD ** (-0.5)
F32 = jnp.float32
BF = jnp.bfloat16
VMEM_LIMIT = 20 << 20

VM = pl.BlockSpec(memory_space=pltpu.VMEM)
SM = pl.BlockSpec(memory_space=pltpu.SMEM)
ANY = pl.BlockSpec(memory_space=pl.ANY)


def sds(shape, dtype):
    return jax.ShapeDtypeStruct(shape, dtype)


STAGE = VM


class Staged:
    def __init__(self, ref, copy):
        self.ref, self.copy, self.waited = ref, copy, False
        self.shape = ref.shape

    def ready(self):
        if not self.waited:
            self.copy.wait()
            self.waited = True
        return self.ref


PENDING = {}


def flush(*refs):
    for r in refs:
        if id(r) in PENDING:
            PENDING[id(r)].start()
            PENDING[id(r)] = None


def ready(*refs):
    out = [r.ready() if isinstance(r, Staged) else r for r in refs]
    return out[0] if len(out) == 1 else out


def kernel_call(body, ins, in_specs, outs, out_specs=None, scratch=(), cost=5, after=(), limit=None):
    n, skip, m, k = len(ins), len(after), len(outs), len(scratch)
    out_specs = [VM] * m if out_specs is None else list(out_specs)
    staged_in = [i for i, spec in enumerate(in_specs) if spec == 'stage']
    staged_out = [i for i, spec in enumerate(out_specs) if spec == 'stage']
    buffers = [pltpu.VMEM(ins[i].shape, ins[i].dtype) for i in staged_in]
    buffers += [pltpu.VMEM(outs[i].shape, outs[i].dtype) for i in staged_out]
    extra = [*buffers, pltpu.SemaphoreType.DMA((len(buffers),))] if buffers else []

    def run(*refs):
        ins, outs = list(refs[:n]), list(refs[n + skip : n + skip + m])
        own = refs[n + skip + m : n + skip + m + k]
        PENDING.clear()
        if not buffers:
            body(*ins, *outs, *own)
            return
        held, sems = refs[n + skip + m + k : -1], refs[-1]
        for j, i in enumerate(staged_in):
            copy = pltpu.make_async_copy(ins[i], held[j], sems.at[j])
            copy.start()
            ins[i] = Staged(held[j], copy)
        copies = []
        for j, i in enumerate(staged_out, len(staged_in)):
            copies.append(pltpu.make_async_copy(held[j], outs[i], sems.at[j]))
            outs[i] = held[j]
            PENDING[id(held[j])] = copies[-1]
        body(*ins, *outs, *own)
        ready(*ins)
        for cp in PENDING.values():
            if cp is not None:
                cp.start()
        for cp in copies:
            cp.wait()

    place = lambda spec: ANY if spec == 'stage' else spec
    return pl.pallas_call(
        run,
        out_shape=list(outs),
        in_specs=[place(spec) for spec in in_specs] + [ANY] * skip,
        out_specs=[place(spec) for spec in out_specs],
        scratch_shapes=[*scratch, *extra],
        compiler_params=pltpu.CompilerParams(vmem_limit_bytes=limit or VMEM_LIMIT),
        cost_estimate=pl.CostEstimate(flops=cost * 16 * 10**9, bytes_accessed=0, transcendentals=0),
    )(*ins, *after)


def tie(x, *earlier):
    return pl.pallas_call(
        lambda *refs: None,
        out_shape=sds(x.shape, x.dtype),
        in_specs=[ANY] * (1 + len(earlier)),
        out_specs=ANY,
        input_output_aliases={0: 0},
        compiler_params=pltpu.CompilerParams(vmem_limit_bytes=1 << 20),
        cost_estimate=pl.CostEstimate(flops=0, bytes_accessed=0, transcendentals=0),
    )(x, *earlier)


def nn(a, b):
    return lax.dot_general(a, b, (((1,), (0,)), ((), ())), preferred_element_type=F32)


def nt(a, b):
    return lax.dot_general(a, b, (((1,), (1,)), ((), ())), preferred_element_type=F32)


def tn(a, b):
    return lax.dot_general(a, b, (((0,), (0,)), ((), ())), preferred_element_type=F32)


def normalise(v):
    mean = jnp.mean(v, -1, keepdims=True)
    cen = v - mean
    inv = lax.rsqrt(jnp.mean(cen * cen, -1, keepdims=True) + EPS)
    return cen * inv, inv


def norm_back(v, gain, dy):
    xhat, inv = normalise(v)
    dxh = dy * gain
    m1 = jnp.mean(dxh, -1, keepdims=True)
    m2 = jnp.mean(dxh * xhat, -1, keepdims=True)
    dx = inv * (dxh - m1 - xhat * m2)
    return dx, jnp.sum(dy * xhat, 0, keepdims=True), jnp.sum(dy, 0, keepdims=True)


def head_of_lane(rows):
    return lax.shift_right_logical(lax.broadcasted_iota(jnp.int32, (rows, DH), 1), 6)


def spread(q):
    head = head_of_lane(1)
    parts = [q * (head == h).astype(F32).astype(q.dtype) for h in range(HALF)]
    return jnp.concatenate(parts, 0)


def fold(o):
    head = head_of_lane(LEN)
    total = jnp.where(head == 0, o[:LEN], 0.0)
    for h in range(1, HALF):
        total = jnp.where(head == h, o[h * LEN : (h + 1) * LEN], total)
    return total


def attend(q, k, v, allowed):
    st = nt(k, spread(q)) * SCALE
    st = jnp.where(allowed, st, NEG)
    e = jnp.exp(st - jnp.max(st, 0, keepdims=True))
    p = (e * (1.0 / jnp.sum(e, 0, keepdims=True))).astype(BF)
    return p, fold(tn(p, v)).astype(BF)


def attend_back(g, q, k, v, p):
    gs, qs = spread(g), spread(q)
    dp = nt(v, gs)
    pf = p.astype(F32)
    t = pf * dp
    ds = (t - pf * jnp.sum(t, 0, keepdims=True)).astype(BF)
    dq = (fold(tn(ds, k)) * SCALE).astype(BF)
    dk = (nn(ds, qs) * SCALE).astype(BF)
    dv = nn(p, gs).astype(BF)
    return dq, dk, dv


def seq_rows(s):
    return pl.ds(pl.multiple_of(s * LEN, LEN), LEN)


def half_lanes(c):
    return pl.ds(pl.multiple_of(c * DH, DH), DH)


def loop(n, body, unroll=1):
    def step(i, carry):
        body(i)
        return carry

    lax.fori_loop(0, n, step, 0, unroll=unroll)


class Rows:
    def __init__(self, pieces, offs_ref, which, cols, targets, sems):
        blk = pieces[0].shape[0] // 4
        self.copies = []
        for i, (lo, hi, o, step, shift) in enumerate(cols):
            for q in range(4):
                for r in range(4):
                    row = pl.multiple_of(offs_ref[which, q * 4 + r] * step + shift, 16)
                    self.copies.append(
                        pltpu.make_async_copy(
                            pieces[q].at[pl.ds(r * blk, blk), pl.ds(lo, hi - lo)],
                            targets[o].at[pl.ds(row, blk), :],
                            sems.at[i * 16 + q * 4 + r],
                        )
                    )
        for cp in self.copies:
            cp.start()

    def wait(self):
        for cp in self.copies:
            cp.wait()


def place_rows(pieces, offs, which, cols, shape):
    def body(offs_ref, *refs):
        Rows(refs[:4], offs_ref, which, cols, refs[4:5], refs[5]).wait()

    return kernel_call(
        body,
        [offs, *pieces],
        [SM] + [ANY] * 4,
        [sds(shape, BF)],
        [VM],
        [pltpu.SemaphoreType.DMA((16 * len(cols),))],
        cost=1,
    )[0]


def out_rows(pieces, offs, lo):
    blk = pieces[0].shape[0] // 4
    return place_rows(pieces, offs, 1, [(lo, lo + DH, 0, blk, 0)], (16 * blk, DH))


def send_out(dw, offs_ref, outs, sems):
    own, to_b, to_a = outs
    blk = dw.shape[0] // 16
    copies = []
    for q, (dst, base) in enumerate(((own, 0), (to_a, 0), (to_b, 0), (to_a, 4))):
        for r in range(4):
            row = pl.multiple_of(offs_ref[0, q * 4 + r] * blk, 16)
            copies.append(
                pltpu.make_async_copy(
                    dw.at[pl.ds(row, blk), :],
                    dst.at[pl.ds((base + r) * blk, blk), :],
                    sems.at[q * 4 + r],
                )
            )
    for cp in copies:
        cp.start()
    for cp in copies:
        cp.wait()


def pack_kernel(core, qkv, out, cq, ckv, cout, win, gains, biases, keep, send, vecs):
    c = core[0]
    qkv, out, cq, ckv, cout, win, gains, biases = ready(qkv, out, cq, ckv, cout, win, gains, biases)
    vecs[...] = jnp.zeros_like(vecs)
    vecs[0:3, 0:24] = gains[...].astype(F32)
    vecs[3:6, 0:24] = biases[...].astype(F32)
    rows = keep.shape[0]
    wide = jnp.transpose(vecs[...])[:rows].astype(BF)
    for dst, which in ((keep, c), (send, 1 - c)):
        at = 0
        for w, groups in ((qkv, 3), (out, 1), (None, 0), (cout, 1), (cq, 1), (ckv, 2)):
            if w is None:
                dst[:, at : at + 128] = wide
                at += 128
            for k in range(groups):
                lanes = pl.ds(pl.multiple_of(k * D + which * DH, 128), DH)
                dst[:, at : at + DH] = w[:, lanes]
                at += DH
    hr = 96
    for k in range(win.shape[1] // (2 * hr)):
        first = win[:, 2 * k * hr : (2 * k + 1) * hr]
        second = win[:, (2 * k + 1) * hr : (2 * k + 2) * hr]
        keep[:, at + k * hr : at + (k + 1) * hr] = jnp.where(c == 0, first, second)
        send[:, at + k * hr : at + (k + 1) * hr] = jnp.where(c == 0, second, first)


def order_kernel(core, keep, got, wout, one, two, rest):
    c = core[0]
    keep, got, wout = ready(keep, got, wout)
    rows = keep.shape[0]
    at = 0
    for dst in (one, two, rest):
        width = min(dst.shape[1], keep.shape[1] - at)
        a, b = keep[:, at : at + width], got[:, at : at + width]
        dst[0:rows, 0:width] = jnp.where(c == 0, a, b)
        dst[rows:, 0:width] = jnp.where(c == 0, b, a)
        at += width
    rest[:, width : width + D] = wout[0 : 2 * rows, :]
    rest[:, width + D :] = wout[2 * rows :, :]


def cat(parts, after=()):
    shape = (sum(p.shape[0] for p in parts), parts[0].shape[1])
    n = len(parts)

    def body(*refs):
        held, sems = refs[n + 1 :]
        copies, at = [], 0
        for i, r in enumerate(refs[:n]):
            copies.append(pltpu.make_async_copy(r, held.at[pl.ds(at, r.shape[0]), :], sems.at[i]))
            at += r.shape[0]
        for cp in copies:
            cp.start()
        for cp in copies:
            cp.wait()
        out = pltpu.make_async_copy(held, refs[n], sems.at[n])
        out.start()
        out.wait()

    scratch = [pltpu.VMEM(shape, BF), pltpu.SemaphoreType.DMA((n + 1,))]
    return kernel_call(body, parts, [ANY] * n, [sds(shape, BF)], [ANY], scratch, cost=1, after=after)[0]


def split_cat(first, second, after=()):
    rows, width = first.shape[0], first.shape[1] // 2

    def body(*refs):
        held, sems = refs[4:]
        copies = []
        for i in range(2):
            copies.append(pltpu.make_async_copy(refs[i], held.at[pl.ds(i * rows, rows), :], sems.at[i]))
        for cp in copies:
            cp.start()
        for cp in copies:
            cp.wait()
        copies = []
        for j in range(2):
            copies.append(pltpu.make_async_copy(held.at[:, pl.ds(j * width, width)], refs[2 + j], sems.at[2 + j]))
        for cp in copies:
            cp.start()
        for cp in copies:
            cp.wait()

    outs = [sds((2 * rows, width), BF)] * 2
    scratch = [pltpu.VMEM((2 * rows, 2 * width), BF), pltpu.SemaphoreType.DMA((4,))]
    return kernel_call(body, [first, second], [ANY] * 2, outs, [ANY] * 2, scratch, cost=1, after=after)


def prepare_kernel(lens, tok_own, tok_other, cot_own, cot_other, mem_own, mem_other, tok, g, mem, xhat):
    tok_own, tok_other = ready(tok_own, tok_other)
    rows = tok.shape[0] // 2
    seqs, length = mem_own.shape[0], mem_own.shape[1]
    pad = mem.shape[0] // (2 * seqs)
    for b, src in ((0, tok_own), (1, tok_other)):
        tok[b * rows : (b + 1) * rows, :] = src[...]
    flush(tok)

    def norm(s):
        xhat[seq_rows(s), :] = normalise(tok[seq_rows(s), :].astype(F32))[0]

    loop(2 * seqs, norm)
    flush(xhat)
    mem_own, mem_other = ready(mem_own, mem_other)
    for b, src in ((0, mem_own), (1, mem_other)):
        for s in range(seqs):
            at = (b * seqs + s) * pad
            mem[at + length - length % 16 : at + pad, :] = jnp.zeros((pad - length + length % 16, D), BF)
            mem[at : at + length, :] = src[s]
    flush(mem)
    cot_own, cot_other = ready(cot_own, cot_other)
    place = lax.broadcasted_iota(jnp.int32, (LEN, D), 0)
    for b, src in ((0, cot_own), (1, cot_other)):
        for s in range(seqs):
            at = (b * seqs + s) * LEN
            live = (place < lens[b * seqs + s]).astype(F32)
            g[at : at + LEN, :] = (src[s * LEN : (s + 1) * LEN, :].astype(F32) * live).astype(BF)


def self_kernel(lens, core, offs, a, b, ab, own, xhat, keep, back, first, packed, probs, comb, vec, wqkv, gcol, sems):
    c = core[0]
    blk = D // 16
    rows = Rows((own, a, b, ab), offs, 0, [(4 * DH, 4 * DH + 128, 1, blk, 0), (0, 3 * DH, 0, blk, 0)], (wqkv, gcol), sems)
    rows.wait()
    flush(wqkv)
    xhat = ready(xhat)
    vec[...] = jnp.transpose(gcol[...].astype(F32))[:8]
    gain, bias = vec[0:1], vec[3:4]

    def norm(s):
        first[seq_rows(s), :] = (xhat[seq_rows(s), :] * gain + bias).astype(BF)

    loop(8, norm)
    flush(first)

    def proj(b):
        rows = pl.ds(pl.multiple_of(b * 256, 256), 256)
        packed[rows, :] = nn(first[rows, :], wqkv[...]).astype(BF)

    loop(2, proj)
    flush(packed)
    key = lax.broadcasted_iota(jnp.int32, (LEN, DH), 0)
    query = lax.broadcasted_iota(jnp.int32, (LEN, DH), 1) & (LEN - 1)

    def att(s):
        allowed = (key <= query) & (key < lens[s])
        rows = seq_rows(s)
        p, m = attend(packed[rows, 0:DH], packed[rows, DH : 2 * DH], packed[rows, 2 * DH :], allowed)
        probs[s] = p
        comb[rows, D:] = m

    loop(8, att, 2)
    flush(probs)
    keep, back = ready(keep, back)
    comb[:, half_lanes(c)] = nn(comb[:, D:], keep[:DH, :]).astype(BF)
    comb[:, half_lanes(1 - c)] = nn(comb[:, D:], back[DH:, :]).astype(BF)


def kv_kernel(offs, a, b, ab, own, mem, kv, wckv, wcq, sems):
    blk = D // 16
    rows = Rows((own, a, b, ab), offs, 0, [(2 * DH, 4 * DH, 0, blk, 0), (DH, 2 * DH, 1, blk, 0)], (wckv, wcq), sems)
    mem = ready(mem)
    rows.wait()
    flush(wckv, wcq)

    def step(b):
        rows = pl.ds(pl.multiple_of(b * 480, 480), 480)
        kv[rows, :] = nn(mem[rows, :], wckv[...]).astype(BF)

    loop(mem.shape[0] // 480, step)


def swapped(s):
    return pl.ds(pl.multiple_of(((s + 4) & 7) * LEN, LEN), LEN)


def cross_kernel(mem_len, core, vec, tok, part, recv, wcq, kv, keep, back, resid, second, cq, probs, comb):
    c = core[0]
    vec, tok, part, recv = ready(vec, tok, part, recv)
    gain, bias = vec[1:2], vec[4:5]

    def norm(s):
        rows = seq_rows(s)
        both = part[rows, 0:D].astype(F32) + recv[swapped(s), 0:D].astype(F32)
        v = tok[rows, :].astype(F32) + both
        resid[rows, :] = v
        xhat, _ = normalise(v)
        second[rows, :] = (xhat * gain + bias).astype(BF)

    loop(8, norm)
    flush(resid, second)
    wcq = ready(wcq)
    cq[...] = nn(second[...], wcq[...]).astype(BF)
    flush(cq)
    kv = ready(kv)
    pad = probs.shape[1]
    allowed = lax.broadcasted_iota(jnp.int32, (pad, DH), 0) < mem_len

    def att(s):
        rows = seq_rows(s)
        keys = pl.ds(pl.multiple_of(s * pad, 16), pad)
        p, m = attend(cq[rows, :], kv[keys, 0:DH], kv[keys, DH:], allowed)
        probs[s] = p
        comb[rows, D:] = m

    loop(8, att, 2)
    flush(probs)
    keep, back = ready(keep, back)
    comb[:, half_lanes(c)] = nn(comb[:, D:], keep[:DH, :]).astype(BF)
    comb[:, half_lanes(1 - c)] = nn(comb[:, D:], back[DH:, :]).astype(BF)


def keys_and_cross_kernel(
    mem_len, offs, a, b, ab, own, mem, core, vec, tok, part, recv, keep, back, kv, wckv, wcq, resid, second, cq, probs, comb, sems
):
    kv_kernel(offs, a, b, ab, own, mem, kv, wckv, wcq, sems)
    cross_kernel(mem_len, core, vec, tok, part, recv, wcq, kv, keep, back, resid, second, cq, probs, comb)


def inner_kernel(resid, part, recv, vec, win, resid_two, third, hidden, slope):
    resid, part, recv, vec = ready(resid, part, recv, vec)
    gain, bias = vec[2:3], vec[5:6]

    def norm(s):
        rows = seq_rows(s)
        both = part[rows, 0:D].astype(F32) + recv[swapped(s), 0:D].astype(F32)
        v = resid[rows, :] + both
        resid_two[rows, :] = v
        xhat, _ = normalise(v)
        third[rows, :] = (xhat * gain + bias).astype(BF)

    loop(8, norm)
    flush(resid_two, third)
    win = ready(win)

    def step(b):
        rows = pl.ds(pl.multiple_of(b * 128, 128), 128)
        x = nn(third[rows, :], win[...])
        cdf = 0.5 + 0.5 * lax.erf(x * (0.5**0.5))
        hidden[rows, :] = (x * cdf).astype(BF)
        density = jnp.exp(x * x * -0.5) * ((2.0 * np.pi) ** -0.5)
        slope[rows, :] = (cdf + x * density).astype(BF)

    loop(4, step)


def mlp_kernel(offs, pa, pb, pab, pown, g, slope, win, hidden, own, comb, ginner, wout, sems):
    half = own.shape[0]
    blk = D // 16
    cols = [(0, D, 0, 2 * blk, 0), (D, 2 * D, 0, 2 * blk, blk)]
    columns = Rows((pown, pa, pb, pab), offs, 0, cols, (wout,), sems)
    g, slope = ready(g, slope)
    columns.wait()
    win = ready(win)

    def back(b):
        rows = pl.ds(pl.multiple_of(b * 256, 256), 256)
        gh = nt(g[rows, :], wout[...])
        ginner[rows, :] = (gh * slope[rows, :].astype(F32)).astype(BF)
        comb[rows, :] = nt(ginner[rows, :], win[...]).astype(BF)

    loop(2, back)
    flush(ginner)
    hidden = ready(hidden)
    own[...] = nn(hidden[0:half, :], wout[...]).astype(BF)
    comb[2 * half :, :] = nn(hidden[half:, :], wout[...]).astype(BF)


def dmlpout_kernel(offs, hidden, g, *refs):
    outs, dw, sems = refs[:3], refs[3], refs[4]
    hidden, g = ready(hidden, g)
    blk = dw.shape[0] // 16
    for b in range(4):
        part = tn(hidden[:, b * 8 * blk : (b + 1) * 8 * blk], g[...]).astype(BF)
        for k in range(8):
            row = (4 * b + k // 2) * blk
            dw[row : row + blk, (k % 2) * D : (k % 2 + 1) * D] = part[k * blk : (k + 1) * blk]
    send_out(dw, offs, outs, sems)


def mlp_and_grad_kernel(
    offs, pa, pb, pab, pown, g, slope, win, hidden, third, own, comb, to_own, to_b, to_a, ginner, wout, dw, sems, more_sems
):
    mlp_kernel(offs, pa, pb, pab, pown, g, slope, win, hidden, own, comb, ginner, wout, sems)
    dmlpin_kernel(offs, third, ginner, to_own, to_b, to_a, dw, more_sems)


def dmlpin_kernel(offs, third, ginner, *refs):
    third, ginner = ready(third, ginner)
    outs, dw, sems = refs[:3], refs[3], refs[4]
    for b in range(0, dw.shape[0], 256):
        dw[b : b + 256, :] = tn(third[:, b : b + 256], ginner[...]).astype(BF)
    send_out(dw, offs, outs, sems)


def cross_back_kernel(
    core, vec, resid, part, recv, own, g, keep, back, kv, cq, probs, wcq, output, gresid, gtwo, dcq, dkv, gsecond, dvec, gm
):
    c = core[0]
    vec, resid, part, recv, own, g = ready(vec, resid, part, recv, own, g)
    gain = vec[2:3]
    dvec[...] = jnp.zeros_like(dvec)

    def norm(s):
        rows = seq_rows(s)
        dy = part[rows, :].astype(F32) + recv[swapped(s), :].astype(F32)
        dx, dg, db = norm_back(resid[rows, :], gain, dy)
        total = g[rows, :].astype(F32) + dx
        gresid[rows, :] = total
        gtwo[rows, :] = total.astype(BF)

        @pl.when(s < 4)
        def _():
            dvec[0:1, :] += dg
            dvec[1:2, :] += db
            extra = own[rows, :].astype(F32) + recv[pl.ds(pl.multiple_of(512 + s * LEN, LEN), LEN), :].astype(F32)
            output[rows, :] = (resid[rows, :] + extra).astype(BF)

    loop(8, norm)
    flush(output, gresid, gtwo, dvec)
    keep, back = ready(keep, back)
    gm[...] = (nt(gtwo[:, half_lanes(c)], keep[:DH, :]) + nt(gtwo[:, half_lanes(1 - c)], back[DH:, :])).astype(BF)
    pad = probs.shape[1]
    kv, cq, probs = ready(kv, cq, probs)

    def att(s):
        rows = seq_rows(s)
        keys = pl.ds(pl.multiple_of(s * pad, 16), pad)
        dq, dk, dv = attend_back(gm[rows, :], cq[rows, :], kv[keys, 0:DH], kv[keys, DH:], probs[s])
        dcq[rows, :] = dq
        dkv[keys, 0:DH] = dk
        dkv[keys, DH:] = dv

    loop(8, att, 2)
    flush(dcq, dkv)
    wcq = ready(wcq)
    gsecond[...] = nt(dcq[...], wcq[...]).astype(BF)


def out_grad(dw, lo, c, mine, other, g):
    cols = half_lanes(c)
    dw[half_lanes(c), lo : lo + DH] = tn(mine[:, D:], g[:, cols]).astype(BF)
    rest = tn(other[256:, D:], g[:256, cols]) + tn(other[:256, D:], g[256:, cols])
    dw[half_lanes(1 - c), lo : lo + DH] = rest.astype(BF)


def dcross_kernel(offs, core, mixed, mixed_other, gtwo, second, dcq, dkv, wckv, mem, *refs):
    outs, gmem, dw, sems = refs[:3], refs[3:5], refs[5], refs[6]
    mixed, mixed_other, gtwo = ready(mixed, mixed_other, gtwo)
    out_grad(dw, 0, core[0], mixed, mixed_other, gtwo)
    second, dcq = ready(second, dcq)
    dw[:, DH : 2 * DH] = tn(second[...], dcq[...]).astype(BF)
    dkv, wckv = ready(dkv, wckv)
    half = dkv.shape[0] // 2
    for i, dst in ((1, gmem[1]), (0, gmem[0])):
        for b in range(0, half, 480):
            dst[b : b + 480, :] = nt(dkv[i * half + b : i * half + b + 480, :], wckv[...]).astype(BF)
    flush(*gmem)
    mem = ready(mem)
    for b in range(0, D, 256):
        dw[b : b + 256, 2 * DH :] = tn(mem[:, b : b + 256], dkv[...]).astype(BF)
    send_out(dw, offs, outs, sems)


def self_back_kernel(
    core, vec, resid, part, recv, gresid_two, keep, back, packed, probs, wqkv, xhat, gresid, gone, dpacked, gfirst_own, gfirst_other, dvec, gm
):
    c = core[0]
    vec, resid, part, recv, gresid_two = ready(vec, resid, part, recv, gresid_two)
    gain = vec[1:2]
    dvec[...] = jnp.zeros_like(dvec)

    def norm(s):
        rows = seq_rows(s)
        dy = part[rows, :].astype(F32) + recv[swapped(s), :].astype(F32)
        dx, dg, db = norm_back(resid[rows, :], gain, dy)
        total = gresid_two[rows, :] + dx
        gone[rows, :] = total.astype(BF)

        @pl.when(s < 4)
        def _():
            gresid[rows, :] = total
            dvec[0:1, :] += dg
            dvec[1:2, :] += db

    loop(8, norm)
    flush(gresid, gone)
    keep, back = ready(keep, back)
    gm[...] = (nt(gone[:, half_lanes(c)], keep[:DH, :]) + nt(gone[:, half_lanes(1 - c)], back[DH:, :])).astype(BF)
    packed, probs = ready(packed, probs)

    def att(s):
        rows = seq_rows(s)
        dq, dk, dv = attend_back(
            gm[rows, :], packed[rows, 0:DH], packed[rows, DH : 2 * DH], packed[rows, 2 * DH :], probs[s]
        )
        dpacked[rows, 0:DH] = dq
        dpacked[rows, DH : 2 * DH] = dk
        dpacked[rows, 2 * DH :] = dv

    loop(8, att, 2)
    flush(dpacked)
    wqkv, xhat = ready(wqkv, xhat)
    half = gfirst_own.shape[0]
    for b, dst in ((half, gfirst_other), (0, gfirst_own)):
        term = nt(dpacked[b : b + half, :], wqkv[...])
        dst[...] = term.astype(BF)
        flush(dst)
        dvec[2:3, :] += jnp.sum(term * xhat[b : b + half, :], 0, keepdims=True)
        dvec[3:4, :] += jnp.sum(term, 0, keepdims=True)


def dself_kernel(offs, core, mixed, mixed_other, gone, first, dpacked, dvec_two, dvec_one, *refs):
    outs, dw, vecs, sems = refs[:3], refs[3], refs[4], refs[5]
    mixed, mixed_other, gone = ready(mixed, mixed_other, gone)
    out_grad(dw, 0, core[0], mixed, mixed_other, gone)
    first, dpacked, dvec_two, dvec_one = ready(first, dpacked, dvec_two, dvec_one)
    for b in range(0, D, 256):
        dw[b : b + 256, DH : 4 * DH] = tn(first[:, b : b + 256], dpacked[...]).astype(BF)
    vecs[...] = jnp.zeros_like(vecs)
    for i, (v, row) in enumerate(((dvec_one, 2), (dvec_one, 0), (dvec_two, 0), (dvec_one, 3), (dvec_one, 1), (dvec_two, 1))):
        vecs[i : i + 1, :] = v[row : row + 1, :]
    dw[:, 4 * DH :] = jnp.transpose(vecs[...]).astype(BF)
    send_out(dw, offs, outs, sems)


def tokens_back_kernel(vec, tok, part, recv, gresid, gmem, gmem_recv, gtok, gmemory):
    vec, tok, part, recv, gresid = ready(vec, tok, part, recv, gresid)
    gain = vec[0:1]

    def norm(s):
        rows = seq_rows(s)
        dy = part[rows, :].astype(F32) + recv[rows, :].astype(F32)
        dx, _, _ = norm_back(tok[rows, :].astype(F32), gain, dy)
        gtok[rows, :] = (gresid[rows, :] + dx).astype(BF)

    loop(4, norm)
    flush(gtok)
    gmem, gmem_recv = ready(gmem, gmem_recv)
    gmemory[...] = (gmem[...].astype(F32) + gmem_recv[...].astype(F32)).astype(BF)


def merge_kernel(kinds, *refs):
    counts = {"pass": (2, 1), "sum": (3, 4), "end": (4, 1)}
    at, out = 0, sum(counts[kind][0] for kind in kinds)
    refs = ready(*refs)
    for kind in kinds:
        ins, outs = refs[at : at + counts[kind][0]], refs[out : out + counts[kind][1]]
        at, out = at + len(ins), out + len(outs)
        if kind == "pass":
            half = ins[0].shape[0]
            outs[0][...] = (ins[0][...].astype(F32) + ins[1][half:, :].astype(F32)).astype(BF)
        elif kind == "end":
            outs[0][...] = ins[0][...] + ins[1][...].astype(F32) + ins[2][...].astype(F32) + ins[3][...].astype(F32)
        else:
            blk = ins[0].shape[0] // 4
            for i in range(4):
                rows = slice(i * blk, (i + 1) * blk)
                total = ins[0][rows, :].astype(F32) + ins[1][rows, :].astype(F32) + ins[2][rows, :].astype(F32)
                outs[i][...] = total.astype(outs[i].dtype)


def merge(jobs, after=()):
    ins, outs = [], []
    for kind, *arrays in jobs:
        ins += arrays
        rows, width = arrays[0].shape
        if kind == "sum":
            outs += [sds((rows // 4, width), F32)] + [sds((rows // 4, width), BF)] * 3
        else:
            outs.append(sds((rows, width), BF if kind == "pass" else F32))
    kinds = [job[0] for job in jobs]
    return kernel_call(
        lambda *refs: merge_kernel(kinds, *refs),
        ins,
        [STAGE] * len(ins),
        outs,
        [STAGE] * len(outs),
        cost=1,
        after=after,
    )


def join_kernel(core, mine, got, *outs):
    c = core[0]
    mine, got = ready(mine, got)
    at = 0
    for out in outs[: 2 if mine.shape[1] > 4 * DH else 3]:
        for k in range(out.shape[1] // D):
            out[:, pl.ds(pl.multiple_of(k * D + c * DH, 128), DH)] = mine[:, at : at + DH]
            out[:, pl.ds(pl.multiple_of(k * D + (1 - c) * DH, 128), DH)] = got[:, at : at + DH]
            at += DH
    if mine.shape[1] > at:
        gains, biases, wide = outs[2:]
        rows = mine.shape[0]
        wide[...] = jnp.zeros_like(wide)
        wide[0:rows, :] = mine[:, at:] + got[:, at:]
        turned = jnp.transpose(wide[...])
        gains[...] = turned[0:3, 0:rows]
        biases[...] = turned[3:6, 0:rows]


class Moves:
    def __init__(self, mesh):
        self.nz, self.nf = mesh.shape["dp"], mesh.shape["fsdp"]
        self.n = self.nz * self.nf
        self.doubling = self.nz == 4 and self.nf == 8

    def permute(self, x, target):
        pairs = [(d, target(d // self.nf, (d % self.nf) // 2, d % 2)) for d in range(self.n)]
        return lax.ppermute(x, AXES, [(a, (z * self.nf) + 2 * yx + c) for a, (z, yx, c) in pairs])

    def sibling(self, x):
        return self.permute(x, lambda z, yx, c: (z, yx, 1 - c))

    def near_z(self, x):
        return self.permute(x, lambda z, yx, c: (z ^ 1, yx, c))

    def far_z(self, x):
        return self.permute(x, lambda z, yx, c: (z ^ 2, yx, c))

    def side_a(self, x):
        return self.permute(x, lambda z, yx, c: (z, yx ^ (1 + c), c))

    def side_b(self, x):
        return self.permute(x, lambda z, yx, c: (z, yx ^ (2 - c), c))

    def opposite_z(self, x):
        return self.permute(x, lambda z, yx, c: (z ^ 3, yx, c))


def per_device(moves, tokens, memory, lengths, cotangent, self_qkv, self_out, cross_q, cross_kv, cross_out, mlp_in, mlp_out, norm_gains, norm_biases):
    seqs, mem_len = memory.shape[0], memory.shape[1]
    rows = seqs * LEN
    place = lax.axis_index(AXES)
    c = place % 2
    chip = place // 2
    core = jnp.reshape(c, (1,)).astype(jnp.int32)
    wr, hr = self_qkv.shape[0], mlp_out.shape[0]
    ff = mlp_in.shape[1]
    fh = ff // 2
    r2, s2 = 2 * rows, 2 * seqs
    wb = D // 16
    pad = -(-mem_len // 16) * 16
    fast = moves.doubling


    def prepare(lens, pairs, after=()):
        return kernel_call(
            prepare_kernel,
            [lens, *pairs],
            [SM] + [STAGE] * 6,
            [sds((r2, D), BF)] * 2 + [sds((s2 * pad, D), BF), sds((r2, D), F32)],
            [STAGE] * 4,
            after=after,
        )

    def self_attention(pieces, lens, xhat, keep, back, after=()):
        own, a, b, ab = pieces
        return kernel_call(
            self_kernel,
            [lens, core, offs, a, b, ab, own, xhat, keep, back],
            [SM] * 3 + [ANY] * 4 + [STAGE] * 3,
            [
                sds((r2, D), BF),
                sds((r2, 3 * DH), BF),
                sds((s2, LEN, DH), BF),
                sds((r2, 3 * DH), BF),
                sds((8, D), F32),
                sds((D, 3 * DH), BF),
            ],
            [STAGE] * 6,
            [pltpu.VMEM((D, 128), BF), pltpu.SemaphoreType.DMA((32,))],
            cost=6,
            after=after,
        )

    def cross_attention(pieces, mem, vec, tok, comb, recv, keep, back, after=()):
        own, a, b, ab = pieces
        kv_rows = s2 * pad
        return kernel_call(
            lambda *refs: keys_and_cross_kernel(mem_len, *refs),
            [offs, a, b, ab, own, mem, core, vec, tok, comb, recv, keep, back],
            [SM] + [ANY] * 4 + [STAGE, SM] + [STAGE] * 6,
            [
                sds((kv_rows, D), BF),
                sds((D, 2 * DH), BF),
                sds((D, DH), BF),
                sds((r2, D), F32),
                sds((r2, D), BF),
                sds((r2, DH), BF),
                sds((s2, pad, DH), BF),
                sds((r2, 3 * DH), BF),
            ],
            [STAGE] * 8,
            [pltpu.SemaphoreType.DMA((32,))],
            cost=12,
            after=after,
        )

    def inner_part(resid_one, comb, recv, vec, w_in, after=()):
        return kernel_call(
            inner_kernel,
            [resid_one, comb, recv, vec, w_in],
            [STAGE] * 5,
            [sds((r2, D), F32), sds((r2, D), BF), sds((r2, fh), BF), sds((r2, fh), BF)],
            [STAGE] * 4,
            cost=5,
            after=after,
        )

    def inner_weight(pieces):
        return place_rows(pieces, offs, 0, [(0, fh, 0, wb, 0)], (D, fh))

    def grads(body, ins, specs, ncols, extra=(), scratch=(), cost=5, after=()):
        return kernel_call(
            body,
            [offs, *ins],
            [SM, *specs],
            [sds((4 * wb, ncols), BF)] * 2 + [sds((8 * wb, ncols), BF)] + list(extra),
            [ANY] * 3 + [STAGE] * len(extra),
            [pltpu.VMEM((D, ncols), BF), *scratch, pltpu.SemaphoreType.DMA((16,))],
            cost=cost,
            after=after,
        )

    def mlp_part(pieces, g, slope, w_in, hidden, third, after=()):
        own, a, b, ab = pieces
        return kernel_call(
            mlp_and_grad_kernel,
            [offs, a, b, ab, own, g, slope, w_in, hidden, third],
            [SM] + [ANY] * 4 + [STAGE] * 5,
            [sds((rows, D), BF), sds((3 * rows, D), BF)]
            + [sds((4 * wb, fh), BF)] * 2
            + [sds((8 * wb, fh), BF)],
            [STAGE] * 2 + [ANY] * 3,
            [
                pltpu.VMEM((r2, fh), BF),
                pltpu.VMEM((fh, D), BF),
                pltpu.VMEM((D, fh), BF),
                pltpu.SemaphoreType.DMA((32,)),
                pltpu.SemaphoreType.DMA((16,)),
            ],
            cost=11,
            after=after,
        )

    def cross_back(resid_two, comb, recv, part, after=()):
        return kernel_call(
            cross_back_kernel,
            [core, vec, resid_two, comb, recv, part, g, *cout, kv, cq, cprobs, w_cq],
            [SM] + [STAGE] * 12,
            [
                sds((rows, D), BF),
                sds((r2, D), F32),
                sds((r2, D), BF),
                sds((r2, DH), BF),
                sds(kv.shape, BF),
                sds((r2, D), BF),
                sds((8, D), F32),
            ],
            [STAGE] * 7,
            scratch=[pltpu.VMEM((r2, DH), BF)],
            cost=11,
            after=after,
        )

    def self_back(gsecond, recv, gresid_two, after=()):
        return kernel_call(
            self_back_kernel,
            [core, vec, resid_one, gsecond, recv, gresid_two, *out, packed, probs, w_qkv, xhat],
            [SM] + [STAGE] * 11,
            [
                sds((rows, D), F32),
                sds((r2, D), BF),
                sds((r2, 3 * DH), BF),
                sds((rows, D), BF),
                sds((rows, D), BF),
                sds((8, D), F32),
            ],
            [STAGE] * 6,
            scratch=[pltpu.VMEM((r2, DH), BF)],
            cost=9,
            after=after,
        )

    def cross_grads(after=()):
        return grads(
            dcross_kernel,
            [core, *cross_mixed, gtwo, second, dcq, dkv, w_ckv, mem],
            [SM] + [STAGE] * 8,
            4 * DH,
            [sds((seqs * pad, D), BF)] * 2,
            cost=10,
            after=after,
        )

    def self_grads(after=()):
        return grads(
            dself_kernel,
            [core, *self_mixed, gone, first, dpacked, dvec_two, dvec_one],
            [SM] + [STAGE] * 7,
            4 * DH + 128,
            scratch=[pltpu.VMEM((128, D), F32)],
            cost=6,
            after=after,
        )

    def tokens_back(recv, gmem_recv, after=()):
        return kernel_call(
            tokens_back_kernel,
            [vec, tokens.reshape(rows, D), gfirst, recv, gresid_one, gmem, gmem_recv],
            [STAGE] * 7,
            [sds((rows, D), BF), sds(gmem.shape, BF)],
            [STAGE] * 2,
            cost=4,
            after=after,
        )

    sib = moves.sibling
    pairs = []
    for x in (tokens.reshape(rows, D), cotangent.reshape(rows, D), memory):
        pairs += [x, sib(x)]
    lens = jnp.concatenate([lengths, sib(lengths)], 0)


    bits = jnp.arange(4, dtype=jnp.int32)
    if fast:
        plane = jnp.stack([jnp.int32(0), 1 + c, 2 - c, jnp.int32(3)]).astype(jnp.int32)
        z, yx = chip // 4, chip % 4
        chips = ((z ^ bits)[None, :] * 4 + (yx ^ plane)[:, None]).reshape(16).astype(jnp.int32)
    else:
        chips = jnp.arange(16, dtype=jnp.int32)
    turned = ((chips // 8) ^ c) * 8 + chips % 8
    offs = jnp.stack([chips, turned]).astype(jnp.int32)
    widths = (4 * DH + 128, 4 * DH, 4 * DH)

    if fast:
        keep, send = kernel_call(
            pack_kernel,
            [core, self_qkv, self_out, cross_q, cross_kv, cross_out, mlp_in, norm_gains, norm_biases],
            [SM] + ["stage"] * 8,
            [sds((wr, sum(widths)), BF)] * 2,
            [STAGE] * 2,
            scratch=[pltpu.VMEM((128, 128), F32)],
            cost=1,
            limit=60 << 20,
        )
        one, two, rest = kernel_call(
            order_kernel,
            [core, keep, sib(send), mlp_out],
            [SM] + [STAGE] * 3,
            [sds((2 * wr, w), BF) for w in (widths[0], widths[1], 8 * DH)],
            [STAGE] * 3,
            cost=1,
            after=[lens, pairs[1], pairs[3]],
        )
        along = [moves.near_z(one), moves.far_z(one), moves.opposite_z(one)]
        near_two = moves.near_z(two)
        tok, g, mem, xhat = prepare(lens, pairs, after=(one,))
        one = cat([one, *along], after=(tok, near_two))
        two = cat([two, near_two], after=(one,))
        rest = tie(rest, two)
        a1, b1, far_two, near_rest = moves.side_a(one), moves.side_b(one), moves.far_z(two), moves.near_z(rest)
        a1 = tie(a1, b1)
        two = cat([two, far_two], after=(a1, near_rest))
        three, four = split_cat(rest, near_rest, after=(two,))
        ab1, a2, b2, far_three = moves.side_b(a1), moves.side_a(two), moves.side_b(two), moves.far_z(three)
        a2 = tie(a2, b2, ab1)
        three = cat([three, far_three], after=(a2,))
        out = out_rows([one, a1, b1, ab1], offs, 3 * DH)
        out = (out, sib(out))
        four, three, a2 = tie(four, out[1], three), tie(three, out[1]), tie(a2, out[1])
        ab2, a3, b3, far_four = moves.side_b(a2), moves.side_a(three), moves.side_b(three), moves.far_z(four)
        first, packed, probs, comb, vec, w_qkv = self_attention([one, a1, b1, ab1], lens, xhat, *out, after=(four,))
        a3 = tie(a3, b3, ab2, comb)
        four = cat([four, far_four], after=(a3,))
        cout = out_rows([two, a2, b2, ab2], offs, 0)
        cout = (cout, sib(cout))
        comb = tie(comb, four)
        self_mixed = (comb, sib(comb))
        ab3, a4, b4 = moves.side_b(a3), moves.side_a(four), moves.side_b(four)
        kv, w_ckv, w_cq, resid_one, second, cq, cprobs, comb = cross_attention(
            [two, a2, b2, ab2], mem, vec, tok, *self_mixed, *cout, after=(four,)
        )
        a4 = tie(a4, b4, ab3, comb)
        ab4 = moves.side_b(a4)
        comb = tie(comb, a4)
        cross_mixed = (comb, sib(comb))
        w_in = inner_weight([three, a3, b3, ab3])
        resid_two, third, hidden, slope = inner_part(resid_one, *cross_mixed, vec, w_in)
        last = [four, a4, b4, ab4]
        after = (ab4,)
    else:
        tok, g, mem, xhat = prepare(lens, pairs)
        whole = lambda w: lax.all_gather(w, AXES, axis=0, tiled=True)
        split = lambda w: [w[i * w.shape[0] // 4 : (i + 1) * w.shape[0] // 4] for i in range(4)]

        def col_half(w, groups):
            w = w.reshape(w.shape[0], groups, 2, w.shape[1] // (2 * groups))
            return lax.dynamic_index_in_dim(w, c, 2, keepdims=False).reshape(w.shape[0], -1)

        vectors = jnp.pad(jnp.concatenate([norm_gains, norm_biases], 0).T, ((0, 0), (0, 122)))
        one = jnp.concatenate([col_half(self_qkv, 3), col_half(self_out, 1), vectors], 1)
        two = jnp.concatenate([col_half(w, w.shape[1] // D) for w in (cross_out, cross_q, cross_kv)], 1)
        one, two = split(whole(one)), split(whole(two))
        three = split(whole(col_half(mlp_in, ff // (2 * hr))))
        out, cout = out_rows(one, offs, 3 * DH), out_rows(two, offs, 0)
        out, cout = (out, sib(out)), (cout, sib(cout))
        rowed = whole(mlp_out).reshape(moves.n // 2, 2, hr, D)
        rowed = lax.dynamic_index_in_dim(rowed, c, 1, keepdims=False).reshape(16, 2, fh // 32, D)
        last = split(rowed.transpose(0, 2, 1, 3).reshape(D, 2 * D))
        first, packed, probs, comb, vec, w_qkv = self_attention(one, lens, xhat, *out)
        self_mixed = (comb, sib(comb))
        kv, w_ckv, w_cq, resid_one, second, cq, cprobs, comb = cross_attention(
            two, mem, vec, tok, *self_mixed, *cout
        )
        cross_mixed = (comb, sib(comb))
        w_in = inner_weight(three)
        resid_two, third, hidden, slope = inner_part(resid_one, *cross_mixed, vec, w_in)
        after = ()


    side_a, side_b = moves.side_a, moves.side_b

    def along_z(blocks):
        return [moves.near_z(blocks[0]), moves.far_z(blocks[1]), moves.opposite_z(blocks[2])]

    d_mlpout = grads(dmlpout_kernel, [hidden, g], [STAGE] * 2, 2 * D, after=after)
    if fast:
        got_a1 = side_a(d_mlpout[2])
    part, comb, *d_mlpin = mlp_part(last, g, slope, w_in, hidden, third, after=d_mlpout[:1])
    if fast:
        (on,) = merge([("pass", d_mlpout[1], got_a1)], after=(part,))
        comb = tie(comb, on)
        got_b1, got_a2 = side_b(on), side_a(tie(d_mlpin[2], on))
        after = (on,)
    recv = sib(comb)
    output, gresid_two, gtwo, dcq, dkv, gsecond, dvec_two = cross_back(resid_two, comb, recv, part, after=after)
    if fast:
        on, kept1, *sums1 = merge([("pass", d_mlpin[1], got_a2), ("sum", d_mlpout[0], got_a1, got_b1)], after=(dcq,))
        got_b2, got_z1 = side_b(on), along_z(sums1)
        gsecond = tie(gsecond, on)
        after = (on,)
    recv = sib(gsecond)
    *d_cross, gmem, gmem_other = cross_grads(after=after)
    if fast:
        kept2, *sums2, total1 = merge([("sum", d_mlpin[0], got_a2, got_b2), ("end", kept1, *got_z1)], after=(gmem,))
        got_z2, got_a3 = along_z(sums2), side_a(tie(d_cross[2], kept2))
        after = (kept2,)
    gresid_one, gone, dpacked, gfirst, gfirst_other, dvec_one = self_back(gsecond, recv, gresid_two, after=after)
    if fast:
        on, total2 = merge([("pass", d_cross[1], got_a3), ("end", kept2, *got_z2)], after=(gone,))
        got_b3 = side_b(on)
        gfirst_other, gmem_other = tie(gfirst_other, on), tie(gmem_other, on)
        after = (on,)
    recv, gmem_recv = sib(gfirst_other), sib(gmem_other)
    d_self = self_grads(after=after)
    if fast:
        kept3, *sums3 = merge([("sum", d_cross[0], got_a3, got_b3)], after=[d_self[0], recv, gmem_recv])
        got_z3, got_a4 = along_z(sums3), side_a(tie(d_self[2], kept3))
        after = (kept3,)
    grad_tokens, grad_memory = tokens_back(recv, gmem_recv, after=after)
    grad_memory = grad_memory.reshape(seqs, pad, D)[:, :mem_len]

    if fast:
        on, total3 = merge([("pass", d_self[1], got_a4), ("end", kept3, *got_z3)], after=(grad_tokens,))
        got_b4 = side_b(on)
        kept4, *sums4 = merge([("sum", d_self[0], got_a4, got_b4)])
        got_z4 = along_z(sums4)
        (total4,) = merge([("end", kept4, *got_z4)])
        total = [total1, total2, total3, total4]

        def own_rows(total):
            mine = lax.dynamic_slice_in_dim(total, c * wr, wr, 0)
            return mine, sib(lax.dynamic_slice_in_dim(total, (1 - c) * wr, wr, 0))

        def join(pair, *shapes, scratch=()):
            return kernel_call(
                join_kernel,
                [core, *pair],
                [SM, STAGE, STAGE],
                [sds(shape, F32) for shape in shapes],
                [STAGE] * len(shapes),
                scratch=scratch,
                cost=1,
            )

        sum_mlpout = jnp.concatenate([total[0][:, :D], total[0][:, D:]], 0)
        mine, got = own_rows(total[1])
        pair = (jnp.where(c == 0, mine, got), jnp.where(c == 0, got, mine))
        parts = [p.reshape(wr, ff // (2 * hr), 1, hr) for p in pair]
        grad_in = jnp.concatenate(parts, 2).reshape(wr, ff)
        grad_cout, grad_cq, grad_ckv = join(own_rows(total[2]), (wr, D), (wr, D), (wr, 2 * D))
        grad_out, grad_qkv, own_gains, own_biases = join(
            own_rows(total[3]), (wr, D), (wr, 3 * D), (3, wr), (3, wr), scratch=[pltpu.VMEM((128, 128), F32)]
        )
    else:

        def placed(parts):
            own, to_b, to_a = parts
            term = jnp.concatenate([own, to_a[: 4 * wb], to_b, to_a[4 * wb :]], 0).astype(F32)
            both = jnp.stack([jnp.where(c == 0, term, 0.0), jnp.where(c == 1, term, 0.0)], 1)
            return lax.psum_scatter(both, AXES, scatter_dimension=0, tiled=True)

        def joined(total, lo, hi, groups):
            return total[:, :, lo:hi].reshape(wr, 2, groups, -1).transpose(0, 2, 1, 3).reshape(wr, -1)

        total = placed(d_cross)
        grad_cout, grad_cq, grad_ckv = (
            joined(total, 0, DH, 1),
            joined(total, DH, 2 * DH, 1),
            joined(total, 2 * DH, 4 * DH, 2),
        )
        total = placed(d_self)
        grad_out, grad_qkv = joined(total, 0, DH, 1), joined(total, DH, 4 * DH, 3)
        vectors = jnp.sum(total[:, :, 4 * DH : 4 * DH + 6], 1).T
        own_gains, own_biases = vectors[:3], vectors[3:]
        grad_in = joined(placed(d_mlpin), 0, fh, ff // (2 * hr))
        own, to_b, to_a = d_mlpout
        term = jnp.concatenate([own, to_a[: 4 * wb], to_b, to_a[4 * wb :]], 0).astype(F32)
        term = term.reshape(16, wb, 2, D).transpose(0, 2, 1, 3).reshape(moves.n // 2, 1, hr, D)
        both = jnp.concatenate([jnp.where(c == 0, term, 0.0), jnp.where(c == 1, term, 0.0)], 1)
        sum_mlpout = lax.psum_scatter(both.reshape(ff, D), AXES, scatter_dimension=0, tiled=True)

    return (
        output.reshape(tokens.shape),
        grad_tokens.reshape(tokens.shape),
        grad_memory,
        grad_qkv,
        grad_out,
        grad_cq,
        grad_ckv,
        grad_cout,
        grad_in,
        sum_mlpout,
        own_gains,
        own_biases,
    )


def solution(mesh):
    batch = P(AXES, None, None)
    rows = P(AXES, None)
    cols = P(None, AXES)
    moves = Moves(mesh)
    in_specs = (batch, batch, P(AXES), batch) + (rows,) * 7 + (cols,) * 2
    out_specs = (batch,) * 3 + (rows,) * 7 + (cols,) * 2
    return jax.shard_map(
        lambda *args: per_device(moves, *args),
        mesh=mesh,
        in_specs=in_specs,
        out_specs=out_specs,
        check_vma=False,
    )
```

time: 322 us -> 277 us (0.86)
  starting transfers between devices: 42.9 us -> 63.3 us
  local copies, waits for them, and re-layouts: 46.8 us -> 26.6 us
  other arithmetic: 22.3 us -> 2.62 us
  Pallas kernels: 117 us -> 104 us
  waiting for transfers between devices: 90.2 us -> 78.1 us
    ppermute x48 -> x56, starting transfers between devices: 42.9 us -> 63.3 us  [permute(): lax.ppermute(x, AXES, [(a, z * self.nf + 2 * yx + c) for a, (z, yx, c) in...]
    unnamed x166 -> x156, local copies, waits for them, and re-layouts: 35.9 us -> 20.8 us
    pallas_call x21 -> x32, Pallas kernels: 117 us -> 104 us  [kernel_call(): pl.pallas_call(run, out_shape=list(outs), in_specs=[place(spec) for spec...]
    ppermute x48 -> x56, waiting for transfers between devices: 90.2 us -> 78.1 us  [permute(): lax.ppermute(x, AXES, [(a, z * self.nf + 2 * yx + c) for a, (z, yx, c) in...]
    concatenate x10 -> x2, other arithmetic: 12.8 us -> 0.81 us  [the longest x1 0.73 us: per_device(): sum_mlpout = jnp.concatenate([total[0][:, :D], total[0][:, D:]], 0)]
    add x15 -> x1, other arithmetic: 4.76 us -> 0.01 us  [per_device(): turned = (chips // 8 ^ c) * 8 + chips % 8]
  transfers between devices with their start and end apart: 48 -> 56, of which waited for: 19 -> 21; matrix products, arithmetic and copies ran while one was open for 9% -> 4% of each run, Pallas kernels for 32% -> 32%
where the time goes in v3:
time: 277 us; the launch traced here: 276 us
  Pallas kernels  104 us (38%)
  waiting for transfers between devices  78.1 us (28%)
  starting transfers between devices  63.3 us (23%)
  local copies, waits for them, and re-layouts  26.6 us (10%)
    pallas_call x32, Pallas kernels, kernel_call(): pl.pallas_call(run, out_shape=list(outs), in_specs=[place(spec) for spec...  104 us
    ppermute x56, waiting for transfers between devices, permute(): lax.ppermute(x, AXES, [(a, z * self.nf + 2 * yx + c) for a, (z, yx, c) in...  78.1 us
    ppermute x56, starting transfers between devices, permute(): lax.ppermute(x, AXES, [(a, z * self.nf + 2 * yx + c) for a, (z, yx, c) in...  63.3 us
    unnamed x156, local copies, waits for them, and re-layouts  20.8 us
  transfers between devices with their start and end apart: 56, of which 21 were waited for; matrix products, arithmetic and copies ran while one was open for 4% of the time, Pallas kernels for 32%

profile of v3, /device:TPU:0, one launch (start us, length us, event | category | flops | bytes accessed | tf_op | source)
XLA Modules:
  0.0 275.9 jit_solution(17552600768345951326)
XLA Ops:
  1.2 2.9 %shard_map.220 = (bf16[24,4736]{1,0:T(8,128)(2,1)}, bf16[24,4736]{1,0:T(8,128)(2,1)}) custom-call(s32[1]{0:T(128)} %bitcast.refs_0_.refs_1_.refs_6_, bf16[24,2304]{1,0:T(8,128)(2,1)} %refs_1_.1, bf16[24,768]{1,0:T(8,128)(2,1)} %refs_2_.1, bf16[24,768]{1,0:T(8,128)(2,1)} %refs_3_.2, bf16[24,1536]{1,0:T(8,128)(2,1)} %refs_4_.1, bf16[24,768]{1,0:T(8,128)(2,1)} %refs_5_.2, ...), custom_call_target="tpu_custom_call" | custom-call | flops 16000000000 | tf_op jit(solution)/shard_map/pallas_call | solution.py:97
  8.3 2.8 %collective-permute-start.4 = (bf16[48,1664]{1,0:T(8,128)(2,1)S(1)}, bf16[48,1664]{1,0:T(8,128)(2,1)S(1)}, u32[]{:S(2)}, u32[]{:S(2)}) collective-permute-start(bf16[48,1664]{1,0:T(8,128)(2,1)S(1)} %get-tuple-element.103.refs_7_.refs_0_), channel_id=1, source_target_pairs={{0,8},{1,9},{2,10},{3,11},{4,12},{5,13},{6,14},{7,15},{8,0},{9,1},... | collective-permute-start | bytes 479240 | tf_op jit(solution)/shard_map/ppermute | solution.py:774
  11.1 2.6 collective-permute-start.5
  16.1 2.5 shard_map.222
  18.6 6.9 %collective-permute-done.8.refs_5_.refs_1_ = bf16[48,1536]{1,0:T(8,128)(2,1)S(1)} collective-permute-done((bf16[48,1536]{1,0:T(8,128)(2,1)S(1)}, bf16[48,1536]{1,0:T(8,128)(2,1)S(1)}, u32[]{:S(2)}, u32[]{:S(2)}) %collective-permute-start.8) | collective-permute-done | bytes 147488 | tf_op jit(solution)/shard_map/ppermute | solution.py:774
  30.5 4.1 %collective-permute-start.14 = (bf16[96,1536]{1,0:T(8,128)(2,1)S(1)}, bf16[96,1536]{1,0:T(8,128)(2,1)S(1)}, u32[]{:S(2)}, u32[]{:S(2)}) collective-permute-start(bf16[96,1536]{1,0:T(8,128)(2,1)S(1)} %shard_map.226.refs_1_.refs_0_), channel_id=1, source_target_pairs={{0,16},{1,17},{2,18},{3,19},{4,20},{5,21},{6,22},{7,23},{8,24},{9,... | collective-permute-start | bytes 884744 | tf_op jit(solution)/shard_map/ppermute | solution.py:774
  34.7 8.5 %collective-permute-done.9.refs_0_ = bf16[192,1664]{1,0:T(8,128)(2,1)S(1)} collective-permute-done((bf16[192,1664]{1,0:T(8,128)(2,1)S(1)}, bf16[192,1664]{1,0:T(8,128)(2,1)S(1)}, u32[]{:S(2)}, u32[]{:S(2)}) %collective-permute-start.9) | collective-permute-done | bytes 639008 | tf_op jit(solution)/shard_map/ppermute | solution.py:774
  43.8 3.3 %collective-permute-done.13.refs_3_.refs_1_ = bf16[48,3072]{1,0:T(8,128)(2,1)S(1)} collective-permute-done((bf16[48,3072]{1,0:T(8,128)(2,1)S(1)}, bf16[48,3072]{1,0:T(8,128)(2,1)S(1)}, u32[]{:S(2)}, u32[]{:S(2)}) %collective-permute-start.13) | collective-permute-done | bytes 294944 | tf_op jit(solution)/shard_map/ppermute | solution.py:774
  48.7 3.3 %collective-permute-start.15 = (bf16[96,1536]{1,0:T(8,128)(2,1)S(1)}, bf16[96,1536]{1,0:T(8,128)(2,1)S(1)}, u32[]{:S(2)}, u32[]{:S(2)}) collective-permute-start(bf16[96,1536]{1,0:T(8,128)(2,1)S(1)} %get-tuple-element.109.refs_0_), channel_id=1, source_target_pairs={{0,16},{1,17},{2,18},{3,19},{4,20},{5,21},{6,22},{7,23},{8,24},{9,... | collective-permute-start | bytes 884744 | tf_op jit(solution)/shard_map/ppermute | solution.py:774
  52.0 6.6 %collective-permute-done.11.refs_4_.refs_2_.refs_5_ = bf16[192,1664]{1,0:T(8,128)(2,1)S(1)} collective-permute-done((bf16[192,1664]{1,0:T(8,128)(2,1)S(1)}, bf16[192,1664]{1,0:T(8,128)(2,1)S(1)}, u32[]{:S(2)}, u32[]{:S(2)}) %collective-permute-start.11) | collective-permute-done | bytes 639008 | tf_op jit(solution)/shard_map/ppermute | solution.py:774
  59.6 4.0 %collective-permute-done.16.refs_0_ = bf16[192,1536]{1,0:T(8,128)(2,1)S(1)} collective-permute-done((bf16[192,1536]{1,0:T(8,128)(2,1)S(1)}, bf16[192,1536]{1,0:T(8,128)(2,1)S(1)}, u32[]{:S(2)}, u32[]{:S(2)}) %collective-permute-start.16) | collective-permute-done | bytes 589856 | tf_op jit(solution)/shard_map/ppermute | solution.py:774
  63.7 2.6 collective-permute-done.17.refs_1_.refs_3_.refs_2_
  66.6 4.7 %collective-permute-start.19 = (bf16[96,1536]{1,0:T(8,128)(2,1)S(1)}, bf16[96,1536]{1,0:T(8,128)(2,1)S(1)}, u32[]{:S(2)}, u32[]{:S(2)}) collective-permute-start(bf16[96,1536]{1,0:T(8,128)(2,1)S(1)} %shard_map.232.refs_10_.refs_0_), channel_id=1, source_target_pairs={{0,16},{1,17},{2,18},{3,19},{4,20},{5,21},{6,22},{7,23},{8,24},{9,... | collective-permute-start | bytes 884744 | tf_op jit(solution)/shard_map/ppermute | solution.py:774
  72.3 1.7 collective-permute-start.18
  74.1 7.7 %shard_map.233 = (bf16[512,768]{1,0:T(8,128)(2,1)S(1)}, bf16[512,1152]{1,0:T(8,128)(2,1)S(1)}, bf16[8,64,384]{2,1,0:T(8,128)(2,1)S(1)}, bf16[512,1152]{1,0:T(8,1...) custom-call(s32[8]{0:T(128)S(1)} %pad_add_fusion.1.refs_4_.refs_0_, s32[1]{0:T(128)} %bitcast.refs_0_.refs_1_.refs_6_, ...), custom_call_target="tpu_custom_call" | custom-call | flops 96000000000 | tf_op jit(solution)/shard_map/pallas_call | solution.py:97
  83.4 7.9 %collective-permute-done.18.refs_2_.refs_4_.refs_3_ = bf16[192,1536]{1,0:T(8,128)(2,1)S(1)} collective-permute-done((bf16[192,1536]{1,0:T(8,128)(2,1)S(1)}, bf16[192,1536]{1,0:T(8,128)(2,1)S(1)}, u32[]{:S(2)}, u32[]{:S(2)}) %collective-permute-start.18) | collective-permute-done | bytes 589856 | tf_op jit(solution)/shard_map/ppermute | solution.py:774
  98.3 12.4 %shard_map.240 = (bf16[1920,768]{1,0:T(8,128)(2,1)S(1)}, bf16[768,768]{1,0:T(8,128)(2,1)S(1)}, bf16[768,384]{1,0:T(8,128)(2,1)S(1)}, f32[512,768]{1,0:T(8,128)S(...) custom-call(s32[2,16]{1,0:T(2,128)S(1)} %pad_add_fusion.refs_0_.refs, ...), custom_call_target="tpu_custom_call" | custom-call | flops 192000000000 | tf_op jit(solution)/shard_map/pallas_call | solution.py:97
  110.8 1.6 copy-done.55
  115.2 1.6 collective-permute-done.26.refs_2_.refs_4_
  118.4 3.5 %shard_map.243.refs_4_.refs_7_ = bf16[768,1536]{1,0:T(8,128)(2,1)S(1)} custom-call(s32[2,16]{1,0:T(2,128)S(1)} %pad_add_fusion.refs_0_.refs_2_, bf16[192,1536]{1,0:T(8,128)(2,1)S(1)} %copy-done.7, bf16[192,1536]{1,0:T(8,128)(2,1)} %shard_map.236.refs_2_, bf16[192,1536]{1,0:T(8,128)(2,1)S(1)} %copy-done.9, ...), custom_call_target="tpu_custom_call" | custom-call | flops 16000000000 | tf_op jit(solution)/shard_map/pallas_call | solution.py:97
  123.5 4.1 %shard_map.244 = (f32[512,768]{1,0:T(8,128)S(1)}, bf16[512,768]{1,0:T(8,128)(2,1)S(1)}, bf16[512,1536]{1,0:T(8,128)(2,1)S(1)}, bf16[512,1536]{1,0:T(8,128)(2,1)S(1)}) custom-call(f32[512,768]{1,0:T(8,128)S(1)} %get-tuple-element.113.refs_0_.refs_2_, bf16[512,1152]{1,0:T(8,128)(2,1)S(1)} %shard_map.242.refs_1_.refs_2_, ...), custom_call_target="tpu_custom_call" | custom-call | flops 80000000000 | tf_op jit(solution)/shard_map/pallas_call | solution.py:97
  128.2 3.9 %collective-permute-done.28.refs_3_ = bf16[192,1536]{1,0:T(8,128)(2,1)S(1)} collective-permute-done((bf16[192,1536]{1,0:T(8,128)(2,1)}, bf16[192,1536]{1,0:T(8,128)(2,1)S(1)}, u32[]{:S(2)}, u32[]{:S(2)}) %collective-permute-start.28) | collective-permute-done | bytes 589856 | tf_op jit(solution)/shard_map/ppermute | solution.py:774
  132.1 4.5 %shard_map.245 = (bf16[192,1536]{1,0:T(8,128)(2,1)S(1)}, bf16[192,1536]{1,0:T(8,128)(2,1)S(1)}, bf16[384,1536]{1,0:T(8,128)(2,1)}) custom-call(s32[2,16]{1,0:T(2,128)S(1)} %pad_add_fusion.refs_0_.refs_2_, bf16[512,1536]{1,0:T(8,128)(2,1)S(1)} %get-tuple-element.118.refs_1_.refs_8_, bf16[512,768]{1,0:T(8,128)(2,1)S(1)} %get-tuple-element.116.refs_2_.refs_5_.refs_6_, ...), custom_call_target="tpu_custom_call" | custom-call | flops 80000000000 | tf_op jit(solution)/shard_map/pallas_call | solution.py:97
  138.2 11.1 %shard_map.246 = (bf16[256,768]{1,0:T(8,128)(2,1)S(1)}, bf16[768,768]{1,0:T(8,128)(2,1)S(1)}, bf16[192,1536]{1,0:T(8,128)(2,1)S(1)}, bf16[192,1536]{1,0:T(8,128)(2,1)S(1)}, bf16[384,1536]{1,0:T(8,128)(2,1)}) custom-call(s32[2,16]{1,0:T(2,128)S(1)} %pad_add_fusion.refs_0_.refs_2_, bf16[192,1536]{1,0:T(8,128)(2,1)} %shard_map.241.refs_1_, ...), custom_call_target="tpu_custom_call" | custom-call | flops 176000008192 | tf_op jit(solution)/shard_map/pallas_call | solution.py:97
  149.3 3.9 %collective-permute-done.29.refs_1_.refs_3_ = bf16[384,1536]{1,0:T(8,128)(2,1)} collective-permute-done((bf16[384,1536]{1,0:T(8,128)(2,1)}, bf16[384,1536]{1,0:T(8,128)(2,1)}, u32[]{:S(2)}, u32[]{:S(2)}) %collective-permute-start.29) | collective-permute-done | bytes 1179680 | tf_op jit(solution)/shard_map/ppermute | solution.py:774
  153.2 2.2 shard_map.247.refs_1_.refs_13_
  160.1 1.8 copy-done.56
  165.0 11.0 %shard_map.249 = (bf16[256,768]{1,0:T(8,128)(2,1)}, f32[512,768]{1,0:T(8,128)S(1)}, bf16[512,768]{1,0:T(8,128)(2,1)S(1)}, bf16[512,384]{1,0:T(8,128)(2,1)S(1)}, ...) custom-call(s32[1]{0:T(128)} %bitcast.refs_0_.refs_1_.refs_6_, ...), custom_call_target="tpu_custom_call" | custom-call | flops 176000008192 | tf_op jit(solution)/shard_map/pallas_call | solution.py:97
  176.1 1.7 collective-permute-done.31.refs_1_
  177.8 3.0 %shard_map.251 = (bf16[192,1536]{1,0:T(8,128)(2,1)}, f32[48,1536]{1,0:T(8,128)S(1)}, bf16[48,1536]{1,0:T(8,128)(2,1)}, bf16[48,1536]{1,0:T(8,128)(2,1)}, bf16[48,1536]{1,0:T(8,128)(2,1)}) custom-call(bf16[192,1536]{1,0:T(8,128)(2,1)S(1)} %get-tuple-element.131.refs_0_, bf16[384,1536]{1,0:T(8,128)(2,1)} %collective-permute-done.31.refs_1_, ...), custom_call_target="tpu_custom_call" | custom-call | flops 16000000000 | tf_op jit(solution)/shard_map/pallas_call | solution.py:97
  184.3 2.5 collective-permute-start.37
  186.8 9.6 %shard_map.253 = (bf16[192,1536]{1,0:T(8,128)(2,1)S(1)}, bf16[192,1536]{1,0:T(8,128)(2,1)S(1)}, bf16[384,1536]{1,0:T(8,128)(2,1)S(1)}, bf16[960,768]{1,0:T(8,128)(2,1)S(1)}, bf16[960,768]{1,0:T(8,128)(2,1)S(1)}) custom-call(s32[2,16]{1,0:T(2,128)S(1)} %copy-done.13, s32[1]{0:T(128)} %bitcast.refs_0_.refs_1_.refs_6_, bf16[512,1152]{1,0:T(8,128)(2,1)S(1)} %copy-done.5, ...), custom_call_target="tpu_custom_call" | custom-call | flops 160000000000 | tf_op jit(solution)/shard_map/pallas_call | solution.py:97
  197.3 2.0 shard_map.254
  200.9 3.0 %collective-permute-start.39 = (bf16[48,1536]{1,0:T(8,128)(2,1)S(1)}, bf16[48,1536]{1,0:T(8,128)(2,1)S(1)}, u32[]{:S(2)}, u32[]{:S(2)}) collective-permute-start(bf16[48,1536]{1,0:T(8,128)(2,1)S(1)} %get-tuple-element.154), channel_id=1, source_target_pairs={{0,8},{1,9},{2,10},{3,11},{4,12},{5,13},{6,14},{7,15},{8,0},{9,1},... | collective-permute-start | bytes 442376 | tf_op jit(solution)/shard_map/ppermute | solution.py:774
  203.9 2.4 collective-permute-start.41
  207.0 10.0 %shard_map.255 = (f32[256,768]{1,0:T(8,128)S(1)}, bf16[512,768]{1,0:T(8,128)(2,1)S(1)}, bf16[512,1152]{1,0:T(8,128)(2,1)S(1)}, bf16[256,768]{1,0:T(8,128)(2,1)S(...) custom-call(s32[1]{0:T(128)} %bitcast.refs_0_.refs_1_.refs_6_, f32[8,768]{1,0:T(8,128)S(1)} %copy-done.73, ...), custom_call_target="tpu_custom_call" | custom-call | flops 143999991808 | tf_op jit(solution)/shard_map/pallas_call | solution.py:97
  219.9 5.7 %shard_map.260 = (bf16[192,1664]{1,0:T(8,128)(2,1)S(1)}, bf16[192,1664]{1,0:T(8,128)(2,1)S(1)}, bf16[384,1664]{1,0:T(8,128)(2,1)S(1)}) custom-call(s32[2,16]{1,0:T(2,128)S(1)} %copy-done.14, s32[1]{0:T(128)} %bitcast.refs_0_.refs_1_.refs_6_, bf16[512,1152]{1,0:T(8,128)(2,1)S(1)} %copy-done.3, bf16[512,1152]{1,0:T(8,128)(2,1)S(1)} %copy-done.16, ...), custom_call_target="tpu_custom_call" | custom-call | flops 96000000000 | tf_op jit(solution)/shard_map/pallas_call | solution.py:97
  225.6 1.6 collective-permute-done.44.refs_2_
  228.1 2.4 collective-permute-start.46
  230.6 2.4 collective-permute-start.48
  232.9 2.2 shard_map.262
  235.1 8.2 %collective-permute-done.47.refs_4_ = bf16[48,1536]{1,0:T(8,128)(2,1)S(1)} collective-permute-done((bf16[48,1536]{1,0:T(8,128)(2,1)S(1)}, bf16[48,1536]{1,0:T(8,128)(2,1)S(1)}, u32[]{:S(2)}, u32[]{:S(2)}) %collective-permute-start.47) | collective-permute-done | bytes 147488 | tf_op jit(solution)/shard_map/ppermute | solution.py:774
  248.2 1.6 dynamic-slice_select_fusion.1
  252.6 1.6 copy.50
  254.2 3.4 %collective-permute-done.49.refs_2_ = bf16[192,1664]{1,0:T(8,128)(2,1)} collective-permute-done((bf16[192,1664]{1,0:T(8,128)(2,1)}, bf16[192,1664]{1,0:T(8,128)(2,1)}, u32[]{:S(2)}, u32[]{:S(2)}) %collective-permute-start.49) | collective-permute-done | bytes 639008 | tf_op jit(solution)/shard_map/ppermute | solution.py:774
  261.0 2.3 collective-permute-start.52
  263.4 1.6 collective-permute-done.50.refs_1_
  265.0 8.5 %collective-permute-done.51.refs_2_ = bf16[48,1664]{1,0:T(8,128)(2,1)S(1)} collective-permute-done((bf16[48,1664]{1,0:T(8,128)(2,1)S(1)}, bf16[48,1664]{1,0:T(8,128)(2,1)S(1)}, u32[]{:S(2)}, u32[]{:S(2)}) %collective-permute-start.51) | collective-permute-done | bytes 159776 | tf_op jit(solution)/shard_map/ppermute | solution.py:774
  (288 shorter events, 64.8 us)
Async XLA Ops:
  0.6 6.3 %collective-permute-start = (s32[4]{0:T(128)}, s32[4]{0:T(128)S(1)}, u32[]{:S(2)}, u32[]{:S(2)}) collective-permute-start(s32[4]{0:T(128)} %param.15), channel_id=1, source_target_pairs={{0,1},{1,0},{2,3},{3,2},{4,5},{5,4},{6,7},{7,6},{8,9},{9,8},{10,11... | collective-permute-start | bytes 56 | tf_op jit(solution)/shard_map/ppermute | solution.py:774
  4.7 9.9 %collective-permute-start.7 = (bf16[4,228,768]{2,0,1:T(4,128)(2,1)}, bf16[4,228,768]{2,0,1:T(4,128)(2,1)}, u32[]{:S(2)}, u32[]{:S(2)}) collective-permute-start(bf16[4,228,768]{2,0,1:T(4,128)(2,1)} %param.14), channel_id=1, source_target_pairs={{0,1},{1,0},{2,3},{3,2},{4,5},{5,4},{6,7},{7,6},{8,9},{9,8},{10,11... | collective-permute-start | bytes 4202504 | tf_op jit(solution)/shard_map/ppermute | solution.py:774
  8.3 17.2 %collective-permute-start.4 = (bf16[48,1664]{1,0:T(8,128)(2,1)S(1)}, bf16[48,1664]{1,0:T(8,128)(2,1)S(1)}, u32[]{:S(2)}, u32[]{:S(2)}) collective-permute-start(bf16[48,1664]{1,0:T(8,128)(2,1)S(1)} %get-tuple-element.103.refs_7_.refs_0_), channel_id=1, source_target_pairs={{0,8},{1,9},{2,10},{3,11},{4,12},{5,13},{6,14},{7,15},{8,0},{9,1},... | collective-permute-start | bytes 479240 | tf_op jit(solution)/shard_map/ppermute | solution.py:774
  11.1 14.8 %collective-permute-start.5 = (bf16[48,1664]{1,0:T(8,128)(2,1)S(1)}, bf16[48,1664]{1,0:T(8,128)(2,1)S(1)}, u32[]{:S(2)}, u32[]{:S(2)}) collective-permute-start(bf16[48,1664]{1,0:T(8,128)(2,1)S(1)} %get-tuple-element.103.refs_7_.refs_0_), channel_id=1, source_target_pairs={{0,16},{1,17},{2,18},{3,19},{4,20},{5,21},{6,22},{7,23},{8,24},{9,... | collective-permute-start | bytes 479240 | tf_op jit(solution)/shard_map/ppermute | solution.py:774
  13.7 12.2 %collective-permute-start.6 = (bf16[48,1664]{1,0:T(8,128)(2,1)S(1)}, bf16[48,1664]{1,0:T(8,128)(2,1)S(1)}, u32[]{:S(2)}, u32[]{:S(2)}) collective-permute-start(bf16[48,1664]{1,0:T(8,128)(2,1)S(1)} %get-tuple-element.103.refs_7_.refs_0_), channel_id=1, source_target_pairs={{0,24},{1,25},{2,26},{3,27},{4,28},{5,29},{6,30},{7,31},{8,16},{9,... | collective-permute-start | bytes 479240 | tf_op jit(solution)/shard_map/ppermute | solution.py:774
  13.7 11.8 %collective-permute-start.8 = (bf16[48,1536]{1,0:T(8,128)(2,1)S(1)}, bf16[48,1536]{1,0:T(8,128)(2,1)S(1)}, u32[]{:S(2)}, u32[]{:S(2)}) collective-permute-start(bf16[48,1536]{1,0:T(8,128)(2,1)S(1)} %get-tuple-element.105.refs_0_), channel_id=1, source_target_pairs={{0,8},{1,9},{2,10},{3,11},{4,12},{5,13},{6,14},{7,15},{8,0},{9,1},... | collective-permute-start | bytes 442376 | tf_op jit(solution)/shard_map/ppermute | solution.py:774
  27.0 16.3 %collective-permute-start.9 = (bf16[192,1664]{1,0:T(8,128)(2,1)S(1)}, bf16[192,1664]{1,0:T(8,128)(2,1)S(1)}, u32[]{:S(2)}, u32[]{:S(2)}) collective-permute-start(bf16[192,1664]{1,0:T(8,128)(2,1)S(1)} %shard_map.223.refs_1_.refs_2_.refs_6_), channel_id=1, source_target_pairs={{0,2},{1,5},{2,0},{3,7},{4,6},{5,1},{6,4},{7,3},{8,10},{9,13},{10,... | collective-permute-start | bytes 1916936 | tf_op jit(solution)/shard_map/ppermute | solution.py:774
  28.5 14.7 %collective-permute-start.10 = (bf16[192,1664]{1,0:T(8,128)(2,1)S(1)}, bf16[192,1664]{1,0:T(8,128)(2,1)S(1)}, u32[]{:S(2)}, u32[]{:S(2)}) collective-permute-start(bf16[192,1664]{1,0:T(8,128)(2,1)S(1)} %shard_map.223.refs_1_.refs_2_.refs_6_), channel_id=1, source_target_pairs={{0,4},{1,3},{2,6},{3,1},{4,0},{5,7},{6,2},{7,5},{8,12},{9,11},{10,... | collective-permute-start | bytes 1916936 | tf_op jit(solution)/shard_map/ppermute | solution.py:774
  30.5 16.6 %collective-permute-start.14 = (bf16[96,1536]{1,0:T(8,128)(2,1)S(1)}, bf16[96,1536]{1,0:T(8,128)(2,1)S(1)}, u32[]{:S(2)}, u32[]{:S(2)}) collective-permute-start(bf16[96,1536]{1,0:T(8,128)(2,1)S(1)} %shard_map.226.refs_1_.refs_0_), channel_id=1, source_target_pairs={{0,16},{1,17},{2,18},{3,19},{4,20},{5,21},{6,22},{7,23},{8,24},{9,... | collective-permute-start | bytes 884744 | tf_op jit(solution)/shard_map/ppermute | solution.py:774
  34.6 12.4 %collective-permute-start.13 = (bf16[48,3072]{1,0:T(8,128)(2,1)S(1)}, bf16[48,3072]{1,0:T(8,128)(2,1)S(1)}, u32[]{:S(2)}, u32[]{:S(2)}) collective-permute-start(bf16[48,3072]{1,0:T(8,128)(2,1)S(1)} %shard_map.227.refs_0_), channel_id=1, source_target_pairs={{0,8},{1,9},{2,10},{3,11},{4,12},{5,13},{6,14},{7,15},{8,0},{9,1},... | collective-permute-start | bytes 884744 | tf_op jit(solution)/shard_map/ppermute | solution.py:774
  43.2 15.4 %collective-permute-start.11 = (bf16[192,1664]{1,0:T(8,128)(2,1)S(1)}, bf16[192,1664]{1,0:T(8,128)(2,1)S(1)}, u32[]{:S(2)}, u32[]{:S(2)}) collective-permute-start(bf16[192,1664]{1,0:T(8,128)(2,1)S(1)} %shard_map.224.refs_2_.refs_3_), channel_id=1, source_target_pairs={{0,4},{1,3},{2,6},{3,1},{4,0},{5,7},{6,2},{7,5},{8,12},{9,11},{10,... | collective-permute-start | bytes 1916936 | tf_op jit(solution)/shard_map/ppermute | solution.py:774
  47.3 16.3 %collective-permute-start.16 = (bf16[192,1536]{1,0:T(8,128)(2,1)S(1)}, bf16[192,1536]{1,0:T(8,128)(2,1)S(1)}, u32[]{:S(2)}, u32[]{:S(2)}) collective-permute-start(bf16[192,1536]{1,0:T(8,128)(2,1)S(1)} %shard_map.228.refs_2_.refs_1_.refs_4_), channel_id=1, source_target_pairs={{0,2},{1,5},{2,0},{3,7},{4,6},{5,1},{6,4},{7,3},{8,10},{9,13},{10,... | collective-permute-start | bytes 1769480 | tf_op jit(solution)/shard_map/ppermute | solution.py:774
  47.9 18.4 %collective-permute-start.17 = (bf16[192,1536]{1,0:T(8,128)(2,1)S(1)}, bf16[192,1536]{1,0:T(8,128)(2,1)S(1)}, u32[]{:S(2)}, u32[]{:S(2)}) collective-permute-start(bf16[192,1536]{1,0:T(8,128)(2,1)S(1)} %shard_map.228.refs_2_.refs_1_.refs_4_), channel_id=1, source_target_pairs={{0,4},{1,3},{2,6},{3,1},{4,0},{5,7},{6,2},{7,5},{8,12},{9,11},{10,... | collective-permute-start | bytes 1769480 | tf_op jit(solution)/shard_map/ppermute | solution.py:774
  48.7 17.6 %collective-permute-start.15 = (bf16[96,1536]{1,0:T(8,128)(2,1)S(1)}, bf16[96,1536]{1,0:T(8,128)(2,1)S(1)}, u32[]{:S(2)}, u32[]{:S(2)}) collective-permute-start(bf16[96,1536]{1,0:T(8,128)(2,1)S(1)} %get-tuple-element.109.refs_0_), channel_id=1, source_target_pairs={{0,16},{1,17},{2,18},{3,19},{4,20},{5,21},{6,22},{7,23},{8,24},{9,... | collective-permute-start | bytes 884744 | tf_op jit(solution)/shard_map/ppermute | solution.py:774
  59.5 7.0 %collective-permute-start.12 = (bf16[768,384]{1,0:T(8,128)(2,1)S(1)}, bf16[768,384]{1,0:T(8,128)(2,1)S(1)}, u32[]{:S(2)}, u32[]{:S(2)}) collective-permute-start(bf16[768,384]{1,0:T(8,128)(2,1)S(1)} %shard_map.225.refs_8_.refs_6_), channel_id=1, source_target_pairs={{0,1},{1,0},{2,3},{3,2},{4,5},{5,4},{6,7},{7,6},{8,9},{9,8},{10,11... | collective-permute-start | bytes 1769480 | tf_op jit(solution)/shard_map/ppermute | solution.py:774
  66.6 25.6 %collective-permute-start.19 = (bf16[96,1536]{1,0:T(8,128)(2,1)S(1)}, bf16[96,1536]{1,0:T(8,128)(2,1)S(1)}, u32[]{:S(2)}, u32[]{:S(2)}) collective-permute-start(bf16[96,1536]{1,0:T(8,128)(2,1)S(1)} %shard_map.232.refs_10_.refs_0_), channel_id=1, source_target_pairs={{0,16},{1,17},{2,18},{3,19},{4,20},{5,21},{6,22},{7,23},{8,24},{9,... | collective-permute-start | bytes 884744 | tf_op jit(solution)/shard_map/ppermute | solution.py:774
  71.3 20.1 %collective-permute-start.20 = (bf16[192,1536]{1,0:T(8,128)(2,1)S(1)}, bf16[192,1536]{1,0:T(8,128)(2,1)}, u32[]{:S(2)}, u32[]{:S(2)}) collective-permute-start(bf16[192,1536]{1,0:T(8,128)(2,1)S(1)} %shard_map.235.refs_1_), channel_id=1, source_target_pairs={{0,2},{1,5},{2,0},{3,7},{4,6},{5,1},{6,4},{7,3},{8,10},{9,13},{10,... | collective-permute-start | bytes 1769480 | tf_op jit(solution)/shard_map/ppermute | solution.py:774
  72.0 19.3 %collective-permute-start.21 = (bf16[192,1536]{1,0:T(8,128)(2,1)S(1)}, bf16[192,1536]{1,0:T(8,128)(2,1)S(1)}, u32[]{:S(2)}, u32[]{:S(2)}) collective-permute-start(bf16[192,1536]{1,0:T(8,128)(2,1)S(1)} %shard_map.235.refs_1_), channel_id=1, source_target_pairs={{0,4},{1,3},{2,6},{3,1},{4,0},{5,7},{6,2},{7,5},{8,12},{9,11},{10,... | collective-permute-start | bytes 1769480 | tf_op jit(solution)/shard_map/ppermute | solution.py:774
  72.3 19.0 %collective-permute-start.18 = (bf16[192,1536]{1,0:T(8,128)(2,1)S(1)}, bf16[192,1536]{1,0:T(8,128)(2,1)S(1)}, u32[]{:S(2)}, u32[]{:S(2)}) collective-permute-start(bf16[192,1536]{1,0:T(8,128)(2,1)S(1)} %shard_map.234.refs_2_.refs_1_), channel_id=1, source_target_pairs={{0,4},{1,3},{2,6},{3,1},{4,0},{5,7},{6,2},{7,5},{8,12},{9,11},{10,... | collective-permute-start | bytes 1769480 | tf_op jit(solution)/shard_map/ppermute | solution.py:774
  94.8 20.4 %collective-permute-start.24 = (bf16[192,1536]{1,0:T(8,128)(2,1)}, bf16[192,1536]{1,0:T(8,128)(2,1)}, u32[]{:S(2)}, u32[]{:S(2)}) collective-permute-start(bf16[192,1536]{1,0:T(8,128)(2,1)} %shard_map.237.refs_1_.refs_13_.refs_4_), channel_id=1, source_target_pairs={{0,2},{1,5},{2,0},{3,7},{4,6},{5,1},{6,4},{7,3},{8,10},{9,13},{10,... | collective-permute-start | bytes 1769480 | tf_op jit(solution)/shard_map/ppermute | solution.py:774
  96.3 18.9 %collective-permute-start.25 = (bf16[192,1536]{1,0:T(8,128)(2,1)}, bf16[192,1536]{1,0:T(8,128)(2,1)}, u32[]{:S(2)}, u32[]{:S(2)}) collective-permute-start(bf16[192,1536]{1,0:T(8,128)(2,1)} %shard_map.237.refs_1_.refs_13_.refs_4_), channel_id=1, source_target_pairs={{0,4},{1,3},{2,6},{3,1},{4,0},{5,7},{6,2},{7,5},{8,12},{9,11},{10,... | collective-permute-start | bytes 1769480 | tf_op jit(solution)/shard_map/ppermute | solution.py:774
  97.4 19.4 %collective-permute-start.26 = (bf16[192,1536]{1,0:T(8,128)(2,1)}, bf16[192,1536]{1,0:T(8,128)(2,1)}, u32[]{:S(2)}, u32[]{:S(2)}) collective-permute-start(bf16[192,1536]{1,0:T(8,128)(2,1)} %shard_map.236.refs_2_), channel_id=1, source_target_pairs={{0,4},{1,3},{2,6},{3,1},{4,0},{5,7},{6,2},{7,5},{8,12},{9,11},{10,... | collective-permute-start | bytes 1769480 | tf_op jit(solution)/shard_map/ppermute | solution.py:774
  116.8 6.7 %collective-permute-start.27 = (bf16[512,1152]{1,0:T(8,128)(2,1)S(1)}, bf16[512,1152]{1,0:T(8,128)(2,1)S(1)}, u32[]{:S(2)}, u32[]{:S(2)}) collective-permute-start(bf16[512,1152]{1,0:T(8,128)(2,1)S(1)} %shard_map.242.refs_1_.refs_2_), channel_id=1, source_target_pairs={{0,1},{1,0},{2,3},{3,2},{4,5},{5,4},{6,7},{7,6},{8,9},{9,8},{10,11... | collective-permute-start | bytes 3538952 | tf_op jit(solution)/shard_map/ppermute | solution.py:774
  122.0 10.2 %collective-permute-start.28 = (bf16[192,1536]{1,0:T(8,128)(2,1)}, bf16[192,1536]{1,0:T(8,128)(2,1)S(1)}, u32[]{:S(2)}, u32[]{:S(2)}) collective-permute-start(bf16[192,1536]{1,0:T(8,128)(2,1)} %shard_map.241.refs_1_), channel_id=1, source_target_pairs={{0,4},{1,3},{2,6},{3,1},{4,0},{5,7},{6,2},{7,5},{8,12},{9,11},{10,... | collective-permute-start | bytes 1769480 | tf_op jit(solution)/shard_map/ppermute | solution.py:774
  136.6 16.6 %collective-permute-start.29 = (bf16[384,1536]{1,0:T(8,128)(2,1)}, bf16[384,1536]{1,0:T(8,128)(2,1)}, u32[]{:S(2)}, u32[]{:S(2)}) collective-permute-start(bf16[384,1536]{1,0:T(8,128)(2,1)} %get-tuple-element.123), channel_id=1, source_target_pairs={{0,2},{1,5},{2,0},{3,7},{4,6},{5,1},{6,4},{7,3},{8,10},{9,13},{10,... | collective-permute-start | bytes 3538952 | tf_op jit(solution)/shard_map/ppermute | solution.py:774
  155.4 20.6 %collective-permute-start.32 = (bf16[192,1536]{1,0:T(8,128)(2,1)}, bf16[192,1536]{1,0:T(8,128)(2,1)}, u32[]{:S(2)}, u32[]{:S(2)}) collective-permute-start(bf16[192,1536]{1,0:T(8,128)(2,1)} %shard_map.247.refs_1_.refs_13_), channel_id=1, source_target_pairs={{0,4},{1,3},{2,6},{3,1},{4,0},{5,7},{6,2},{7,5},{8,12},{9,11},{10,... | collective-permute-start | bytes 1769480 | tf_op jit(solution)/shard_map/ppermute | solution.py:774
  156.9 20.9 %collective-permute-start.31 = (bf16[384,1536]{1,0:T(8,128)(2,1)}, bf16[384,1536]{1,0:T(8,128)(2,1)}, u32[]{:S(2)}, u32[]{:S(2)}) collective-permute-start(bf16[384,1536]{1,0:T(8,128)(2,1)} %shard_map.250), channel_id=1, source_target_pairs={{0,2},{1,5},{2,0},{3,7},{4,6},{5,1},{6,4},{7,3},{8,10},{9,13},{10,... | collective-permute-start | bytes 3538952 | tf_op jit(solution)/shard_map/ppermute | solution.py:774
  180.8 16.4 %collective-permute-start.34 = (bf16[192,1536]{1,0:T(8,128)(2,1)}, bf16[192,1536]{1,0:T(8,128)(2,1)}, u32[]{:S(2)}, u32[]{:S(2)}) collective-permute-start(bf16[192,1536]{1,0:T(8,128)(2,1)} %get-tuple-element.134.refs_1_.refs_10_), channel_id=1, source_target_pairs={{0,4},{1,3},{2,6},{3,1},{4,0},{5,7},{6,2},{7,5},{8,12},{9,11},{10,... | collective-permute-start | bytes 1769480 | tf_op jit(solution)/shard_map/ppermute | solution.py:774
  182.4 24.6 %collective-permute-start.33 = (bf16[512,768]{1,0:T(8,128)(2,1)}, bf16[512,768]{1,0:T(8,128)(2,1)}, u32[]{:S(2)}, u32[]{:S(2)}) collective-permute-start(bf16[512,768]{1,0:T(8,128)(2,1)} %shard_map.252.refs_3_), channel_id=1, source_target_pairs={{0,1},{1,0},{2,3},{3,2},{4,5},{5,4},{6,7},{7,6},{8,9},{9,8},{10,11... | collective-permute-start | bytes 2359304 | tf_op jit(solution)/shard_map/ppermute | solution.py:774
  182.4 14.0 %collective-permute-start.35 = (bf16[48,1536]{1,0:T(8,128)(2,1)}, bf16[48,1536]{1,0:T(8,128)(2,1)}, u32[]{:S(2)}, u32[]{:S(2)}) collective-permute-start(bf16[48,1536]{1,0:T(8,128)(2,1)} %get-tuple-element.141), channel_id=1, source_target_pairs={{0,8},{1,9},{2,10},{3,11},{4,12},{5,13},{6,14},{7,15},{8,0},{9,1},... | collective-permute-start | bytes 442376 | tf_op jit(solution)/shard_map/ppermute | solution.py:774
  183.0 14.3 %collective-permute-start.36 = (bf16[48,1536]{1,0:T(8,128)(2,1)}, bf16[48,1536]{1,0:T(8,128)(2,1)}, u32[]{:S(2)}, u32[]{:S(2)}) collective-permute-start(bf16[48,1536]{1,0:T(8,128)(2,1)} %get-tuple-element.142), channel_id=1, source_target_pairs={{0,16},{1,17},{2,18},{3,19},{4,20},{5,21},{6,22},{7,23},{8,24},{9,... | collective-permute-start | bytes 442376 | tf_op jit(solution)/shard_map/ppermute | solution.py:774
  184.3 13.0 %collective-permute-start.37 = (bf16[48,1536]{1,0:T(8,128)(2,1)}, bf16[48,1536]{1,0:T(8,128)(2,1)}, u32[]{:S(2)}, u32[]{:S(2)}) collective-permute-start(bf16[48,1536]{1,0:T(8,128)(2,1)} %get-tuple-element.143), channel_id=1, source_target_pairs={{0,24},{1,25},{2,26},{3,27},{4,28},{5,29},{6,30},{7,31},{8,16},{9,... | collective-permute-start | bytes 442376 | tf_op jit(solution)/shard_map/ppermute | solution.py:774
  199.3 17.8 %collective-permute-start.38 = (bf16[384,1536]{1,0:T(8,128)(2,1)S(1)}, bf16[384,1536]{1,0:T(8,128)(2,1)S(1)}, u32[]{:S(2)}, u32[]{:S(2)}) collective-permute-start(bf16[384,1536]{1,0:T(8,128)(2,1)S(1)} %shard_map.256), channel_id=1, source_target_pairs={{0,2},{1,5},{2,0},{3,7},{4,6},{5,1},{6,4},{7,3},{8,10},{9,13},{10,... | collective-permute-start | bytes 3538952 | tf_op jit(solution)/shard_map/ppermute | solution.py:774
  200.9 16.2 %collective-permute-start.39 = (bf16[48,1536]{1,0:T(8,128)(2,1)S(1)}, bf16[48,1536]{1,0:T(8,128)(2,1)S(1)}, u32[]{:S(2)}, u32[]{:S(2)}) collective-permute-start(bf16[48,1536]{1,0:T(8,128)(2,1)S(1)} %get-tuple-element.154), channel_id=1, source_target_pairs={{0,8},{1,9},{2,10},{3,11},{4,12},{5,13},{6,14},{7,15},{8,0},{9,1},... | collective-permute-start | bytes 442376 | tf_op jit(solution)/shard_map/ppermute | solution.py:774
  203.9 13.2 %collective-permute-start.40 = (bf16[48,1536]{1,0:T(8,128)(2,1)S(1)}, bf16[48,1536]{1,0:T(8,128)(2,1)S(1)}, u32[]{:S(2)}, u32[]{:S(2)}) collective-permute-start(bf16[48,1536]{1,0:T(8,128)(2,1)S(1)} %get-tuple-element.155), channel_id=1, source_target_pairs={{0,16},{1,17},{2,18},{3,19},{4,20},{5,21},{6,22},{7,23},{8,24},{9,... | collective-permute-start | bytes 442376 | tf_op jit(solution)/shard_map/ppermute | solution.py:774
  203.9 13.2 %collective-permute-start.41 = (bf16[48,1536]{1,0:T(8,128)(2,1)S(1)}, bf16[48,1536]{1,0:T(8,128)(2,1)S(1)}, u32[]{:S(2)}, u32[]{:S(2)}) collective-permute-start(bf16[48,1536]{1,0:T(8,128)(2,1)S(1)} %get-tuple-element.156), channel_id=1, source_target_pairs={{0,24},{1,25},{2,26},{3,27},{4,28},{5,29},{6,30},{7,31},{8,16},{9,... | collective-permute-start | bytes 442376 | tf_op jit(solution)/shard_map/ppermute | solution.py:774
  217.3 9.9 %collective-permute-start.44 = (bf16[192,1536]{1,0:T(8,128)(2,1)S(1)}, bf16[192,1536]{1,0:T(8,128)(2,1)S(1)}, u32[]{:S(2)}, u32[]{:S(2)}) collective-permute-start(bf16[192,1536]{1,0:T(8,128)(2,1)S(1)} %get-tuple-element.158.refs_1_.refs_9_), channel_id=1, source_target_pairs={{0,4},{1,3},{2,6},{3,1},{4,0},{5,7},{6,2},{7,5},{8,12},{9,11},{10,... | collective-permute-start | bytes 1769480 | tf_op jit(solution)/shard_map/ppermute | solution.py:774
  218.0 7.6 %collective-permute-start.42 = (bf16[256,768]{1,0:T(8,128)(2,1)S(1)}, bf16[256,768]{1,0:T(8,128)(2,1)S(1)}, u32[]{:S(2)}, u32[]{:S(2)}) collective-permute-start(bf16[256,768]{1,0:T(8,128)(2,1)S(1)} %shard_map.258), channel_id=1, source_target_pairs={{0,1},{1,0},{2,3},{3,2},{4,5},{5,4},{6,7},{7,6},{8,9},{9,8},{10,11... | collective-permute-start | bytes 1179656 | tf_op jit(solution)/shard_map/ppermute | solution.py:774
  218.0 9.3 %collective-permute-start.43 = (bf16[960,768]{1,0:T(8,128)(2,1)S(1)}, bf16[960,768]{1,0:T(8,128)(2,1)S(1)}, u32[]{:S(2)}, u32[]{:S(2)}) collective-permute-start(bf16[960,768]{1,0:T(8,128)(2,1)S(1)} %shard_map.259), channel_id=1, source_target_pairs={{0,1},{1,0},{2,3},{3,2},{4,5},{5,4},{6,7},{7,6},{8,9},{9,8},{10,11... | collective-permute-start | bytes 4423688 | tf_op jit(solution)/shard_map/ppermute | solution.py:774
  219.2 28.9 %collective-permute-start.55 = (f32[24,1536]{1,0:T(8,128)}, f32[24,1536]{1,0:T(8,128)}, u32[]{:S(2)}, u32[]{:S(2)}) collective-permute-start(f32[24,1536]{1,0:T(8,128)} %constant_dynamic-slice_fusion), channel_id=1, source_target_pairs={{0,1},{1,0},{2,3},{3,2},{4,5},{5,4},{6,7},{7,6},{8,9},{9,8},{10,11... | collective-permute-start | bytes 442376 | tf_op jit(solution)/shard_map/ppermute | solution.py:774
  227.5 17.3 %collective-permute-start.45 = (bf16[384,1664]{1,0:T(8,128)(2,1)S(1)}, bf16[384,1664]{1,0:T(8,128)(2,1)S(1)}, u32[]{:S(2)}, u32[]{:S(2)}) collective-permute-start(bf16[384,1664]{1,0:T(8,128)(2,1)S(1)} %shard_map.263), channel_id=1, source_target_pairs={{0,2},{1,5},{2,0},{3,7},{4,6},{5,1},{6,4},{7,3},{8,10},{9,13},{10,... | collective-permute-start | bytes 3833864 | tf_op jit(solution)/shard_map/ppermute | solution.py:774
  228.1 7.0 %collective-permute-start.46 = (bf16[48,1536]{1,0:T(8,128)(2,1)S(1)}, bf16[48,1536]{1,0:T(8,128)(2,1)S(1)}, u32[]{:S(2)}, u32[]{:S(2)}) collective-permute-start(bf16[48,1536]{1,0:T(8,128)(2,1)S(1)} %get-tuple-element.172), channel_id=1, source_target_pairs={{0,8},{1,9},{2,10},{3,11},{4,12},{5,13},{6,14},{7,15},{8,0},{9,1},... | collective-permute-start | bytes 442376 | tf_op jit(solution)/shard_map/ppermute | solution.py:774
  230.6 12.7 %collective-permute-start.47 = (bf16[48,1536]{1,0:T(8,128)(2,1)S(1)}, bf16[48,1536]{1,0:T(8,128)(2,1)S(1)}, u32[]{:S(2)}, u32[]{:S(2)}) collective-permute-start(bf16[48,1536]{1,0:T(8,128)(2,1)S(1)} %get-tuple-element.173), channel_id=1, source_target_pairs={{0,16},{1,17},{2,18},{3,19},{4,20},{5,21},{6,22},{7,23},{8,24},{9,... | collective-permute-start | bytes 442376 | tf_op jit(solution)/shard_map/ppermute | solution.py:774
  230.6 12.7 %collective-permute-start.48 = (bf16[48,1536]{1,0:T(8,128)(2,1)S(1)}, bf16[48,1536]{1,0:T(8,128)(2,1)S(1)}, u32[]{:S(2)}, u32[]{:S(2)}) collective-permute-start(bf16[48,1536]{1,0:T(8,128)(2,1)S(1)} %get-tuple-element.174), channel_id=1, source_target_pairs={{0,24},{1,25},{2,26},{3,27},{4,28},{5,29},{6,30},{7,31},{8,16},{9,... | collective-permute-start | bytes 442376 | tf_op jit(solution)/shard_map/ppermute | solution.py:774
  246.8 10.7 %collective-permute-start.49 = (bf16[192,1664]{1,0:T(8,128)(2,1)}, bf16[192,1664]{1,0:T(8,128)(2,1)}, u32[]{:S(2)}, u32[]{:S(2)}) collective-permute-start(bf16[192,1664]{1,0:T(8,128)(2,1)} %get-tuple-element.175), channel_id=1, source_target_pairs={{0,4},{1,3},{2,6},{3,1},{4,0},{5,7},{6,2},{7,5},{8,12},{9,11},{10,... | collective-permute-start | bytes 1916936 | tf_op jit(solution)/shard_map/ppermute | solution.py:774
  260.4 13.1 %collective-permute-start.51 = (bf16[48,1664]{1,0:T(8,128)(2,1)S(1)}, bf16[48,1664]{1,0:T(8,128)(2,1)S(1)}, u32[]{:S(2)}, u32[]{:S(2)}) collective-permute-start(bf16[48,1664]{1,0:T(8,128)(2,1)S(1)} %get-tuple-element.178), channel_id=1, source_target_pairs={{0,16},{1,17},{2,18},{3,19},{4,20},{5,21},{6,22},{7,23},{8,24},{9,... | collective-permute-start | bytes 479240 | tf_op jit(solution)/shard_map/ppermute | solution.py:774
  261.0 12.5 %collective-permute-start.52 = (bf16[48,1664]{1,0:T(8,128)(2,1)S(1)}, bf16[48,1664]{1,0:T(8,128)(2,1)S(1)}, u32[]{:S(2)}, u32[]{:S(2)}) collective-permute-start(bf16[48,1664]{1,0:T(8,128)(2,1)S(1)} %get-tuple-element.179), channel_id=1, source_target_pairs={{0,24},{1,25},{2,26},{3,27},{4,28},{5,29},{6,30},{7,31},{8,16},{9,... | collective-permute-start | bytes 479240 | tf_op jit(solution)/shard_map/ppermute | solution.py:774
  263.4 10.4 %collective-permute-start.54 = (f32[24,1536]{1,0:T(8,128)S(1)}, f32[24,1536]{1,0:T(8,128)S(1)}, u32[]{:S(2)}, u32[]{:S(2)}) collective-permute-start(f32[24,1536]{1,0:T(8,128)S(1)} %get-tuple-element.196), channel_id=1, source_target_pairs={{0,1},{1,0},{2,3},{3,2},{4,5},{5,4},{6,7},{7,6},{8,9},{9,8},{10,11... | collective-permute-start | bytes 442376 | tf_op jit(solution)/shard_map/ppermute | solution.py:774
  (85 other events, 740.7 us)

commit v4 on v3

--- a/solution.py
+++ b/solution.py
@@ -18,7 +18,7 @@
 SCALE = HEAD ** (-0.5)
 F32 = jnp.float32
 BF = jnp.bfloat16
-VMEM_LIMIT = 20 << 20
+VMEM_LIMIT = 14 << 20
 
 VM = pl.BlockSpec(memory_space=pltpu.VMEM)
 SM = pl.BlockSpec(memory_space=pltpu.SMEM)
@@ -59,8 +59,8 @@
     return out[0] if len(out) == 1 else out
 
 
-def kernel_call(body, ins, in_specs, outs, out_specs=None, scratch=(), cost=5, after=(), limit=None):
-    n, skip, m, k = len(ins), len(after), len(outs), len(scratch)
+def kernel_call(body, ins, in_specs, outs, out_specs=None, scratch=(), cost=5, after=(), limit=None, hold=()):
+    n, skip, m, k = len(ins), len(after) + len(hold), len(outs), len(scratch)
     out_specs = [VM] * m if out_specs is None else list(out_specs)
     staged_in = [i for i, spec in enumerate(in_specs) if spec == 'stage']
     staged_out = [i for i, spec in enumerate(out_specs) if spec == 'stage']
@@ -93,16 +93,16 @@
         for cp in copies:
             cp.wait()
 
-    place = lambda spec: ANY if spec == 'stage' else spec
+    space = lambda spec: ANY if spec == 'stage' else spec
     return pl.pallas_call(
         run,
         out_shape=list(outs),
-        in_specs=[place(spec) for spec in in_specs] + [ANY] * skip,
-        out_specs=[place(spec) for spec in out_specs],
+        in_specs=[space(spec) for spec in in_specs] + [ANY] * len(after) + [VM] * len(hold),
+        out_specs=[space(spec) for spec in out_specs],
         scratch_shapes=[*scratch, *extra],
         compiler_params=pltpu.CompilerParams(vmem_limit_bytes=limit or VMEM_LIMIT),
-        cost_estimate=pl.CostEstimate(flops=cost * 16 * 10**9, bytes_accessed=0, transcendentals=0),
-    )(*ins, *after)
+        cost_estimate=pl.CostEstimate(flops=cost * 7 * 10**9, bytes_accessed=0, transcendentals=0),
+    )(*ins, *after, *hold)
 
 
 def tie(x, *earlier):
@@ -199,42 +199,38 @@
     lax.fori_loop(0, n, step, 0, unroll=unroll)
 
 
-class Rows:
-    def __init__(self, pieces, offs_ref, which, cols, targets, sems):
-        blk = pieces[0].shape[0] // 4
-        self.copies = []
-        for i, (lo, hi, o, step, shift) in enumerate(cols):
-            for q in range(4):
-                for r in range(4):
-                    row = pl.multiple_of(offs_ref[which, q * 4 + r] * step + shift, 16)
-                    self.copies.append(
-                        pltpu.make_async_copy(
-                            pieces[q].at[pl.ds(r * blk, blk), pl.ds(lo, hi - lo)],
-                            targets[o].at[pl.ds(row, blk), :],
-                            sems.at[i * 16 + q * 4 + r],
-                        )
-                    )
-        for cp in self.copies:
-            cp.start()
-
-    def wait(self):
-        for cp in self.copies:
-            cp.wait()
-
-
-def place_rows(pieces, offs, which, cols, shape):
+def columns_first(pieces, q, r):
+    blk = pieces[0].shape[0] // 4
+    return pieces[q], r * blk
+
+
+def place(pieces, offs_ref, which, cols, targets):
+    blk = pieces[0].shape[0] // 4
+    for lo, hi, o, step, shift in cols:
+        for q in range(4):
+            for r in range(4):
+                row = pl.multiple_of(offs_ref[which, q * 4 + r] * step + shift, 16)
+                targets[o][pl.ds(row, blk), :] = pieces[q][r * blk : (r + 1) * blk, lo:hi]
+
+
+def place_levels(near, far, offs_ref, step, shift, target):
+    blk = near.shape[0] // 8
+    lo = 0
+    for level, src in ((0, near), *((2, part) for part in far)):
+        at = 0 if level == 0 else lo
+        for q in range(4):
+            for r in range(2):
+                row = pl.multiple_of(offs_ref[0, q * 4 + level + r] * step + shift, 16)
+                rows = slice((r * 4 + q) * blk, (r * 4 + q + 1) * blk)
+                target[pl.ds(row, blk), at : at + src.shape[1]] = src[rows, :]
+        lo += src.shape[1] if level else 0
+
+
+def place_rows(pieces, offs, which, cols, shape, hold=()):
     def body(offs_ref, *refs):
-        Rows(refs[:4], offs_ref, which, cols, refs[4:5], refs[5]).wait()
-
-    return kernel_call(
-        body,
-        [offs, *pieces],
-        [SM] + [ANY] * 4,
-        [sds(shape, BF)],
-        [VM],
-        [pltpu.SemaphoreType.DMA((16 * len(cols),))],
-        cost=1,
-    )[0]
+        place(refs[:4], offs_ref, which, cols, refs[4:5])
+
+    return kernel_call(body, [offs, *pieces], [SM] + [VM] * 4, [sds(shape, BF)], cost=1, hold=hold)[0]
 
 
 def out_rows(pieces, offs, lo):
@@ -242,24 +238,13 @@
     return place_rows(pieces, offs, 1, [(lo, lo + DH, 0, blk, 0)], (16 * blk, DH))
 
 
-def send_out(dw, offs_ref, outs, sems):
+def send_out(dw, offs_ref, outs):
     own, to_b, to_a = outs
     blk = dw.shape[0] // 16
-    copies = []
     for q, (dst, base) in enumerate(((own, 0), (to_a, 0), (to_b, 0), (to_a, 4))):
         for r in range(4):
             row = pl.multiple_of(offs_ref[0, q * 4 + r] * blk, 16)
-            copies.append(
-                pltpu.make_async_copy(
-                    dw.at[pl.ds(row, blk), :],
-                    dst.at[pl.ds((base + r) * blk, blk), :],
-                    sems.at[q * 4 + r],
-                )
-            )
-    for cp in copies:
-        cp.start()
-    for cp in copies:
-        cp.wait()
+            dst[(base + r) * blk : (base + r + 1) * blk, :] = dw[pl.ds(row, blk), :]
 
 
 def pack_kernel(core, qkv, out, cq, ckv, cout, win, gains, biases, keep, send, vecs):
@@ -288,66 +273,36 @@
         send[:, at + k * hr : at + (k + 1) * hr] = jnp.where(c == 0, second, first)
 
 
-def order_kernel(core, keep, got, wout, one, two, rest):
+def order_kernel(core, keep, got, wout, both, one, three, last):
     c = core[0]
     keep, got, wout = ready(keep, got, wout)
     rows = keep.shape[0]
-    at = 0
-    for dst in (one, two, rest):
-        width = min(dst.shape[1], keep.shape[1] - at)
-        a, b = keep[:, at : at + width], got[:, at : at + width]
-        dst[0:rows, 0:width] = jnp.where(c == 0, a, b)
-        dst[rows:, 0:width] = jnp.where(c == 0, b, a)
-        at += width
-    rest[:, width : width + D] = wout[0 : 2 * rows, :]
-    rest[:, width + D :] = wout[2 * rows :, :]
-
-
-def cat(parts, after=()):
-    shape = (sum(p.shape[0] for p in parts), parts[0].shape[1])
-    n = len(parts)
+    for b, (top, under) in enumerate(((keep, got), (got, keep))):
+        for dst, at, width in ((both, 0, both.shape[1]), (one, 0, one.shape[1]), (three, both.shape[1], 4 * DH)):
+            dst[b * rows : (b + 1) * rows, :width] = jnp.where(c == 0, top[:, at : at + width], under[:, at : at + width])
+    three[:, 4 * DH :] = wout[0 : 2 * rows, :]
+    last[...] = wout[2 * rows :, :]
+
+
+def cats(jobs, after=()):
+    arrays, places, outs = [], [], []
+    for job in jobs:
+        at, outs = 0, [*outs, sds((sum(x.shape[0] for x, _, _ in job), job[0][2]), BF)]
+        for x, lo, width in job:
+            arrays.append(x)
+            places.append((len(outs) - 1, at, lo, width))
+            at += x.shape[0]
+    n = len(arrays)
 
     def body(*refs):
-        held, sems = refs[n + 1 :]
-        copies, at = [], 0
-        for i, r in enumerate(refs[:n]):
-            copies.append(pltpu.make_async_copy(r, held.at[pl.ds(at, r.shape[0]), :], sems.at[i]))
-            at += r.shape[0]
-        for cp in copies:
-            cp.start()
-        for cp in copies:
-            cp.wait()
-        out = pltpu.make_async_copy(held, refs[n], sems.at[n])
-        out.start()
-        out.wait()
-
-    scratch = [pltpu.VMEM(shape, BF), pltpu.SemaphoreType.DMA((n + 1,))]
-    return kernel_call(body, parts, [ANY] * n, [sds(shape, BF)], [ANY], scratch, cost=1, after=after)[0]
-
-
-def split_cat(first, second, after=()):
-    rows, width = first.shape[0], first.shape[1] // 2
-
-    def body(*refs):
-        held, sems = refs[4:]
-        copies = []
-        for i in range(2):
-            copies.append(pltpu.make_async_copy(refs[i], held.at[pl.ds(i * rows, rows), :], sems.at[i]))
-        for cp in copies:
-            cp.start()
-        for cp in copies:
-            cp.wait()
-        copies = []
-        for j in range(2):
-            copies.append(pltpu.make_async_copy(held.at[:, pl.ds(j * width, width)], refs[2 + j], sems.at[2 + j]))
-        for cp in copies:
-            cp.start()
-        for cp in copies:
-            cp.wait()
-
-    outs = [sds((2 * rows, width), BF)] * 2
-    scratch = [pltpu.VMEM((2 * rows, 2 * width), BF), pltpu.SemaphoreType.DMA((4,))]
-    return kernel_call(body, [first, second], [ANY] * 2, outs, [ANY] * 2, scratch, cost=1, after=after)
+        for src, (o, at, lo, width) in zip(refs[:n], places):
+            refs[n + o][at : at + src.shape[0], :] = src[:, lo : lo + width]
+
+    return kernel_call(body, arrays, [VM] * n, outs, cost=1, after=after)
+
+
+def whole(*arrays):
+    return [(x, 0, x.shape[1]) for x in arrays]
 
 
 def prepare_kernel(lens, tok_own, tok_other, cot_own, cot_other, mem_own, mem_other, tok, g, mem, xhat):
@@ -380,12 +335,10 @@
             g[at : at + LEN, :] = (src[s * LEN : (s + 1) * LEN, :].astype(F32) * live).astype(BF)
 
 
-def self_kernel(lens, core, offs, a, b, ab, own, xhat, keep, back, first, packed, probs, comb, vec, wqkv, gcol, sems):
+def self_kernel(lens, core, offs, own, a, b, ab, xhat, keep, back, first, packed, probs, comb, vec, wqkv, gcol):
     c = core[0]
     blk = D // 16
-    rows = Rows((own, a, b, ab), offs, 0, [(4 * DH, 4 * DH + 128, 1, blk, 0), (0, 3 * DH, 0, blk, 0)], (wqkv, gcol), sems)
-    rows.wait()
-    flush(wqkv)
+    place((own, a, b, ab), offs, 0, [(4 * DH, 4 * DH + 128, 1, blk, 0), (0, 3 * DH, 0, blk, 0)], (wqkv, gcol))
     xhat = ready(xhat)
     vec[...] = jnp.transpose(gcol[...].astype(F32))[:8]
     gain, bias = vec[0:1], vec[3:4]
@@ -419,12 +372,10 @@
     comb[:, half_lanes(1 - c)] = nn(comb[:, D:], back[DH:, :]).astype(BF)
 
 
-def kv_kernel(offs, a, b, ab, own, mem, kv, wckv, wcq, sems):
+def kv_kernel(offs, own, a, b, ab, mem, kv, wckv, wcq):
     blk = D // 16
-    rows = Rows((own, a, b, ab), offs, 0, [(2 * DH, 4 * DH, 0, blk, 0), (DH, 2 * DH, 1, blk, 0)], (wckv, wcq), sems)
+    place((own, a, b, ab), offs, 0, [(2 * DH, 4 * DH, 0, blk, 0), (DH, 2 * DH, 1, blk, 0)], (wckv, wcq))
     mem = ready(mem)
-    rows.wait()
-    flush(wckv, wcq)
 
     def step(b):
         rows = pl.ds(pl.multiple_of(b * 480, 480), 480)
@@ -474,9 +425,9 @@
 
 
 def keys_and_cross_kernel(
-    mem_len, offs, a, b, ab, own, mem, core, vec, tok, part, recv, keep, back, kv, wckv, wcq, resid, second, cq, probs, comb, sems
+    mem_len, offs, own, a, b, ab, mem, core, vec, tok, part, recv, keep, back, kv, wckv, wcq, resid, second, cq, probs, comb
 ):
-    kv_kernel(offs, a, b, ab, own, mem, kv, wckv, wcq, sems)
+    kv_kernel(offs, own, a, b, ab, mem, kv, wckv, wcq)
     cross_kernel(mem_len, core, vec, tok, part, recv, wcq, kv, keep, back, resid, second, cq, probs, comb)
 
 
@@ -507,14 +458,12 @@
     loop(4, step)
 
 
-def mlp_kernel(offs, pa, pb, pab, pown, g, slope, win, hidden, own, comb, ginner, wout, sems):
+def mlp_kernel(offs, pieces, near, far, g, slope, win, hidden, own, comb, ginner, wout):
     half = own.shape[0]
     blk = D // 16
-    cols = [(0, D, 0, 2 * blk, 0), (D, 2 * D, 0, 2 * blk, blk)]
-    columns = Rows((pown, pa, pb, pab), offs, 0, cols, (wout,), sems)
-    g, slope = ready(g, slope)
-    columns.wait()
-    win = ready(win)
+    place(pieces, offs, 0, [(0, D, 0, 2 * blk, 0)], (wout,))
+    place_levels(near, far, offs, 2 * blk, blk, wout)
+    g, slope, win = ready(g, slope, win)
 
     def back(b):
         rows = pl.ds(pl.multiple_of(b * 256, 256), 256)
@@ -529,8 +478,7 @@
     comb[2 * half :, :] = nn(hidden[half:, :], wout[...]).astype(BF)
 
 
-def dmlpout_kernel(offs, hidden, g, *refs):
-    outs, dw, sems = refs[:3], refs[3], refs[4]
+def dmlpout_kernel(offs, hidden, g, to_own, to_b, to_a, dw):
     hidden, g = ready(hidden, g)
     blk = dw.shape[0] // 16
     for b in range(4):
@@ -538,22 +486,22 @@
         for k in range(8):
             row = (4 * b + k // 2) * blk
             dw[row : row + blk, (k % 2) * D : (k % 2 + 1) * D] = part[k * blk : (k + 1) * blk]
-    send_out(dw, offs, outs, sems)
+    send_out(dw, offs, (to_own, to_b, to_a))
 
 
 def mlp_and_grad_kernel(
-    offs, pa, pb, pab, pown, g, slope, win, hidden, third, own, comb, to_own, to_b, to_a, ginner, wout, dw, sems, more_sems
+    offs, pown, pa, pb, pab, near, far_a, far_b, g, slope, win, hidden, third, own, comb, to_own, to_b, to_a, ginner, wout, dw
 ):
-    mlp_kernel(offs, pa, pb, pab, pown, g, slope, win, hidden, own, comb, ginner, wout, sems)
-    dmlpin_kernel(offs, third, ginner, to_own, to_b, to_a, dw, more_sems)
+    mlp_kernel(offs, (pown, pa, pb, pab), near, (far_a, far_b), g, slope, win, hidden, own, comb, ginner, wout)
+    dmlpin_kernel(offs, third, ginner, to_own, to_b, to_a, dw)
 
 
 def dmlpin_kernel(offs, third, ginner, *refs):
     third, ginner = ready(third, ginner)
-    outs, dw, sems = refs[:3], refs[3], refs[4]
+    outs, dw = refs[:3], refs[3]
     for b in range(0, dw.shape[0], 256):
         dw[b : b + 256, :] = tn(third[:, b : b + 256], ginner[...]).astype(BF)
-    send_out(dw, offs, outs, sems)
+    send_out(dw, offs, outs)
 
 
 def cross_back_kernel(
@@ -608,7 +556,7 @@
 
 
 def dcross_kernel(offs, core, mixed, mixed_other, gtwo, second, dcq, dkv, wckv, mem, *refs):
-    outs, gmem, dw, sems = refs[:3], refs[3:5], refs[5], refs[6]
+    outs, gmem, dw = refs[:3], refs[3:5], refs[5]
     mixed, mixed_other, gtwo = ready(mixed, mixed_other, gtwo)
     out_grad(dw, 0, core[0], mixed, mixed_other, gtwo)
     second, dcq = ready(second, dcq)
@@ -622,7 +570,7 @@
     mem = ready(mem)
     for b in range(0, D, 256):
         dw[b : b + 256, 2 * DH :] = tn(mem[:, b : b + 256], dkv[...]).astype(BF)
-    send_out(dw, offs, outs, sems)
+    send_out(dw, offs, outs)
 
 
 def self_back_kernel(
@@ -674,7 +622,7 @@
 
 
 def dself_kernel(offs, core, mixed, mixed_other, gone, first, dpacked, dvec_two, dvec_one, *refs):
-    outs, dw, vecs, sems = refs[:3], refs[3], refs[4], refs[5]
+    outs, dw, vecs = refs[:3], refs[3], refs[4]
     mixed, mixed_other, gone = ready(mixed, mixed_other, gone)
     out_grad(dw, 0, core[0], mixed, mixed_other, gone)
     first, dpacked, dvec_two, dvec_one = ready(first, dpacked, dvec_two, dvec_one)
@@ -684,7 +632,7 @@
     for i, (v, row) in enumerate(((dvec_one, 2), (dvec_one, 0), (dvec_two, 0), (dvec_one, 3), (dvec_one, 1), (dvec_two, 1))):
         vecs[i : i + 1, :] = v[row : row + 1, :]
     dw[:, 4 * DH :] = jnp.transpose(vecs[...]).astype(BF)
-    send_out(dw, offs, outs, sems)
+    send_out(dw, offs, outs)
 
 
 def tokens_back_kernel(vec, tok, part, recv, gresid, gmem, gmem_recv, gtok, gmemory):
@@ -819,11 +767,10 @@
         )
 
     def self_attention(pieces, lens, xhat, keep, back, after=()):
-        own, a, b, ab = pieces
         return kernel_call(
             self_kernel,
-            [lens, core, offs, a, b, ab, own, xhat, keep, back],
-            [SM] * 3 + [ANY] * 4 + [STAGE] * 3,
+            [lens, core, offs, *pieces, xhat, keep, back],
+            [SM] * 3 + [VM] * 4 + [STAGE] * 3,
             [
                 sds((r2, D), BF),
                 sds((r2, 3 * DH), BF),
@@ -833,18 +780,17 @@
                 sds((D, 3 * DH), BF),
             ],
             [STAGE] * 6,
-            [pltpu.VMEM((D, 128), BF), pltpu.SemaphoreType.DMA((32,))],
+            [pltpu.VMEM((D, 128), BF)],
             cost=6,
             after=after,
         )
 
     def cross_attention(pieces, mem, vec, tok, comb, recv, keep, back, after=()):
-        own, a, b, ab = pieces
         kv_rows = s2 * pad
         return kernel_call(
             lambda *refs: keys_and_cross_kernel(mem_len, *refs),
-            [offs, a, b, ab, own, mem, core, vec, tok, comb, recv, keep, back],
-            [SM] + [ANY] * 4 + [STAGE, SM] + [STAGE] * 6,
+            [offs, *pieces, mem, core, vec, tok, comb, recv, keep, back],
+            [SM] + [VM] * 4 + [STAGE, SM] + [STAGE] * 6,
             [
                 sds((kv_rows, D), BF),
                 sds((D, 2 * DH), BF),
@@ -856,12 +802,11 @@
                 sds((r2, 3 * DH), BF),
             ],
             [STAGE] * 8,
-            [pltpu.SemaphoreType.DMA((32,))],
             cost=12,
             after=after,
         )
 
-    def inner_part(resid_one, comb, recv, vec, w_in, after=()):
+    def inner_part(resid_one, comb, recv, vec, w_in, hold=()):
         return kernel_call(
             inner_kernel,
             [resid_one, comb, recv, vec, w_in],
@@ -869,43 +814,34 @@
             [sds((r2, D), F32), sds((r2, D), BF), sds((r2, fh), BF), sds((r2, fh), BF)],
             [STAGE] * 4,
             cost=5,
-            after=after,
-        )
-
-    def inner_weight(pieces):
-        return place_rows(pieces, offs, 0, [(0, fh, 0, wb, 0)], (D, fh))
-
-    def grads(body, ins, specs, ncols, extra=(), scratch=(), cost=5, after=()):
+            hold=hold,
+        )
+
+    def inner_weight(pieces, hold=()):
+        return place_rows(pieces, offs, 0, [(0, fh, 0, wb, 0)], (D, fh), hold)
+
+    def grads(body, ins, specs, ncols, extra=(), scratch=(), cost=5, after=(), hold=()):
         return kernel_call(
             body,
             [offs, *ins],
             [SM, *specs],
-            [sds((4 * wb, ncols), BF)] * 2 + [sds((8 * wb, ncols), BF)] + list(extra),
-            [ANY] * 3 + [STAGE] * len(extra),
-            [pltpu.VMEM((D, ncols), BF), *scratch, pltpu.SemaphoreType.DMA((16,))],
+            [sds((n * wb, ncols), BF) for n in (4, 4, 8)] + list(extra),
+            scratch=[pltpu.VMEM((D, ncols), BF), *scratch],
             cost=cost,
             after=after,
-        )
-
-    def mlp_part(pieces, g, slope, w_in, hidden, third, after=()):
-        own, a, b, ab = pieces
+            hold=hold,
+        )
+
+    def mlp_part(pieces, g, slope, w_in, hidden, third, after=(), hold=()):
         return kernel_call(
             mlp_and_grad_kernel,
-            [offs, a, b, ab, own, g, slope, w_in, hidden, third],
-            [SM] + [ANY] * 4 + [STAGE] * 5,
-            [sds((rows, D), BF), sds((3 * rows, D), BF)]
-            + [sds((4 * wb, fh), BF)] * 2
-            + [sds((8 * wb, fh), BF)],
-            [STAGE] * 2 + [ANY] * 3,
-            [
-                pltpu.VMEM((r2, fh), BF),
-                pltpu.VMEM((fh, D), BF),
-                pltpu.VMEM((D, fh), BF),
-                pltpu.SemaphoreType.DMA((32,)),
-                pltpu.SemaphoreType.DMA((16,)),
-            ],
+            [offs, *pieces, g, slope, w_in, hidden, third],
+            [SM] + [VM] * 12,
+            [sds((rows, D), BF), sds((3 * rows, D), BF)] + [sds((n * wb, fh), BF) for n in (4, 4, 8)],
+            scratch=[pltpu.VMEM((r2, fh), BF), pltpu.VMEM((fh, D), BF), pltpu.VMEM((D, fh), BF)],
             cost=11,
             after=after,
+            hold=hold,
         )
 
     def cross_back(resid_two, comb, recv, part, after=()):
@@ -1009,54 +945,72 @@
             cost=1,
             limit=60 << 20,
         )
-        one, two, rest = kernel_call(
+        both, one, three, last = kernel_call(
             order_kernel,
             [core, keep, sib(send), mlp_out],
             [SM] + [STAGE] * 3,
-            [sds((2 * wr, w), BF) for w in (widths[0], widths[1], 8 * DH)],
-            [STAGE] * 3,
+            [sds((2 * wr, w), BF) for w in (widths[0] + widths[1], widths[0], 6 * DH, 2 * DH)],
+            [STAGE] * 4,
             cost=1,
             after=[lens, pairs[1], pairs[3]],
         )
-        along = [moves.near_z(one), moves.far_z(one), moves.opposite_z(one)]
-        near_two = moves.near_z(two)
+        near, far, side_a, side_b = moves.near_z, moves.far_z, moves.side_a, moves.side_b
+        near_both, along, a_last, b_last = near(both), [far(one), moves.opposite_z(one)], side_a(last), side_b(last)
         tok, g, mem, xhat = prepare(lens, pairs, after=(one,))
-        one = cat([one, *along], after=(tok, near_two))
-        two = cat([two, near_two], after=(one,))
-        rest = tie(rest, two)
-        a1, b1, far_two, near_rest = moves.side_a(one), moves.side_b(one), moves.far_z(two), moves.near_z(rest)
+        one, two = cats(
+            [
+                [(one, 0, widths[0]), (near_both, 0, widths[0]), *whole(*along)],
+                [(both, widths[0], widths[1]), (near_both, widths[0], widths[1])],
+            ],
+            after=(tok, a_last, b_last),
+        )
+        three, ab_last = tie(three, one), tie(a_last, one)
+        a1, b1, far_two, near_three, ab_last = side_a(one), side_b(one), far(two), near(three), side_b(ab_last)
         a1 = tie(a1, b1)
-        two = cat([two, far_two], after=(a1, near_rest))
-        three, four = split_cat(rest, near_rest, after=(two,))
-        ab1, a2, b2, far_three = moves.side_b(a1), moves.side_a(two), moves.side_b(two), moves.far_z(three)
+        two, last, four, three = cats(
+            [
+                whole(two, far_two),
+                whole(last, a_last, b_last, ab_last),
+                [(three, 4 * DH, D), (near_three, 4 * DH, D)],
+                [(three, 0, 4 * DH), (near_three, 0, 4 * DH)],
+            ],
+            after=(a1,),
+        )
+        ab1, a2, b2, far_three, near_last = side_b(a1), side_a(two), side_b(two), far(three), near(last)
         a2 = tie(a2, b2, ab1)
-        three = cat([three, far_three], after=(a2,))
+        three, last, *parts = cats(
+            [
+                whole(three, far_three),
+                whole(last, near_last),
+                [(last, 0, DH), (near_last, 0, DH)],
+                [(last, DH, DH), (near_last, DH, DH)],
+            ],
+            after=(a2,),
+        )
         out = out_rows([one, a1, b1, ab1], offs, 3 * DH)
         out = (out, sib(out))
-        four, three, a2 = tie(four, out[1], three), tie(three, out[1]), tie(a2, out[1])
-        ab2, a3, b3, far_four = moves.side_b(a2), moves.side_a(three), moves.side_b(three), moves.far_z(four)
-        first, packed, probs, comb, vec, w_qkv = self_attention([one, a1, b1, ab1], lens, xhat, *out, after=(four,))
-        a3 = tie(a3, b3, ab2, comb)
-        four = cat([four, far_four], after=(a3,))
+        three, a2, four = tie(three, out[1]), tie(a2, out[1]), tie(four, out[1])
+        ab2, a3, b3, far_four, far_a = side_b(a2), side_a(three), side_b(three), far(four), far(tie(parts[0], out[1]))
+        first, packed, probs, comb, vec, w_qkv = self_attention([one, a1, b1, ab1], lens, xhat, *out, after=(three,))
+        a3 = tie(a3, b3, ab2, comb, far_a)
+        (four,) = cats([whole(four, far_four)], after=(a3,))
+        comb = tie(comb, four)
         cout = out_rows([two, a2, b2, ab2], offs, 0)
         cout = (cout, sib(cout))
-        comb = tie(comb, four)
         self_mixed = (comb, sib(comb))
-        ab3, a4, b4 = moves.side_b(a3), moves.side_a(four), moves.side_b(four)
+        ab3, a4, b4, far_b = side_b(a3), side_a(four), side_b(four), far(tie(parts[1], four))
         kv, w_ckv, w_cq, resid_one, second, cq, cprobs, comb = cross_attention(
-            [two, a2, b2, ab2], mem, vec, tok, *self_mixed, *cout, after=(four,)
-        )
-        a4 = tie(a4, b4, ab3, comb)
-        ab4 = moves.side_b(a4)
-        comb = tie(comb, a4)
-        cross_mixed = (comb, sib(comb))
-        w_in = inner_weight([three, a3, b3, ab3])
-        resid_two, third, hidden, slope = inner_part(resid_one, *cross_mixed, vec, w_in)
-        last = [four, a4, b4, ab4]
-        after = (ab4,)
+            [two, a2, b2, ab2], mem, vec, tok, *self_mixed, *cout
+        )
+        comb = tie(comb, ab3, a4, b4, far_b)
+        cross_mixed, ab4 = (comb, sib(comb)), side_b(tie(a4, comb))
+        hold = [kv, cprobs, cq, w_cq, *cout, w_ckv, second]
+        w_in = inner_weight([three, a3, b3, ab3], hold)
+        resid_two, third, hidden, slope = inner_part(resid_one, *cross_mixed, vec, w_in, hold)
+        last = [four, a4, b4, ab4, last, far_a, far_b]
     else:
         tok, g, mem, xhat = prepare(lens, pairs)
-        whole = lambda w: lax.all_gather(w, AXES, axis=0, tiled=True)
+        everywhere = lambda w: lax.all_gather(w, AXES, axis=0, tiled=True)
         split = lambda w: [w[i * w.shape[0] // 4 : (i + 1) * w.shape[0] // 4] for i in range(4)]
 
         def col_half(w, groups):
@@ -1066,13 +1020,16 @@
         vectors = jnp.pad(jnp.concatenate([norm_gains, norm_biases], 0).T, ((0, 0), (0, 122)))
         one = jnp.concatenate([col_half(self_qkv, 3), col_half(self_out, 1), vectors], 1)
         two = jnp.concatenate([col_half(w, w.shape[1] // D) for w in (cross_out, cross_q, cross_kv)], 1)
-        one, two = split(whole(one)), split(whole(two))
-        three = split(whole(col_half(mlp_in, ff // (2 * hr))))
+        one, two = split(everywhere(one)), split(everywhere(two))
+        three = split(everywhere(col_half(mlp_in, ff // (2 * hr))))
         out, cout = out_rows(one, offs, 3 * DH), out_rows(two, offs, 0)
         out, cout = (out, sib(out)), (cout, sib(cout))
-        rowed = whole(mlp_out).reshape(moves.n // 2, 2, hr, D)
+        rowed = everywhere(mlp_out).reshape(moves.n // 2, 2, hr, D)
         rowed = lax.dynamic_index_in_dim(rowed, c, 1, keepdims=False).reshape(16, 2, fh // 32, D)
-        last = split(rowed.transpose(0, 2, 1, 3).reshape(D, 2 * D))
+        rowed = rowed.transpose(1, 0, 2, 3)
+        levels = rowed[1].reshape(4, 4, wb, D).transpose(1, 0, 2, 3).reshape(D, D)
+        last = split(rowed[0].reshape(D, D)) + [levels[: D // 2], levels[D // 2 :, :DH], levels[D // 2 :, DH:]]
+        hold = ()
         first, packed, probs, comb, vec, w_qkv = self_attention(one, lens, xhat, *out)
         self_mixed = (comb, sib(comb))
         kv, w_ckv, w_cq, resid_one, second, cq, cprobs, comb = cross_attention(
@@ -1081,18 +1038,19 @@
         cross_mixed = (comb, sib(comb))
         w_in = inner_weight(three)
         resid_two, third, hidden, slope = inner_part(resid_one, *cross_mixed, vec, w_in)
-        after = ()
-
-
-    side_a, side_b = moves.side_a, moves.side_b
+
+
+    near, far, side_a, side_b = moves.near_z, moves.far_z, moves.side_a, moves.side_b
+    after = ()
 
     def along_z(blocks):
-        return [moves.near_z(blocks[0]), moves.far_z(blocks[1]), moves.opposite_z(blocks[2])]
-
-    d_mlpout = grads(dmlpout_kernel, [hidden, g], [STAGE] * 2, 2 * D, after=after)
+        return [near(blocks[0]), far(blocks[1]), moves.opposite_z(blocks[2])]
+
+    held = [resid_two, vec]
+    d_mlpout = grads(dmlpout_kernel, [hidden, g], [STAGE] * 2, 2 * D, hold=[*hold, *held, third])
     if fast:
         got_a1 = side_a(d_mlpout[2])
-    part, comb, *d_mlpin = mlp_part(last, g, slope, w_in, hidden, third, after=d_mlpout[:1])
+    part, comb, *d_mlpin = mlp_part(last, g, slope, w_in, hidden, third, after=d_mlpout[:1], hold=[*hold, *held])
     if fast:
         (on,) = merge([("pass", d_mlpout[1], got_a1)], after=(part,))
         comb = tie(comb, on)

time: 277 us -> 253 us (0.913)
  Pallas kernels: 104 us -> 73.7 us
  waiting for transfers between devices: 78.1 us -> 93.3 us
  local copies, waits for them, and re-layouts: 26.6 us -> 19.7 us
    pallas_call x32 -> x30, Pallas kernels: 104 us -> 73.7 us  [kernel_call(): pl.pallas_call(run, out_shape=list(outs), in_specs=[space(spec) for spec...]
    ppermute x56 -> x61, waiting for transfers between devices: 78.1 us -> 93.3 us  [permute(): lax.ppermute(x, AXES, [(a, z * self.nf + 2 * yx + c) for a, (z, yx, c) in...]
    unnamed x156, local copies, waits for them, and re-layouts: 20.8 us -> 14.5 us
    ppermute x56 -> x61, starting transfers between devices: 63.3 us -> 61.8 us  [permute(): lax.ppermute(x, AXES, [(a, z * self.nf + 2 * yx + c) for a, (z, yx, c) in...]
  transfers between devices with their start and end apart: 56 -> 61, of which waited for: 21 -> 23; matrix products, arithmetic and copies ran while one was open for 4% -> 4% of each run, Pallas kernels for 32% -> 29%
where the time goes in v4:
time: 253 us; the launch traced here: 252 us
  waiting for transfers between devices  93.3 us (37%)
  Pallas kernels  73.7 us (29%)
  starting transfers between devices  61.8 us (24%)
  local copies, waits for them, and re-layouts  19.7 us (8%)
    ppermute x61, waiting for transfers between devices, permute(): lax.ppermute(x, AXES, [(a, z * self.nf + 2 * yx + c) for a, (z, yx, c) in...  93.3 us
    pallas_call x30, Pallas kernels, kernel_call(): pl.pallas_call(run, out_shape=list(outs), in_specs=[space(spec) for spec...  73.7 us
    ppermute x61, starting transfers between devices, permute(): lax.ppermute(x, AXES, [(a, z * self.nf + 2 * yx + c) for a, (z, yx, c) in...  61.8 us
    unnamed x156, local copies, waits for them, and re-layouts  14.5 us
  transfers between devices with their start and end apart: 61, of which 23 were waited for; matrix products, arithmetic and copies ran while one was open for 4% of the time, Pallas kernels for 29%

profile of v4, /device:TPU:0, one launch (start us, length us, event | category | flops | bytes accessed | tf_op | source)
XLA Modules:
  0.0 252.0 jit_solution(11293274835247628952)
XLA Ops:
  1.7 2.8 %shard_map.220 = (bf16[24,4736]{1,0:T(8,128)(2,1)}, bf16[24,4736]{1,0:T(8,128)(2,1)}) custom-call(s32[1]{0:T(128)} %bitcast.refs_0_.refs_1_.refs_6_, bf16[24,2304]{1,0:T(8,128)(2,1)} %refs_1_.1, bf16[24,768]{1,0:T(8,128)(2,1)} %refs_2_.1, bf16[24,768]{1,0:T(8,128)(2,1)} %refs_3_.2, bf16[24,1536]{1,0:T(8,128)(2,1)} %refs_4_.1, bf16[24,768]{1,0:T(8,128)(2,1)} %refs_5_.2, ...), custom_call_target="tpu_custom_call" | custom-call | flops 7000000000 | tf_op jit(solution)/shard_map/pallas_call | solution.py:97
  5.1 1.5 copy.49.refs_5_
  6.9 3.7 %collective-permute-start.5 = (bf16[48,1664]{1,0:T(8,128)(2,1)S(1)}, bf16[48,1664]{1,0:T(8,128)(2,1)S(1)}, u32[]{:S(2)}, u32[]{:S(2)}) collective-permute-start(bf16[48,1664]{1,0:T(8,128)(2,1)S(1)} %get-tuple-element.112.refs_7_.refs_0_), channel_id=1, source_target_pairs={{0,16},{1,17},{2,18},{3,19},{4,20},{5,21},{6,22},{7,23},{8,24},{9,... | collective-permute-start | bytes 479240 | tf_op jit(solution)/shard_map/ppermute | solution.py:722
  15.2 1.5 copy.50.refs_6_
  16.8 2.5 shard_map.222
  19.3 3.1 %collective-permute-done.5.refs_2_ = bf16[48,1664]{1,0:T(8,128)(2,1)S(1)} collective-permute-done((bf16[48,1664]{1,0:T(8,128)(2,1)S(1)}, bf16[48,1664]{1,0:T(8,128)(2,1)S(1)}, u32[]{:S(2)}, u32[]{:S(2)}) %collective-permute-start.5) | collective-permute-done | bytes 159776 | tf_op jit(solution)/shard_map/ppermute | solution.py:722
  22.5 6.2 %collective-permute-done.4.refs_1_.refs_5_ = bf16[48,3200]{1,0:T(8,128)(2,1)S(1)} collective-permute-done((bf16[48,3200]{1,0:T(8,128)(2,1)S(1)}, bf16[48,3200]{1,0:T(8,128)(2,1)S(1)}, u32[]{:S(2)}, u32[]{:S(2)}) %collective-permute-start.4) | collective-permute-done | bytes 307232 | tf_op jit(solution)/shard_map/ppermute | solution.py:722
  30.7 4.0 %collective-permute-start.14 = (bf16[96,1536]{1,0:T(8,128)(2,1)S(1)}, bf16[96,1536]{1,0:T(8,128)(2,1)S(1)}, u32[]{:S(2)}, u32[]{:S(2)}) collective-permute-start(bf16[96,1536]{1,0:T(8,128)(2,1)S(1)} %get-tuple-element.118.refs_0_), channel_id=1, source_target_pairs={{0,16},{1,17},{2,18},{3,19},{4,20},{5,21},{6,22},{7,23},{8,24},{9,... | collective-permute-start | bytes 884744 | tf_op jit(solution)/shard_map/ppermute | solution.py:722
  34.7 1.6 collective-permute-start.15
  36.3 9.7 %collective-permute-done.10.refs_0_ = bf16[192,1664]{1,0:T(8,128)(2,1)S(1)} collective-permute-done((bf16[192,1664]{1,0:T(8,128)(2,1)S(1)}, bf16[192,1664]{1,0:T(8,128)(2,1)S(1)}, u32[]{:S(2)}, u32[]{:S(2)}) %collective-permute-start.10) | collective-permute-done | bytes 639008 | tf_op jit(solution)/shard_map/ppermute | solution.py:722
  48.4 1.7 collective-permute-start.20
  50.5 2.6 %collective-permute-start.18 = (bf16[192,768]{1,0:T(8,128)(2,1)S(1)}, bf16[192,768]{1,0:T(8,128)(2,1)S(1)}, u32[]{:S(2)}, u32[]{:S(2)}) collective-permute-start(bf16[192,768]{1,0:T(8,128)(2,1)S(1)} %get-tuple-element.121.refs_2_.refs_4_.refs_6_), channel_id=1, source_target_pairs={{0,8},{1,9},{2,10},{3,11},{4,12},{5,13},{6,14},{7,15},{8,0},{9,1},... | collective-permute-start | bytes 884744 | tf_op jit(solution)/shard_map/ppermute | solution.py:722
  53.1 8.9 %collective-permute-done.12.refs_4_.refs_2_.refs_6_ = bf16[192,1664]{1,0:T(8,128)(2,1)S(1)} collective-permute-done((bf16[192,1664]{1,0:T(8,128)(2,1)S(1)}, bf16[192,1664]{1,0:T(8,128)(2,1)S(1)}, u32[]{:S(2)}, u32[]{:S(2)}) %collective-permute-start.12) | collective-permute-done | bytes 639008 | tf_op jit(solution)/shard_map/ppermute | solution.py:722
  63.6 4.7 %collective-permute-done.20.refs_1_.refs_3_ = bf16[192,1536]{1,0:T(8,128)(2,1)S(1)} collective-permute-done((bf16[192,1536]{1,0:T(8,128)(2,1)S(1)}, bf16[192,1536]{1,0:T(8,128)(2,1)S(1)}, u32[]{:S(2)}, u32[]{:S(2)}) %collective-permute-start.20) | collective-permute-done | bytes 589856 | tf_op jit(solution)/shard_map/ppermute | solution.py:722
  69.3 1.7 collective-permute-start.24
  71.3 1.7 collective-permute-start.25
  74.2 6.9 %shard_map.232 = (bf16[512,768]{1,0:T(8,128)(2,1)S(1)}, bf16[512,1152]{1,0:T(8,128)(2,1)S(1)}, bf16[8,64,384]{2,1,0:T(8,128)(2,1)S(1)}, bf16[512,1152]{1,0:T(8,1...) custom-call(s32[8]{0:T(128)S(1)} %pad_add_fusion.1.refs_4_.refs_0_, s32[1]{0:T(128)} %bitcast.refs_0_.refs_1_.refs_6_, ...), custom_call_target="tpu_custom_call" | custom-call | flops 41999998976 | tf_op jit(solution)/shard_map/pallas_call | solution.py:97
  82.1 8.7 %collective-permute-done.25.refs_4_.refs_6_ = bf16[384,384]{1,0:T(8,128)(2,1)S(1)} collective-permute-done((bf16[384,384]{1,0:T(8,128)(2,1)S(1)}, bf16[384,384]{1,0:T(8,128)(2,1)S(1)}, u32[]{:S(2)}, u32[]{:S(2)}) %collective-permute-start.25) | collective-permute-done | bytes 294944 | tf_op jit(solution)/shard_map/ppermute | solution.py:722
  94.9 1.7 collective-permute-start.30
  96.7 11.6 %shard_map.240 = (bf16[1920,768]{1,0:T(8,128)(2,1)S(1)}, bf16[768,768]{1,0:T(8,128)(2,1)S(1)}, bf16[768,384]{1,0:T(8,128)(2,1)S(1)}, f32[512,768]{1,0:T(8,128)S(...) custom-call(s32[2,16]{1,0:T(2,128)S(1)} %pad_add_fusion.refs_0_.refs, ...), custom_call_target="tpu_custom_call" | custom-call | flops 83999997952 | tf_op jit(solution)/shard_map/pallas_call | solution.py:97
  108.4 4.5 %collective-permute-done.31.refs_4_.refs_7_ = bf16[384,384]{1,0:T(8,128)(2,1)S(1)} collective-permute-done((bf16[384,384]{1,0:T(8,128)(2,1)S(1)}, bf16[384,384]{1,0:T(8,128)(2,1)S(1)}, u32[]{:S(2)}, u32[]{:S(2)}) %collective-permute-start.31) | collective-permute-done | bytes 294944 | tf_op jit(solution)/shard_map/ppermute | solution.py:722
  115.8 4.1 %shard_map.244 = (f32[512,768]{1,0:T(8,128)S(1)}, bf16[512,768]{1,0:T(8,128)(2,1)S(1)}, bf16[512,1536]{1,0:T(8,128)(2,1)S(1)}, bf16[512,1536]{1,0:T(8,128)(2,1)S(1)}) custom-call(f32[512,768]{1,0:T(8,128)S(1)} %get-tuple-element.129.refs_0_.refs_2_, bf16[512,1152]{1,0:T(8,128)(2,1)S(1)} %shard_map.242.refs_1_.refs_2_, ...), custom_call_target="tpu_custom_call" | custom-call | flops 35000000512 | tf_op jit(solution)/shard_map/pallas_call | solution.py:97
  120.0 2.1 shard_map.246
  122.6 6.8 %shard_map.247 = (bf16[256,768]{1,0:T(8,128)(2,1)S(1)}, bf16[768,768]{1,0:T(8,128)(2,1)S(1)}, bf16[192,1536]{1,0:T(8,128)(2,1)S(1)}, bf16[192,1536]{1,0:T(8,128)(2,1)S(1)}, bf16[384,1536]{1,0:T(8,128)(2,1)S(1)}) custom-call(s32[2,16]{1,0:T(2,128)S(1)} %pad_add_fusion.refs_0_.refs_2_, bf16[192,768]{1,0:T(8,128)(2,1)S(1)} %shard_map.237.refs_1_, ...), custom_call_target="tpu_custom_call" | custom-call | flops 76999999488 | tf_op jit(solution)/shard_map/pallas_call | solution.py:97
  129.4 9.0 %collective-permute-done.34.refs_1_.refs_3_ = bf16[384,1536]{1,0:T(8,128)(2,1)S(1)} collective-permute-done((bf16[384,1536]{1,0:T(8,128)(2,1)S(1)}, bf16[384,1536]{1,0:T(8,128)(2,1)S(1)}, u32[]{:S(2)}, u32[]{:S(2)}) %collective-permute-start.34) | collective-permute-done | bytes 1179680 | tf_op jit(solution)/shard_map/ppermute | solution.py:722
  140.5 1.8 collective-permute-done.35.refs_4_
  142.4 1.8 copy-done.26
  148.8 11.5 %shard_map.250 = (bf16[256,768]{1,0:T(8,128)(2,1)}, f32[512,768]{1,0:T(8,128)S(1)}, bf16[512,768]{1,0:T(8,128)(2,1)S(1)}, bf16[512,384]{1,0:T(8,128)(2,1)S(1)}, ...) custom-call(s32[1]{0:T(128)} %bitcast.refs_0_.refs_1_.refs_6_, ...), custom_call_target="tpu_custom_call" | custom-call | flops 76999999488 | tf_op jit(solution)/shard_map/pallas_call | solution.py:97
  162.6 1.8 collective-permute-start.41
  164.4 2.6 %collective-permute-start.42 = (bf16[48,1536]{1,0:T(8,128)(2,1)S(1)}, bf16[48,1536]{1,0:T(8,128)(2,1)S(1)}, u32[]{:S(2)}, u32[]{:S(2)}) collective-permute-start(bf16[48,1536]{1,0:T(8,128)(2,1)S(1)} %get-tuple-element.163), channel_id=1, source_target_pairs={{0,24},{1,25},{2,26},{3,27},{4,28},{5,29},{6,30},{7,31},{8,16},{9,... | collective-permute-start | bytes 442376 | tf_op jit(solution)/shard_map/ppermute | solution.py:722
  167.0 6.5 %shard_map.254 = (bf16[192,1536]{1,0:T(8,128)(2,1)S(1)}, bf16[192,1536]{1,0:T(8,128)(2,1)S(1)}, bf16[384,1536]{1,0:T(8,128)(2,1)S(1)}, bf16[960,768]{1,0:T(8,128)(2,1)S(1)}, bf16[960,768]{1,0:T(8,128)(2,1)S(1)}) custom-call(s32[2,16]{1,0:T(2,128)S(1)} %pad_add_fusion.refs_0_.refs_2_, s32[1]{0:T(128)} %bitcast.refs_0_.refs_1_.refs_6_, ...), custom_call_target="tpu_custom_call" | custom-call | flops 70000001024 | tf_op jit(solution)/shard_map/pallas_call | solution.py:97
  173.6 3.0 %collective-permute-done.41.refs_5_ = bf16[48,1536]{1,0:T(8,128)(2,1)S(1)} collective-permute-done((bf16[48,1536]{1,0:T(8,128)(2,1)S(1)}, bf16[48,1536]{1,0:T(8,128)(2,1)S(1)}, u32[]{:S(2)}, u32[]{:S(2)}) %collective-permute-start.41) | collective-permute-done | bytes 147488 | tf_op jit(solution)/shard_map/ppermute | solution.py:722
  177.4 3.6 %collective-permute-start.44 = (bf16[48,1536]{1,0:T(8,128)(2,1)S(1)}, bf16[48,1536]{1,0:T(8,128)(2,1)S(1)}, u32[]{:S(2)}, u32[]{:S(2)}) collective-permute-start(bf16[48,1536]{1,0:T(8,128)(2,1)S(1)} %get-tuple-element.172), channel_id=1, source_target_pairs={{0,8},{1,9},{2,10},{3,11},{4,12},{5,13},{6,14},{7,15},{8,0},{9,1},... | collective-permute-start | bytes 442376 | tf_op jit(solution)/shard_map/ppermute | solution.py:722
  181.0 2.4 collective-permute-start.46
  184.1 8.8 %shard_map.256 = (f32[256,768]{1,0:T(8,128)S(1)}, bf16[512,768]{1,0:T(8,128)(2,1)S(1)}, bf16[512,1152]{1,0:T(8,128)(2,1)S(1)}, bf16[256,768]{1,0:T(8,128)(2,1)S(...) custom-call(s32[1]{0:T(128)} %bitcast.refs_0_.refs_1_.refs_6_, f32[8,768]{1,0:T(8,128)S(1)} %copy-done.72, ...), custom_call_target="tpu_custom_call" | custom-call | flops 62999998464 | tf_op jit(solution)/shard_map/pallas_call | solution.py:97
  196.4 2.4 shard_map.261
  198.9 4.6 %collective-permute-done.49.refs_2_ = bf16[192,1536]{1,0:T(8,128)(2,1)S(1)} collective-permute-done((bf16[192,1536]{1,0:T(8,128)(2,1)S(1)}, bf16[192,1536]{1,0:T(8,128)(2,1)S(1)}, u32[]{:S(2)}, u32[]{:S(2)}) %collective-permute-start.49) | collective-permute-done | bytes 589856 | tf_op jit(solution)/shard_map/ppermute | solution.py:722
  203.7 1.8 collective-permute-start.50
  205.4 2.6 %collective-permute-start.51 = (bf16[48,1536]{1,0:T(8,128)(2,1)S(1)}, bf16[48,1536]{1,0:T(8,128)(2,1)S(1)}, u32[]{:S(2)}, u32[]{:S(2)}) collective-permute-start(bf16[48,1536]{1,0:T(8,128)(2,1)S(1)} %get-tuple-element.190), channel_id=1, source_target_pairs={{0,8},{1,9},{2,10},{3,11},{4,12},{5,13},{6,14},{7,15},{8,0},{9,1},... | collective-permute-start | bytes 442376 | tf_op jit(solution)/shard_map/ppermute | solution.py:722
  208.1 2.3 collective-permute-start.53
  210.4 2.2 shard_map.263
  212.5 8.3 %collective-permute-done.52.refs_4_ = bf16[48,1536]{1,0:T(8,128)(2,1)S(1)} collective-permute-done((bf16[48,1536]{1,0:T(8,128)(2,1)S(1)}, bf16[48,1536]{1,0:T(8,128)(2,1)S(1)}, u32[]{:S(2)}, u32[]{:S(2)}) %collective-permute-start.52) | collective-permute-done | bytes 147488 | tf_op jit(solution)/shard_map/ppermute | solution.py:722
  227.9 1.6 copy.53
  229.5 3.5 %collective-permute-done.54.refs_2_ = bf16[192,1664]{1,0:T(8,128)(2,1)S(1)} collective-permute-done((bf16[192,1664]{1,0:T(8,128)(2,1)S(1)}, bf16[192,1664]{1,0:T(8,128)(2,1)S(1)}, u32[]{:S(2)}, u32[]{:S(2)}) %collective-permute-start.54) | collective-permute-done | bytes 639008 | tf_op jit(solution)/shard_map/ppermute | solution.py:722
  233.3 2.5 collective-permute-start.55
  235.8 2.4 collective-permute-start.57
  238.3 2.3 collective-permute-done.55.refs_1_
  240.6 9.1 %collective-permute-done.56.refs_2_ = bf16[48,1664]{1,0:T(8,128)(2,1)S(1)} collective-permute-done((bf16[48,1664]{1,0:T(8,128)(2,1)S(1)}, bf16[48,1664]{1,0:T(8,128)(2,1)S(1)}, u32[]{:S(2)}, u32[]{:S(2)}) %collective-permute-start.56) | collective-permute-done | bytes 159776 | tf_op jit(solution)/shard_map/ppermute | solution.py:722
  (299 shorter events, 47.6 us)
Async XLA Ops:
  1.2 13.7 %collective-permute-start.7 = (bf16[4,228,768]{2,0,1:T(4,128)(2,1)}, bf16[4,228,768]{2,0,1:T(4,128)(2,1)}, u32[]{:S(2)}, u32[]{:S(2)}) collective-permute-start(bf16[4,228,768]{2,0,1:T(4,128)(2,1)} %param.14), channel_id=1, source_target_pairs={{0,1},{1,0},{2,3},{3,2},{4,5},{5,4},{6,7},{7,6},{8,9},{9,8},{10,11... | collective-permute-start | bytes 4202504 | tf_op jit(solution)/shard_map/ppermute | solution.py:722
  6.9 15.6 %collective-permute-start.5 = (bf16[48,1664]{1,0:T(8,128)(2,1)S(1)}, bf16[48,1664]{1,0:T(8,128)(2,1)S(1)}, u32[]{:S(2)}, u32[]{:S(2)}) collective-permute-start(bf16[48,1664]{1,0:T(8,128)(2,1)S(1)} %get-tuple-element.112.refs_7_.refs_0_), channel_id=1, source_target_pairs={{0,16},{1,17},{2,18},{3,19},{4,20},{5,21},{6,22},{7,23},{8,24},{9,... | collective-permute-start | bytes 479240 | tf_op jit(solution)/shard_map/ppermute | solution.py:722
  10.6 11.9 %collective-permute-start.6 = (bf16[48,1664]{1,0:T(8,128)(2,1)S(1)}, bf16[48,1664]{1,0:T(8,128)(2,1)S(1)}, u32[]{:S(2)}, u32[]{:S(2)}) collective-permute-start(bf16[48,1664]{1,0:T(8,128)(2,1)S(1)} %get-tuple-element.112.refs_7_.refs_0_), channel_id=1, source_target_pairs={{0,24},{1,25},{2,26},{3,27},{4,28},{5,29},{6,30},{7,31},{8,16},{9,... | collective-permute-start | bytes 479240 | tf_op jit(solution)/shard_map/ppermute | solution.py:722
  11.9 7.3 %collective-permute-start.8 = (bf16[48,768]{1,0:T(8,128)(2,1)S(1)}, bf16[48,768]{1,0:T(8,128)(2,1)S(1)}, u32[]{:S(2)}, u32[]{:S(2)}) collective-permute-start(bf16[48,768]{1,0:T(8,128)(2,1)S(1)} %get-tuple-element.115.refs_2_), channel_id=1, source_target_pairs={{0,2},{1,5},{2,0},{3,7},{4,6},{5,1},{6,4},{7,3},{8,10},{9,13},{10,... | collective-permute-start | bytes 221192 | tf_op jit(solution)/shard_map/ppermute | solution.py:722
  15.0 13.7 %collective-permute-start.4 = (bf16[48,3200]{1,0:T(8,128)(2,1)S(1)}, bf16[48,3200]{1,0:T(8,128)(2,1)S(1)}, u32[]{:S(2)}, u32[]{:S(2)}) collective-permute-start(bf16[48,3200]{1,0:T(8,128)(2,1)S(1)} %get-tuple-element.113.refs_4_), channel_id=1, source_target_pairs={{0,8},{1,9},{2,10},{3,11},{4,12},{5,13},{6,14},{7,15},{8,0},{9,1},... | collective-permute-start | bytes 921608 | tf_op jit(solution)/shard_map/ppermute | solution.py:722
  28.8 17.2 %collective-permute-start.10 = (bf16[192,1664]{1,0:T(8,128)(2,1)S(1)}, bf16[192,1664]{1,0:T(8,128)(2,1)S(1)}, u32[]{:S(2)}, u32[]{:S(2)}) collective-permute-start(bf16[192,1664]{1,0:T(8,128)(2,1)S(1)} %get-tuple-element.116.refs_1_.refs_3_), channel_id=1, source_target_pairs={{0,2},{1,5},{2,0},{3,7},{4,6},{5,1},{6,4},{7,3},{8,10},{9,13},{10,... | collective-permute-start | bytes 1916936 | tf_op jit(solution)/shard_map/ppermute | solution.py:722
  29.9 16.1 %collective-permute-start.11 = (bf16[192,1664]{1,0:T(8,128)(2,1)S(1)}, bf16[192,1664]{1,0:T(8,128)(2,1)S(1)}, u32[]{:S(2)}, u32[]{:S(2)}) collective-permute-start(bf16[192,1664]{1,0:T(8,128)(2,1)S(1)} %get-tuple-element.116.refs_1_.refs_3_), channel_id=1, source_target_pairs={{0,4},{1,3},{2,6},{3,1},{4,0},{5,7},{6,2},{7,5},{8,12},{9,11},{10,... | collective-permute-start | bytes 1916936 | tf_op jit(solution)/shard_map/ppermute | solution.py:722
  30.7 16.5 %collective-permute-start.16 = (bf16[48,2304]{1,0:T(8,128)(2,1)S(1)}, bf16[48,2304]{1,0:T(8,128)(2,1)S(1)}, u32[]{:S(2)}, u32[]{:S(2)}) collective-permute-start(bf16[48,2304]{1,0:T(8,128)(2,1)S(1)} %shard_map.227.refs_6_.refs_8_), channel_id=1, source_target_pairs={{0,8},{1,9},{2,10},{3,11},{4,12},{5,13},{6,14},{7,15},{8,0},{9,1},... | collective-permute-start | bytes 663560 | tf_op jit(solution)/shard_map/ppermute | solution.py:722
  30.7 16.5 %collective-permute-start.14 = (bf16[96,1536]{1,0:T(8,128)(2,1)S(1)}, bf16[96,1536]{1,0:T(8,128)(2,1)S(1)}, u32[]{:S(2)}, u32[]{:S(2)}) collective-permute-start(bf16[96,1536]{1,0:T(8,128)(2,1)S(1)} %get-tuple-element.118.refs_0_), channel_id=1, source_target_pairs={{0,16},{1,17},{2,18},{3,19},{4,20},{5,21},{6,22},{7,23},{8,24},{9,... | collective-permute-start | bytes 884744 | tf_op jit(solution)/shard_map/ppermute | solution.py:722
  34.7 12.4 %collective-permute-start.15 = (bf16[48,768]{1,0:T(8,128)(2,1)S(1)}, bf16[48,768]{1,0:T(8,128)(2,1)S(1)}, u32[]{:S(2)}, u32[]{:S(2)}) collective-permute-start(bf16[48,768]{1,0:T(8,128)(2,1)S(1)} %shard_map.226), channel_id=1, source_target_pairs={{0,4},{1,3},{2,6},{3,1},{4,0},{5,7},{6,2},{7,5},{8,12},{9,11},{10,... | collective-permute-start | bytes 221192 | tf_op jit(solution)/shard_map/ppermute | solution.py:722
  46.0 16.0 %collective-permute-start.12 = (bf16[192,1664]{1,0:T(8,128)(2,1)S(1)}, bf16[192,1664]{1,0:T(8,128)(2,1)S(1)}, u32[]{:S(2)}, u32[]{:S(2)}) collective-permute-start(bf16[192,1664]{1,0:T(8,128)(2,1)S(1)} %shard_map.224.refs_2_.refs_10_.refs_4_), channel_id=1, source_target_pairs={{0,4},{1,3},{2,6},{3,1},{4,0},{5,7},{6,2},{7,5},{8,12},{9,11},{10,... | collective-permute-start | bytes 1916936 | tf_op jit(solution)/shard_map/ppermute | solution.py:722
  47.3 16.3 %collective-permute-start.19 = (bf16[192,1536]{1,0:T(8,128)(2,1)S(1)}, bf16[192,1536]{1,0:T(8,128)(2,1)S(1)}, u32[]{:S(2)}, u32[]{:S(2)}) collective-permute-start(bf16[192,1536]{1,0:T(8,128)(2,1)S(1)} %get-tuple-element.122.refs_1_), channel_id=1, source_target_pairs={{0,2},{1,5},{2,0},{3,7},{4,6},{5,1},{6,4},{7,3},{8,10},{9,13},{10,... | collective-permute-start | bytes 1769480 | tf_op jit(solution)/shard_map/ppermute | solution.py:722
  48.4 19.9 %collective-permute-start.20 = (bf16[192,1536]{1,0:T(8,128)(2,1)S(1)}, bf16[192,1536]{1,0:T(8,128)(2,1)S(1)}, u32[]{:S(2)}, u32[]{:S(2)}) collective-permute-start(bf16[192,1536]{1,0:T(8,128)(2,1)S(1)} %get-tuple-element.122.refs_1_), channel_id=1, source_target_pairs={{0,4},{1,3},{2,6},{3,1},{4,0},{5,7},{6,2},{7,5},{8,12},{9,11},{10,... | collective-permute-start | bytes 1769480 | tf_op jit(solution)/shard_map/ppermute | solution.py:722
  50.1 18.2 %collective-permute-start.17 = (bf16[96,1536]{1,0:T(8,128)(2,1)S(1)}, bf16[96,1536]{1,0:T(8,128)(2,1)S(1)}, u32[]{:S(2)}, u32[]{:S(2)}) collective-permute-start(bf16[96,1536]{1,0:T(8,128)(2,1)S(1)} %get-tuple-element.120.refs_0_), channel_id=1, source_target_pairs={{0,16},{1,17},{2,18},{3,19},{4,20},{5,21},{6,22},{7,23},{8,24},{9,... | collective-permute-start | bytes 884744 | tf_op jit(solution)/shard_map/ppermute | solution.py:722
  50.5 17.8 %collective-permute-start.18 = (bf16[192,768]{1,0:T(8,128)(2,1)S(1)}, bf16[192,768]{1,0:T(8,128)(2,1)S(1)}, u32[]{:S(2)}, u32[]{:S(2)}) collective-permute-start(bf16[192,768]{1,0:T(8,128)(2,1)S(1)} %get-tuple-element.121.refs_2_.refs_4_.refs_6_), channel_id=1, source_target_pairs={{0,8},{1,9},{2,10},{3,11},{4,12},{5,13},{6,14},{7,15},{8,0},{9,1},... | collective-permute-start | bytes 884744 | tf_op jit(solution)/shard_map/ppermute | solution.py:722
  68.5 22.3 %collective-permute-start.23 = (bf16[192,1536]{1,0:T(8,128)(2,1)S(1)}, bf16[192,1536]{1,0:T(8,128)(2,1)S(1)}, u32[]{:S(2)}, u32[]{:S(2)}) collective-permute-start(bf16[192,1536]{1,0:T(8,128)(2,1)S(1)} %shard_map.231.refs_10_.refs_1_), channel_id=1, source_target_pairs={{0,2},{1,5},{2,0},{3,7},{4,6},{5,1},{6,4},{7,3},{8,10},{9,13},{10,... | collective-permute-start | bytes 1769480 | tf_op jit(solution)/shard_map/ppermute | solution.py:722
  69.3 21.6 %collective-permute-start.24 = (bf16[192,1536]{1,0:T(8,128)(2,1)S(1)}, bf16[192,1536]{1,0:T(8,128)(2,1)S(1)}, u32[]{:S(2)}, u32[]{:S(2)}) collective-permute-start(bf16[192,1536]{1,0:T(8,128)(2,1)S(1)} %shard_map.231.refs_10_.refs_1_), channel_id=1, source_target_pairs={{0,4},{1,3},{2,6},{3,1},{4,0},{5,7},{6,2},{7,5},{8,12},{9,11},{10,... | collective-permute-start | bytes 1769480 | tf_op jit(solution)/shard_map/ppermute | solution.py:722
  71.0 19.9 %collective-permute-start.21 = (bf16[192,1536]{1,0:T(8,128)(2,1)S(1)}, bf16[192,1536]{1,0:T(8,128)(2,1)S(1)}, u32[]{:S(2)}, u32[]{:S(2)}) collective-permute-start(bf16[192,1536]{1,0:T(8,128)(2,1)S(1)} %shard_map.233.refs_2_), channel_id=1, source_target_pairs={{0,4},{1,3},{2,6},{3,1},{4,0},{5,7},{6,2},{7,5},{8,12},{9,11},{10,... | collective-permute-start | bytes 1769480 | tf_op jit(solution)/shard_map/ppermute | solution.py:722
  71.3 19.5 %collective-permute-start.25 = (bf16[384,384]{1,0:T(8,128)(2,1)S(1)}, bf16[384,384]{1,0:T(8,128)(2,1)S(1)}, u32[]{:S(2)}, u32[]{:S(2)}) collective-permute-start(bf16[384,384]{1,0:T(8,128)(2,1)S(1)} %shard_map.235), channel_id=1, source_target_pairs={{0,16},{1,17},{2,18},{3,19},{4,20},{5,21},{6,22},{7,23},{8,24},{9,... | collective-permute-start | bytes 884744 | tf_op jit(solution)/shard_map/ppermute | solution.py:722
  73.0 19.8 %collective-permute-start.22 = (bf16[96,768]{1,0:T(8,128)(2,1)S(1)}, bf16[96,768]{1,0:T(8,128)(2,1)S(1)}, u32[]{:S(2)}, u32[]{:S(2)}) collective-permute-start(bf16[96,768]{1,0:T(8,128)(2,1)S(1)} %shard_map.234.refs_0_), channel_id=1, source_target_pairs={{0,16},{1,17},{2,18},{3,19},{4,20},{5,21},{6,22},{7,23},{8,24},{9,... | collective-permute-start | bytes 442376 | tf_op jit(solution)/shard_map/ppermute | solution.py:722
  94.2 18.7 %collective-permute-start.28 = (bf16[192,1536]{1,0:T(8,128)(2,1)S(1)}, bf16[192,1536]{1,0:T(8,128)(2,1)S(1)}, u32[]{:S(2)}, u32[]{:S(2)}) collective-permute-start(bf16[192,1536]{1,0:T(8,128)(2,1)S(1)} %shard_map.236.refs_2_), channel_id=1, source_target_pairs={{0,4},{1,3},{2,6},{3,1},{4,0},{5,7},{6,2},{7,5},{8,12},{9,11},{10,... | collective-permute-start | bytes 1769480 | tf_op jit(solution)/shard_map/ppermute | solution.py:722
  94.5 18.4 %collective-permute-start.29 = (bf16[192,768]{1,0:T(8,128)(2,1)S(1)}, bf16[192,768]{1,0:T(8,128)(2,1)S(1)}, u32[]{:S(2)}, u32[]{:S(2)}) collective-permute-start(bf16[192,768]{1,0:T(8,128)(2,1)S(1)} %shard_map.237.refs_1_), channel_id=1, source_target_pairs={{0,2},{1,5},{2,0},{3,7},{4,6},{5,1},{6,4},{7,3},{8,10},{9,13},{10,... | collective-permute-start | bytes 884744 | tf_op jit(solution)/shard_map/ppermute | solution.py:722
  94.9 18.0 %collective-permute-start.30 = (bf16[192,768]{1,0:T(8,128)(2,1)S(1)}, bf16[192,768]{1,0:T(8,128)(2,1)S(1)}, u32[]{:S(2)}, u32[]{:S(2)}) collective-permute-start(bf16[192,768]{1,0:T(8,128)(2,1)S(1)} %shard_map.237.refs_1_), channel_id=1, source_target_pairs={{0,4},{1,3},{2,6},{3,1},{4,0},{5,7},{6,2},{7,5},{8,12},{9,11},{10,... | collective-permute-start | bytes 884744 | tf_op jit(solution)/shard_map/ppermute | solution.py:722
  96.7 16.2 %collective-permute-start.31 = (bf16[384,384]{1,0:T(8,128)(2,1)S(1)}, bf16[384,384]{1,0:T(8,128)(2,1)S(1)}, u32[]{:S(2)}, u32[]{:S(2)}) collective-permute-start(bf16[384,384]{1,0:T(8,128)(2,1)S(1)} %shard_map.241), channel_id=1, source_target_pairs={{0,16},{1,17},{2,18},{3,19},{4,20},{5,21},{6,22},{7,23},{8,24},{9,... | collective-permute-start | bytes 884744 | tf_op jit(solution)/shard_map/ppermute | solution.py:722
  113.1 9.4 %collective-permute-start.33 = (bf16[192,768]{1,0:T(8,128)(2,1)S(1)}, bf16[192,768]{1,0:T(8,128)(2,1)S(1)}, u32[]{:S(2)}, u32[]{:S(2)}) collective-permute-start(bf16[192,768]{1,0:T(8,128)(2,1)S(1)} %shard_map.245), channel_id=1, source_target_pairs={{0,4},{1,3},{2,6},{3,1},{4,0},{5,7},{6,2},{7,5},{8,12},{9,11},{10,... | collective-permute-start | bytes 884744 | tf_op jit(solution)/shard_map/ppermute | solution.py:722
  122.1 16.3 %collective-permute-start.34 = (bf16[384,1536]{1,0:T(8,128)(2,1)S(1)}, bf16[384,1536]{1,0:T(8,128)(2,1)S(1)}, u32[]{:S(2)}, u32[]{:S(2)}) collective-permute-start(bf16[384,1536]{1,0:T(8,128)(2,1)S(1)} %get-tuple-element.147), channel_id=1, source_target_pairs={{0,2},{1,5},{2,0},{3,7},{4,6},{5,1},{6,4},{7,3},{8,10},{9,13},{10,... | collective-permute-start | bytes 3538952 | tf_op jit(solution)/shard_map/ppermute | solution.py:722
  139.4 20.9 %collective-permute-start.37 = (bf16[192,1536]{1,0:T(8,128)(2,1)S(1)}, bf16[192,1536]{1,0:T(8,128)(2,1)S(1)}, u32[]{:S(2)}, u32[]{:S(2)}) collective-permute-start(bf16[192,1536]{1,0:T(8,128)(2,1)S(1)} %shard_map.248.refs_1_.refs_13_), channel_id=1, source_target_pairs={{0,4},{1,3},{2,6},{3,1},{4,0},{5,7},{6,2},{7,5},{8,12},{9,11},{10,... | collective-permute-start | bytes 1769480 | tf_op jit(solution)/shard_map/ppermute | solution.py:722
  140.1 21.4 %collective-permute-start.36 = (bf16[384,1536]{1,0:T(8,128)(2,1)S(1)}, bf16[384,1536]{1,0:T(8,128)(2,1)S(1)}, u32[]{:S(2)}, u32[]{:S(2)}) collective-permute-start(bf16[384,1536]{1,0:T(8,128)(2,1)S(1)} %shard_map.251), channel_id=1, source_target_pairs={{0,2},{1,5},{2,0},{3,7},{4,6},{5,1},{6,4},{7,3},{8,10},{9,13},{10,... | collective-permute-start | bytes 3538952 | tf_op jit(solution)/shard_map/ppermute | solution.py:722
  161.9 14.7 %collective-permute-start.39 = (bf16[192,1536]{1,0:T(8,128)(2,1)S(1)}, bf16[192,1536]{1,0:T(8,128)(2,1)S(1)}, u32[]{:S(2)}, u32[]{:S(2)}) collective-permute-start(bf16[192,1536]{1,0:T(8,128)(2,1)S(1)} %get-tuple-element.154.refs_1_.refs_10_), channel_id=1, source_target_pairs={{0,4},{1,3},{2,6},{3,1},{4,0},{5,7},{6,2},{7,5},{8,12},{9,11},{10,... | collective-permute-start | bytes 1769480 | tf_op jit(solution)/shard_map/ppermute | solution.py:722
  162.6 11.0 %collective-permute-start.40 = (bf16[48,1536]{1,0:T(8,128)(2,1)S(1)}, bf16[48,1536]{1,0:T(8,128)(2,1)S(1)}, u32[]{:S(2)}, u32[]{:S(2)}) collective-permute-start(bf16[48,1536]{1,0:T(8,128)(2,1)S(1)} %get-tuple-element.161), channel_id=1, source_target_pairs={{0,8},{1,9},{2,10},{3,11},{4,12},{5,13},{6,14},{7,15},{8,0},{9,1},... | collective-permute-start | bytes 442376 | tf_op jit(solution)/shard_map/ppermute | solution.py:722
  162.6 13.9 %collective-permute-start.41 = (bf16[48,1536]{1,0:T(8,128)(2,1)S(1)}, bf16[48,1536]{1,0:T(8,128)(2,1)S(1)}, u32[]{:S(2)}, u32[]{:S(2)}) collective-permute-start(bf16[48,1536]{1,0:T(8,128)(2,1)S(1)} %get-tuple-element.162), channel_id=1, source_target_pairs={{0,16},{1,17},{2,18},{3,19},{4,20},{5,21},{6,22},{7,23},{8,24},{9,... | collective-permute-start | bytes 442376 | tf_op jit(solution)/shard_map/ppermute | solution.py:722
  164.4 12.2 %collective-permute-start.42 = (bf16[48,1536]{1,0:T(8,128)(2,1)S(1)}, bf16[48,1536]{1,0:T(8,128)(2,1)S(1)}, u32[]{:S(2)}, u32[]{:S(2)}) collective-permute-start(bf16[48,1536]{1,0:T(8,128)(2,1)S(1)} %get-tuple-element.163), channel_id=1, source_target_pairs={{0,24},{1,25},{2,26},{3,27},{4,28},{5,29},{6,30},{7,31},{8,16},{9,... | collective-permute-start | bytes 442376 | tf_op jit(solution)/shard_map/ppermute | solution.py:722
  167.0 17.1 %collective-permute-start.38 = (bf16[512,768]{1,0:T(8,128)(2,1)S(1)}, bf16[512,768]{1,0:T(8,128)(2,1)S(1)}, u32[]{:S(2)}, u32[]{:S(2)}) collective-permute-start(bf16[512,768]{1,0:T(8,128)(2,1)S(1)} %shard_map.253.refs_3_), channel_id=1, source_target_pairs={{0,1},{1,0},{2,3},{3,2},{4,5},{5,4},{6,7},{7,6},{8,9},{9,8},{10,11... | collective-permute-start | bytes 2359304 | tf_op jit(solution)/shard_map/ppermute | solution.py:722
  176.9 16.3 %collective-permute-start.43 = (bf16[384,1536]{1,0:T(8,128)(2,1)S(1)}, bf16[384,1536]{1,0:T(8,128)(2,1)S(1)}, u32[]{:S(2)}, u32[]{:S(2)}) collective-permute-start(bf16[384,1536]{1,0:T(8,128)(2,1)S(1)} %shard_map.257), channel_id=1, source_target_pairs={{0,2},{1,5},{2,0},{3,7},{4,6},{5,1},{6,4},{7,3},{8,10},{9,13},{10,... | collective-permute-start | bytes 3538952 | tf_op jit(solution)/shard_map/ppermute | solution.py:722
  177.4 15.6 %collective-permute-start.44 = (bf16[48,1536]{1,0:T(8,128)(2,1)S(1)}, bf16[48,1536]{1,0:T(8,128)(2,1)S(1)}, u32[]{:S(2)}, u32[]{:S(2)}) collective-permute-start(bf16[48,1536]{1,0:T(8,128)(2,1)S(1)} %get-tuple-element.172), channel_id=1, source_target_pairs={{0,8},{1,9},{2,10},{3,11},{4,12},{5,13},{6,14},{7,15},{8,0},{9,1},... | collective-permute-start | bytes 442376 | tf_op jit(solution)/shard_map/ppermute | solution.py:722
  181.0 12.0 %collective-permute-start.45 = (bf16[48,1536]{1,0:T(8,128)(2,1)S(1)}, bf16[48,1536]{1,0:T(8,128)(2,1)S(1)}, u32[]{:S(2)}, u32[]{:S(2)}) collective-permute-start(bf16[48,1536]{1,0:T(8,128)(2,1)S(1)} %get-tuple-element.173), channel_id=1, source_target_pairs={{0,16},{1,17},{2,18},{3,19},{4,20},{5,21},{6,22},{7,23},{8,24},{9,... | collective-permute-start | bytes 442376 | tf_op jit(solution)/shard_map/ppermute | solution.py:722
  181.0 12.0 %collective-permute-start.46 = (bf16[48,1536]{1,0:T(8,128)(2,1)S(1)}, bf16[48,1536]{1,0:T(8,128)(2,1)S(1)}, u32[]{:S(2)}, u32[]{:S(2)}) collective-permute-start(bf16[48,1536]{1,0:T(8,128)(2,1)S(1)} %get-tuple-element.174), channel_id=1, source_target_pairs={{0,24},{1,25},{2,26},{3,27},{4,28},{5,29},{6,30},{7,31},{8,16},{9,... | collective-permute-start | bytes 442376 | tf_op jit(solution)/shard_map/ppermute | solution.py:722
  193.4 30.9 %collective-permute-start.60 = (f32[24,1536]{1,0:T(8,128)S(1)}, f32[24,1536]{1,0:T(8,128)S(1)}, u32[]{:S(2)}, u32[]{:S(2)}) collective-permute-start(f32[24,1536]{1,0:T(8,128)S(1)} %constant_dynamic-slice_fusion), channel_id=1, source_target_pairs={{0,1},{1,0},{2,3},{3,2},{4,5},{5,4},{6,7},{7,6},{8,9},{9,8},{10,11... | collective-permute-start | bytes 442376 | tf_op jit(solution)/shard_map/ppermute | solution.py:722
  193.5 9.9 %collective-permute-start.49 = (bf16[192,1536]{1,0:T(8,128)(2,1)S(1)}, bf16[192,1536]{1,0:T(8,128)(2,1)S(1)}, u32[]{:S(2)}, u32[]{:S(2)}) collective-permute-start(bf16[192,1536]{1,0:T(8,128)(2,1)S(1)} %get-tuple-element.176.refs_1_.refs_9_), channel_id=1, source_target_pairs={{0,4},{1,3},{2,6},{3,1},{4,0},{5,7},{6,2},{7,5},{8,12},{9,11},{10,... | collective-permute-start | bytes 1769480 | tf_op jit(solution)/shard_map/ppermute | solution.py:722
  194.6 8.8 %collective-permute-start.48 = (bf16[960,768]{1,0:T(8,128)(2,1)S(1)}, bf16[960,768]{1,0:T(8,128)(2,1)S(1)}, u32[]{:S(2)}, u32[]{:S(2)}) collective-permute-start(bf16[960,768]{1,0:T(8,128)(2,1)S(1)} %shard_map.260), channel_id=1, source_target_pairs={{0,1},{1,0},{2,3},{3,2},{4,5},{5,4},{6,7},{7,6},{8,9},{9,8},{10,11... | collective-permute-start | bytes 4423688 | tf_op jit(solution)/shard_map/ppermute | solution.py:722
  203.7 17.3 %collective-permute-start.50 = (bf16[384,1664]{1,0:T(8,128)(2,1)S(1)}, bf16[384,1664]{1,0:T(8,128)(2,1)S(1)}, u32[]{:S(2)}, u32[]{:S(2)}) collective-permute-start(bf16[384,1664]{1,0:T(8,128)(2,1)S(1)} %shard_map.264), channel_id=1, source_target_pairs={{0,2},{1,5},{2,0},{3,7},{4,6},{5,1},{6,4},{7,3},{8,10},{9,13},{10,... | collective-permute-start | bytes 3833864 | tf_op jit(solution)/shard_map/ppermute | solution.py:722
  208.0 12.8 %collective-permute-start.52 = (bf16[48,1536]{1,0:T(8,128)(2,1)S(1)}, bf16[48,1536]{1,0:T(8,128)(2,1)S(1)}, u32[]{:S(2)}, u32[]{:S(2)}) collective-permute-start(bf16[48,1536]{1,0:T(8,128)(2,1)S(1)} %get-tuple-element.191), channel_id=1, source_target_pairs={{0,16},{1,17},{2,18},{3,19},{4,20},{5,21},{6,22},{7,23},{8,24},{9,... | collective-permute-start | bytes 442376 | tf_op jit(solution)/shard_map/ppermute | solution.py:722
  208.1 12.8 %collective-permute-start.53 = (bf16[48,1536]{1,0:T(8,128)(2,1)S(1)}, bf16[48,1536]{1,0:T(8,128)(2,1)S(1)}, u32[]{:S(2)}, u32[]{:S(2)}) collective-permute-start(bf16[48,1536]{1,0:T(8,128)(2,1)S(1)} %get-tuple-element.192), channel_id=1, source_target_pairs={{0,24},{1,25},{2,26},{3,27},{4,28},{5,29},{6,30},{7,31},{8,16},{9,... | collective-permute-start | bytes 442376 | tf_op jit(solution)/shard_map/ppermute | solution.py:722
  222.5 10.5 %collective-permute-start.54 = (bf16[192,1664]{1,0:T(8,128)(2,1)S(1)}, bf16[192,1664]{1,0:T(8,128)(2,1)S(1)}, u32[]{:S(2)}, u32[]{:S(2)}) collective-permute-start(bf16[192,1664]{1,0:T(8,128)(2,1)S(1)} %get-tuple-element.193), channel_id=1, source_target_pairs={{0,4},{1,3},{2,6},{3,1},{4,0},{5,7},{6,2},{7,5},{8,12},{9,11},{10,... | collective-permute-start | bytes 1916936 | tf_op jit(solution)/shard_map/ppermute | solution.py:722
  233.3 7.4 %collective-permute-start.55 = (bf16[48,1664]{1,0:T(8,128)(2,1)S(1)}, bf16[48,1664]{1,0:T(8,128)(2,1)S(1)}, u32[]{:S(2)}, u32[]{:S(2)}) collective-permute-start(bf16[48,1664]{1,0:T(8,128)(2,1)S(1)} %get-tuple-element.195), channel_id=1, source_target_pairs={{0,8},{1,9},{2,10},{3,11},{4,12},{5,13},{6,14},{7,15},{8,0},{9,1},... | collective-permute-start | bytes 479240 | tf_op jit(solution)/shard_map/ppermute | solution.py:722
  235.8 13.9 %collective-permute-start.56 = (bf16[48,1664]{1,0:T(8,128)(2,1)S(1)}, bf16[48,1664]{1,0:T(8,128)(2,1)S(1)}, u32[]{:S(2)}, u32[]{:S(2)}) collective-permute-start(bf16[48,1664]{1,0:T(8,128)(2,1)S(1)} %get-tuple-element.196), channel_id=1, source_target_pairs={{0,16},{1,17},{2,18},{3,19},{4,20},{5,21},{6,22},{7,23},{8,24},{9,... | collective-permute-start | bytes 479240 | tf_op jit(solution)/shard_map/ppermute | solution.py:722
  235.8 13.9 %collective-permute-start.57 = (bf16[48,1664]{1,0:T(8,128)(2,1)S(1)}, bf16[48,1664]{1,0:T(8,128)(2,1)S(1)}, u32[]{:S(2)}, u32[]{:S(2)}) collective-permute-start(bf16[48,1664]{1,0:T(8,128)(2,1)S(1)} %get-tuple-element.197), channel_id=1, source_target_pairs={{0,24},{1,25},{2,26},{3,27},{4,28},{5,29},{6,30},{7,31},{8,16},{9,... | collective-permute-start | bytes 479240 | tf_op jit(solution)/shard_map/ppermute | solution.py:722
  238.2 11.7 %collective-permute-start.59 = (f32[24,1536]{1,0:T(8,128)S(1)}, f32[24,1536]{1,0:T(8,128)S(1)}, u32[]{:S(2)}, u32[]{:S(2)}) collective-permute-start(f32[24,1536]{1,0:T(8,128)S(1)} %get-tuple-element.214), channel_id=1, source_target_pairs={{0,1},{1,0},{2,3},{3,2},{4,5},{5,4},{6,7},{7,6},{8,9},{9,8},{10,11... | collective-permute-start | bytes 442376 | tf_op jit(solution)/shard_map/ppermute | solution.py:722
  (89 other events, 566.2 us)

commit v5 on v4

--- a/solution.py
+++ b/solution.py
@@ -145,42 +145,51 @@
     return dx, jnp.sum(dy * xhat, 0, keepdims=True), jnp.sum(dy, 0, keepdims=True)
 
 
-def head_of_lane(rows):
-    return lax.shift_right_logical(lax.broadcasted_iota(jnp.int32, (rows, DH), 1), 6)
+GROUPS = ((0, 256), (256, DH))
+
+
+def head_of_lane(rows, width):
+    return lax.shift_right_logical(lax.broadcasted_iota(jnp.int32, (rows, width), 1), 6)
 
 
 def spread(q):
-    head = head_of_lane(1)
-    parts = [q * (head == h).astype(F32).astype(q.dtype) for h in range(HALF)]
+    head = head_of_lane(1, q.shape[1])
+    parts = [q * (head == h).astype(F32).astype(q.dtype) for h in range(q.shape[1] // HEAD)]
     return jnp.concatenate(parts, 0)
 
 
 def fold(o):
-    head = head_of_lane(LEN)
+    head = head_of_lane(LEN, o.shape[1])
     total = jnp.where(head == 0, o[:LEN], 0.0)
-    for h in range(1, HALF):
+    for h in range(1, o.shape[1] // HEAD):
         total = jnp.where(head == h, o[h * LEN : (h + 1) * LEN], total)
     return total
 
 
 def attend(q, k, v, allowed):
-    st = nt(k, spread(q)) * SCALE
-    st = jnp.where(allowed, st, NEG)
-    e = jnp.exp(st - jnp.max(st, 0, keepdims=True))
-    p = (e * (1.0 / jnp.sum(e, 0, keepdims=True))).astype(BF)
-    return p, fold(tn(p, v)).astype(BF)
+    probs, mixed = [], []
+    for lo, hi in GROUPS:
+        st = nt(k[:, lo:hi], spread(q[:, lo:hi])) * SCALE
+        st = jnp.where(allowed[:, lo:hi], st, NEG)
+        e = jnp.exp(st - jnp.max(st, 0, keepdims=True))
+        p = (e * (1.0 / jnp.sum(e, 0, keepdims=True))).astype(BF)
+        probs.append(p)
+        mixed.append(fold(tn(p, v[:, lo:hi])).astype(BF))
+    return jnp.concatenate(probs, 1), jnp.concatenate(mixed, 1)
 
 
 def attend_back(g, q, k, v, p):
-    gs, qs = spread(g), spread(q)
-    dp = nt(v, gs)
-    pf = p.astype(F32)
-    t = pf * dp
-    ds = (t - pf * jnp.sum(t, 0, keepdims=True)).astype(BF)
-    dq = (fold(tn(ds, k)) * SCALE).astype(BF)
-    dk = (nn(ds, qs) * SCALE).astype(BF)
-    dv = nn(p, gs).astype(BF)
-    return dq, dk, dv
+    dq, dk, dv = [], [], []
+    for lo, hi in GROUPS:
+        gs, qs, low = spread(g[:, lo:hi]), spread(q[:, lo:hi]), p[:, lo:hi]
+        dp = nt(v[:, lo:hi], gs)
+        pf = low.astype(F32)
+        t = pf * dp
+        ds = (t - pf * jnp.sum(t, 0, keepdims=True)).astype(BF)
+        dq.append((fold(tn(ds, k[:, lo:hi])) * SCALE).astype(BF))
+        dk.append((nn(ds, qs) * SCALE).astype(BF))
+        dv.append(nn(low, gs).astype(BF))
+    return [jnp.concatenate(x, 1) for x in (dq, dk, dv)]
 
 
 def seq_rows(s):
@@ -239,12 +248,11 @@
 
 
 def send_out(dw, offs_ref, outs):
-    own, to_b, to_a = outs
     blk = dw.shape[0] // 16
-    for q, (dst, base) in enumerate(((own, 0), (to_a, 0), (to_b, 0), (to_a, 4))):
+    for q in range(4):
         for r in range(4):
             row = pl.multiple_of(offs_ref[0, q * 4 + r] * blk, 16)
-            dst[(base + r) * blk : (base + r + 1) * blk, :] = dw[pl.ds(row, blk), :]
+            outs[q][r * blk : (r + 1) * blk, :] = dw[pl.ds(row, blk), :]
 
 
 def pack_kernel(core, qkv, out, cq, ckv, cout, win, gains, biases, keep, send, vecs):
@@ -317,7 +325,7 @@
     def norm(s):
         xhat[seq_rows(s), :] = normalise(tok[seq_rows(s), :].astype(F32))[0]
 
-    loop(2 * seqs, norm)
+    loop(2 * seqs, norm, 2)
     flush(xhat)
     mem_own, mem_other = ready(mem_own, mem_other)
     for b, src in ((0, mem_own), (1, mem_other)):
@@ -346,7 +354,7 @@
     def norm(s):
         first[seq_rows(s), :] = (xhat[seq_rows(s), :] * gain + bias).astype(BF)
 
-    loop(8, norm)
+    loop(8, norm, 2)
     flush(first)
 
     def proj(b):
@@ -401,7 +409,7 @@
         xhat, _ = normalise(v)
         second[rows, :] = (xhat * gain + bias).astype(BF)
 
-    loop(8, norm)
+    loop(8, norm, 2)
     flush(resid, second)
     wcq = ready(wcq)
     cq[...] = nn(second[...], wcq[...]).astype(BF)
@@ -443,7 +451,7 @@
         xhat, _ = normalise(v)
         third[rows, :] = (xhat * gain + bias).astype(BF)
 
-    loop(8, norm)
+    loop(8, norm, 2)
     flush(resid_two, third)
     win = ready(win)
 
@@ -478,7 +486,8 @@
     comb[2 * half :, :] = nn(hidden[half:, :], wout[...]).astype(BF)
 
 
-def dmlpout_kernel(offs, hidden, g, to_own, to_b, to_a, dw):
+def dmlpout_kernel(offs, hidden, g, *refs):
+    outs, dw = refs[:4], refs[4]
     hidden, g = ready(hidden, g)
     blk = dw.shape[0] // 16
     for b in range(4):
@@ -486,19 +495,19 @@
         for k in range(8):
             row = (4 * b + k // 2) * blk
             dw[row : row + blk, (k % 2) * D : (k % 2 + 1) * D] = part[k * blk : (k + 1) * blk]
-    send_out(dw, offs, (to_own, to_b, to_a))
+    send_out(dw, offs, outs)
 
 
 def mlp_and_grad_kernel(
-    offs, pown, pa, pb, pab, near, far_a, far_b, g, slope, win, hidden, third, own, comb, to_own, to_b, to_a, ginner, wout, dw
+    offs, pown, pa, pb, pab, near, far_a, far_b, g, slope, win, hidden, third, own, comb, d_own, d_a, d_b, d_ab, ginner, wout, dw
 ):
     mlp_kernel(offs, (pown, pa, pb, pab), near, (far_a, far_b), g, slope, win, hidden, own, comb, ginner, wout)
-    dmlpin_kernel(offs, third, ginner, to_own, to_b, to_a, dw)
+    dmlpin_kernel(offs, third, ginner, d_own, d_a, d_b, d_ab, dw)
 
 
 def dmlpin_kernel(offs, third, ginner, *refs):
     third, ginner = ready(third, ginner)
-    outs, dw = refs[:3], refs[3]
+    outs, dw = refs[:4], refs[4]
     for b in range(0, dw.shape[0], 256):
         dw[b : b + 256, :] = tn(third[:, b : b + 256], ginner[...]).astype(BF)
     send_out(dw, offs, outs)
@@ -527,7 +536,7 @@
             extra = own[rows, :].astype(F32) + recv[pl.ds(pl.multiple_of(512 + s * LEN, LEN), LEN), :].astype(F32)
             output[rows, :] = (resid[rows, :] + extra).astype(BF)
 
-    loop(8, norm)
+    loop(8, norm, 2)
     flush(output, gresid, gtwo, dvec)
     keep, back = ready(keep, back)
     gm[...] = (nt(gtwo[:, half_lanes(c)], keep[:DH, :]) + nt(gtwo[:, half_lanes(1 - c)], back[DH:, :])).astype(BF)
@@ -556,7 +565,7 @@
 
 
 def dcross_kernel(offs, core, mixed, mixed_other, gtwo, second, dcq, dkv, wckv, mem, *refs):
-    outs, gmem, dw = refs[:3], refs[3:5], refs[5]
+    outs, gmem, dw = refs[:4], refs[4:6], refs[6]
     mixed, mixed_other, gtwo = ready(mixed, mixed_other, gtwo)
     out_grad(dw, 0, core[0], mixed, mixed_other, gtwo)
     second, dcq = ready(second, dcq)
@@ -573,6 +582,18 @@
     send_out(dw, offs, outs)
 
 
+def cross_back_and_grads_kernel(
+    offs, core, vec, resid, part, recv, own, g, keep, back, kv, cq, probs, wcq, mixed, mixed_other, second, wckv, mem,
+    output, gresid, gsecond, dvec, gmem_own, gmem_other, d_own, d_a, d_b, d_ab, gtwo, dcq, dkv, gm, dw
+):
+    cross_back_kernel(
+        core, vec, resid, part, recv, own, g, keep, back, kv, cq, probs, wcq, output, gresid, gtwo, dcq, dkv, gsecond, dvec, gm
+    )
+    dcross_kernel(
+        offs, core, mixed, mixed_other, gtwo, second, dcq, dkv, wckv, mem, d_own, d_a, d_b, d_ab, gmem_own, gmem_other, dw
+    )
+
+
 def self_back_kernel(
     core, vec, resid, part, recv, gresid_two, keep, back, packed, probs, wqkv, xhat, gresid, gone, dpacked, gfirst_own, gfirst_other, dvec, gm
 ):
@@ -594,7 +615,7 @@
             dvec[0:1, :] += dg
             dvec[1:2, :] += db
 
-    loop(8, norm)
+    loop(8, norm, 2)
     flush(gresid, gone)
     keep, back = ready(keep, back)
     gm[...] = (nt(gone[:, half_lanes(c)], keep[:DH, :]) + nt(gone[:, half_lanes(1 - c)], back[DH:, :])).astype(BF)
@@ -622,7 +643,7 @@
 
 
 def dself_kernel(offs, core, mixed, mixed_other, gone, first, dpacked, dvec_two, dvec_one, *refs):
-    outs, dw, vecs = refs[:3], refs[3], refs[4]
+    outs, dw, vecs = refs[:4], refs[4], refs[5]
     mixed, mixed_other, gone = ready(mixed, mixed_other, gone)
     out_grad(dw, 0, core[0], mixed, mixed_other, gone)
     first, dpacked, dvec_two, dvec_one = ready(first, dpacked, dvec_two, dvec_one)
@@ -635,6 +656,17 @@
     send_out(dw, offs, outs)
 
 
+def self_back_and_grads_kernel(
+    offs, core, vec, resid, part, recv, gresid_two, keep, back, packed, probs, wqkv, xhat, mixed, mixed_other, first, dvec_two,
+    gresid, gfirst_own, gfirst_other, d_own, d_a, d_b, d_ab, gone, dpacked, dvec, gm, dw, vecs
+):
+    self_back_kernel(
+        core, vec, resid, part, recv, gresid_two, keep, back, packed, probs, wqkv, xhat,
+        gresid, gone, dpacked, gfirst_own, gfirst_other, dvec, gm
+    )
+    dself_kernel(offs, core, mixed, mixed_other, gone, first, dpacked, dvec_two, dvec, d_own, d_a, d_b, d_ab, dw, vecs)
+
+
 def tokens_back_kernel(vec, tok, part, recv, gresid, gmem, gmem_recv, gtok, gmemory):
     vec, tok, part, recv, gresid = ready(vec, tok, part, recv, gresid)
     gain = vec[0:1]
@@ -651,24 +683,21 @@
     gmemory[...] = (gmem[...].astype(F32) + gmem_recv[...].astype(F32)).astype(BF)
 
 
+MERGES = {"pass": (2, 1), "sum": (3, 4), "end": (4, 1), "half": (3, 2), "near": (2, 2), "last": (2, 1)}
+
+
 def merge_kernel(kinds, *refs):
-    counts = {"pass": (2, 1), "sum": (3, 4), "end": (4, 1)}
-    at, out = 0, sum(counts[kind][0] for kind in kinds)
-    refs = ready(*refs)
+    at, out = 0, sum(MERGES[kind][0] for kind in kinds)
     for kind in kinds:
-        ins, outs = refs[at : at + counts[kind][0]], refs[out : out + counts[kind][1]]
+        ins, outs = refs[at : at + MERGES[kind][0]], refs[out : out + MERGES[kind][1]]
         at, out = at + len(ins), out + len(outs)
-        if kind == "pass":
-            half = ins[0].shape[0]
-            outs[0][...] = (ins[0][...].astype(F32) + ins[1][half:, :].astype(F32)).astype(BF)
-        elif kind == "end":
-            outs[0][...] = ins[0][...] + ins[1][...].astype(F32) + ins[2][...].astype(F32) + ins[3][...].astype(F32)
+        if kind == "sum" or kind == "half" or kind == "near":
+            blk = outs[0].shape[0]
+            for i, dst in enumerate(outs):
+                rows = slice(i * blk, (i + 1) * blk)
+                dst[...] = sum(x[rows, :].astype(F32) for x in ins).astype(dst.dtype)
         else:
-            blk = ins[0].shape[0] // 4
-            for i in range(4):
-                rows = slice(i * blk, (i + 1) * blk)
-                total = ins[0][rows, :].astype(F32) + ins[1][rows, :].astype(F32) + ins[2][rows, :].astype(F32)
-                outs[i][...] = total.astype(outs[i].dtype)
+            outs[0][...] = sum(x[...].astype(F32) for x in ins).astype(outs[0].dtype)
 
 
 def merge(jobs, after=()):
@@ -676,19 +705,12 @@
     for kind, *arrays in jobs:
         ins += arrays
         rows, width = arrays[0].shape
-        if kind == "sum":
-            outs += [sds((rows // 4, width), F32)] + [sds((rows // 4, width), BF)] * 3
-        else:
-            outs.append(sds((rows, width), BF if kind == "pass" else F32))
+        parts = {"sum": 4, "half": 2, "near": 2}.get(kind, 1)
+        outs.append(sds((rows // parts, width), BF if kind == "pass" else F32))
+        outs += [sds((rows // parts, width), BF)] * (parts - 1)
     kinds = [job[0] for job in jobs]
     return kernel_call(
-        lambda *refs: merge_kernel(kinds, *refs),
-        ins,
-        [STAGE] * len(ins),
-        outs,
-        [STAGE] * len(outs),
-        cost=1,
-        after=after,
+        lambda *refs: merge_kernel(kinds, *refs), ins, [VM] * len(ins), outs, cost=1, after=after
     )
 
 
@@ -711,6 +733,9 @@
         biases[...] = turned[3:6, 0:rows]
 
 
+CUTS = ((0, 512), (512, 256))
+
+
 class Moves:
     def __init__(self, mesh):
         self.nz, self.nf = mesh.shape["dp"], mesh.shape["fsdp"]
@@ -756,7 +781,7 @@
     fast = moves.doubling
 
 
-    def prepare(lens, pairs, after=()):
+    def prepare(lens, pairs, after=(), hold=()):
         return kernel_call(
             prepare_kernel,
             [lens, *pairs],
@@ -764,6 +789,7 @@
             [sds((r2, D), BF)] * 2 + [sds((s2 * pad, D), BF), sds((r2, D), F32)],
             [STAGE] * 4,
             after=after,
+            hold=hold,
         )
 
     def self_attention(pieces, lens, xhat, keep, back, after=()):
@@ -825,7 +851,7 @@
             body,
             [offs, *ins],
             [SM, *specs],
-            [sds((n * wb, ncols), BF) for n in (4, 4, 8)] + list(extra),
+            [sds((4 * wb, ncols), BF)] * 4 + list(extra),
             scratch=[pltpu.VMEM((D, ncols), BF), *scratch],
             cost=cost,
             after=after,
@@ -837,7 +863,7 @@
             mlp_and_grad_kernel,
             [offs, *pieces, g, slope, w_in, hidden, third],
             [SM] + [VM] * 12,
-            [sds((rows, D), BF), sds((3 * rows, D), BF)] + [sds((n * wb, fh), BF) for n in (4, 4, 8)],
+            [sds((rows, D), BF), sds((3 * rows, D), BF)] + [sds((4 * wb, fh), BF)] * 4,
             scratch=[pltpu.VMEM((r2, fh), BF), pltpu.VMEM((fh, D), BF), pltpu.VMEM((D, fh), BF)],
             cost=11,
             after=after,
@@ -846,62 +872,52 @@
 
     def cross_back(resid_two, comb, recv, part, after=()):
         return kernel_call(
-            cross_back_kernel,
-            [core, vec, resid_two, comb, recv, part, g, *cout, kv, cq, cprobs, w_cq],
-            [SM] + [STAGE] * 12,
+            cross_back_and_grads_kernel,
+            [
+                offs, core, vec, resid_two, comb, recv, part, g, *cout, kv, cq, cprobs, w_cq,
+                *cross_mixed, second, w_ckv, mem,
+            ],
+            [SM] * 2 + [VM] * 17,
             [
                 sds((rows, D), BF),
                 sds((r2, D), F32),
                 sds((r2, D), BF),
-                sds((r2, DH), BF),
-                sds(kv.shape, BF),
-                sds((r2, D), BF),
                 sds((8, D), F32),
+                sds((seqs * pad, D), BF),
+                sds((seqs * pad, D), BF),
+            ]
+            + [sds((4 * wb, 4 * DH), BF)] * 4,
+            scratch=[
+                pltpu.VMEM((r2, D), BF),
+                pltpu.VMEM((r2, DH), BF),
+                pltpu.VMEM(kv.shape, BF),
+                pltpu.VMEM((r2, DH), BF),
+                pltpu.VMEM((D, 4 * DH), BF),
             ],
-            [STAGE] * 7,
-            scratch=[pltpu.VMEM((r2, DH), BF)],
-            cost=11,
+            cost=16,
             after=after,
+            limit=24 << 20,
         )
 
     def self_back(gsecond, recv, gresid_two, after=()):
         return kernel_call(
-            self_back_kernel,
-            [core, vec, resid_one, gsecond, recv, gresid_two, *out, packed, probs, w_qkv, xhat],
-            [SM] + [STAGE] * 11,
+            self_back_and_grads_kernel,
             [
-                sds((rows, D), F32),
-                sds((r2, D), BF),
-                sds((r2, 3 * DH), BF),
-                sds((rows, D), BF),
-                sds((rows, D), BF),
-                sds((8, D), F32),
+                offs, core, vec, resid_one, gsecond, recv, gresid_two, *out, packed, probs, w_qkv, xhat,
+                *self_mixed, first, dvec_two,
             ],
-            [STAGE] * 6,
-            scratch=[pltpu.VMEM((r2, DH), BF)],
-            cost=9,
-            after=after,
-        )
-
-    def cross_grads(after=()):
-        return grads(
-            dcross_kernel,
-            [core, *cross_mixed, gtwo, second, dcq, dkv, w_ckv, mem],
-            [SM] + [STAGE] * 8,
-            4 * DH,
-            [sds((seqs * pad, D), BF)] * 2,
-            cost=10,
-            after=after,
-        )
-
-    def self_grads(after=()):
-        return grads(
-            dself_kernel,
-            [core, *self_mixed, gone, first, dpacked, dvec_two, dvec_one],
-            [SM] + [STAGE] * 7,
-            4 * DH + 128,
-            scratch=[pltpu.VMEM((128, D), F32)],
-            cost=6,
+            [SM] * 2 + [STAGE] * 15,
+            [sds((rows, D), F32), sds((rows, D), BF), sds((rows, D), BF)]
+            + [sds((4 * wb, 4 * DH + 128), BF)] * 4,
+            scratch=[
+                pltpu.VMEM((r2, D), BF),
+                pltpu.VMEM((r2, 3 * DH), BF),
+                pltpu.VMEM((8, D), F32),
+                pltpu.VMEM((r2, DH), BF),
+                pltpu.VMEM((D, 4 * DH + 128), BF),
+                pltpu.VMEM((128, D), F32),
+            ],
+            cost=11,
             after=after,
         )
 
@@ -955,8 +971,10 @@
             after=[lens, pairs[1], pairs[3]],
         )
         near, far, side_a, side_b = moves.near_z, moves.far_z, moves.side_a, moves.side_b
-        near_both, along, a_last, b_last = near(both), [far(one), moves.opposite_z(one)], side_a(last), side_b(last)
-        tok, g, mem, xhat = prepare(lens, pairs, after=(one,))
+        near_both, along = near(both), [far(one), moves.opposite_z(one)]
+        tok, g, mem, xhat = prepare(lens, pairs, hold=(one, both, three, last))
+        last = tie(last, tok)
+        a_last, b_last = side_a(last), side_b(last)
         one, two = cats(
             [
                 [(one, 0, widths[0]), (near_both, 0, widths[0]), *whole(*along)],
@@ -967,33 +985,27 @@
         three, ab_last = tie(three, one), tie(a_last, one)
         a1, b1, far_two, near_three, ab_last = side_a(one), side_b(one), far(two), near(three), side_b(ab_last)
         a1 = tie(a1, b1)
-        two, last, four, three = cats(
-            [
-                whole(two, far_two),
-                whole(last, a_last, b_last, ab_last),
-                [(three, 4 * DH, D), (near_three, 4 * DH, D)],
-                [(three, 0, 4 * DH), (near_three, 0, 4 * DH)],
-            ],
-            after=(a1,),
+        two, last, three = cats(
+            [whole(two, far_two), whole(last, a_last, b_last, ab_last), whole(three, near_three)], after=(a1,)
         )
         ab1, a2, b2, far_three, near_last = side_b(a1), side_a(two), side_b(two), far(three), near(last)
         a2 = tie(a2, b2, ab1)
-        three, last, *parts = cats(
+        three, four, last, *parts = cats(
             [
-                whole(three, far_three),
+                [(three, 0, 4 * DH), (far_three, 0, 4 * DH)],
+                [(three, 4 * DH, D), (far_three, 4 * DH, D)],
                 whole(last, near_last),
-                [(last, 0, DH), (near_last, 0, DH)],
-                [(last, DH, DH), (near_last, DH, DH)],
+                *([(last, lo, width), (near_last, lo, width)] for lo, width in CUTS),
             ],
             after=(a2,),
         )
         out = out_rows([one, a1, b1, ab1], offs, 3 * DH)
         out = (out, sib(out))
-        three, a2, four = tie(three, out[1]), tie(a2, out[1]), tie(four, out[1])
-        ab2, a3, b3, far_four, far_a = side_b(a2), side_a(three), side_b(three), far(four), far(tie(parts[0], out[1]))
+        three, a2 = tie(three, out[1]), tie(a2, out[1])
+        ab2, a3, b3, far_a = side_b(a2), side_a(three), side_b(three), far(tie(parts[0], out[1]))
         first, packed, probs, comb, vec, w_qkv = self_attention([one, a1, b1, ab1], lens, xhat, *out, after=(three,))
         a3 = tie(a3, b3, ab2, comb, far_a)
-        (four,) = cats([whole(four, far_four)], after=(a3,))
+        four = tie(four, a3)
         comb = tie(comb, four)
         cout = out_rows([two, a2, b2, ab2], offs, 0)
         cout = (cout, sib(cout))
@@ -1028,7 +1040,8 @@
         rowed = lax.dynamic_index_in_dim(rowed, c, 1, keepdims=False).reshape(16, 2, fh // 32, D)
         rowed = rowed.transpose(1, 0, 2, 3)
         levels = rowed[1].reshape(4, 4, wb, D).transpose(1, 0, 2, 3).reshape(D, D)
-        last = split(rowed[0].reshape(D, D)) + [levels[: D // 2], levels[D // 2 :, :DH], levels[D // 2 :, DH:]]
+        last = split(rowed[0].reshape(D, D)) + [levels[: D // 2]]
+        last += [levels[D // 2 :, lo : lo + width] for lo, width in CUTS]
         hold = ()
         first, packed, probs, comb, vec, w_qkv = self_attention(one, lens, xhat, *out)
         self_mixed = (comb, sib(comb))
@@ -1043,52 +1056,58 @@
     near, far, side_a, side_b = moves.near_z, moves.far_z, moves.side_a, moves.side_b
     after = ()
 
-    def along_z(blocks):
-        return [near(blocks[0]), far(blocks[1]), moves.opposite_z(blocks[2])]
-
     held = [resid_two, vec]
     d_mlpout = grads(dmlpout_kernel, [hidden, g], [STAGE] * 2, 2 * D, hold=[*hold, *held, third])
     if fast:
-        got_a1 = side_a(d_mlpout[2])
+        got_ab1 = side_a(d_mlpout[3])
     part, comb, *d_mlpin = mlp_part(last, g, slope, w_in, hidden, third, after=d_mlpout[:1], hold=[*hold, *held])
     if fast:
-        (on,) = merge([("pass", d_mlpout[1], got_a1)], after=(part,))
+        (on,) = merge([("pass", d_mlpout[2], got_ab1)], after=(part,))
         comb = tie(comb, on)
-        got_b1, got_a2 = side_b(on), side_a(tie(d_mlpin[2], on))
+        got_b1, got_ab2, got_a1 = side_b(on), side_a(tie(d_mlpin[3], on)), side_a(tie(d_mlpout[1], on))
         after = (on,)
     recv = sib(comb)
-    output, gresid_two, gtwo, dcq, dkv, gsecond, dvec_two = cross_back(resid_two, comb, recv, part, after=after)
+    output, gresid_two, gsecond, dvec_two, gmem, gmem_other, *d_cross = cross_back(
+        resid_two, comb, recv, part, after=after
+    )
     if fast:
-        on, kept1, *sums1 = merge([("pass", d_mlpin[1], got_a2), ("sum", d_mlpout[0], got_a1, got_b1)], after=(dcq,))
-        got_b2, got_z1 = side_b(on), along_z(sums1)
+        on, kept1, on_far = merge(
+            [("pass", d_mlpin[2], got_ab2), ("half", d_mlpout[0], got_a1, got_b1)], after=(dvec_two,)
+        )
         gsecond = tie(gsecond, on)
+        got_b2, got_far1 = side_b(on), far(on_far)
+        got_a2, got_ab3 = side_a(tie(d_mlpin[1], on)), side_a(tie(d_cross[3], on))
         after = (on,)
     recv = sib(gsecond)
-    *d_cross, gmem, gmem_other = cross_grads(after=after)
+    gresid_one, gfirst, gfirst_other, *d_self = self_back(gsecond, recv, gresid_two, after=after)
     if fast:
-        kept2, *sums2, total1 = merge([("sum", d_mlpin[0], got_a2, got_b2), ("end", kept1, *got_z1)], after=(gmem,))
-        got_z2, got_a3 = along_z(sums2), side_a(tie(d_cross[2], kept2))
-        after = (kept2,)
-    gresid_one, gone, dpacked, gfirst, gfirst_other, dvec_one = self_back(gsecond, recv, gresid_two, after=after)
+        on, kept2, on_far, kept1, on_near = merge(
+            [("pass", d_cross[2], got_ab3), ("half", d_mlpin[0], got_a2, got_b2), ("near", kept1, got_far1)],
+            after=(gfirst,),
+        )
+        got_b3, got_a3, got_ab4 = side_b(on), side_a(tie(d_cross[1], on)), side_a(tie(d_self[3], on))
+        got_far2, got_near1 = far(on_far), near(on_near)
+        on, kept3, on_far, kept2, on_near, total1 = merge(
+            [
+                ("pass", d_self[2], got_ab4),
+                ("half", d_cross[0], got_a3, got_b3),
+                ("near", kept2, got_far2),
+                ("last", kept1, got_near1),
+            ]
+        )
+        gfirst_other, gmem_other = tie(gfirst_other, on), tie(gmem_other, on)
+        got_b4, got_a4 = side_b(on), side_a(tie(d_self[1], on))
+        got_far3, got_near2 = far(on_far), near(on_near)
+    recv, gmem_recv = sib(gfirst_other), sib(gmem_other)
+    grad_tokens, grad_memory = tokens_back(recv, gmem_recv)
+    grad_memory = grad_memory.reshape(seqs, pad, D)[:, :mem_len]
+
     if fast:
-        on, total2 = merge([("pass", d_cross[1], got_a3), ("end", kept2, *got_z2)], after=(gone,))
-        got_b3 = side_b(on)
-        gfirst_other, gmem_other = tie(gfirst_other, on), tie(gmem_other, on)
-        after = (on,)
-    recv, gmem_recv = sib(gfirst_other), sib(gmem_other)
-    d_self = self_grads(after=after)
-    if fast:
-        kept3, *sums3 = merge([("sum", d_cross[0], got_a3, got_b3)], after=[d_self[0], recv, gmem_recv])
-        got_z3, got_a4 = along_z(sums3), side_a(tie(d_self[2], kept3))
-        after = (kept3,)
-    grad_tokens, grad_memory = tokens_back(recv, gmem_recv, after=after)
-    grad_memory = grad_memory.reshape(seqs, pad, D)[:, :mem_len]
-
-    if fast:
-        on, total3 = merge([("pass", d_self[1], got_a4), ("end", kept3, *got_z3)], after=(grad_tokens,))
-        got_b4 = side_b(on)
-        kept4, *sums4 = merge([("sum", d_self[0], got_a4, got_b4)])
-        got_z4 = along_z(sums4)
+        kept4, *blocks, kept3, on_near, total2 = merge(
+            [("sum", d_self[0], got_a4, got_b4), ("near", kept3, got_far3), ("last", kept2, got_near2)], after=(grad_tokens,)
+        )
+        got_z4, got_near3 = [near(blocks[0]), far(blocks[1]), moves.opposite_z(blocks[2])], near(on_near)
+        (total3,) = merge([("last", kept3, got_near3)])
         (total4,) = merge([("end", kept4, *got_z4)])
         total = [total1, total2, total3, total4]
 
@@ -1119,8 +1138,7 @@
     else:
 
         def placed(parts):
-            own, to_b, to_a = parts
-            term = jnp.concatenate([own, to_a[: 4 * wb], to_b, to_a[4 * wb :]], 0).astype(F32)
+            term = jnp.concatenate(parts, 0).astype(F32)
             both = jnp.stack([jnp.where(c == 0, term, 0.0), jnp.where(c == 1, term, 0.0)], 1)
             return lax.psum_scatter(both, AXES, scatter_dimension=0, tiled=True)
 
@@ -1138,8 +1156,7 @@
         vectors = jnp.sum(total[:, :, 4 * DH : 4 * DH + 6], 1).T
         own_gains, own_biases = vectors[:3], vectors[3:]
         grad_in = joined(placed(d_mlpin), 0, fh, ff // (2 * hr))
-        own, to_b, to_a = d_mlpout
-        term = jnp.concatenate([own, to_a[: 4 * wb], to_b, to_a[4 * wb :]], 0).astype(F32)
+        term = jnp.concatenate(d_mlpout, 0).astype(F32)
         term = term.reshape(16, wb, 2, D).transpose(0, 2, 1, 3).reshape(moves.n // 2, 1, hr, D)
         both = jnp.concatenate([jnp.where(c == 0, term, 0.0), jnp.where(c == 1, term, 0.0)], 1)
         sum_mlpout = lax.psum_scatter(both.reshape(ff, D), AXES, scatter_dimension=0, tiled=True)

time: 253 us -> 239 us (0.945)
  starting transfers between devices: 61.8 us -> 56.4 us
  waiting for transfers between devices: 93.3 us -> 89.9 us
  local copies, waits for them, and re-layouts: 19.7 us -> 16.5 us
    ppermute x61, starting transfers between devices: 61.8 us -> 56.4 us  [permute(): lax.ppermute(x, AXES, [(a, z * self.nf + 2 * yx + c) for a, (z, yx, c) in...]
    ppermute x61, waiting for transfers between devices: 93.3 us -> 89.9 us  [permute(): lax.ppermute(x, AXES, [(a, z * self.nf + 2 * yx + c) for a, (z, yx, c) in...]
    unnamed x156 -> x116, local copies, waits for them, and re-layouts: 14.5 us -> 12.9 us
    pallas_call x30 -> x26, Pallas kernels: 73.7 us -> 73 us  [kernel_call(): pl.pallas_call(run, out_shape=list(outs), in_specs=[space(spec) for spec...]
  transfers between devices with their start and end apart: 61 -> 61, of which waited for: 23 -> 29; matrix products, arithmetic and copies ran while one was open for 4% -> 3% of each run, Pallas kernels for 29% -> 29%
where the time goes in v5:
time: 239 us; the launch traced here: 238 us
  waiting for transfers between devices  89.9 us (38%)
  Pallas kernels  73.1 us (31%)
  starting transfers between devices  56.4 us (24%)
  local copies, waits for them, and re-layouts  16.5 us (7%)
    ppermute x61, waiting for transfers between devices, permute(): lax.ppermute(x, AXES, [(a, z * self.nf + 2 * yx + c) for a, (z, yx, c) in...  89.9 us
    pallas_call x26, Pallas kernels, kernel_call(): pl.pallas_call(run, out_shape=list(outs), in_specs=[space(spec) for spec...  73 us
    ppermute x61, starting transfers between devices, permute(): lax.ppermute(x, AXES, [(a, z * self.nf + 2 * yx + c) for a, (z, yx, c) in...  56.4 us
    unnamed x116, local copies, waits for them, and re-layouts  12.9 us
  transfers between devices with their start and end apart: 61, of which 29 were waited for; matrix products, arithmetic and copies ran while one was open for 3% of the time, Pallas kernels for 29%

profile of v5, /device:TPU:0, one launch (start us, length us, event | category | flops | bytes accessed | tf_op | source)
XLA Modules:
  0.0 238.5 jit_solution(13253501928745216493)
XLA Ops:
  1.7 2.9 %shard_map.220 = (bf16[24,4736]{1,0:T(8,128)(2,1)}, bf16[24,4736]{1,0:T(8,128)(2,1)}) custom-call(s32[1]{0:T(128)} %bitcast.2.refs_0_.refs_1_.refs_6_, bf16[24,2304]{1,0:T(8,128)(2,1)} %refs_1_.1, bf16[24,768]{1,0:T(8,128)(2,1)} %refs_2_.1, bf16[24,768]{1,0:T(8,128)(2,1)} %refs_3_.2, bf16[24,1536]{1,0:T(8,128)(2,1)} %refs_4_.1, bf16[24,768]{1,0:T(8,128)(2,1)} %refs_5_.2, ...), custom_call_target="tpu_custom_call" | custom-call | flops 7000000000 | tf_op jit(solution)/shard_map/pallas_call | solution.py:97
  6.5 3.8 %collective-permute-start.5 = (bf16[48,1664]{1,0:T(8,128)(2,1)S(1)}, bf16[48,1664]{1,0:T(8,128)(2,1)S(1)}, u32[]{:S(2)}, u32[]{:S(2)}) collective-permute-start(bf16[48,1664]{1,0:T(8,128)(2,1)S(1)} %get-tuple-element.109.refs_7_.refs_0_), channel_id=1, source_target_pairs={{0,16},{1,17},{2,18},{3,19},{4,20},{5,21},{6,22},{7,23},{8,24},{9,... | collective-permute-start | bytes 479240 | tf_op jit(solution)/shard_map/ppermute | solution.py:747
  10.3 1.3 collective-permute-start.6
  11.9 1.5 copy.55.refs_6_
  13.4 1.8 shard_map.222
  15.3 1.6 copy-done.32
  19.0 1.5 collective-permute-start.8
  20.5 1.5 collective-permute-start.9
  22.8 3.6 %collective-permute-done.4.refs_1_.refs_5_ = bf16[48,3200]{1,0:T(8,128)(2,1)} collective-permute-done((bf16[48,3200]{1,0:T(8,128)(2,1)S(1)}, bf16[48,3200]{1,0:T(8,128)(2,1)}, u32[]{:S(2)}, u32[]{:S(2)}) %collective-permute-start.4) | collective-permute-done | bytes 307232 | tf_op jit(solution)/shard_map/ppermute | solution.py:747
  29.3 1.5 collective-permute-start.10
  30.9 1.5 collective-permute-start.11
  33.0 3.6 %collective-permute-start.14 = (bf16[96,1536]{1,0:T(8,128)(2,1)}, bf16[96,1536]{1,0:T(8,128)(2,1)S(1)}, u32[]{:S(2)}, u32[]{:S(2)}) collective-permute-start(bf16[96,1536]{1,0:T(8,128)(2,1)} %copy-done.13), channel_id=1, source_target_pairs={{0,16},{1,17},{2,18},{3,19},{4,20},{5,21},{6,22},{7,23},{8,24},{9,... | collective-permute-start | bytes 884744 | tf_op jit(solution)/shard_map/ppermute | solution.py:747
  37.3 9.2 %collective-permute-done.10.refs_0_ = bf16[192,1664]{1,0:T(8,128)(2,1)S(1)} collective-permute-done((bf16[192,1664]{1,0:T(8,128)(2,1)S(1)}, bf16[192,1664]{1,0:T(8,128)(2,1)S(1)}, u32[]{:S(2)}, u32[]{:S(2)}) %collective-permute-start.10) | collective-permute-done | bytes 639008 | tf_op jit(solution)/shard_map/ppermute | solution.py:747
  47.1 1.4 collective-permute-done.14.refs_1_
  51.5 2.8 %collective-permute-start.18 = (bf16[192,768]{1,0:T(8,128)(2,1)S(1)}, bf16[192,768]{1,0:T(8,128)(2,1)S(1)}, u32[]{:S(2)}, u32[]{:S(2)}) collective-permute-start(bf16[192,768]{1,0:T(8,128)(2,1)S(1)} %get-tuple-element.118.refs_4_.refs_6_.refs_8_), channel_id=1, source_target_pairs={{0,8},{1,9},{2,10},{3,11},{4,12},{5,13},{6,14},{7,15},{8,0},{9,1},... | collective-permute-start | bytes 884744 | tf_op jit(solution)/shard_map/ppermute | solution.py:747
  54.3 8.3 %collective-permute-done.12.refs_4_.refs_2_.refs_6_ = bf16[192,1664]{1,0:T(8,128)(2,1)S(1)} collective-permute-done((bf16[192,1664]{1,0:T(8,128)(2,1)S(1)}, bf16[192,1664]{1,0:T(8,128)(2,1)S(1)}, u32[]{:S(2)}, u32[]{:S(2)}) %collective-permute-start.12) | collective-permute-done | bytes 639008 | tf_op jit(solution)/shard_map/ppermute | solution.py:747
  63.4 1.5 collective-permute-done.19.refs_0_
  64.9 4.1 %collective-permute-done.20.refs_1_.refs_3_ = bf16[192,1536]{1,0:T(8,128)(2,1)S(1)} collective-permute-done((bf16[192,1536]{1,0:T(8,128)(2,1)S(1)}, bf16[192,1536]{1,0:T(8,128)(2,1)S(1)}, u32[]{:S(2)}, u32[]{:S(2)}) %collective-permute-start.20) | collective-permute-done | bytes 589856 | tf_op jit(solution)/shard_map/ppermute | solution.py:747
  69.0 1.7 collective-permute-done.17.refs_1_.refs_3_
  71.5 1.7 collective-permute-start.23
  74.6 7.4 %shard_map.233 = (bf16[512,768]{1,0:T(8,128)(2,1)S(1)}, bf16[512,1152]{1,0:T(8,128)(2,1)S(1)}, bf16[8,64,384]{2,1,0:T(8,128)(2,1)S(1)}, bf16[512,1152]{1,0:T(8,1...) custom-call(s32[8]{0:T(128)S(1)} %pad_add_fusion.1.refs_4_.refs_0_, s32[1]{0:T(128)} %bitcast.2.refs_0_.refs_1_.refs_6_, ...), custom_call_target="tpu_custom_call" | custom-call | flops 41999998976 | tf_op jit(solution)/shard_map/pallas_call | solution.py:97
  82.1 11.1 %collective-permute-done.24.refs_4_.refs_6_ = bf16[384,512]{1,0:T(8,128)(2,1)S(1)} collective-permute-done((bf16[384,512]{1,0:T(8,128)(2,1)S(1)}, bf16[384,512]{1,0:T(8,128)(2,1)S(1)}, u32[]{:S(2)}, u32[]{:S(2)}) %collective-permute-start.24) | collective-permute-done | bytes 393248 | tf_op jit(solution)/shard_map/ppermute | solution.py:747
  95.5 1.7 collective-permute-start.29
  97.2 10.3 %shard_map.240 = (bf16[1920,768]{1,0:T(8,128)(2,1)S(1)}, bf16[768,768]{1,0:T(8,128)(2,1)S(1)}, bf16[768,384]{1,0:T(8,128)(2,1)S(1)}, f32[512,768]{1,0:T(8,128)S(...) custom-call(s32[2,16]{1,0:T(2,128)S(1)} %pad_add_fusion.refs_0_.refs, ...), custom_call_target="tpu_custom_call" | custom-call | flops 83999997952 | tf_op jit(solution)/shard_map/pallas_call | solution.py:97
  107.6 1.6 collective-permute-done.30.refs_4_.refs_7_
  111.4 1.7 collective-permute-done.31.refs_2_.refs_15_
  113.0 3.3 %shard_map.244 = (f32[512,768]{1,0:T(8,128)S(1)}, bf16[512,768]{1,0:T(8,128)(2,1)S(1)}, bf16[512,1536]{1,0:T(8,128)(2,1)S(1)}, bf16[512,1536]{1,0:T(8,128)(2,1)S(1)}) custom-call(f32[512,768]{1,0:T(8,128)S(1)} %get-tuple-element.126.refs_0_.refs_3_, bf16[512,1152]{1,0:T(8,128)(2,1)S(1)} %shard_map.242.refs_1_.refs_14_, ...), custom_call_target="tpu_custom_call" | custom-call | flops 35000000512 | tf_op jit(solution)/shard_map/pallas_call | solution.py:97
  116.4 2.1 shard_map.246
  119.8 6.8 %shard_map.247 = (bf16[256,768]{1,0:T(8,128)(2,1)S(1)}, bf16[768,768]{1,0:T(8,128)(2,1)S(1)}, bf16[192,1536]{1,0:T(8,128)(2,1)S(1)}, bf16[192,1536]{1,0:T(8,128)...) custom-call(s32[2,16]{1,0:T(2,128)S(1)} %pad_add_fusion.refs_0_.refs_2_, ...), custom_call_target="tpu_custom_call" | custom-call | flops 76999999488 | tf_op jit(solution)/shard_map/pallas_call | solution.py:97
  126.5 1.9 collective-permute-done.33.refs_1_
  131.5 16.7 %shard_map.250 = (bf16[256,768]{1,0:T(8,128)(2,1)}, f32[512,768]{1,0:T(8,128)S(1)}, bf16[512,768]{1,0:T(8,128)(2,1)S(1)}, f32[8,768]{1,0:T(8,128)S(1)}, bf16[960...) custom-call(s32[2,16]{1,0:T(2,128)S(1)} %pad_add_fusion.refs_0_.refs, ...), custom_call_target="tpu_custom_call" | custom-call | flops 112000000000 | tf_op jit(solution)/shard_map/pallas_call | solution.py:97
  148.2 2.5 %collective-permute-done.35.refs_1_ = bf16[192,1536]{1,0:T(8,128)(2,1)S(1)} collective-permute-done((bf16[192,1536]{1,0:T(8,128)(2,1)S(1)}, bf16[192,1536]{1,0:T(8,128)(2,1)S(1)}, u32[]{:S(2)}, u32[]{:S(2)}) %collective-permute-start.35) | collective-permute-done | bytes 589856 | tf_op jit(solution)/shard_map/ppermute | solution.py:747
  154.9 11.6 %shard_map.255 = (f32[256,768]{1,0:T(8,128)S(1)}, bf16[256,768]{1,0:T(8,128)(2,1)S(1)}, bf16[256,768]{1,0:T(8,128)(2,1)S(1)}, bf16[192,1664]{1,0:T(8,128)(2,1)S(...) custom-call(s32[2,16]{1,0:T(2,128)S(1)} %pad_add_fusion.refs_0_.refs_2_, ...), custom_call_target="tpu_custom_call" | custom-call | flops 76999999488 | tf_op jit(solution)/shard_map/pallas_call | solution.py:97
  166.5 3.8 %collective-permute-done.42.refs_6_ = bf16[96,1536]{1,0:T(8,128)(2,1)S(1)} collective-permute-done((bf16[96,1536]{1,0:T(8,128)(2,1)S(1)}, bf16[96,1536]{1,0:T(8,128)(2,1)S(1)}, u32[]{:S(2)}, u32[]{:S(2)}) %collective-permute-start.42) | collective-permute-done | bytes 294944 | tf_op jit(solution)/shard_map/ppermute | solution.py:747
  170.3 3.0 %collective-permute-done.39.refs_1_ = bf16[192,1536]{1,0:T(8,128)(2,1)S(1)} collective-permute-done((bf16[192,1536]{1,0:T(8,128)(2,1)S(1)}, bf16[192,1536]{1,0:T(8,128)(2,1)S(1)}, u32[]{:S(2)}, u32[]{:S(2)}) %collective-permute-start.39) | collective-permute-done | bytes 589856 | tf_op jit(solution)/shard_map/ppermute | solution.py:747
  176.6 4.1 %collective-permute-start.47 = (bf16[48,1536]{1,0:T(8,128)(2,1)S(1)}, bf16[48,1536]{1,0:T(8,128)(2,1)S(1)}, u32[]{:S(2)}, u32[]{:S(2)}) collective-permute-start(bf16[48,1536]{1,0:T(8,128)(2,1)S(1)} %get-tuple-element.174), channel_id=1, source_target_pairs={{0,8},{1,9},{2,10},{3,11},{4,12},{5,13},{6,14},{7,15},{8,0},{9,1},... | collective-permute-start | bytes 442376 | tf_op jit(solution)/shard_map/ppermute | solution.py:747
  180.6 6.0 %collective-permute-done.47.refs_8_ = bf16[48,1536]{1,0:T(8,128)(2,1)S(1)} collective-permute-done((bf16[48,1536]{1,0:T(8,128)(2,1)S(1)}, bf16[48,1536]{1,0:T(8,128)(2,1)S(1)}, u32[]{:S(2)}, u32[]{:S(2)}) %collective-permute-start.47) | collective-permute-done | bytes 147488 | tf_op jit(solution)/shard_map/ppermute | solution.py:747
  186.6 6.1 %collective-permute-done.46.refs_6_ = bf16[96,1536]{1,0:T(8,128)(2,1)S(1)} collective-permute-done((bf16[96,1536]{1,0:T(8,128)(2,1)S(1)}, bf16[96,1536]{1,0:T(8,128)(2,1)S(1)}, u32[]{:S(2)}, u32[]{:S(2)}) %collective-permute-start.46) | collective-permute-done | bytes 294944 | tf_op jit(solution)/shard_map/ppermute | solution.py:747
  192.8 4.1 %collective-permute-done.44.refs_3_ = bf16[192,1536]{1,0:T(8,128)(2,1)S(1)} collective-permute-done((bf16[192,1536]{1,0:T(8,128)(2,1)S(1)}, bf16[192,1536]{1,0:T(8,128)(2,1)S(1)}, u32[]{:S(2)}, u32[]{:S(2)}) %collective-permute-start.44) | collective-permute-done | bytes 589856 | tf_op jit(solution)/shard_map/ppermute | solution.py:747
  202.3 2.6 %collective-permute-start.53 = (bf16[48,1536]{1,0:T(8,128)(2,1)S(1)}, bf16[48,1536]{1,0:T(8,128)(2,1)S(1)}, u32[]{:S(2)}, u32[]{:S(2)}) collective-permute-start(bf16[48,1536]{1,0:T(8,128)(2,1)S(1)} %copy-done.19), channel_id=1, source_target_pairs={{0,8},{1,9},{2,10},{3,11},{4,12},{5,13},{6,14},{7,15},{8,0},{9,1},... | collective-permute-start | bytes 442376 | tf_op jit(solution)/shard_map/ppermute | solution.py:747
  204.9 1.4 copy-done.36
  207.4 3.5 %shard_map.264 = (bf16[256,768]{1,0:T(8,128)(2,1)}, bf16[960,768]{1,0:T(8,128)(2,1)S(1)}) custom-call(f32[8,768]{1,0:T(8,128)S(1)} %copy-done.53, bf16[256,768]{1,0:T(8,128)(2,1)S(1)} %bitcast.13, bf16[256,768]{1,0:T(8,128)(2,1)S(1)} %copy-done.28, bf16[256,768]{1,0:T(8,128)(2,1)} %collective-permute-done.48.refs_3_, f32[256,768]{1,0:T(8,128)S(1)} %copy-done.43, ...), custom_call_target="tpu_custom_call" | custom-call | flops 28000000000 | tf_op jit(solution)/shard_map/pallas_call | solution.py:97
  211.0 5.1 %collective-permute-done.52.refs_4_ = bf16[96,1536]{1,0:T(8,128)(2,1)S(1)} collective-permute-done((bf16[96,1536]{1,0:T(8,128)(2,1)S(1)}, bf16[96,1536]{1,0:T(8,128)(2,1)S(1)}, u32[]{:S(2)}, u32[]{:S(2)}) %collective-permute-start.52) | collective-permute-done | bytes 294944 | tf_op jit(solution)/shard_map/ppermute | solution.py:747
  220.4 1.5 collective-permute-start.55
  221.9 1.8 collective-permute-start.56
  223.8 1.6 copy.58
  228.6 2.8 %collective-permute-done.54.refs_1_ = bf16[48,1664]{1,0:T(8,128)(2,1)S(1)} collective-permute-done((bf16[48,1664]{1,0:T(8,128)(2,1)S(1)}, bf16[48,1664]{1,0:T(8,128)(2,1)S(1)}, u32[]{:S(2)}, u32[]{:S(2)}) %collective-permute-start.54) | collective-permute-done | bytes 159776 | tf_op jit(solution)/shard_map/ppermute | solution.py:747
  231.4 4.8 %collective-permute-done.56.refs_3_ = bf16[48,1664]{1,0:T(8,128)(2,1)S(1)} collective-permute-done((bf16[48,1664]{1,0:T(8,128)(2,1)S(1)}, bf16[48,1664]{1,0:T(8,128)(2,1)S(1)}, u32[]{:S(2)}, u32[]{:S(2)}) %collective-permute-start.56) | collective-permute-done | bytes 159776 | tf_op jit(solution)/shard_map/ppermute | solution.py:747
  (260 shorter events, 48.9 us)
Async XLA Ops:
  1.2 10.6 %collective-permute-start.7 = (bf16[4,228,768]{2,0,1:T(4,128)(2,1)}, bf16[4,228,768]{2,0,1:T(4,128)(2,1)}, u32[]{:S(2)}, u32[]{:S(2)}) collective-permute-start(bf16[4,228,768]{2,0,1:T(4,128)(2,1)} %param.14), channel_id=1, source_target_pairs={{0,1},{1,0},{2,3},{3,2},{4,5},{5,4},{6,7},{7,6},{8,9},{9,8},{10,11... | collective-permute-start | bytes 4202504 | tf_op jit(solution)/shard_map/ppermute | solution.py:747
  6.5 15.6 %collective-permute-start.5 = (bf16[48,1664]{1,0:T(8,128)(2,1)S(1)}, bf16[48,1664]{1,0:T(8,128)(2,1)S(1)}, u32[]{:S(2)}, u32[]{:S(2)}) collective-permute-start(bf16[48,1664]{1,0:T(8,128)(2,1)S(1)} %get-tuple-element.109.refs_7_.refs_0_), channel_id=1, source_target_pairs={{0,16},{1,17},{2,18},{3,19},{4,20},{5,21},{6,22},{7,23},{8,24},{9,... | collective-permute-start | bytes 479240 | tf_op jit(solution)/shard_map/ppermute | solution.py:747
  10.3 12.5 %collective-permute-start.6 = (bf16[48,1664]{1,0:T(8,128)(2,1)S(1)}, bf16[48,1664]{1,0:T(8,128)(2,1)}, u32[]{:S(2)}, u32[]{:S(2)}) collective-permute-start(bf16[48,1664]{1,0:T(8,128)(2,1)S(1)} %get-tuple-element.109.refs_7_.refs_0_), channel_id=1, source_target_pairs={{0,24},{1,25},{2,26},{3,27},{4,28},{5,29},{6,30},{7,31},{8,16},{9,... | collective-permute-start | bytes 479240 | tf_op jit(solution)/shard_map/ppermute | solution.py:747
  11.6 14.8 %collective-permute-start.4 = (bf16[48,3200]{1,0:T(8,128)(2,1)S(1)}, bf16[48,3200]{1,0:T(8,128)(2,1)}, u32[]{:S(2)}, u32[]{:S(2)}) collective-permute-start(bf16[48,3200]{1,0:T(8,128)(2,1)S(1)} %get-tuple-element.110.refs_8_.refs_4_), channel_id=1, source_target_pairs={{0,8},{1,9},{2,10},{3,11},{4,12},{5,13},{6,14},{7,15},{8,0},{9,1},... | collective-permute-start | bytes 921608 | tf_op jit(solution)/shard_map/ppermute | solution.py:747
  19.0 7.5 %collective-permute-start.8 = (bf16[48,768]{1,0:T(8,128)(2,1)S(1)}, bf16[48,768]{1,0:T(8,128)(2,1)S(1)}, u32[]{:S(2)}, u32[]{:S(2)}) collective-permute-start(bf16[48,768]{1,0:T(8,128)(2,1)S(1)} %shard_map.223.refs_2_), channel_id=1, source_target_pairs={{0,2},{1,5},{2,0},{3,7},{4,6},{5,1},{6,4},{7,3},{8,10},{9,13},{10,... | collective-permute-start | bytes 221192 | tf_op jit(solution)/shard_map/ppermute | solution.py:747
  29.3 17.2 %collective-permute-start.10 = (bf16[192,1664]{1,0:T(8,128)(2,1)S(1)}, bf16[192,1664]{1,0:T(8,128)(2,1)S(1)}, u32[]{:S(2)}, u32[]{:S(2)}) collective-permute-start(bf16[192,1664]{1,0:T(8,128)(2,1)S(1)} %get-tuple-element.114.refs_1_.refs_3_), channel_id=1, source_target_pairs={{0,2},{1,5},{2,0},{3,7},{4,6},{5,1},{6,4},{7,3},{8,10},{9,13},{10,... | collective-permute-start | bytes 1916936 | tf_op jit(solution)/shard_map/ppermute | solution.py:747
  30.9 15.7 %collective-permute-start.11 = (bf16[192,1664]{1,0:T(8,128)(2,1)S(1)}, bf16[192,1664]{1,0:T(8,128)(2,1)S(1)}, u32[]{:S(2)}, u32[]{:S(2)}) collective-permute-start(bf16[192,1664]{1,0:T(8,128)(2,1)S(1)} %get-tuple-element.114.refs_1_.refs_3_), channel_id=1, source_target_pairs={{0,4},{1,3},{2,6},{3,1},{4,0},{5,7},{6,2},{7,5},{8,12},{9,11},{10,... | collective-permute-start | bytes 1916936 | tf_op jit(solution)/shard_map/ppermute | solution.py:747
  32.6 14.5 %collective-permute-start.16 = (bf16[48,2304]{1,0:T(8,128)(2,1)S(1)}, bf16[48,2304]{1,0:T(8,128)(2,1)S(1)}, u32[]{:S(2)}, u32[]{:S(2)}) collective-permute-start(bf16[48,2304]{1,0:T(8,128)(2,1)S(1)} %shard_map.228.refs_6_), channel_id=1, source_target_pairs={{0,8},{1,9},{2,10},{3,11},{4,12},{5,13},{6,14},{7,15},{8,0},{9,1},... | collective-permute-start | bytes 663560 | tf_op jit(solution)/shard_map/ppermute | solution.py:747
  33.0 15.5 %collective-permute-start.14 = (bf16[96,1536]{1,0:T(8,128)(2,1)}, bf16[96,1536]{1,0:T(8,128)(2,1)S(1)}, u32[]{:S(2)}, u32[]{:S(2)}) collective-permute-start(bf16[96,1536]{1,0:T(8,128)(2,1)} %copy-done.13), channel_id=1, source_target_pairs={{0,16},{1,17},{2,18},{3,19},{4,20},{5,21},{6,22},{7,23},{8,24},{9,... | collective-permute-start | bytes 884744 | tf_op jit(solution)/shard_map/ppermute | solution.py:747
  36.7 10.4 %collective-permute-start.15 = (bf16[48,768]{1,0:T(8,128)(2,1)S(1)}, bf16[48,768]{1,0:T(8,128)(2,1)S(1)}, u32[]{:S(2)}, u32[]{:S(2)}) collective-permute-start(bf16[48,768]{1,0:T(8,128)(2,1)S(1)} %shard_map.227), channel_id=1, source_target_pairs={{0,4},{1,3},{2,6},{3,1},{4,0},{5,7},{6,2},{7,5},{8,12},{9,11},{10,... | collective-permute-start | bytes 221192 | tf_op jit(solution)/shard_map/ppermute | solution.py:747
  46.5 16.2 %collective-permute-start.12 = (bf16[192,1664]{1,0:T(8,128)(2,1)S(1)}, bf16[192,1664]{1,0:T(8,128)(2,1)S(1)}, u32[]{:S(2)}, u32[]{:S(2)}) collective-permute-start(bf16[192,1664]{1,0:T(8,128)(2,1)S(1)} %shard_map.225.refs_2_.refs_8_.refs_4_), channel_id=1, source_target_pairs={{0,4},{1,3},{2,6},{3,1},{4,0},{5,7},{6,2},{7,5},{8,12},{9,11},{10,... | collective-permute-start | bytes 1916936 | tf_op jit(solution)/shard_map/ppermute | solution.py:747
  48.6 16.3 %collective-permute-start.19 = (bf16[192,1536]{1,0:T(8,128)(2,1)S(1)}, bf16[192,1536]{1,0:T(8,128)(2,1)S(1)}, u32[]{:S(2)}, u32[]{:S(2)}) collective-permute-start(bf16[192,1536]{1,0:T(8,128)(2,1)S(1)} %get-tuple-element.119.refs_1_), channel_id=1, source_target_pairs={{0,2},{1,5},{2,0},{3,7},{4,6},{5,1},{6,4},{7,3},{8,10},{9,13},{10,... | collective-permute-start | bytes 1769480 | tf_op jit(solution)/shard_map/ppermute | solution.py:747
  49.2 19.8 %collective-permute-start.20 = (bf16[192,1536]{1,0:T(8,128)(2,1)S(1)}, bf16[192,1536]{1,0:T(8,128)(2,1)S(1)}, u32[]{:S(2)}, u32[]{:S(2)}) collective-permute-start(bf16[192,1536]{1,0:T(8,128)(2,1)S(1)} %get-tuple-element.119.refs_1_), channel_id=1, source_target_pairs={{0,4},{1,3},{2,6},{3,1},{4,0},{5,7},{6,2},{7,5},{8,12},{9,11},{10,... | collective-permute-start | bytes 1769480 | tf_op jit(solution)/shard_map/ppermute | solution.py:747
  50.3 20.4 %collective-permute-start.17 = (bf16[96,2304]{1,0:T(8,128)(2,1)S(1)}, bf16[96,2304]{1,0:T(8,128)(2,1)S(1)}, u32[]{:S(2)}, u32[]{:S(2)}) collective-permute-start(bf16[96,2304]{1,0:T(8,128)(2,1)S(1)} %get-tuple-element.117.refs_0_.refs_2_), channel_id=1, source_target_pairs={{0,16},{1,17},{2,18},{3,19},{4,20},{5,21},{6,22},{7,23},{8,24},{9,... | collective-permute-start | bytes 1327112 | tf_op jit(solution)/shard_map/ppermute | solution.py:747
  51.5 17.5 %collective-permute-start.18 = (bf16[192,768]{1,0:T(8,128)(2,1)S(1)}, bf16[192,768]{1,0:T(8,128)(2,1)S(1)}, u32[]{:S(2)}, u32[]{:S(2)}) collective-permute-start(bf16[192,768]{1,0:T(8,128)(2,1)S(1)} %get-tuple-element.118.refs_4_.refs_6_.refs_8_), channel_id=1, source_target_pairs={{0,8},{1,9},{2,10},{3,11},{4,12},{5,13},{6,14},{7,15},{8,0},{9,1},... | collective-permute-start | bytes 884744 | tf_op jit(solution)/shard_map/ppermute | solution.py:747
  63.3 7.5 %collective-permute-start.13 = (bf16[768,384]{1,0:T(8,128)(2,1)S(1)}, bf16[768,384]{1,0:T(8,128)(2,1)S(1)}, u32[]{:S(2)}, u32[]{:S(2)}) collective-permute-start(bf16[768,384]{1,0:T(8,128)(2,1)S(1)} %shard_map.226.refs_8_.refs_7_), channel_id=1, source_target_pairs={{0,1},{1,0},{2,3},{3,2},{4,5},{5,4},{6,7},{7,6},{8,9},{9,8},{10,11... | collective-permute-start | bytes 1769480 | tf_op jit(solution)/shard_map/ppermute | solution.py:747
  70.9 22.4 %collective-permute-start.22 = (bf16[192,1536]{1,0:T(8,128)(2,1)S(1)}, bf16[192,1536]{1,0:T(8,128)(2,1)S(1)}, u32[]{:S(2)}, u32[]{:S(2)}) collective-permute-start(bf16[192,1536]{1,0:T(8,128)(2,1)S(1)} %shard_map.232.refs_10_.refs_1_), channel_id=1, source_target_pairs={{0,2},{1,5},{2,0},{3,7},{4,6},{5,1},{6,4},{7,3},{8,10},{9,13},{10,... | collective-permute-start | bytes 1769480 | tf_op jit(solution)/shard_map/ppermute | solution.py:747
  71.5 21.8 %collective-permute-start.23 = (bf16[192,1536]{1,0:T(8,128)(2,1)S(1)}, bf16[192,1536]{1,0:T(8,128)(2,1)S(1)}, u32[]{:S(2)}, u32[]{:S(2)}) collective-permute-start(bf16[192,1536]{1,0:T(8,128)(2,1)S(1)} %shard_map.232.refs_10_.refs_1_), channel_id=1, source_target_pairs={{0,4},{1,3},{2,6},{3,1},{4,0},{5,7},{6,2},{7,5},{8,12},{9,11},{10,... | collective-permute-start | bytes 1769480 | tf_op jit(solution)/shard_map/ppermute | solution.py:747
  73.1 20.2 %collective-permute-start.21 = (bf16[192,1536]{1,0:T(8,128)(2,1)S(1)}, bf16[192,1536]{1,0:T(8,128)(2,1)S(1)}, u32[]{:S(2)}, u32[]{:S(2)}) collective-permute-start(bf16[192,1536]{1,0:T(8,128)(2,1)S(1)} %shard_map.234.refs_2_), channel_id=1, source_target_pairs={{0,4},{1,3},{2,6},{3,1},{4,0},{5,7},{6,2},{7,5},{8,12},{9,11},{10,... | collective-permute-start | bytes 1769480 | tf_op jit(solution)/shard_map/ppermute | solution.py:747
  73.5 19.8 %collective-permute-start.24 = (bf16[384,512]{1,0:T(8,128)(2,1)S(1)}, bf16[384,512]{1,0:T(8,128)(2,1)S(1)}, u32[]{:S(2)}, u32[]{:S(2)}) collective-permute-start(bf16[384,512]{1,0:T(8,128)(2,1)S(1)} %shard_map.235), channel_id=1, source_target_pairs={{0,16},{1,17},{2,18},{3,19},{4,20},{5,21},{6,22},{7,23},{8,24},{9,... | collective-permute-start | bytes 1179656 | tf_op jit(solution)/shard_map/ppermute | solution.py:747
  94.6 15.6 %collective-permute-start.27 = (bf16[192,1536]{1,0:T(8,128)(2,1)S(1)}, bf16[192,1536]{1,0:T(8,128)(2,1)S(1)}, u32[]{:S(2)}, u32[]{:S(2)}) collective-permute-start(bf16[192,1536]{1,0:T(8,128)(2,1)S(1)} %shard_map.236.refs_1_.refs_2_), channel_id=1, source_target_pairs={{0,4},{1,3},{2,6},{3,1},{4,0},{5,7},{6,2},{7,5},{8,12},{9,11},{10,... | collective-permute-start | bytes 1769480 | tf_op jit(solution)/shard_map/ppermute | solution.py:747
  95.0 14.2 %collective-permute-start.28 = (bf16[192,768]{1,0:T(8,128)(2,1)S(1)}, bf16[192,768]{1,0:T(8,128)(2,1)S(1)}, u32[]{:S(2)}, u32[]{:S(2)}) collective-permute-start(bf16[192,768]{1,0:T(8,128)(2,1)S(1)} %shard_map.237.refs_1_), channel_id=1, source_target_pairs={{0,2},{1,5},{2,0},{3,7},{4,6},{5,1},{6,4},{7,3},{8,10},{9,13},{10,... | collective-permute-start | bytes 884744 | tf_op jit(solution)/shard_map/ppermute | solution.py:747
  95.5 14.7 %collective-permute-start.29 = (bf16[192,768]{1,0:T(8,128)(2,1)S(1)}, bf16[192,768]{1,0:T(8,128)(2,1)S(1)}, u32[]{:S(2)}, u32[]{:S(2)}) collective-permute-start(bf16[192,768]{1,0:T(8,128)(2,1)S(1)} %shard_map.237.refs_1_), channel_id=1, source_target_pairs={{0,4},{1,3},{2,6},{3,1},{4,0},{5,7},{6,2},{7,5},{8,12},{9,11},{10,... | collective-permute-start | bytes 884744 | tf_op jit(solution)/shard_map/ppermute | solution.py:747
  97.2 12.0 %collective-permute-start.30 = (bf16[384,256]{1,0:T(8,128)(2,1)S(1)}, bf16[384,256]{1,0:T(8,128)(2,1)S(1)}, u32[]{:S(2)}, u32[]{:S(2)}) collective-permute-start(bf16[384,256]{1,0:T(8,128)(2,1)S(1)} %shard_map.241), channel_id=1, source_target_pairs={{0,16},{1,17},{2,18},{3,19},{4,20},{5,21},{6,22},{7,23},{8,24},{9,... | collective-permute-start | bytes 589832 | tf_op jit(solution)/shard_map/ppermute | solution.py:747
  110.2 9.5 %collective-permute-start.32 = (bf16[192,768]{1,0:T(8,128)(2,1)S(1)}, bf16[192,768]{1,0:T(8,128)(2,1)S(1)}, u32[]{:S(2)}, u32[]{:S(2)}) collective-permute-start(bf16[192,768]{1,0:T(8,128)(2,1)S(1)} %shard_map.245), channel_id=1, source_target_pairs={{0,4},{1,3},{2,6},{3,1},{4,0},{5,7},{6,2},{7,5},{8,12},{9,11},{10,... | collective-permute-start | bytes 884744 | tf_op jit(solution)/shard_map/ppermute | solution.py:747
  118.5 9.9 %collective-permute-start.33 = (bf16[192,1536]{1,0:T(8,128)(2,1)S(1)}, bf16[192,1536]{1,0:T(8,128)(2,1)S(1)}, u32[]{:S(2)}, u32[]{:S(2)}) collective-permute-start(bf16[192,1536]{1,0:T(8,128)(2,1)S(1)} %get-tuple-element.144), channel_id=1, source_target_pairs={{0,2},{1,5},{2,0},{3,7},{4,6},{5,1},{6,4},{7,3},{8,10},{9,13},{10,... | collective-permute-start | bytes 1769480 | tf_op jit(solution)/shard_map/ppermute | solution.py:747
  128.7 22.1 %collective-permute-start.37 = (bf16[192,1536]{1,0:T(8,128)(2,1)S(1)}, bf16[192,1536]{1,0:T(8,128)(2,1)S(1)}, u32[]{:S(2)}, u32[]{:S(2)}) collective-permute-start(bf16[192,1536]{1,0:T(8,128)(2,1)S(1)} %shard_map.248.refs_1_.refs_19_), channel_id=1, source_target_pairs={{0,4},{1,3},{2,6},{3,1},{4,0},{5,7},{6,2},{7,5},{8,12},{9,11},{10,... | collective-permute-start | bytes 1769480 | tf_op jit(solution)/shard_map/ppermute | solution.py:747
  129.1 19.1 %collective-permute-start.36 = (bf16[192,1536]{1,0:T(8,128)(2,1)S(1)}, bf16[192,1536]{1,0:T(8,128)(2,1)S(1)}, u32[]{:S(2)}, u32[]{:S(2)}) collective-permute-start(bf16[192,1536]{1,0:T(8,128)(2,1)S(1)} %shard_map.252), channel_id=1, source_target_pairs={{0,2},{1,5},{2,0},{3,7},{4,6},{5,1},{6,4},{7,3},{8,10},{9,13},{10,... | collective-permute-start | bytes 1769480 | tf_op jit(solution)/shard_map/ppermute | solution.py:747
  130.3 20.4 %collective-permute-start.35 = (bf16[192,1536]{1,0:T(8,128)(2,1)S(1)}, bf16[192,1536]{1,0:T(8,128)(2,1)S(1)}, u32[]{:S(2)}, u32[]{:S(2)}) collective-permute-start(bf16[192,1536]{1,0:T(8,128)(2,1)S(1)} %shard_map.251), channel_id=1, source_target_pairs={{0,2},{1,5},{2,0},{3,7},{4,6},{5,1},{6,4},{7,3},{8,10},{9,13},{10,... | collective-permute-start | bytes 1769480 | tf_op jit(solution)/shard_map/ppermute | solution.py:747
  151.6 21.7 %collective-permute-start.41 = (bf16[192,1536]{1,0:T(8,128)(2,1)S(1)}, bf16[192,1536]{1,0:T(8,128)(2,1)S(1)}, u32[]{:S(2)}, u32[]{:S(2)}) collective-permute-start(bf16[192,1536]{1,0:T(8,128)(2,1)S(1)} %get-tuple-element.152.refs_1_.refs_17_), channel_id=1, source_target_pairs={{0,4},{1,3},{2,6},{3,1},{4,0},{5,7},{6,2},{7,5},{8,12},{9,11},{10,... | collective-permute-start | bytes 1769480 | tf_op jit(solution)/shard_map/ppermute | solution.py:747
  152.0 18.4 %collective-permute-start.40 = (bf16[192,1536]{1,0:T(8,128)(2,1)S(1)}, bf16[192,1536]{1,0:T(8,128)(2,1)S(1)}, u32[]{:S(2)}, u32[]{:S(2)}) collective-permute-start(bf16[192,1536]{1,0:T(8,128)(2,1)S(1)} %shard_map.257), channel_id=1, source_target_pairs={{0,2},{1,5},{2,0},{3,7},{4,6},{5,1},{6,4},{7,3},{8,10},{9,13},{10,... | collective-permute-start | bytes 1769480 | tf_op jit(solution)/shard_map/ppermute | solution.py:747
  153.2 20.1 %collective-permute-start.39 = (bf16[192,1536]{1,0:T(8,128)(2,1)S(1)}, bf16[192,1536]{1,0:T(8,128)(2,1)S(1)}, u32[]{:S(2)}, u32[]{:S(2)}) collective-permute-start(bf16[192,1536]{1,0:T(8,128)(2,1)S(1)} %shard_map.256), channel_id=1, source_target_pairs={{0,2},{1,5},{2,0},{3,7},{4,6},{5,1},{6,4},{7,3},{8,10},{9,13},{10,... | collective-permute-start | bytes 1769480 | tf_op jit(solution)/shard_map/ppermute | solution.py:747
  154.0 16.3 %collective-permute-start.42 = (bf16[96,1536]{1,0:T(8,128)(2,1)S(1)}, bf16[96,1536]{1,0:T(8,128)(2,1)S(1)}, u32[]{:S(2)}, u32[]{:S(2)}) collective-permute-start(bf16[96,1536]{1,0:T(8,128)(2,1)S(1)} %get-tuple-element.167), channel_id=1, source_target_pairs={{0,16},{1,17},{2,18},{3,19},{4,20},{5,21},{6,22},{7,23},{8,24},{9,... | collective-permute-start | bytes 884744 | tf_op jit(solution)/shard_map/ppermute | solution.py:747
  173.7 23.1 %collective-permute-start.43 = (bf16[192,1664]{1,0:T(8,128)(2,1)S(1)}, bf16[192,1664]{1,0:T(8,128)(2,1)S(1)}, u32[]{:S(2)}, u32[]{:S(2)}) collective-permute-start(bf16[192,1664]{1,0:T(8,128)(2,1)S(1)} %shard_map.259), channel_id=1, source_target_pairs={{0,2},{1,5},{2,0},{3,7},{4,6},{5,1},{6,4},{7,3},{8,10},{9,13},{10,... | collective-permute-start | bytes 1916936 | tf_op jit(solution)/shard_map/ppermute | solution.py:747
  174.9 21.9 %collective-permute-start.44 = (bf16[192,1536]{1,0:T(8,128)(2,1)S(1)}, bf16[192,1536]{1,0:T(8,128)(2,1)S(1)}, u32[]{:S(2)}, u32[]{:S(2)}) collective-permute-start(bf16[192,1536]{1,0:T(8,128)(2,1)S(1)} %shard_map.260), channel_id=1, source_target_pairs={{0,2},{1,5},{2,0},{3,7},{4,6},{5,1},{6,4},{7,3},{8,10},{9,13},{10,... | collective-permute-start | bytes 1769480 | tf_op jit(solution)/shard_map/ppermute | solution.py:747
  175.8 21.0 %collective-permute-start.45 = (bf16[192,1536]{1,0:T(8,128)(2,1)S(1)}, bf16[192,1536]{1,0:T(8,128)(2,1)S(1)}, u32[]{:S(2)}, u32[]{:S(2)}) collective-permute-start(bf16[192,1536]{1,0:T(8,128)(2,1)S(1)} %get-tuple-element.168.refs_1_), channel_id=1, source_target_pairs={{0,4},{1,3},{2,6},{3,1},{4,0},{5,7},{6,2},{7,5},{8,12},{9,11},{10,... | collective-permute-start | bytes 1769480 | tf_op jit(solution)/shard_map/ppermute | solution.py:747
  176.2 16.6 %collective-permute-start.46 = (bf16[96,1536]{1,0:T(8,128)(2,1)S(1)}, bf16[96,1536]{1,0:T(8,128)(2,1)S(1)}, u32[]{:S(2)}, u32[]{:S(2)}) collective-permute-start(bf16[96,1536]{1,0:T(8,128)(2,1)S(1)} %get-tuple-element.172), channel_id=1, source_target_pairs={{0,16},{1,17},{2,18},{3,19},{4,20},{5,21},{6,22},{7,23},{8,24},{9,... | collective-permute-start | bytes 884744 | tf_op jit(solution)/shard_map/ppermute | solution.py:747
  176.6 10.1 %collective-permute-start.47 = (bf16[48,1536]{1,0:T(8,128)(2,1)S(1)}, bf16[48,1536]{1,0:T(8,128)(2,1)S(1)}, u32[]{:S(2)}, u32[]{:S(2)}) collective-permute-start(bf16[48,1536]{1,0:T(8,128)(2,1)S(1)} %get-tuple-element.174), channel_id=1, source_target_pairs={{0,8},{1,9},{2,10},{3,11},{4,12},{5,13},{6,14},{7,15},{8,0},{9,1},... | collective-permute-start | bytes 442376 | tf_op jit(solution)/shard_map/ppermute | solution.py:747
  198.8 17.3 %collective-permute-start.51 = (bf16[192,1664]{1,0:T(8,128)(2,1)S(1)}, bf16[192,1664]{1,0:T(8,128)(2,1)S(1)}, u32[]{:S(2)}, u32[]{:S(2)}) collective-permute-start(bf16[192,1664]{1,0:T(8,128)(2,1)S(1)} %get-tuple-element.175.refs_1_), channel_id=1, source_target_pairs={{0,4},{1,3},{2,6},{3,1},{4,0},{5,7},{6,2},{7,5},{8,12},{9,11},{10,... | collective-permute-start | bytes 1916936 | tf_op jit(solution)/shard_map/ppermute | solution.py:747
  199.3 16.8 %collective-permute-start.50 = (bf16[192,1664]{1,0:T(8,128)(2,1)S(1)}, bf16[192,1664]{1,0:T(8,128)(2,1)S(1)}, u32[]{:S(2)}, u32[]{:S(2)}) collective-permute-start(bf16[192,1664]{1,0:T(8,128)(2,1)S(1)} %shard_map.265), channel_id=1, source_target_pairs={{0,2},{1,5},{2,0},{3,7},{4,6},{5,1},{6,4},{7,3},{8,10},{9,13},{10,... | collective-permute-start | bytes 1916936 | tf_op jit(solution)/shard_map/ppermute | solution.py:747
  200.4 15.6 %collective-permute-start.52 = (bf16[96,1536]{1,0:T(8,128)(2,1)S(1)}, bf16[96,1536]{1,0:T(8,128)(2,1)S(1)}, u32[]{:S(2)}, u32[]{:S(2)}) collective-permute-start(bf16[96,1536]{1,0:T(8,128)(2,1)S(1)} %copy-done.12), channel_id=1, source_target_pairs={{0,16},{1,17},{2,18},{3,19},{4,20},{5,21},{6,22},{7,23},{8,24},{9,... | collective-permute-start | bytes 884744 | tf_op jit(solution)/shard_map/ppermute | solution.py:747
  202.3 8.7 %collective-permute-start.53 = (bf16[48,1536]{1,0:T(8,128)(2,1)S(1)}, bf16[48,1536]{1,0:T(8,128)(2,1)S(1)}, u32[]{:S(2)}, u32[]{:S(2)}) collective-permute-start(bf16[48,1536]{1,0:T(8,128)(2,1)S(1)} %copy-done.19), channel_id=1, source_target_pairs={{0,8},{1,9},{2,10},{3,11},{4,12},{5,13},{6,14},{7,15},{8,0},{9,1},... | collective-permute-start | bytes 442376 | tf_op jit(solution)/shard_map/ppermute | solution.py:747
  217.4 8.0 %collective-permute-start.60 = (f32[24,1536]{1,0:T(8,128)S(1)}, f32[24,1536]{1,0:T(8,128)S(1)}, u32[]{:S(2)}, u32[]{:S(2)}) collective-permute-start(f32[24,1536]{1,0:T(8,128)S(1)} %constant_dynamic-slice_fusion), channel_id=1, source_target_pairs={{0,1},{1,0},{2,3},{3,2},{4,5},{5,4},{6,7},{7,6},{8,9},{9,8},{10,11... | collective-permute-start | bytes 442376 | tf_op jit(solution)/shard_map/ppermute | solution.py:747
  218.3 10.1 %collective-permute-start.58 = (bf16[48,1536]{1,0:T(8,128)(2,1)S(1)}, bf16[48,1536]{1,0:T(8,128)(2,1)S(1)}, u32[]{:S(2)}, u32[]{:S(2)}) collective-permute-start(bf16[48,1536]{1,0:T(8,128)(2,1)S(1)} %get-tuple-element.194), channel_id=1, source_target_pairs={{0,8},{1,9},{2,10},{3,11},{4,12},{5,13},{6,14},{7,15},{8,0},{9,1},... | collective-permute-start | bytes 442376 | tf_op jit(solution)/shard_map/ppermute | solution.py:747
  219.3 12.1 %collective-permute-start.54 = (bf16[48,1664]{1,0:T(8,128)(2,1)S(1)}, bf16[48,1664]{1,0:T(8,128)(2,1)S(1)}, u32[]{:S(2)}, u32[]{:S(2)}) collective-permute-start(bf16[48,1664]{1,0:T(8,128)(2,1)S(1)} %get-tuple-element.188), channel_id=1, source_target_pairs={{0,8},{1,9},{2,10},{3,11},{4,12},{5,13},{6,14},{7,15},{8,0},{9,1},... | collective-permute-start | bytes 479240 | tf_op jit(solution)/shard_map/ppermute | solution.py:747
  220.4 11.0 %collective-permute-start.55 = (bf16[48,1664]{1,0:T(8,128)(2,1)S(1)}, bf16[48,1664]{1,0:T(8,128)(2,1)S(1)}, u32[]{:S(2)}, u32[]{:S(2)}) collective-permute-start(bf16[48,1664]{1,0:T(8,128)(2,1)S(1)} %get-tuple-element.189), channel_id=1, source_target_pairs={{0,16},{1,17},{2,18},{3,19},{4,20},{5,21},{6,22},{7,23},{8,24},{9,... | collective-permute-start | bytes 479240 | tf_op jit(solution)/shard_map/ppermute | solution.py:747
  221.9 14.3 %collective-permute-start.56 = (bf16[48,1664]{1,0:T(8,128)(2,1)S(1)}, bf16[48,1664]{1,0:T(8,128)(2,1)S(1)}, u32[]{:S(2)}, u32[]{:S(2)}) collective-permute-start(bf16[48,1664]{1,0:T(8,128)(2,1)S(1)} %get-tuple-element.190), channel_id=1, source_target_pairs={{0,24},{1,25},{2,26},{3,27},{4,28},{5,29},{6,30},{7,31},{8,16},{9,... | collective-permute-start | bytes 479240 | tf_op jit(solution)/shard_map/ppermute | solution.py:747
  228.5 7.9 %collective-permute-start.59 = (f32[24,1536]{1,0:T(8,128)S(1)}, f32[24,1536]{1,0:T(8,128)S(1)}, u32[]{:S(2)}, u32[]{:S(2)}) collective-permute-start(f32[24,1536]{1,0:T(8,128)S(1)} %get-tuple-element.208), channel_id=1, source_target_pairs={{0,1},{1,0},{2,3},{3,2},{4,5},{5,4},{6,7},{7,6},{8,9},{9,8},{10,11... | collective-permute-start | bytes 442376 | tf_op jit(solution)/shard_map/ppermute | solution.py:747
  (69 other events, 368.0 us)

commit v6 on v5

--- a/solution.py
+++ b/solution.py
@@ -255,9 +255,9 @@
             outs[q][r * blk : (r + 1) * blk, :] = dw[pl.ds(row, blk), :]
 
 
-def pack_kernel(core, qkv, out, cq, ckv, cout, win, gains, biases, keep, send, vecs):
+def pack_kernel(core, qkv, out, cq, ckv, cout, gains, biases, keep, send, vecs):
     c = core[0]
-    qkv, out, cq, ckv, cout, win, gains, biases = ready(qkv, out, cq, ckv, cout, win, gains, biases)
+    qkv, out, cq, ckv, cout, gains, biases = ready(qkv, out, cq, ckv, cout, gains, biases)
     vecs[...] = jnp.zeros_like(vecs)
     vecs[0:3, 0:24] = gains[...].astype(F32)
     vecs[3:6, 0:24] = biases[...].astype(F32)
@@ -273,23 +273,35 @@
                 lanes = pl.ds(pl.multiple_of(k * D + which * DH, 128), DH)
                 dst[:, at : at + DH] = w[:, lanes]
                 at += DH
+
+
+def pack_inner_kernel(core, win, keep, send):
+    c = core[0]
+    win = ready(win)
     hr = 96
     for k in range(win.shape[1] // (2 * hr)):
         first = win[:, 2 * k * hr : (2 * k + 1) * hr]
         second = win[:, (2 * k + 1) * hr : (2 * k + 2) * hr]
-        keep[:, at + k * hr : at + (k + 1) * hr] = jnp.where(c == 0, first, second)
-        send[:, at + k * hr : at + (k + 1) * hr] = jnp.where(c == 0, second, first)
-
-
-def order_kernel(core, keep, got, wout, both, one, three, last):
+        keep[:, k * hr : (k + 1) * hr] = jnp.where(c == 0, first, second)
+        send[:, k * hr : (k + 1) * hr] = jnp.where(c == 0, second, first)
+
+
+def order_kernel(core, keep, got, wout, last, *outs):
     c = core[0]
-    keep, got, wout = ready(keep, got, wout)
     rows = keep.shape[0]
     for b, (top, under) in enumerate(((keep, got), (got, keep))):
-        for dst, at, width in ((both, 0, both.shape[1]), (one, 0, one.shape[1]), (three, both.shape[1], 4 * DH)):
-            dst[b * rows : (b + 1) * rows, :width] = jnp.where(c == 0, top[:, at : at + width], under[:, at : at + width])
-    three[:, 4 * DH :] = wout[0 : 2 * rows, :]
+        for dst in outs:
+            width = dst.shape[1]
+            dst[b * rows : (b + 1) * rows, :] = jnp.where(c == 0, top[:, :width], under[:, :width])
     last[...] = wout[2 * rows :, :]
+
+
+def order_mlp_kernel(core, keep, got, wout, three):
+    c = core[0]
+    rows, width = keep.shape
+    for b, (top, under) in enumerate(((keep, got), (got, keep))):
+        three[b * rows : (b + 1) * rows, :width] = jnp.where(c == 0, top[...], under[...])
+    three[:, width:] = wout[0 : 2 * rows, :]
 
 
 def cats(jobs, after=()):
@@ -486,16 +498,25 @@
     comb[2 * half :, :] = nn(hidden[half:, :], wout[...]).astype(BF)
 
 
-def dmlpout_kernel(offs, hidden, g, *refs):
-    outs, dw = refs[:4], refs[4]
-    hidden, g = ready(hidden, g)
+def dmlpout_kernel(offs, hidden, g, own, a, b, ab, near, *refs):
+    far, dw, dz = refs[:-2], refs[-2], refs[-1]
     blk = dw.shape[0] // 16
-    for b in range(4):
-        part = tn(hidden[:, b * 8 * blk : (b + 1) * 8 * blk], g[...]).astype(BF)
+    for i in range(4):
+        part = tn(hidden[:, i * 8 * blk : (i + 1) * 8 * blk], g[...]).astype(BF)
         for k in range(8):
-            row = (4 * b + k // 2) * blk
-            dw[row : row + blk, (k % 2) * D : (k % 2 + 1) * D] = part[k * blk : (k + 1) * blk]
-    send_out(dw, offs, outs)
+            dst = dz if k % 2 else dw
+            row = (4 * i + k // 2) * blk
+            dst[row : row + blk, :] = part[k * blk : (k + 1) * blk]
+    send_out(dw, offs, (own, a, b, ab))
+    for q in range(4):
+        for r in range(4):
+            rows = pl.ds(pl.multiple_of(offs[0, q * 4 + r] * blk, 16), blk)
+            at = ((r % 2) * 4 + q) * blk
+            if r < 2:
+                near[at : at + blk, :] = dz[rows, :]
+                continue
+            for dst, (lo, width) in zip(far, FAR_CUTS):
+                dst[at : at + blk, :] = dz[rows, lo : lo + width]
 
 
 def mlp_and_grad_kernel(
@@ -564,33 +585,34 @@
     dw[half_lanes(1 - c), lo : lo + DH] = rest.astype(BF)
 
 
-def dcross_kernel(offs, core, mixed, mixed_other, gtwo, second, dcq, dkv, wckv, mem, *refs):
-    outs, gmem, dw = refs[:4], refs[4:6], refs[6]
+def dcross_kernel(offs, core, mixed, mixed_other, gtwo, second, dcq, dkv, mem, *refs):
+    outs, dw = refs[:4], refs[4]
     mixed, mixed_other, gtwo = ready(mixed, mixed_other, gtwo)
     out_grad(dw, 0, core[0], mixed, mixed_other, gtwo)
     second, dcq = ready(second, dcq)
     dw[:, DH : 2 * DH] = tn(second[...], dcq[...]).astype(BF)
-    dkv, wckv = ready(dkv, wckv)
-    half = dkv.shape[0] // 2
-    for i, dst in ((1, gmem[1]), (0, gmem[0])):
-        for b in range(0, half, 480):
-            dst[b : b + 480, :] = nt(dkv[i * half + b : i * half + b + 480, :], wckv[...]).astype(BF)
-    flush(*gmem)
     mem = ready(mem)
     for b in range(0, D, 256):
         dw[b : b + 256, 2 * DH :] = tn(mem[:, b : b + 256], dkv[...]).astype(BF)
     send_out(dw, offs, outs)
 
 
+def memory_kernel(dkv, wckv, own, other):
+    half = own.shape[0]
+    for i, dst in ((1, other), (0, own)):
+        for b in range(0, half, 480):
+            dst[b : b + 480, :] = nt(dkv[i * half + b : i * half + b + 480, :], wckv[...]).astype(BF)
+
+
 def cross_back_and_grads_kernel(
-    offs, core, vec, resid, part, recv, own, g, keep, back, kv, cq, probs, wcq, mixed, mixed_other, second, wckv, mem,
-    output, gresid, gsecond, dvec, gmem_own, gmem_other, d_own, d_a, d_b, d_ab, gtwo, dcq, dkv, gm, dw
+    offs, core, vec, resid, part, recv, own, g, keep, back, kv, cq, probs, wcq, mixed, mixed_other, second, mem,
+    output, gresid, gsecond, dvec, dkv, d_own, d_a, d_b, d_ab, gtwo, dcq, gm, dw
 ):
     cross_back_kernel(
         core, vec, resid, part, recv, own, g, keep, back, kv, cq, probs, wcq, output, gresid, gtwo, dcq, dkv, gsecond, dvec, gm
     )
     dcross_kernel(
-        offs, core, mixed, mixed_other, gtwo, second, dcq, dkv, wckv, mem, d_own, d_a, d_b, d_ab, gmem_own, gmem_other, dw
+        offs, core, mixed, mixed_other, gtwo, second, dcq, dkv, mem, d_own, d_a, d_b, d_ab, dw
     )
 
 
@@ -667,7 +689,8 @@
     dself_kernel(offs, core, mixed, mixed_other, gone, first, dpacked, dvec_two, dvec, d_own, d_a, d_b, d_ab, dw, vecs)
 
 
-def tokens_back_kernel(vec, tok, part, recv, gresid, gmem, gmem_recv, gtok, gmemory):
+def tokens_back_kernel(vec, tok, part, recv, gresid, gmem, gmem_recv, gtok, gmemory, token):
+    token[...] = jnp.zeros_like(token)
     vec, tok, part, recv, gresid = ready(vec, tok, part, recv, gresid)
     gain = vec[0:1]
 
@@ -683,15 +706,47 @@
     gmemory[...] = (gmem[...].astype(F32) + gmem_recv[...].astype(F32)).astype(BF)
 
 
-MERGES = {"pass": (2, 1), "sum": (3, 4), "end": (4, 1), "half": (3, 2), "near": (2, 2), "last": (2, 1)}
-
-
-def merge_kernel(kinds, *refs):
+MERGES = {"pass": (2, 1), "half": (3, 2), "near": (2, 2), "last": (2, 1)}
+MERGES.update({"tail": (6, 1), "tail_near": (3, 1), "send": (3, 3), "send_near": (2, 1), "levels": (3, 2), "columns": (2, 3), "side": (3, 2)})
+
+
+def merge_kernel(kinds, beside, *refs):
+    if beside:
+        n_in, (i, j) = sum(MERGES[kind][0] for kind in kinds), beside
+        outs = list(refs[n_in:])
+        wide, width = outs[i], outs[i].shape[1] - refs[n_in - 2].shape[1]
+        outs[i] = wide.at[:, :width]
+        outs.insert(j, wide.at[:, width:])
+        refs = (*refs[:n_in], *outs)
     at, out = 0, sum(MERGES[kind][0] for kind in kinds)
     for kind in kinds:
         ins, outs = refs[at : at + MERGES[kind][0]], refs[out : out + MERGES[kind][1]]
         at, out = at + len(ins), out + len(outs)
-        if kind == "sum" or kind == "half" or kind == "near":
+        if kind == "levels":
+            half = outs[0].shape[0]
+            for i, dst in enumerate(outs):
+                rows = slice(i * half, (i + 1) * half)
+                for src, (lo, width) in zip(ins[1:], FAR_CUTS):
+                    total = ins[0][rows, lo : lo + width].astype(F32) + src[rows, :].astype(F32)
+                    dst[:, lo : lo + width] = total.astype(dst.dtype)
+        elif kind == "columns":
+            blk = outs[0].shape[0]
+            for i, (dst, at) in enumerate(((outs[0], 0), (outs[2], 0), (outs[1], 0), (outs[2], blk))):
+                rows = slice(i * blk, (i + 1) * blk)
+                dst[at : at + blk, :] = (ins[0][rows, :] + ins[1][rows, :].astype(F32)).astype(dst.dtype)
+        elif kind == "send" or kind == "send_near":
+            blk = outs[0].shape[0]
+            for i, dst in enumerate(outs):
+                rows = slice((i + 1) * blk, (i + 2) * blk)
+                dst[...] = sum(x[rows, :].astype(F32) for x in ins).astype(dst.dtype)
+        elif kind == "tail" or kind == "tail_near":
+            blk = outs[0].shape[0]
+            outs[0][...] = sum(x[:blk, :].astype(F32) for x in ins)
+        elif kind == "side":
+            blk = outs[0].shape[0]
+            outs[0][...] = ins[0][...] + ins[2][:blk, :].astype(F32)
+            outs[1][...] = (ins[1][...] + ins[2][blk:, :].astype(F32)).astype(BF)
+        elif kind == "half" or kind == "near":
             blk = outs[0].shape[0]
             for i, dst in enumerate(outs):
                 rows = slice(i * blk, (i + 1) * blk)
@@ -700,17 +755,39 @@
             outs[0][...] = sum(x[...].astype(F32) for x in ins).astype(outs[0].dtype)
 
 
-def merge(jobs, after=()):
+def merge(jobs, after=(), beside=None):
     ins, outs = [], []
     for kind, *arrays in jobs:
         ins += arrays
         rows, width = arrays[0].shape
-        parts = {"sum": 4, "half": 2, "near": 2}.get(kind, 1)
+        if kind == "levels":
+            outs += [sds((rows // 2, width), F32), sds((rows // 2, width), BF)]
+            continue
+        if kind == "columns":
+            outs += [sds((rows // 4, width), F32)] * 2 + [sds((rows // 2, width), BF)]
+            continue
+        if kind == "send":
+            outs += [sds((rows // 4, width), BF)] * 3
+            continue
+        if kind == "send_near":
+            outs.append(sds((rows // 2, width), BF))
+            continue
+        if kind == "tail" or kind == "tail_near":
+            outs.append(sds((rows // (4 if kind == "tail" else 2), width), F32))
+            continue
+        if kind == "side":
+            outs += [sds((rows, width), F32), sds((rows, width), BF)]
+            continue
+        parts = 1 if kind in ("pass", "last") else 2
         outs.append(sds((rows // parts, width), BF if kind == "pass" else F32))
         outs += [sds((rows // parts, width), BF)] * (parts - 1)
     kinds = [job[0] for job in jobs]
+    if beside:
+        i, j = beside
+        outs[i] = sds((outs[i].shape[0], outs[i].shape[1] + outs[j].shape[1]), outs[i].dtype)
+        del outs[j]
     return kernel_call(
-        lambda *refs: merge_kernel(kinds, *refs), ins, [VM] * len(ins), outs, cost=1, after=after
+        lambda *refs: merge_kernel(kinds, beside, *refs), ins, [VM] * len(ins), outs, cost=1, after=after
     )
 
 
@@ -734,6 +811,7 @@
 
 
 CUTS = ((0, 512), (512, 256))
+FAR_CUTS = ((0, 256), (256, 512))
 
 
 class Moves:
@@ -875,26 +953,24 @@
             cross_back_and_grads_kernel,
             [
                 offs, core, vec, resid_two, comb, recv, part, g, *cout, kv, cq, cprobs, w_cq,
-                *cross_mixed, second, w_ckv, mem,
+                *cross_mixed, second, mem,
             ],
-            [SM] * 2 + [VM] * 17,
+            [SM] * 2 + [VM] * 16,
             [
                 sds((rows, D), BF),
                 sds((r2, D), F32),
                 sds((r2, D), BF),
                 sds((8, D), F32),
-                sds((seqs * pad, D), BF),
-                sds((seqs * pad, D), BF),
+                sds(kv.shape, BF),
             ]
             + [sds((4 * wb, 4 * DH), BF)] * 4,
             scratch=[
                 pltpu.VMEM((r2, D), BF),
                 pltpu.VMEM((r2, DH), BF),
-                pltpu.VMEM(kv.shape, BF),
                 pltpu.VMEM((r2, DH), BF),
                 pltpu.VMEM((D, 4 * DH), BF),
             ],
-            cost=16,
+            cost=14,
             after=after,
             limit=24 << 20,
         )
@@ -926,8 +1002,8 @@
             tokens_back_kernel,
             [vec, tokens.reshape(rows, D), gfirst, recv, gresid_one, gmem, gmem_recv],
             [STAGE] * 7,
-            [sds((rows, D), BF), sds(gmem.shape, BF)],
-            [STAGE] * 2,
+            [sds((rows, D), BF), sds(gmem.shape, BF), sds((8, 128), F32)],
+            [STAGE] * 3,
             cost=4,
             after=after,
         )
@@ -951,28 +1027,27 @@
     widths = (4 * DH + 128, 4 * DH, 4 * DH)
 
     if fast:
+        width = widths[0] + widths[1]
         keep, send = kernel_call(
             pack_kernel,
-            [core, self_qkv, self_out, cross_q, cross_kv, cross_out, mlp_in, norm_gains, norm_biases],
-            [SM] + ["stage"] * 8,
-            [sds((wr, sum(widths)), BF)] * 2,
-            [STAGE] * 2,
+            [core, self_qkv, self_out, cross_q, cross_kv, cross_out, norm_gains, norm_biases],
+            [SM] + ["stage"] * 7,
+            [sds((wr, width), BF)] * 2,
             scratch=[pltpu.VMEM((128, 128), F32)],
             cost=1,
             limit=60 << 20,
         )
-        both, one, three, last = kernel_call(
+        last, both, one = kernel_call(
             order_kernel,
             [core, keep, sib(send), mlp_out],
-            [SM] + [STAGE] * 3,
-            [sds((2 * wr, w), BF) for w in (widths[0] + widths[1], widths[0], 6 * DH, 2 * DH)],
-            [STAGE] * 4,
+            [SM] + [VM] * 3,
+            [sds((2 * wr, D), BF), sds((2 * wr, width), BF), sds((2 * wr, widths[0]), BF)],
             cost=1,
-            after=[lens, pairs[1], pairs[3]],
+            after=[pairs[1], pairs[3]],
         )
         near, far, side_a, side_b = moves.near_z, moves.far_z, moves.side_a, moves.side_b
         near_both, along = near(both), [far(one), moves.opposite_z(one)]
-        tok, g, mem, xhat = prepare(lens, pairs, hold=(one, both, three, last))
+        tok, g, mem, xhat = prepare(lens, pairs, hold=(one, both))
         last = tie(last, tok)
         a_last, b_last = side_a(last), side_b(last)
         one, two = cats(
@@ -982,7 +1057,13 @@
             ],
             after=(tok, a_last, b_last),
         )
-        three, ab_last = tie(three, one), tie(a_last, one)
+        keep, send = kernel_call(
+            pack_inner_kernel, [core, mlp_in], [SM, VM], [sds((wr, fh), BF)] * 2, cost=1, after=(one,)
+        )
+        (three,) = kernel_call(
+            order_mlp_kernel, [core, keep, sib(send), mlp_out], [SM] + [VM] * 3, [sds((2 * wr, 6 * DH), BF)], cost=1
+        )
+        ab_last = tie(a_last, one)
         a1, b1, far_two, near_three, ab_last = side_a(one), side_b(one), far(two), near(three), side_b(ab_last)
         a1 = tie(a1, b1)
         two, last, three = cats(
@@ -1057,58 +1138,90 @@
     after = ()
 
     held = [resid_two, vec]
-    d_mlpout = grads(dmlpout_kernel, [hidden, g], [STAGE] * 2, 2 * D, hold=[*hold, *held, third])
+    d_mlpout = kernel_call(
+        dmlpout_kernel,
+        [offs, hidden, g],
+        [SM, VM, VM],
+        [sds((4 * wb, D), BF)] * 4 + [sds((8 * wb, D), BF)] + [sds((8 * wb, width), BF) for _, width in FAR_CUTS],
+        scratch=[pltpu.VMEM((D, D), BF)] * 2,
+        cost=3,
+        hold=[*hold, *held, third],
+    )
     if fast:
-        got_ab1 = side_a(d_mlpout[3])
+        got_ab1, got_z1 = side_a(d_mlpout[3]), far(d_mlpout[5])
     part, comb, *d_mlpin = mlp_part(last, g, slope, w_in, hidden, third, after=d_mlpout[:1], hold=[*hold, *held])
     if fast:
-        (on,) = merge([("pass", d_mlpout[2], got_ab1)], after=(part,))
+        (on,) = merge([("pass", d_mlpout[2], got_ab1)], after=(part, got_z1))
         comb = tie(comb, on)
-        got_b1, got_ab2, got_a1 = side_b(on), side_a(tie(d_mlpin[3], on)), side_a(tie(d_mlpout[1], on))
+        got_b1, got_a1, got_z2 = side_b(on), side_a(tie(d_mlpout[1], on)), far(tie(d_mlpout[6], on))
+        got_ab2, got_a2 = side_a(tie(d_mlpin[3], on)), side_a(tie(d_mlpin[1], on))
         after = (on,)
     recv = sib(comb)
-    output, gresid_two, gsecond, dvec_two, gmem, gmem_other, *d_cross = cross_back(
-        resid_two, comb, recv, part, after=after
-    )
+    output, gresid_two, gsecond, dvec_two, dkv, *d_cross = cross_back(resid_two, comb, recv, part, after=after)
     if fast:
-        on, kept1, on_far = merge(
-            [("pass", d_mlpin[2], got_ab2), ("half", d_mlpout[0], got_a1, got_b1)], after=(dvec_two,)
+        on, kept1, on_far, kept_z, on_z = merge(
+            [
+                ("pass", d_mlpin[2], got_ab2),
+                ("half", d_mlpout[0], got_a1, got_b1),
+                ("levels", d_mlpout[4], got_z1, got_z2),
+            ],
+            after=(dvec_two, got_a2),
         )
         gsecond = tie(gsecond, on)
-        got_b2, got_far1 = side_b(on), far(on_far)
-        got_a2, got_ab3 = side_a(tie(d_mlpin[1], on)), side_a(tie(d_cross[3], on))
+        got_b2, got_far1, got_near_z = side_b(on), far(on_far), near(on_z)
+        got_ab3, got_a3 = side_a(tie(d_cross[3], on)), side_a(tie(d_cross[1], on))
         after = (on,)
     recv = sib(gsecond)
     gresid_one, gfirst, gfirst_other, *d_self = self_back(gsecond, recv, gresid_two, after=after)
     if fast:
-        on, kept2, on_far, kept1, on_near = merge(
-            [("pass", d_cross[2], got_ab3), ("half", d_mlpin[0], got_a2, got_b2), ("near", kept1, got_far1)],
-            after=(gfirst,),
-        )
-        got_b3, got_a3, got_ab4 = side_b(on), side_a(tie(d_cross[1], on)), side_a(tie(d_self[3], on))
-        got_far2, got_near1 = far(on_far), near(on_near)
-        on, kept3, on_far, kept2, on_near, total1 = merge(
+        on, kept2, on_far, kept1, on_near, own_z, pass_z, on_z = merge(
+            [
+                ("pass", d_cross[2], got_ab3),
+                ("half", d_mlpin[0], got_a2, got_b2),
+                ("near", kept1, got_far1),
+                ("columns", kept_z, got_near_z),
+            ],
+            after=(gfirst, got_a3),
+        )
+        got_b3, got_ab4 = side_b(on), side_a(tie(d_self[3], on))
+        got_far2, got_near1, got_a_z = far(on_far), near(on_near), side_a(on_z)
+        after = (on,)
+    gmem, gmem_other = kernel_call(
+        memory_kernel, [dkv, w_ckv], [VM, VM], [sds((seqs * pad, D), BF)] * 2, cost=3, after=after
+    )
+    if fast:
+        on, kept3, on_far, kept2, on_near, total1, own_z, on_z = merge(
             [
                 ("pass", d_self[2], got_ab4),
                 ("half", d_cross[0], got_a3, got_b3),
                 ("near", kept2, got_far2),
                 ("last", kept1, got_near1),
-            ]
+                ("side", own_z, pass_z, got_a_z),
+            ],
+            after=(gmem,),
         )
         gfirst_other, gmem_other = tie(gfirst_other, on), tie(gmem_other, on)
         got_b4, got_a4 = side_b(on), side_a(tie(d_self[1], on))
-        got_far3, got_near2 = far(on_far), near(on_near)
+        got_far3, got_near2, got_b_z = far(on_far), near(on_near), side_b(on_z)
     recv, gmem_recv = sib(gfirst_other), sib(gmem_other)
-    grad_tokens, grad_memory = tokens_back(recv, gmem_recv)
+    grad_tokens, grad_memory, token = tokens_back(recv, gmem_recv)
     grad_memory = grad_memory.reshape(seqs, pad, D)[:, :mem_len]
 
     if fast:
-        kept4, *blocks, kept3, on_near, total2 = merge(
-            [("sum", d_self[0], got_a4, got_b4), ("near", kept3, got_far3), ("last", kept2, got_near2)], after=(grad_tokens,)
-        )
-        got_z4, got_near3 = [near(blocks[0]), far(blocks[1]), moves.opposite_z(blocks[2])], near(on_near)
-        (total3,) = merge([("last", kept3, got_near3)])
-        (total4,) = merge([("end", kept4, *got_z4)])
+        *blocks, total_z, total2 = merge(
+            [
+                ("send", d_self[0], got_a4, got_b4),
+                ("send_near", kept3, got_far3),
+                ("last", own_z, got_b_z),
+                ("last", kept2, got_near2),
+            ],
+            after=(token,),
+            beside=(0, 3),
+        )
+        got_far4, got_opp4, got_near = far(blocks[1]), moves.opposite_z(blocks[2]), near(blocks[0])
+        width = 4 * DH + 128
+        (total3,) = merge([("tail_near", kept3, got_far3, got_near[:, width:])])
+        (total4,) = merge([("tail", d_self[0], got_a4, got_b4, got_near[:, :width], got_far4, got_opp4)])
         total = [total1, total2, total3, total4]
 
         def own_rows(total):
@@ -1126,7 +1239,7 @@
                 cost=1,
             )
 
-        sum_mlpout = jnp.concatenate([total[0][:, :D], total[0][:, D:]], 0)
+        sum_mlpout = jnp.concatenate([total[0], total_z], 0)
         mine, got = own_rows(total[1])
         pair = (jnp.where(c == 0, mine, got), jnp.where(c == 0, got, mine))
         parts = [p.reshape(wr, ff // (2 * hr), 1, hr) for p in pair]
@@ -1156,8 +1269,10 @@
         vectors = jnp.sum(total[:, :, 4 * DH : 4 * DH + 6], 1).T
         own_gains, own_biases = vectors[:3], vectors[3:]
         grad_in = joined(placed(d_mlpin), 0, fh, ff // (2 * hr))
-        term = jnp.concatenate(d_mlpout, 0).astype(F32)
-        term = term.reshape(16, wb, 2, D).transpose(0, 2, 1, 3).reshape(moves.n // 2, 1, hr, D)
+        first_rows = jnp.concatenate(d_mlpout[:4], 0).reshape(16, 1, wb, D)
+        levels = jnp.concatenate([d_mlpout[4], jnp.concatenate(d_mlpout[5:], 1)], 0).reshape(4, 4, wb, D)
+        term = jnp.concatenate([first_rows, levels.transpose(1, 0, 2, 3).reshape(16, 1, wb, D)], 1).astype(F32)
+        term = term.reshape(moves.n // 2, 1, hr, D)
         both = jnp.concatenate([jnp.where(c == 0, term, 0.0), jnp.where(c == 1, term, 0.0)], 1)
         sum_mlpout = lax.psum_scatter(both.reshape(ff, D), AXES, scatter_dimension=0, tiled=True)
 

time: 239 us -> 234 us (0.979)
  local copies, waits for them, and re-layouts: 16.5 us -> 11.8 us
  starting transfers between devices: 56.4 us -> 59.9 us
  waiting for transfers between devices: 89.9 us -> 86.7 us
    unnamed x116 -> x122, local copies, waits for them, and re-layouts: 12.9 us -> 8.22 us
    ppermute x61 -> x66, starting transfers between devices: 56.4 us -> 59.9 us  [permute(): lax.ppermute(x, AXES, [(a, z * self.nf + 2 * yx + c) for a, (z, yx, c) in...]
    ppermute x61 -> x66, waiting for transfers between devices: 89.9 us -> 86.7 us  [permute(): lax.ppermute(x, AXES, [(a, z * self.nf + 2 * yx + c) for a, (z, yx, c) in...]
    pallas_call x26 -> x29, Pallas kernels: 73 us -> 71.5 us  [kernel_call(): pl.pallas_call(run, out_shape=list(outs), in_specs=[space(spec) for spec...]
  transfers between devices with their start and end apart: 61 -> 66, of which waited for: 29 -> 24; matrix products, arithmetic and copies ran while one was open for 3% -> 4% of each run, Pallas kernels for 29% -> 29%
where the time goes in v6:
time: 234 us
  waiting for transfers between devices  86.7 us (37%)
  Pallas kernels  71.6 us (31%)
  starting transfers between devices  59.9 us (26%)
  local copies, waits for them, and re-layouts  11.8 us (5%)
    ppermute x66, waiting for transfers between devices, permute(): lax.ppermute(x, AXES, [(a, z * self.nf + 2 * yx + c) for a, (z, yx, c) in...  86.7 us
    pallas_call x29, Pallas kernels, kernel_call(): pl.pallas_call(run, out_shape=list(outs), in_specs=[space(spec) for spec...  71.5 us
    ppermute x66, starting transfers between devices, permute(): lax.ppermute(x, AXES, [(a, z * self.nf + 2 * yx + c) for a, (z, yx, c) in...  59.9 us
    unnamed x122, local copies, waits for them, and re-layouts  8.22 us
  transfers between devices with their start and end apart: 66, of which 24 were waited for; matrix products, arithmetic and copies ran while one was open for 4% of the time, Pallas kernels for 29%

profile of v6, /device:TPU:0, one launch (start us, length us, event | category | flops | bytes accessed | tf_op | source)
XLA Modules:
  0.0 233.7 jit_solution(14415304745140218219)
XLA Ops:
  1.7 1.9 shard_map.220
  4.1 1.5 copy.54.refs_5_
  5.9 3.7 %collective-permute-start.5 = (bf16[48,1664]{1,0:T(8,128)(2,1)S(1)}, bf16[48,1664]{1,0:T(8,128)(2,1)S(1)}, u32[]{:S(2)}, u32[]{:S(2)}) collective-permute-start(bf16[48,1664]{1,0:T(8,128)(2,1)S(1)} %get-tuple-element.120.refs_7_.refs_0_), channel_id=1, source_target_pairs={{0,16},{1,17},{2,18},{3,19},{4,20},{5,21},{6,22},{7,23},{8,24},{9,... | collective-permute-start | bytes 479240 | tf_op jit(solution)/shard_map/ppermute | solution.py:825
  9.6 1.3 collective-permute-start.6
  11.2 1.5 copy.55.refs_6_
  12.8 1.8 shard_map.222
  14.6 1.6 collective-permute-start.8
  16.2 1.5 collective-permute-start.9
  17.8 3.7 %collective-permute-done.5.refs_2_ = bf16[48,1664]{1,0:T(8,128)(2,1)S(1)} collective-permute-done((bf16[48,1664]{1,0:T(8,128)(2,1)S(1)}, bf16[48,1664]{1,0:T(8,128)(2,1)S(1)}, u32[]{:S(2)}, u32[]{:S(2)}) %collective-permute-start.5) | collective-permute-done | bytes 159776 | tf_op jit(solution)/shard_map/ppermute | solution.py:825
  21.5 4.2 %collective-permute-done.4.refs_1_.refs_5_ = bf16[48,3200]{1,0:T(8,128)(2,1)S(1)} collective-permute-done((bf16[48,3200]{1,0:T(8,128)(2,1)S(1)}, bf16[48,3200]{1,0:T(8,128)(2,1)S(1)}, u32[]{:S(2)}, u32[]{:S(2)}) %collective-permute-start.4) | collective-permute-done | bytes 307232 | tf_op jit(solution)/shard_map/ppermute | solution.py:825
  26.7 1.6 collective-permute-start.10
  28.2 1.5 collective-permute-start.11
  29.8 1.6 collective-permute-start.14
  31.4 2.5 %collective-permute-start.17 = (bf16[48,2304]{1,0:T(8,128)(2,1)S(1)}, bf16[48,2304]{1,0:T(8,128)(2,1)S(1)}, u32[]{:S(2)}, u32[]{:S(2)}) collective-permute-start(bf16[48,2304]{1,0:T(8,128)(2,1)S(1)} %shard_map.229.refs_6_), channel_id=1, source_target_pairs={{0,8},{1,9},{2,10},{3,11},{4,12},{5,13},{6,14},{7,15},{8,0},{9,1},... | collective-permute-start | bytes 663560 | tf_op jit(solution)/shard_map/ppermute | solution.py:825
  34.5 8.6 %collective-permute-done.10.refs_0_ = bf16[192,1664]{1,0:T(8,128)(2,1)S(1)} collective-permute-done((bf16[192,1664]{1,0:T(8,128)(2,1)S(1)}, bf16[192,1664]{1,0:T(8,128)(2,1)S(1)}, u32[]{:S(2)}, u32[]{:S(2)}) %collective-permute-start.10) | collective-permute-done | bytes 639008 | tf_op jit(solution)/shard_map/ppermute | solution.py:825
  43.5 2.1 collective-permute-start.12
  47.5 1.6 collective-permute-start.18
  49.1 2.5 %collective-permute-start.19 = (bf16[192,768]{1,0:T(8,128)(2,1)S(1)}, bf16[192,768]{1,0:T(8,128)(2,1)S(1)}, u32[]{:S(2)}, u32[]{:S(2)}) collective-permute-start(bf16[192,768]{1,0:T(8,128)(2,1)S(1)} %get-tuple-element.130.refs_4_.refs_6_.refs_8_), channel_id=1, source_target_pairs={{0,8},{1,9},{2,10},{3,11},{4,12},{5,13},{6,14},{7,15},{8,0},{9,1},... | collective-permute-start | bytes 884744 | tf_op jit(solution)/shard_map/ppermute | solution.py:825
  51.5 8.2 %collective-permute-done.12.refs_4_.refs_2_.refs_6_ = bf16[192,1664]{1,0:T(8,128)(2,1)S(1)} collective-permute-done((bf16[192,1664]{1,0:T(8,128)(2,1)S(1)}, bf16[192,1664]{1,0:T(8,128)(2,1)S(1)}, u32[]{:S(2)}, u32[]{:S(2)}) %collective-permute-start.12) | collective-permute-done | bytes 639008 | tf_op jit(solution)/shard_map/ppermute | solution.py:825
  60.5 1.8 collective-permute-done.20.refs_0_
  62.3 4.3 %collective-permute-done.21.refs_1_.refs_3_ = bf16[192,1536]{1,0:T(8,128)(2,1)S(1)} collective-permute-done((bf16[192,1536]{1,0:T(8,128)(2,1)S(1)}, bf16[192,1536]{1,0:T(8,128)(2,1)S(1)}, u32[]{:S(2)}, u32[]{:S(2)}) %collective-permute-start.21) | collective-permute-done | bytes 589856 | tf_op jit(solution)/shard_map/ppermute | solution.py:825
  66.6 2.9 %collective-permute-done.18.refs_1_.refs_3_ = bf16[96,2304]{1,0:T(8,128)(2,1)S(1)} collective-permute-done((bf16[96,2304]{1,0:T(8,128)(2,1)S(1)}, bf16[96,2304]{1,0:T(8,128)(2,1)S(1)}, u32[]{:S(2)}, u32[]{:S(2)}) %collective-permute-start.18) | collective-permute-done | bytes 442400 | tf_op jit(solution)/shard_map/ppermute | solution.py:825
  72.7 7.4 %shard_map.234 = (bf16[512,768]{1,0:T(8,128)(2,1)S(1)}, bf16[512,1152]{1,0:T(8,128)(2,1)S(1)}, bf16[8,64,384]{2,1,0:T(8,128)(2,1)S(1)}, bf16[512,1152]{1,0:T(8,1...) custom-call(s32[8]{0:T(128)S(1)} %pad_add_fusion.1.refs_0_, s32[1]{0:T(128)} %bitcast.2.refs_0_.refs_1_.refs_6_, ...), custom_call_target="tpu_custom_call" | custom-call | flops 41999998976 | tf_op jit(solution)/shard_map/pallas_call | solution.py:97
  81.1 10.5 %collective-permute-done.25.refs_4_.refs_6_ = bf16[384,512]{1,0:T(8,128)(2,1)S(1)} collective-permute-done((bf16[384,512]{1,0:T(8,128)(2,1)S(1)}, bf16[384,512]{1,0:T(8,128)(2,1)S(1)}, u32[]{:S(2)}, u32[]{:S(2)}) %collective-permute-start.25) | collective-permute-done | bytes 393248 | tf_op jit(solution)/shard_map/ppermute | solution.py:825
  96.3 10.3 %shard_map.241 = (bf16[1920,768]{1,0:T(8,128)(2,1)S(1)}, bf16[768,768]{1,0:T(8,128)(2,1)S(1)}, bf16[768,384]{1,0:T(8,128)(2,1)S(1)}, f32[512,768]{1,0:T(8,128)S(...) custom-call(s32[2,16]{1,0:T(2,128)S(1)} %pad_add_fusion.refs_0_.refs, ...), custom_call_target="tpu_custom_call" | custom-call | flops 83999997952 | tf_op jit(solution)/shard_map/pallas_call | solution.py:97
  107.1 2.2 collective-permute-done.30.refs_3_
  112.2 3.3 %shard_map.245 = (f32[512,768]{1,0:T(8,128)S(1)}, bf16[512,768]{1,0:T(8,128)(2,1)S(1)}, bf16[512,1536]{1,0:T(8,128)(2,1)S(1)}, bf16[512,1536]{1,0:T(8,128)(2,1)S(1)}) custom-call(f32[512,768]{1,0:T(8,128)S(1)} %get-tuple-element.138.refs_0_.refs_3_, bf16[512,1152]{1,0:T(8,128)(2,1)S(1)} %shard_map.243.refs_1_.refs_14_, ...), custom_call_target="tpu_custom_call" | custom-call | flops 35000000512 | tf_op jit(solution)/shard_map/pallas_call | solution.py:97
  115.5 2.1 shard_map.247
  119.5 6.8 %shard_map.248 = (bf16[256,768]{1,0:T(8,128)(2,1)S(1)}, bf16[768,768]{1,0:T(8,128)(2,1)S(1)}, bf16[192,1536]{1,0:T(8,128)(2,1)S(1)}, bf16[192,1536]{1,0:T(8,128)...) custom-call(s32[2,16]{1,0:T(2,128)S(1)} %pad_add_fusion.refs_0_.refs_2_, ...), custom_call_target="tpu_custom_call" | custom-call | flops 76999999488 | tf_op jit(solution)/shard_map/pallas_call | solution.py:97
  126.3 3.6 %collective-permute-done.35.refs_3_.refs_6_ = bf16[384,256]{1,0:T(8,128)(2,1)S(1)} collective-permute-done((bf16[384,256]{1,0:T(8,128)(2,1)S(1)}, bf16[384,256]{1,0:T(8,128)(2,1)S(1)}, u32[]{:S(2)}, u32[]{:S(2)}) %collective-permute-start.35) | collective-permute-done | bytes 196640 | tf_op jit(solution)/shard_map/ppermute | solution.py:825
  134.2 14.3 %shard_map.251 = (bf16[256,768]{1,0:T(8,128)(2,1)}, f32[512,768]{1,0:T(8,128)S(1)}, bf16[512,768]{1,0:T(8,128)(2,1)S(1)}, f32[8,768]{1,0:T(8,128)S(1)}, bf16[192...) custom-call(s32[2,16]{1,0:T(2,128)S(1)} %pad_add_fusion.refs_0_.refs, ...), custom_call_target="tpu_custom_call" | custom-call | flops 98000003072 | tf_op jit(solution)/shard_map/pallas_call | solution.py:97
  148.5 3.5 %collective-permute-done.40.refs_7_ = bf16[384,512]{1,0:T(8,128)(2,1)S(1)} collective-permute-done((bf16[384,512]{1,0:T(8,128)(2,1)S(1)}, bf16[384,512]{1,0:T(8,128)(2,1)S(1)}, u32[]{:S(2)}, u32[]{:S(2)}) %collective-permute-start.40) | collective-permute-done | bytes 393248 | tf_op jit(solution)/shard_map/ppermute | solution.py:825
  156.1 2.5 %collective-permute-start.45 = (bf16[96,768]{1,0:T(8,128)(2,1)S(1)}, bf16[96,768]{1,0:T(8,128)(2,1)S(1)}, u32[]{:S(2)}, u32[]{:S(2)}) collective-permute-start(bf16[96,768]{1,0:T(8,128)(2,1)S(1)} %get-tuple-element.182), channel_id=1, source_target_pairs={{0,16},{1,17},{2,18},{3,19},{4,20},{5,21},{6,22},{7,23},{8,24},{9,... | collective-permute-start | bytes 442376 | tf_op jit(solution)/shard_map/ppermute | solution.py:825
  158.7 11.5 %shard_map.258 = (f32[256,768]{1,0:T(8,128)S(1)}, bf16[256,768]{1,0:T(8,128)(2,1)S(1)}, bf16[256,768]{1,0:T(8,128)(2,1)S(1)}, bf16[192,1664]{1,0:T(8,128)(2,1)S(...) custom-call(s32[2,16]{1,0:T(2,128)S(1)} %pad_add_fusion.refs_0_.refs_2_, ...), custom_call_target="tpu_custom_call" | custom-call | flops 76999999488 | tf_op jit(solution)/shard_map/pallas_call | solution.py:97
  170.2 4.4 %collective-permute-done.43.refs_1_ = bf16[192,1536]{1,0:T(8,128)(2,1)S(1)} collective-permute-done((bf16[192,1536]{1,0:T(8,128)(2,1)S(1)}, bf16[192,1536]{1,0:T(8,128)(2,1)S(1)}, u32[]{:S(2)}, u32[]{:S(2)}) %collective-permute-start.43) | collective-permute-done | bytes 589856 | tf_op jit(solution)/shard_map/ppermute | solution.py:825
  178.2 2.5 %collective-permute-start.51 = (bf16[48,768]{1,0:T(8,128)(2,1)S(1)}, bf16[48,768]{1,0:T(8,128)(2,1)S(1)}, u32[]{:S(2)}, u32[]{:S(2)}) collective-permute-start(bf16[48,768]{1,0:T(8,128)(2,1)S(1)} %get-tuple-element.191), channel_id=1, source_target_pairs={{0,8},{1,9},{2,10},{3,11},{4,12},{5,13},{6,14},{7,15},{8,0},{9,1},... | collective-permute-start | bytes 221192 | tf_op jit(solution)/shard_map/ppermute | solution.py:825
  180.7 2.5 %shard_map.263 = (bf16[960,768]{1,0:T(8,128)(2,1)S(1)}, bf16[960,768]{1,0:T(8,128)(2,1)S(1)}) custom-call(bf16[1920,768]{1,0:T(8,128)(2,1)S(1)} %get-tuple-element.195.refs_0_, bf16[768,768]{1,0:T(8,128)(2,1)S(1)} %get-tuple-element.145.refs_11_.refs_9_.refs_20_.refs_1_, bf16[192,1536]{1,0:T(8,128)(2,1)S(1)} %get-tuple-element.186.refs_1_.refs_2_), custom_call_target="tpu_custom_call" | custom-call | flops 20999999488 | tf_op jit(solution)/shard_map/pallas_call | solution.py:97
  183.2 2.4 %collective-permute-done.51.refs_8_ = bf16[48,768]{1,0:T(8,128)(2,1)S(1)} collective-permute-done((bf16[48,768]{1,0:T(8,128)(2,1)S(1)}, bf16[48,768]{1,0:T(8,128)(2,1)S(1)}, u32[]{:S(2)}, u32[]{:S(2)}) %collective-permute-start.51) | collective-permute-done | bytes 73760 | tf_op jit(solution)/shard_map/ppermute | solution.py:825
  185.6 7.6 %collective-permute-done.52.refs_11_ = bf16[96,768]{1,0:T(8,128)(2,1)S(1)} collective-permute-done((bf16[96,768]{1,0:T(8,128)(2,1)S(1)}, bf16[96,768]{1,0:T(8,128)(2,1)S(1)}, u32[]{:S(2)}, u32[]{:S(2)}) %collective-permute-start.52) | collective-permute-done | bytes 147488 | tf_op jit(solution)/shard_map/ppermute | solution.py:825
  197.3 1.4 collective-permute-done.53.refs_3_
  200.8 1.4 copy-done.24
  202.2 3.5 %shard_map.267 = (bf16[256,768]{1,0:T(8,128)(2,1)}, bf16[960,768]{1,0:T(8,128)(2,1)S(1)}, f32[8,128]{1,0:T(8,128)S(1)}) custom-call(f32[8,768]{1,0:T(8,128)S(1)} %get-tuple-element.133.refs_7_.refs_3_.refs_12_.refs_23_.refs_2_.refs_0_, bf16[256,768]{1,0:T(8,128)(2,1)S(1)} %bitcast.13, bf16[256,768]{1,0:T(8,128)(2,1)S(1)} %copy-done.32, ...), custom_call_target="tpu_custom_call" | custom-call | flops 28000000000 | tf_op jit(solution)/shard_map/pallas_call | solution.py:97
  205.7 7.5 %collective-permute-done.58.refs_6_ = bf16[48,768]{1,0:T(8,128)(2,1)S(1)} collective-permute-done((bf16[48,768]{1,0:T(8,128)(2,1)S(1)}, bf16[48,768]{1,0:T(8,128)(2,1)S(1)}, u32[]{:S(2)}, u32[]{:S(2)}) %collective-permute-start.58) | collective-permute-done | bytes 73760 | tf_op jit(solution)/shard_map/ppermute | solution.py:825
  214.6 2.5 %collective-permute-start.61 = (bf16[48,1664]{1,0:T(8,128)(2,1)S(1)}, bf16[48,1664]{1,0:T(8,128)(2,1)S(1)}, u32[]{:S(2)}, u32[]{:S(2)}) collective-permute-start(bf16[48,1664]{1,0:T(8,128)(2,1)S(1)} %get-tuple-element.212), channel_id=1, source_target_pairs={{0,16},{1,17},{2,18},{3,19},{4,20},{5,21},{6,22},{7,23},{8,24},{9,... | collective-permute-start | bytes 479240 | tf_op jit(solution)/shard_map/ppermute | solution.py:825
  217.1 1.8 collective-permute-start.62
  219.0 1.6 copy.58
  224.2 3.4 %collective-permute-done.60 = bf16[48,3200]{1,0:T(8,128)(2,1)S(1)} collective-permute-done((bf16[48,3200]{1,0:T(8,128)(2,1)S(1)}, bf16[48,3200]{1,0:T(8,128)(2,1)S(1)}, u32[]{:S(2)}, u32[]{:S(2)}) %collective-permute-start.60) | collective-permute-done | bytes 307232 | tf_op jit(solution)/shard_map/ppermute | solution.py:825
  227.9 3.5 %collective-permute-done.62.refs_5_ = bf16[48,1664]{1,0:T(8,128)(2,1)S(1)} collective-permute-done((bf16[48,1664]{1,0:T(8,128)(2,1)S(1)}, bf16[48,1664]{1,0:T(8,128)(2,1)S(1)}, u32[]{:S(2)}, u32[]{:S(2)}) %collective-permute-start.62) | collective-permute-done | bytes 159776 | tf_op jit(solution)/shard_map/ppermute | solution.py:825
  (280 shorter events, 45.8 us)
Async XLA Ops:
  1.2 10.0 %collective-permute-start.7 = (bf16[4,228,768]{2,0,1:T(4,128)(2,1)}, bf16[4,228,768]{2,0,1:T(4,128)(2,1)}, u32[]{:S(2)}, u32[]{:S(2)}) collective-permute-start(bf16[4,228,768]{2,0,1:T(4,128)(2,1)} %param.14), channel_id=1, source_target_pairs={{0,1},{1,0},{2,3},{3,2},{4,5},{5,4},{6,7},{7,6},{8,9},{9,8},{10,11... | collective-permute-start | bytes 4202504 | tf_op jit(solution)/shard_map/ppermute | solution.py:825
  5.9 15.6 %collective-permute-start.5 = (bf16[48,1664]{1,0:T(8,128)(2,1)S(1)}, bf16[48,1664]{1,0:T(8,128)(2,1)S(1)}, u32[]{:S(2)}, u32[]{:S(2)}) collective-permute-start(bf16[48,1664]{1,0:T(8,128)(2,1)S(1)} %get-tuple-element.120.refs_7_.refs_0_), channel_id=1, source_target_pairs={{0,16},{1,17},{2,18},{3,19},{4,20},{5,21},{6,22},{7,23},{8,24},{9,... | collective-permute-start | bytes 479240 | tf_op jit(solution)/shard_map/ppermute | solution.py:825
  9.6 11.9 %collective-permute-start.6 = (bf16[48,1664]{1,0:T(8,128)(2,1)S(1)}, bf16[48,1664]{1,0:T(8,128)(2,1)S(1)}, u32[]{:S(2)}, u32[]{:S(2)}) collective-permute-start(bf16[48,1664]{1,0:T(8,128)(2,1)S(1)} %get-tuple-element.120.refs_7_.refs_0_), channel_id=1, source_target_pairs={{0,24},{1,25},{2,26},{3,27},{4,28},{5,29},{6,30},{7,31},{8,16},{9,... | collective-permute-start | bytes 479240 | tf_op jit(solution)/shard_map/ppermute | solution.py:825
  11.0 14.7 %collective-permute-start.4 = (bf16[48,3200]{1,0:T(8,128)(2,1)S(1)}, bf16[48,3200]{1,0:T(8,128)(2,1)S(1)}, u32[]{:S(2)}, u32[]{:S(2)}) collective-permute-start(bf16[48,3200]{1,0:T(8,128)(2,1)S(1)} %get-tuple-element.121.refs_8_.refs_4_), channel_id=1, source_target_pairs={{0,8},{1,9},{2,10},{3,11},{4,12},{5,13},{6,14},{7,15},{8,0},{9,1},... | collective-permute-start | bytes 921608 | tf_op jit(solution)/shard_map/ppermute | solution.py:825
  14.6 11.1 %collective-permute-start.8 = (bf16[48,768]{1,0:T(8,128)(2,1)S(1)}, bf16[48,768]{1,0:T(8,128)(2,1)S(1)}, u32[]{:S(2)}, u32[]{:S(2)}) collective-permute-start(bf16[48,768]{1,0:T(8,128)(2,1)S(1)} %shard_map.223.refs_2_), channel_id=1, source_target_pairs={{0,2},{1,5},{2,0},{3,7},{4,6},{5,1},{6,4},{7,3},{8,10},{9,13},{10,... | collective-permute-start | bytes 221192 | tf_op jit(solution)/shard_map/ppermute | solution.py:825
  26.7 16.5 %collective-permute-start.10 = (bf16[192,1664]{1,0:T(8,128)(2,1)S(1)}, bf16[192,1664]{1,0:T(8,128)(2,1)S(1)}, u32[]{:S(2)}, u32[]{:S(2)}) collective-permute-start(bf16[192,1664]{1,0:T(8,128)(2,1)S(1)} %get-tuple-element.124.refs_1_.refs_2_.refs_3_), channel_id=1, source_target_pairs={{0,2},{1,5},{2,0},{3,7},{4,6},{5,1},{6,4},{7,3},{8,10},{9,13},{10,... | collective-permute-start | bytes 1916936 | tf_op jit(solution)/shard_map/ppermute | solution.py:825
  28.2 15.2 %collective-permute-start.11 = (bf16[192,1664]{1,0:T(8,128)(2,1)S(1)}, bf16[192,1664]{1,0:T(8,128)(2,1)S(1)}, u32[]{:S(2)}, u32[]{:S(2)}) collective-permute-start(bf16[192,1664]{1,0:T(8,128)(2,1)S(1)} %get-tuple-element.124.refs_1_.refs_2_.refs_3_), channel_id=1, source_target_pairs={{0,4},{1,3},{2,6},{3,1},{4,0},{5,7},{6,2},{7,5},{8,12},{9,11},{10,... | collective-permute-start | bytes 1916936 | tf_op jit(solution)/shard_map/ppermute | solution.py:825
  29.8 16.1 %collective-permute-start.14 = (bf16[96,1536]{1,0:T(8,128)(2,1)S(1)}, bf16[96,1536]{1,0:T(8,128)(2,1)S(1)}, u32[]{:S(2)}, u32[]{:S(2)}) collective-permute-start(bf16[96,1536]{1,0:T(8,128)(2,1)S(1)} %get-tuple-element.126.refs_0_), channel_id=1, source_target_pairs={{0,16},{1,17},{2,18},{3,19},{4,20},{5,21},{6,22},{7,23},{8,24},{9,... | collective-permute-start | bytes 884744 | tf_op jit(solution)/shard_map/ppermute | solution.py:825
  31.4 14.2 %collective-permute-start.17 = (bf16[48,2304]{1,0:T(8,128)(2,1)S(1)}, bf16[48,2304]{1,0:T(8,128)(2,1)S(1)}, u32[]{:S(2)}, u32[]{:S(2)}) collective-permute-start(bf16[48,2304]{1,0:T(8,128)(2,1)S(1)} %shard_map.229.refs_6_), channel_id=1, source_target_pairs={{0,8},{1,9},{2,10},{3,11},{4,12},{5,13},{6,14},{7,15},{8,0},{9,1},... | collective-permute-start | bytes 663560 | tf_op jit(solution)/shard_map/ppermute | solution.py:825
  33.9 11.6 %collective-permute-start.15 = (bf16[48,768]{1,0:T(8,128)(2,1)S(1)}, bf16[48,768]{1,0:T(8,128)(2,1)S(1)}, u32[]{:S(2)}, u32[]{:S(2)}) collective-permute-start(bf16[48,768]{1,0:T(8,128)(2,1)S(1)} %shard_map.227), channel_id=1, source_target_pairs={{0,4},{1,3},{2,6},{3,1},{4,0},{5,7},{6,2},{7,5},{8,12},{9,11},{10,... | collective-permute-start | bytes 221192 | tf_op jit(solution)/shard_map/ppermute | solution.py:825
  43.5 16.3 %collective-permute-start.12 = (bf16[192,1664]{1,0:T(8,128)(2,1)S(1)}, bf16[192,1664]{1,0:T(8,128)(2,1)S(1)}, u32[]{:S(2)}, u32[]{:S(2)}) collective-permute-start(bf16[192,1664]{1,0:T(8,128)(2,1)S(1)} %shard_map.225.refs_2_.refs_8_.refs_4_), channel_id=1, source_target_pairs={{0,4},{1,3},{2,6},{3,1},{4,0},{5,7},{6,2},{7,5},{8,12},{9,11},{10,... | collective-permute-start | bytes 1916936 | tf_op jit(solution)/shard_map/ppermute | solution.py:825
  45.9 16.3 %collective-permute-start.20 = (bf16[192,1536]{1,0:T(8,128)(2,1)S(1)}, bf16[192,1536]{1,0:T(8,128)(2,1)S(1)}, u32[]{:S(2)}, u32[]{:S(2)}) collective-permute-start(bf16[192,1536]{1,0:T(8,128)(2,1)S(1)} %get-tuple-element.131.refs_1_), channel_id=1, source_target_pairs={{0,2},{1,5},{2,0},{3,7},{4,6},{5,1},{6,4},{7,3},{8,10},{9,13},{10,... | collective-permute-start | bytes 1769480 | tf_op jit(solution)/shard_map/ppermute | solution.py:825
  47.2 19.4 %collective-permute-start.21 = (bf16[192,1536]{1,0:T(8,128)(2,1)S(1)}, bf16[192,1536]{1,0:T(8,128)(2,1)S(1)}, u32[]{:S(2)}, u32[]{:S(2)}) collective-permute-start(bf16[192,1536]{1,0:T(8,128)(2,1)S(1)} %get-tuple-element.131.refs_1_), channel_id=1, source_target_pairs={{0,4},{1,3},{2,6},{3,1},{4,0},{5,7},{6,2},{7,5},{8,12},{9,11},{10,... | collective-permute-start | bytes 1769480 | tf_op jit(solution)/shard_map/ppermute | solution.py:825
  47.5 22.0 %collective-permute-start.18 = (bf16[96,2304]{1,0:T(8,128)(2,1)S(1)}, bf16[96,2304]{1,0:T(8,128)(2,1)S(1)}, u32[]{:S(2)}, u32[]{:S(2)}) collective-permute-start(bf16[96,2304]{1,0:T(8,128)(2,1)S(1)} %get-tuple-element.129.refs_0_.refs_2_), channel_id=1, source_target_pairs={{0,16},{1,17},{2,18},{3,19},{4,20},{5,21},{6,22},{7,23},{8,24},{9,... | collective-permute-start | bytes 1327112 | tf_op jit(solution)/shard_map/ppermute | solution.py:825
  49.1 17.5 %collective-permute-start.19 = (bf16[192,768]{1,0:T(8,128)(2,1)S(1)}, bf16[192,768]{1,0:T(8,128)(2,1)S(1)}, u32[]{:S(2)}, u32[]{:S(2)}) collective-permute-start(bf16[192,768]{1,0:T(8,128)(2,1)S(1)} %get-tuple-element.130.refs_4_.refs_6_.refs_8_), channel_id=1, source_target_pairs={{0,8},{1,9},{2,10},{3,11},{4,12},{5,13},{6,14},{7,15},{8,0},{9,1},... | collective-permute-start | bytes 884744 | tf_op jit(solution)/shard_map/ppermute | solution.py:825
  69.7 22.0 %collective-permute-start.23 = (bf16[192,1536]{1,0:T(8,128)(2,1)S(1)}, bf16[192,1536]{1,0:T(8,128)(2,1)S(1)}, u32[]{:S(2)}, u32[]{:S(2)}) collective-permute-start(bf16[192,1536]{1,0:T(8,128)(2,1)S(1)} %shard_map.233.refs_10_.refs_1_), channel_id=1, source_target_pairs={{0,2},{1,5},{2,0},{3,7},{4,6},{5,1},{6,4},{7,3},{8,10},{9,13},{10,... | collective-permute-start | bytes 1769480 | tf_op jit(solution)/shard_map/ppermute | solution.py:825
  70.7 21.0 %collective-permute-start.24 = (bf16[192,1536]{1,0:T(8,128)(2,1)S(1)}, bf16[192,1536]{1,0:T(8,128)(2,1)S(1)}, u32[]{:S(2)}, u32[]{:S(2)}) collective-permute-start(bf16[192,1536]{1,0:T(8,128)(2,1)S(1)} %shard_map.233.refs_10_.refs_1_), channel_id=1, source_target_pairs={{0,4},{1,3},{2,6},{3,1},{4,0},{5,7},{6,2},{7,5},{8,12},{9,11},{10,... | collective-permute-start | bytes 1769480 | tf_op jit(solution)/shard_map/ppermute | solution.py:825
  71.7 20.0 %collective-permute-start.22 = (bf16[192,1536]{1,0:T(8,128)(2,1)S(1)}, bf16[192,1536]{1,0:T(8,128)(2,1)S(1)}, u32[]{:S(2)}, u32[]{:S(2)}) collective-permute-start(bf16[192,1536]{1,0:T(8,128)(2,1)S(1)} %shard_map.235.refs_2_), channel_id=1, source_target_pairs={{0,4},{1,3},{2,6},{3,1},{4,0},{5,7},{6,2},{7,5},{8,12},{9,11},{10,... | collective-permute-start | bytes 1769480 | tf_op jit(solution)/shard_map/ppermute | solution.py:825
  72.7 18.9 %collective-permute-start.25 = (bf16[384,512]{1,0:T(8,128)(2,1)S(1)}, bf16[384,512]{1,0:T(8,128)(2,1)S(1)}, u32[]{:S(2)}, u32[]{:S(2)}) collective-permute-start(bf16[384,512]{1,0:T(8,128)(2,1)S(1)} %shard_map.236), channel_id=1, source_target_pairs={{0,16},{1,17},{2,18},{3,19},{4,20},{5,21},{6,22},{7,23},{8,24},{9,... | collective-permute-start | bytes 1179656 | tf_op jit(solution)/shard_map/ppermute | solution.py:825
  93.6 15.7 %collective-permute-start.28 = (bf16[192,1536]{1,0:T(8,128)(2,1)S(1)}, bf16[192,1536]{1,0:T(8,128)(2,1)S(1)}, u32[]{:S(2)}, u32[]{:S(2)}) collective-permute-start(bf16[192,1536]{1,0:T(8,128)(2,1)S(1)} %shard_map.237.refs_1_.refs_2_), channel_id=1, source_target_pairs={{0,4},{1,3},{2,6},{3,1},{4,0},{5,7},{6,2},{7,5},{8,12},{9,11},{10,... | collective-permute-start | bytes 1769480 | tf_op jit(solution)/shard_map/ppermute | solution.py:825
  94.4 12.8 %collective-permute-start.29 = (bf16[192,768]{1,0:T(8,128)(2,1)S(1)}, bf16[192,768]{1,0:T(8,128)(2,1)S(1)}, u32[]{:S(2)}, u32[]{:S(2)}) collective-permute-start(bf16[192,768]{1,0:T(8,128)(2,1)S(1)} %shard_map.238.refs_1_), channel_id=1, source_target_pairs={{0,2},{1,5},{2,0},{3,7},{4,6},{5,1},{6,4},{7,3},{8,10},{9,13},{10,... | collective-permute-start | bytes 884744 | tf_op jit(solution)/shard_map/ppermute | solution.py:825
  95.3 14.0 %collective-permute-start.30 = (bf16[192,768]{1,0:T(8,128)(2,1)S(1)}, bf16[192,768]{1,0:T(8,128)(2,1)S(1)}, u32[]{:S(2)}, u32[]{:S(2)}) collective-permute-start(bf16[192,768]{1,0:T(8,128)(2,1)S(1)} %shard_map.238.refs_1_), channel_id=1, source_target_pairs={{0,4},{1,3},{2,6},{3,1},{4,0},{5,7},{6,2},{7,5},{8,12},{9,11},{10,... | collective-permute-start | bytes 884744 | tf_op jit(solution)/shard_map/ppermute | solution.py:825
  96.3 10.8 %collective-permute-start.31 = (bf16[384,256]{1,0:T(8,128)(2,1)S(1)}, bf16[384,256]{1,0:T(8,128)(2,1)S(1)}, u32[]{:S(2)}, u32[]{:S(2)}) collective-permute-start(bf16[384,256]{1,0:T(8,128)(2,1)S(1)} %shard_map.242), channel_id=1, source_target_pairs={{0,16},{1,17},{2,18},{3,19},{4,20},{5,21},{6,22},{7,23},{8,24},{9,... | collective-permute-start | bytes 589832 | tf_op jit(solution)/shard_map/ppermute | solution.py:825
  109.4 10.1 %collective-permute-start.33 = (bf16[192,768]{1,0:T(8,128)(2,1)S(1)}, bf16[192,768]{1,0:T(8,128)(2,1)S(1)}, u32[]{:S(2)}, u32[]{:S(2)}) collective-permute-start(bf16[192,768]{1,0:T(8,128)(2,1)S(1)} %shard_map.246), channel_id=1, source_target_pairs={{0,4},{1,3},{2,6},{3,1},{4,0},{5,7},{6,2},{7,5},{8,12},{9,11},{10,... | collective-permute-start | bytes 884744 | tf_op jit(solution)/shard_map/ppermute | solution.py:825
  117.7 12.3 %collective-permute-start.34 = (bf16[192,768]{1,0:T(8,128)(2,1)S(1)}, bf16[192,768]{1,0:T(8,128)(2,1)S(1)}, u32[]{:S(2)}, u32[]{:S(2)}) collective-permute-start(bf16[192,768]{1,0:T(8,128)(2,1)S(1)} %get-tuple-element.156), channel_id=1, source_target_pairs={{0,2},{1,5},{2,0},{3,7},{4,6},{5,1},{6,4},{7,3},{8,10},{9,13},{10,... | collective-permute-start | bytes 884744 | tf_op jit(solution)/shard_map/ppermute | solution.py:825
  118.9 11.0 %collective-permute-start.35 = (bf16[384,256]{1,0:T(8,128)(2,1)S(1)}, bf16[384,256]{1,0:T(8,128)(2,1)S(1)}, u32[]{:S(2)}, u32[]{:S(2)}) collective-permute-start(bf16[384,256]{1,0:T(8,128)(2,1)S(1)} %get-tuple-element.158), channel_id=1, source_target_pairs={{0,16},{1,17},{2,18},{3,19},{4,20},{5,21},{6,22},{7,23},{8,24},{9,... | collective-permute-start | bytes 589832 | tf_op jit(solution)/shard_map/ppermute | solution.py:825
  130.1 18.4 %collective-permute-start.39 = (bf16[192,768]{1,0:T(8,128)(2,1)S(1)}, bf16[192,768]{1,0:T(8,128)(2,1)S(1)}, u32[]{:S(2)}, u32[]{:S(2)}) collective-permute-start(bf16[192,768]{1,0:T(8,128)(2,1)S(1)} %shard_map.249.refs_1_.refs_18_), channel_id=1, source_target_pairs={{0,4},{1,3},{2,6},{3,1},{4,0},{5,7},{6,2},{7,5},{8,12},{9,11},{10,... | collective-permute-start | bytes 884744 | tf_op jit(solution)/shard_map/ppermute | solution.py:825
  131.2 20.8 %collective-permute-start.41 = (bf16[192,1536]{1,0:T(8,128)(2,1)S(1)}, bf16[192,1536]{1,0:T(8,128)(2,1)S(1)}, u32[]{:S(2)}, u32[]{:S(2)}) collective-permute-start(bf16[192,1536]{1,0:T(8,128)(2,1)S(1)} %shard_map.255), channel_id=1, source_target_pairs={{0,2},{1,5},{2,0},{3,7},{4,6},{5,1},{6,4},{7,3},{8,10},{9,13},{10,... | collective-permute-start | bytes 1769480 | tf_op jit(solution)/shard_map/ppermute | solution.py:825
  132.2 19.8 %collective-permute-start.40 = (bf16[384,512]{1,0:T(8,128)(2,1)S(1)}, bf16[384,512]{1,0:T(8,128)(2,1)S(1)}, u32[]{:S(2)}, u32[]{:S(2)}) collective-permute-start(bf16[384,512]{1,0:T(8,128)(2,1)S(1)} %shard_map.254), channel_id=1, source_target_pairs={{0,16},{1,17},{2,18},{3,19},{4,20},{5,21},{6,22},{7,23},{8,24},{9,... | collective-permute-start | bytes 1179656 | tf_op jit(solution)/shard_map/ppermute | solution.py:825
  132.2 16.4 %collective-permute-start.38 = (bf16[192,768]{1,0:T(8,128)(2,1)S(1)}, bf16[192,768]{1,0:T(8,128)(2,1)S(1)}, u32[]{:S(2)}, u32[]{:S(2)}) collective-permute-start(bf16[192,768]{1,0:T(8,128)(2,1)S(1)} %shard_map.253), channel_id=1, source_target_pairs={{0,2},{1,5},{2,0},{3,7},{4,6},{5,1},{6,4},{7,3},{8,10},{9,13},{10,... | collective-permute-start | bytes 884744 | tf_op jit(solution)/shard_map/ppermute | solution.py:825
  133.2 18.9 %collective-permute-start.37 = (bf16[192,1536]{1,0:T(8,128)(2,1)S(1)}, bf16[192,1536]{1,0:T(8,128)(2,1)S(1)}, u32[]{:S(2)}, u32[]{:S(2)}) collective-permute-start(bf16[192,1536]{1,0:T(8,128)(2,1)S(1)} %shard_map.252), channel_id=1, source_target_pairs={{0,2},{1,5},{2,0},{3,7},{4,6},{5,1},{6,4},{7,3},{8,10},{9,13},{10,... | collective-permute-start | bytes 1769480 | tf_op jit(solution)/shard_map/ppermute | solution.py:825
  153.0 21.7 %collective-permute-start.44 = (bf16[192,1536]{1,0:T(8,128)(2,1)S(1)}, bf16[192,1536]{1,0:T(8,128)(2,1)S(1)}, u32[]{:S(2)}, u32[]{:S(2)}) collective-permute-start(bf16[192,1536]{1,0:T(8,128)(2,1)S(1)} %get-tuple-element.168.refs_1_.refs_17_), channel_id=1, source_target_pairs={{0,4},{1,3},{2,6},{3,1},{4,0},{5,7},{6,2},{7,5},{8,12},{9,11},{10,... | collective-permute-start | bytes 1769480 | tf_op jit(solution)/shard_map/ppermute | solution.py:825
  154.0 16.2 %collective-permute-start.47 = (bf16[192,1536]{1,0:T(8,128)(2,1)S(1)}, bf16[192,1536]{1,0:T(8,128)(2,1)S(1)}, u32[]{:S(2)}, u32[]{:S(2)}) collective-permute-start(bf16[192,1536]{1,0:T(8,128)(2,1)S(1)} %shard_map.260), channel_id=1, source_target_pairs={{0,2},{1,5},{2,0},{3,7},{4,6},{5,1},{6,4},{7,3},{8,10},{9,13},{10,... | collective-permute-start | bytes 1769480 | tf_op jit(solution)/shard_map/ppermute | solution.py:825
  155.1 19.6 %collective-permute-start.43 = (bf16[192,1536]{1,0:T(8,128)(2,1)S(1)}, bf16[192,1536]{1,0:T(8,128)(2,1)S(1)}, u32[]{:S(2)}, u32[]{:S(2)}) collective-permute-start(bf16[192,1536]{1,0:T(8,128)(2,1)S(1)} %shard_map.259), channel_id=1, source_target_pairs={{0,2},{1,5},{2,0},{3,7},{4,6},{5,1},{6,4},{7,3},{8,10},{9,13},{10,... | collective-permute-start | bytes 1769480 | tf_op jit(solution)/shard_map/ppermute | solution.py:825
  156.1 14.1 %collective-permute-start.46 = (bf16[192,768]{1,0:T(8,128)(2,1)S(1)}, bf16[192,768]{1,0:T(8,128)(2,1)S(1)}, u32[]{:S(2)}, u32[]{:S(2)}) collective-permute-start(bf16[192,768]{1,0:T(8,128)(2,1)S(1)} %get-tuple-element.184), channel_id=1, source_target_pairs={{0,8},{1,9},{2,10},{3,11},{4,12},{5,13},{6,14},{7,15},{8,0},{9,1},... | collective-permute-start | bytes 884744 | tf_op jit(solution)/shard_map/ppermute | solution.py:825
  156.1 14.1 %collective-permute-start.45 = (bf16[96,768]{1,0:T(8,128)(2,1)S(1)}, bf16[96,768]{1,0:T(8,128)(2,1)S(1)}, u32[]{:S(2)}, u32[]{:S(2)}) collective-permute-start(bf16[96,768]{1,0:T(8,128)(2,1)S(1)} %get-tuple-element.182), channel_id=1, source_target_pairs={{0,16},{1,17},{2,18},{3,19},{4,20},{5,21},{6,22},{7,23},{8,24},{9,... | collective-permute-start | bytes 442376 | tf_op jit(solution)/shard_map/ppermute | solution.py:825
  175.1 18.0 %collective-permute-start.49 = (bf16[192,1536]{1,0:T(8,128)(2,1)S(1)}, bf16[192,1536]{1,0:T(8,128)(2,1)S(1)}, u32[]{:S(2)}, u32[]{:S(2)}) collective-permute-start(bf16[192,1536]{1,0:T(8,128)(2,1)S(1)} %get-tuple-element.186.refs_1_.refs_2_), channel_id=1, source_target_pairs={{0,4},{1,3},{2,6},{3,1},{4,0},{5,7},{6,2},{7,5},{8,12},{9,11},{10,... | collective-permute-start | bytes 1769480 | tf_op jit(solution)/shard_map/ppermute | solution.py:825
  176.2 17.0 %collective-permute-start.48 = (bf16[192,1664]{1,0:T(8,128)(2,1)S(1)}, bf16[192,1664]{1,0:T(8,128)(2,1)S(1)}, u32[]{:S(2)}, u32[]{:S(2)}) collective-permute-start(bf16[192,1664]{1,0:T(8,128)(2,1)S(1)} %shard_map.262), channel_id=1, source_target_pairs={{0,2},{1,5},{2,0},{3,7},{4,6},{5,1},{6,4},{7,3},{8,10},{9,13},{10,... | collective-permute-start | bytes 1916936 | tf_op jit(solution)/shard_map/ppermute | solution.py:825
  177.2 16.0 %collective-permute-start.50 = (bf16[96,1536]{1,0:T(8,128)(2,1)S(1)}, bf16[96,1536]{1,0:T(8,128)(2,1)S(1)}, u32[]{:S(2)}, u32[]{:S(2)}) collective-permute-start(bf16[96,1536]{1,0:T(8,128)(2,1)S(1)} %get-tuple-element.189), channel_id=1, source_target_pairs={{0,16},{1,17},{2,18},{3,19},{4,20},{5,21},{6,22},{7,23},{8,24},{9,... | collective-permute-start | bytes 884744 | tf_op jit(solution)/shard_map/ppermute | solution.py:825
  177.2 16.0 %collective-permute-start.52 = (bf16[96,768]{1,0:T(8,128)(2,1)S(1)}, bf16[96,768]{1,0:T(8,128)(2,1)S(1)}, u32[]{:S(2)}, u32[]{:S(2)}) collective-permute-start(bf16[96,768]{1,0:T(8,128)(2,1)S(1)} %get-tuple-element.194), channel_id=1, source_target_pairs={{0,2},{1,5},{2,0},{3,7},{4,6},{5,1},{6,4},{7,3},{8,10},{9,13},{10,... | collective-permute-start | bytes 442376 | tf_op jit(solution)/shard_map/ppermute | solution.py:825
  195.2 18.1 %collective-permute-start.56 = (bf16[192,1664]{1,0:T(8,128)(2,1)S(1)}, bf16[192,1664]{1,0:T(8,128)(2,1)S(1)}, u32[]{:S(2)}, u32[]{:S(2)}) collective-permute-start(bf16[192,1664]{1,0:T(8,128)(2,1)S(1)} %get-tuple-element.197.refs_1_), channel_id=1, source_target_pairs={{0,4},{1,3},{2,6},{3,1},{4,0},{5,7},{6,2},{7,5},{8,12},{9,11},{10,... | collective-permute-start | bytes 1916936 | tf_op jit(solution)/shard_map/ppermute | solution.py:825
  196.3 17.0 %collective-permute-start.55 = (bf16[192,1664]{1,0:T(8,128)(2,1)S(1)}, bf16[192,1664]{1,0:T(8,128)(2,1)S(1)}, u32[]{:S(2)}, u32[]{:S(2)}) collective-permute-start(bf16[192,1664]{1,0:T(8,128)(2,1)S(1)} %shard_map.268), channel_id=1, source_target_pairs={{0,2},{1,5},{2,0},{3,7},{4,6},{5,1},{6,4},{7,3},{8,10},{9,13},{10,... | collective-permute-start | bytes 1916936 | tf_op jit(solution)/shard_map/ppermute | solution.py:825
  197.3 16.0 %collective-permute-start.57 = (bf16[96,1536]{1,0:T(8,128)(2,1)S(1)}, bf16[96,1536]{1,0:T(8,128)(2,1)S(1)}, u32[]{:S(2)}, u32[]{:S(2)}) collective-permute-start(bf16[96,1536]{1,0:T(8,128)(2,1)S(1)} %copy-done.20), channel_id=1, source_target_pairs={{0,16},{1,17},{2,18},{3,19},{4,20},{5,21},{6,22},{7,23},{8,24},{9,... | collective-permute-start | bytes 884744 | tf_op jit(solution)/shard_map/ppermute | solution.py:825
  198.6 14.6 %collective-permute-start.59 = (bf16[48,1536]{1,0:T(8,128)(2,1)S(1)}, bf16[48,1536]{1,0:T(8,128)(2,1)S(1)}, u32[]{:S(2)}, u32[]{:S(2)}) collective-permute-start(bf16[48,1536]{1,0:T(8,128)(2,1)S(1)} %get-tuple-element.209), channel_id=1, source_target_pairs={{0,8},{1,9},{2,10},{3,11},{4,12},{5,13},{6,14},{7,15},{8,0},{9,1},... | collective-permute-start | bytes 442376 | tf_op jit(solution)/shard_map/ppermute | solution.py:825
  199.8 13.4 %collective-permute-start.58 = (bf16[48,768]{1,0:T(8,128)(2,1)S(1)}, bf16[48,768]{1,0:T(8,128)(2,1)S(1)}, u32[]{:S(2)}, u32[]{:S(2)}) collective-permute-start(bf16[48,768]{1,0:T(8,128)(2,1)S(1)} %get-tuple-element.207), channel_id=1, source_target_pairs={{0,4},{1,3},{2,6},{3,1},{4,0},{5,7},{6,2},{7,5},{8,12},{9,11},{10,... | collective-permute-start | bytes 221192 | tf_op jit(solution)/shard_map/ppermute | solution.py:825
  214.5 13.1 %collective-permute-start.60 = (bf16[48,3200]{1,0:T(8,128)(2,1)S(1)}, bf16[48,3200]{1,0:T(8,128)(2,1)S(1)}, u32[]{:S(2)}, u32[]{:S(2)}) collective-permute-start(bf16[48,3200]{1,0:T(8,128)(2,1)S(1)} %get-tuple-element.211), channel_id=1, source_target_pairs={{0,8},{1,9},{2,10},{3,11},{4,12},{5,13},{6,14},{7,15},{8,0},{9,1},... | collective-permute-start | bytes 921608 | tf_op jit(solution)/shard_map/ppermute | solution.py:825
  214.6 13.3 %collective-permute-start.61 = (bf16[48,1664]{1,0:T(8,128)(2,1)S(1)}, bf16[48,1664]{1,0:T(8,128)(2,1)S(1)}, u32[]{:S(2)}, u32[]{:S(2)}) collective-permute-start(bf16[48,1664]{1,0:T(8,128)(2,1)S(1)} %get-tuple-element.212), channel_id=1, source_target_pairs={{0,16},{1,17},{2,18},{3,19},{4,20},{5,21},{6,22},{7,23},{8,24},{9,... | collective-permute-start | bytes 479240 | tf_op jit(solution)/shard_map/ppermute | solution.py:825
  217.1 14.2 %collective-permute-start.62 = (bf16[48,1664]{1,0:T(8,128)(2,1)S(1)}, bf16[48,1664]{1,0:T(8,128)(2,1)S(1)}, u32[]{:S(2)}, u32[]{:S(2)}) collective-permute-start(bf16[48,1664]{1,0:T(8,128)(2,1)S(1)} %get-tuple-element.213), channel_id=1, source_target_pairs={{0,24},{1,25},{2,26},{3,27},{4,28},{5,29},{6,30},{7,31},{8,16},{9,... | collective-permute-start | bytes 479240 | tf_op jit(solution)/shard_map/ppermute | solution.py:825
  (77 other events, 405.0 us)

commit v7 on v6

--- a/solution.py
+++ b/solution.py
@@ -504,9 +504,12 @@
     for i in range(4):
         part = tn(hidden[:, i * 8 * blk : (i + 1) * 8 * blk], g[...]).astype(BF)
         for k in range(8):
-            dst = dz if k % 2 else dw
-            row = (4 * i + k // 2) * blk
-            dst[row : row + blk, :] = part[k * blk : (k + 1) * blk]
+            row, rows = (4 * i + k // 2) * blk, slice(k * blk, (k + 1) * blk)
+            if k % 2:
+                dz[row : row + blk, :] = part[rows, :LEVELS]
+                dw[row : row + blk, D:] = part[rows, LEVELS:]
+            else:
+                dw[row : row + blk, :D] = part[rows]
     send_out(dw, offs, (own, a, b, ab))
     for q in range(4):
         for r in range(4):
@@ -810,8 +813,18 @@
         biases[...] = turned[3:6, 0:rows]
 
 
+def join_inner_kernel(core, mine, got, out):
+    c = core[0]
+    hr = 96
+    for k in range(mine.shape[1] // hr):
+        a, b = mine[:, k * hr : (k + 1) * hr], got[:, k * hr : (k + 1) * hr]
+        out[:, 2 * k * hr : (2 * k + 1) * hr] = jnp.where(c == 0, a, b)
+        out[:, (2 * k + 1) * hr : (2 * k + 2) * hr] = jnp.where(c == 0, b, a)
+
+
 CUTS = ((0, 512), (512, 256))
-FAR_CUTS = ((0, 256), (256, 512))
+FAR_CUTS = ((0, 128), (128, 512))
+LEVELS = 640
 
 
 class Moves:
@@ -1142,8 +1155,10 @@
         dmlpout_kernel,
         [offs, hidden, g],
         [SM, VM, VM],
-        [sds((4 * wb, D), BF)] * 4 + [sds((8 * wb, D), BF)] + [sds((8 * wb, width), BF) for _, width in FAR_CUTS],
-        scratch=[pltpu.VMEM((D, D), BF)] * 2,
+        [sds((4 * wb, 2 * D - LEVELS), BF)] * 4
+        + [sds((8 * wb, LEVELS), BF)]
+        + [sds((8 * wb, width), BF) for _, width in FAR_CUTS],
+        scratch=[pltpu.VMEM((D, 2 * D - LEVELS), BF), pltpu.VMEM((D, LEVELS), BF)],
         cost=3,
         hold=[*hold, *held, third],
     )
@@ -1220,6 +1235,7 @@
         )
         got_far4, got_opp4, got_near = far(blocks[1]), moves.opposite_z(blocks[2]), near(blocks[0])
         width = 4 * DH + 128
+        total2 = tie(total2, got_near)
         (total3,) = merge([("tail_near", kept3, got_far3, got_near[:, width:])])
         (total4,) = merge([("tail", d_self[0], got_a4, got_b4, got_near[:, :width], got_far4, got_opp4)])
         total = [total1, total2, total3, total4]
@@ -1239,11 +1255,10 @@
                 cost=1,
             )
 
-        sum_mlpout = jnp.concatenate([total[0], total_z], 0)
-        mine, got = own_rows(total[1])
-        pair = (jnp.where(c == 0, mine, got), jnp.where(c == 0, got, mine))
-        parts = [p.reshape(wr, ff // (2 * hr), 1, hr) for p in pair]
-        grad_in = jnp.concatenate(parts, 2).reshape(wr, ff)
+        sum_mlpout = jnp.concatenate([total[0][:, :D], jnp.concatenate([total_z, total[0][:, D:]], 1)], 0)
+        (grad_in,) = kernel_call(
+            join_inner_kernel, [core, *own_rows(total[1])], [SM, VM, VM], [sds((wr, ff), F32)], cost=1
+        )
         grad_cout, grad_cq, grad_ckv = join(own_rows(total[2]), (wr, D), (wr, D), (wr, 2 * D))
         grad_out, grad_qkv, own_gains, own_biases = join(
             own_rows(total[3]), (wr, D), (wr, 3 * D), (3, wr), (3, wr), scratch=[pltpu.VMEM((128, 128), F32)]
@@ -1269,9 +1284,10 @@
         vectors = jnp.sum(total[:, :, 4 * DH : 4 * DH + 6], 1).T
         own_gains, own_biases = vectors[:3], vectors[3:]
         grad_in = joined(placed(d_mlpin), 0, fh, ff // (2 * hr))
-        first_rows = jnp.concatenate(d_mlpout[:4], 0).reshape(16, 1, wb, D)
-        levels = jnp.concatenate([d_mlpout[4], jnp.concatenate(d_mlpout[5:], 1)], 0).reshape(4, 4, wb, D)
-        term = jnp.concatenate([first_rows, levels.transpose(1, 0, 2, 3).reshape(16, 1, wb, D)], 1).astype(F32)
+        first_rows = jnp.concatenate(d_mlpout[:4], 0)
+        levels = jnp.concatenate([d_mlpout[4], jnp.concatenate(d_mlpout[5:], 1)], 0).reshape(4, 4, wb, LEVELS)
+        levels = jnp.concatenate([levels.transpose(1, 0, 2, 3).reshape(D, LEVELS), first_rows[:, D:]], 1)
+        term = jnp.stack([first_rows[:, :D].reshape(16, wb, D), levels.reshape(16, wb, D)], 1).astype(F32)
         term = term.reshape(moves.n // 2, 1, hr, D)
         both = jnp.concatenate([jnp.where(c == 0, term, 0.0), jnp.where(c == 1, term, 0.0)], 1)
         sum_mlpout = lax.psum_scatter(both.reshape(ff, D), AXES, scatter_dimension=0, tiled=True)

time: 234 us -> 231 us (0.987)
  starting transfers between devices: 59.9 us -> 64.1 us
  local copies, waits for them, and re-layouts: 11.8 us -> 8.78 us
  waiting for transfers between devices: 86.7 us -> 83.9 us
    ppermute x66, starting transfers between devices: 59.9 us -> 64.1 us  [permute(): lax.ppermute(x, AXES, [(a, z * self.nf + 2 * yx + c) for a, (z, yx, c) in...]
    ppermute x66, waiting for transfers between devices: 86.7 us -> 83.9 us  [permute(): lax.ppermute(x, AXES, [(a, z * self.nf + 2 * yx + c) for a, (z, yx, c) in...]
    unnamed x122 -> x82, local copies, waits for them, and re-layouts: 8.22 us -> 6.95 us
    pallas_call x29 -> x30, Pallas kernels: 71.5 us -> 71.2 us  [kernel_call(): pl.pallas_call(run, out_shape=list(outs), in_specs=[space(spec) for spec...]
  transfers between devices with their start and end apart: 66 -> 66, of which waited for: 24 -> 23; matrix products, arithmetic and copies ran while one was open for 4% -> 3% of each run, Pallas kernels for 29% -> 30%
where the time goes in v7:
time: 231 us
  waiting for transfers between devices  83.9 us (36%)
  Pallas kernels  71.3 us (31%)
  starting transfers between devices  64.1 us (28%)
  local copies, waits for them, and re-layouts  8.78 us (4%)
    ppermute x66, waiting for transfers between devices, permute(): lax.ppermute(x, AXES, [(a, z * self.nf + 2 * yx + c) for a, (z, yx, c) in...  83.9 us
    pallas_call x30, Pallas kernels, kernel_call(): pl.pallas_call(run, out_shape=list(outs), in_specs=[space(spec) for spec...  71.2 us
    ppermute x66, starting transfers between devices, permute(): lax.ppermute(x, AXES, [(a, z * self.nf + 2 * yx + c) for a, (z, yx, c) in...  64.1 us
    unnamed x82, local copies, waits for them, and re-layouts  6.95 us
  transfers between devices with their start and end apart: 66, of which 23 were waited for; matrix products, arithmetic and copies ran while one was open for 3% of the time, Pallas kernels for 30%

profile of v7, /device:TPU:0, one launch (start us, length us, event | category | flops | bytes accessed | tf_op | source)
XLA Modules:
  0.0 230.5 jit_solution(687242590948233872)
XLA Ops:
  1.7 1.9 shard_map.220
  4.1 1.5 copy.54.refs_5_
  5.9 3.7 %collective-permute-start.5 = (bf16[48,1664]{1,0:T(8,128)(2,1)S(1)}, bf16[48,1664]{1,0:T(8,128)(2,1)S(1)}, u32[]{:S(2)}, u32[]{:S(2)}) collective-permute-start(bf16[48,1664]{1,0:T(8,128)(2,1)S(1)} %get-tuple-element.120.refs_7_.refs_0_), channel_id=1, source_target_pairs={{0,16},{1,17},{2,18},{3,19},{4,20},{5,21},{6,22},{7,23},{8,24},{9,... | collective-permute-start | bytes 479240 | tf_op jit(solution)/shard_map/ppermute | solution.py:838
  9.6 1.3 collective-permute-start.6
  11.2 1.5 copy.55.refs_6_
  12.8 1.8 shard_map.222
  14.6 1.6 copy-done.27
  16.2 1.5 collective-permute-start.8
  17.7 1.5 collective-permute-start.9
  19.3 2.2 collective-permute-done.5.refs_2_
  21.5 4.2 %collective-permute-done.4.refs_1_.refs_5_ = bf16[48,3200]{1,0:T(8,128)(2,1)S(1)} collective-permute-done((bf16[48,3200]{1,0:T(8,128)(2,1)S(1)}, bf16[48,3200]{1,0:T(8,128)(2,1)S(1)}, u32[]{:S(2)}, u32[]{:S(2)}) %collective-permute-start.4) | collective-permute-done | bytes 307232 | tf_op jit(solution)/shard_map/ppermute | solution.py:838
  26.7 1.6 collective-permute-start.10
  28.2 1.5 collective-permute-start.11
  29.7 1.6 collective-permute-start.14
  31.4 2.5 %collective-permute-start.17 = (bf16[48,2304]{1,0:T(8,128)(2,1)S(1)}, bf16[48,2304]{1,0:T(8,128)(2,1)S(1)}, u32[]{:S(2)}, u32[]{:S(2)}) collective-permute-start(bf16[48,2304]{1,0:T(8,128)(2,1)S(1)} %shard_map.229.refs_6_), channel_id=1, source_target_pairs={{0,8},{1,9},{2,10},{3,11},{4,12},{5,13},{6,14},{7,15},{8,0},{9,1},... | collective-permute-start | bytes 663560 | tf_op jit(solution)/shard_map/ppermute | solution.py:838
  34.5 8.6 %collective-permute-done.10.refs_0_ = bf16[192,1664]{1,0:T(8,128)(2,1)S(1)} collective-permute-done((bf16[192,1664]{1,0:T(8,128)(2,1)S(1)}, bf16[192,1664]{1,0:T(8,128)(2,1)S(1)}, u32[]{:S(2)}, u32[]{:S(2)}) %collective-permute-start.10) | collective-permute-done | bytes 639008 | tf_op jit(solution)/shard_map/ppermute | solution.py:838
  43.5 2.1 collective-permute-start.12
  45.9 1.3 collective-permute-start.20
  47.5 1.6 collective-permute-start.18
  49.0 2.5 %collective-permute-start.19 = (bf16[192,768]{1,0:T(8,128)(2,1)S(1)}, bf16[192,768]{1,0:T(8,128)(2,1)S(1)}, u32[]{:S(2)}, u32[]{:S(2)}) collective-permute-start(bf16[192,768]{1,0:T(8,128)(2,1)S(1)} %get-tuple-element.130.refs_4_.refs_6_.refs_8_), channel_id=1, source_target_pairs={{0,8},{1,9},{2,10},{3,11},{4,12},{5,13},{6,14},{7,15},{8,0},{9,1},... | collective-permute-start | bytes 884744 | tf_op jit(solution)/shard_map/ppermute | solution.py:838
  51.5 8.2 %collective-permute-done.12.refs_4_.refs_2_.refs_6_ = bf16[192,1664]{1,0:T(8,128)(2,1)S(1)} collective-permute-done((bf16[192,1664]{1,0:T(8,128)(2,1)S(1)}, bf16[192,1664]{1,0:T(8,128)(2,1)S(1)}, u32[]{:S(2)}, u32[]{:S(2)}) %collective-permute-start.12) | collective-permute-done | bytes 639008 | tf_op jit(solution)/shard_map/ppermute | solution.py:838
  60.5 1.8 collective-permute-done.20.refs_0_
  62.2 4.3 %collective-permute-done.21.refs_1_.refs_3_ = bf16[192,1536]{1,0:T(8,128)(2,1)S(1)} collective-permute-done((bf16[192,1536]{1,0:T(8,128)(2,1)S(1)}, bf16[192,1536]{1,0:T(8,128)(2,1)S(1)}, u32[]{:S(2)}, u32[]{:S(2)}) %collective-permute-start.21) | collective-permute-done | bytes 589856 | tf_op jit(solution)/shard_map/ppermute | solution.py:838
  66.5 2.9 %collective-permute-done.18.refs_1_.refs_3_ = bf16[96,2304]{1,0:T(8,128)(2,1)S(1)} collective-permute-done((bf16[96,2304]{1,0:T(8,128)(2,1)S(1)}, bf16[96,2304]{1,0:T(8,128)(2,1)S(1)}, u32[]{:S(2)}, u32[]{:S(2)}) %collective-permute-start.18) | collective-permute-done | bytes 442400 | tf_op jit(solution)/shard_map/ppermute | solution.py:838
  72.7 7.4 %shard_map.234 = (bf16[512,768]{1,0:T(8,128)(2,1)S(1)}, bf16[512,1152]{1,0:T(8,128)(2,1)S(1)}, bf16[8,64,384]{2,1,0:T(8,128)(2,1)S(1)}, bf16[512,1152]{1,0:T(8,1...) custom-call(s32[8]{0:T(128)S(1)} %pad_add_fusion.1.refs_0_, s32[1]{0:T(128)} %bitcast.2.refs_0_.refs_1_.refs_6_, ...), custom_call_target="tpu_custom_call" | custom-call | flops 41999998976 | tf_op jit(solution)/shard_map/pallas_call | solution.py:97
  80.2 11.5 %collective-permute-done.25.refs_4_.refs_6_ = bf16[384,512]{1,0:T(8,128)(2,1)S(1)} collective-permute-done((bf16[384,512]{1,0:T(8,128)(2,1)S(1)}, bf16[384,512]{1,0:T(8,128)(2,1)S(1)}, u32[]{:S(2)}, u32[]{:S(2)}) %collective-permute-start.25) | collective-permute-done | bytes 393248 | tf_op jit(solution)/shard_map/ppermute | solution.py:838
  96.3 10.3 %shard_map.241 = (bf16[1920,768]{1,0:T(8,128)(2,1)S(1)}, bf16[768,768]{1,0:T(8,128)(2,1)S(1)}, bf16[768,384]{1,0:T(8,128)(2,1)S(1)}, f32[512,768]{1,0:T(8,128)S(...) custom-call(s32[2,16]{1,0:T(2,128)S(1)} %pad_add_fusion.refs_0_.refs, ...), custom_call_target="tpu_custom_call" | custom-call | flops 83999997952 | tf_op jit(solution)/shard_map/pallas_call | solution.py:97
  107.1 2.2 collective-permute-done.30.refs_3_
  112.2 3.3 %shard_map.245 = (f32[512,768]{1,0:T(8,128)S(1)}, bf16[512,768]{1,0:T(8,128)(2,1)S(1)}, bf16[512,1536]{1,0:T(8,128)(2,1)S(1)}, bf16[512,1536]{1,0:T(8,128)(2,1)S(1)}) custom-call(f32[512,768]{1,0:T(8,128)S(1)} %get-tuple-element.138.refs_0_.refs_3_, bf16[512,1152]{1,0:T(8,128)(2,1)S(1)} %shard_map.243.refs_1_.refs_14_, ...), custom_call_target="tpu_custom_call" | custom-call | flops 35000000512 | tf_op jit(solution)/shard_map/pallas_call | solution.py:97
  115.5 2.2 shard_map.247
  119.5 6.8 %shard_map.248 = (bf16[256,768]{1,0:T(8,128)(2,1)S(1)}, bf16[768,768]{1,0:T(8,128)(2,1)S(1)}, bf16[192,1536]{1,0:T(8,128)(2,1)S(1)}, bf16[192,1536]{1,0:T(8,128)...) custom-call(s32[2,16]{1,0:T(2,128)S(1)} %pad_add_fusion.refs_0_.refs_2_, ...), custom_call_target="tpu_custom_call" | custom-call | flops 76999999488 | tf_op jit(solution)/shard_map/pallas_call | solution.py:97
  128.3 2.6 %collective-permute-start.40 = (bf16[384,512]{1,0:T(8,128)(2,1)S(1)}, bf16[384,512]{1,0:T(8,128)(2,1)S(1)}, u32[]{:S(2)}, u32[]{:S(2)}) collective-permute-start(bf16[384,512]{1,0:T(8,128)(2,1)S(1)} %shard_map.254), channel_id=1, source_target_pairs={{0,16},{1,17},{2,18},{3,19},{4,20},{5,21},{6,22},{7,23},{8,24},{9,... | collective-permute-start | bytes 1179656 | tf_op jit(solution)/shard_map/ppermute | solution.py:838
  132.9 14.3 %shard_map.251 = (bf16[256,768]{1,0:T(8,128)(2,1)}, f32[512,768]{1,0:T(8,128)S(1)}, bf16[512,768]{1,0:T(8,128)(2,1)S(1)}, f32[8,768]{1,0:T(8,128)S(1)}, bf16[192...) custom-call(s32[2,16]{1,0:T(2,128)S(1)} %pad_add_fusion.refs_0_.refs, ...), custom_call_target="tpu_custom_call" | custom-call | flops 98000003072 | tf_op jit(solution)/shard_map/pallas_call | solution.py:97
  153.3 2.1 collective-permute-start.46
  155.9 11.6 %shard_map.258 = (f32[256,768]{1,0:T(8,128)S(1)}, bf16[256,768]{1,0:T(8,128)(2,1)S(1)}, bf16[256,768]{1,0:T(8,128)(2,1)S(1)}, bf16[192,1664]{1,0:T(8,128)(2,1)S(...) custom-call(s32[2,16]{1,0:T(2,128)S(1)} %pad_add_fusion.refs_0_.refs_2_, ...), custom_call_target="tpu_custom_call" | custom-call | flops 76999999488 | tf_op jit(solution)/shard_map/pallas_call | solution.py:97
  167.6 4.6 %collective-permute-done.43.refs_1_ = bf16[192,1536]{1,0:T(8,128)(2,1)S(1)} collective-permute-done((bf16[192,1536]{1,0:T(8,128)(2,1)S(1)}, bf16[192,1536]{1,0:T(8,128)(2,1)S(1)}, u32[]{:S(2)}, u32[]{:S(2)}) %collective-permute-start.43) | collective-permute-done | bytes 589856 | tf_op jit(solution)/shard_map/ppermute | solution.py:838
  174.3 2.6 %collective-permute-start.50 = (bf16[96,1536]{1,0:T(8,128)(2,1)S(1)}, bf16[96,1536]{1,0:T(8,128)(2,1)S(1)}, u32[]{:S(2)}, u32[]{:S(2)}) collective-permute-start(bf16[96,1536]{1,0:T(8,128)(2,1)S(1)} %get-tuple-element.189), channel_id=1, source_target_pairs={{0,16},{1,17},{2,18},{3,19},{4,20},{5,21},{6,22},{7,23},{8,24},{9,... | collective-permute-start | bytes 884744 | tf_op jit(solution)/shard_map/ppermute | solution.py:838
  178.0 2.5 %shard_map.263 = (bf16[960,768]{1,0:T(8,128)(2,1)S(1)}, bf16[960,768]{1,0:T(8,128)(2,1)S(1)}) custom-call(bf16[1920,768]{1,0:T(8,128)(2,1)S(1)} %get-tuple-element.195.refs_0_, bf16[768,768]{1,0:T(8,128)(2,1)S(1)} %copy-done.21, bf16[192,1536]{1,0:T(8,128)(2,1)S(1)} %get-tuple-element.186.refs_1_.refs_2_), custom_call_target="tpu_custom_call" | custom-call | flops 20999999488 | tf_op jit(solution)/shard_map/pallas_call | solution.py:97
  180.5 4.8 %collective-permute-done.51.refs_8_ = bf16[48,896]{1,0:T(8,128)(2,1)S(1)} collective-permute-done((bf16[48,896]{1,0:T(8,128)(2,1)S(1)}, bf16[48,896]{1,0:T(8,128)(2,1)S(1)}, u32[]{:S(2)}, u32[]{:S(2)}) %collective-permute-start.51) | collective-permute-done | bytes 86048 | tf_op jit(solution)/shard_map/ppermute | solution.py:838
  185.3 4.7 %collective-permute-done.52.refs_11_ = bf16[96,640]{1,0:T(8,128)(2,1)S(1)} collective-permute-done((bf16[96,640]{1,0:T(8,128)(2,1)S(1)}, bf16[96,640]{1,0:T(8,128)(2,1)S(1)}, u32[]{:S(2)}, u32[]{:S(2)}) %collective-permute-start.52) | collective-permute-done | bytes 122912 | tf_op jit(solution)/shard_map/ppermute | solution.py:838
  193.6 2.1 collective-permute-start.57
  197.6 2.2 shard_map.267
  199.8 9.5 %collective-permute-done.58.refs_6_ = bf16[48,640]{1,0:T(8,128)(2,1)S(1)} collective-permute-done((bf16[48,640]{1,0:T(8,128)(2,1)S(1)}, bf16[48,640]{1,0:T(8,128)(2,1)S(1)}, u32[]{:S(2)}, u32[]{:S(2)}) %collective-permute-start.58) | collective-permute-done | bytes 61472 | tf_op jit(solution)/shard_map/ppermute | solution.py:838
  211.0 1.7 collective-permute-start.60
  213.6 1.9 collective-permute-start.62
  215.5 1.6 copy.57
  217.9 5.0 %collective-permute-done.60.refs_1_ = bf16[48,3200]{1,0:T(8,128)(2,1)S(1)} collective-permute-done((bf16[48,3200]{1,0:T(8,128)(2,1)S(1)}, bf16[48,3200]{1,0:T(8,128)(2,1)S(1)}, u32[]{:S(2)}, u32[]{:S(2)}) %collective-permute-start.60) | collective-permute-done | bytes 307232 | tf_op jit(solution)/shard_map/ppermute | solution.py:838
  223.9 4.0 %collective-permute-done.62.refs_5_ = bf16[48,1664]{1,0:T(8,128)(2,1)S(1)} collective-permute-done((bf16[48,1664]{1,0:T(8,128)(2,1)S(1)}, bf16[48,1664]{1,0:T(8,128)(2,1)S(1)}, u32[]{:S(2)}, u32[]{:S(2)}) %collective-permute-start.62) | collective-permute-done | bytes 159776 | tf_op jit(solution)/shard_map/ppermute | solution.py:838
  (238 shorter events, 44.3 us)
Async XLA Ops:
  1.2 10.0 %collective-permute-start.7 = (bf16[4,228,768]{2,0,1:T(4,128)(2,1)}, bf16[4,228,768]{2,0,1:T(4,128)(2,1)}, u32[]{:S(2)}, u32[]{:S(2)}) collective-permute-start(bf16[4,228,768]{2,0,1:T(4,128)(2,1)} %param.14), channel_id=1, source_target_pairs={{0,1},{1,0},{2,3},{3,2},{4,5},{5,4},{6,7},{7,6},{8,9},{9,8},{10,11... | collective-permute-start | bytes 4202504 | tf_op jit(solution)/shard_map/ppermute | solution.py:838
  5.9 15.6 %collective-permute-start.5 = (bf16[48,1664]{1,0:T(8,128)(2,1)S(1)}, bf16[48,1664]{1,0:T(8,128)(2,1)S(1)}, u32[]{:S(2)}, u32[]{:S(2)}) collective-permute-start(bf16[48,1664]{1,0:T(8,128)(2,1)S(1)} %get-tuple-element.120.refs_7_.refs_0_), channel_id=1, source_target_pairs={{0,16},{1,17},{2,18},{3,19},{4,20},{5,21},{6,22},{7,23},{8,24},{9,... | collective-permute-start | bytes 479240 | tf_op jit(solution)/shard_map/ppermute | solution.py:838
  9.6 11.9 %collective-permute-start.6 = (bf16[48,1664]{1,0:T(8,128)(2,1)S(1)}, bf16[48,1664]{1,0:T(8,128)(2,1)S(1)}, u32[]{:S(2)}, u32[]{:S(2)}) collective-permute-start(bf16[48,1664]{1,0:T(8,128)(2,1)S(1)} %get-tuple-element.120.refs_7_.refs_0_), channel_id=1, source_target_pairs={{0,24},{1,25},{2,26},{3,27},{4,28},{5,29},{6,30},{7,31},{8,16},{9,... | collective-permute-start | bytes 479240 | tf_op jit(solution)/shard_map/ppermute | solution.py:838
  11.0 14.7 %collective-permute-start.4 = (bf16[48,3200]{1,0:T(8,128)(2,1)S(1)}, bf16[48,3200]{1,0:T(8,128)(2,1)S(1)}, u32[]{:S(2)}, u32[]{:S(2)}) collective-permute-start(bf16[48,3200]{1,0:T(8,128)(2,1)S(1)} %get-tuple-element.121.refs_8_.refs_4_), channel_id=1, source_target_pairs={{0,8},{1,9},{2,10},{3,11},{4,12},{5,13},{6,14},{7,15},{8,0},{9,1},... | collective-permute-start | bytes 921608 | tf_op jit(solution)/shard_map/ppermute | solution.py:838
  16.2 9.5 %collective-permute-start.8 = (bf16[48,768]{1,0:T(8,128)(2,1)S(1)}, bf16[48,768]{1,0:T(8,128)(2,1)S(1)}, u32[]{:S(2)}, u32[]{:S(2)}) collective-permute-start(bf16[48,768]{1,0:T(8,128)(2,1)S(1)} %shard_map.223.refs_2_), channel_id=1, source_target_pairs={{0,2},{1,5},{2,0},{3,7},{4,6},{5,1},{6,4},{7,3},{8,10},{9,13},{10,... | collective-permute-start | bytes 221192 | tf_op jit(solution)/shard_map/ppermute | solution.py:838
  26.7 16.5 %collective-permute-start.10 = (bf16[192,1664]{1,0:T(8,128)(2,1)S(1)}, bf16[192,1664]{1,0:T(8,128)(2,1)S(1)}, u32[]{:S(2)}, u32[]{:S(2)}) collective-permute-start(bf16[192,1664]{1,0:T(8,128)(2,1)S(1)} %get-tuple-element.124.refs_1_.refs_2_.refs_3_), channel_id=1, source_target_pairs={{0,2},{1,5},{2,0},{3,7},{4,6},{5,1},{6,4},{7,3},{8,10},{9,13},{10,... | collective-permute-start | bytes 1916936 | tf_op jit(solution)/shard_map/ppermute | solution.py:838
  28.2 15.2 %collective-permute-start.11 = (bf16[192,1664]{1,0:T(8,128)(2,1)S(1)}, bf16[192,1664]{1,0:T(8,128)(2,1)S(1)}, u32[]{:S(2)}, u32[]{:S(2)}) collective-permute-start(bf16[192,1664]{1,0:T(8,128)(2,1)S(1)} %get-tuple-element.124.refs_1_.refs_2_.refs_3_), channel_id=1, source_target_pairs={{0,4},{1,3},{2,6},{3,1},{4,0},{5,7},{6,2},{7,5},{8,12},{9,11},{10,... | collective-permute-start | bytes 1916936 | tf_op jit(solution)/shard_map/ppermute | solution.py:838
  29.7 16.1 %collective-permute-start.14 = (bf16[96,1536]{1,0:T(8,128)(2,1)S(1)}, bf16[96,1536]{1,0:T(8,128)(2,1)S(1)}, u32[]{:S(2)}, u32[]{:S(2)}) collective-permute-start(bf16[96,1536]{1,0:T(8,128)(2,1)S(1)} %get-tuple-element.126.refs_0_), channel_id=1, source_target_pairs={{0,16},{1,17},{2,18},{3,19},{4,20},{5,21},{6,22},{7,23},{8,24},{9,... | collective-permute-start | bytes 884744 | tf_op jit(solution)/shard_map/ppermute | solution.py:838
  31.4 14.2 %collective-permute-start.17 = (bf16[48,2304]{1,0:T(8,128)(2,1)S(1)}, bf16[48,2304]{1,0:T(8,128)(2,1)S(1)}, u32[]{:S(2)}, u32[]{:S(2)}) collective-permute-start(bf16[48,2304]{1,0:T(8,128)(2,1)S(1)} %shard_map.229.refs_6_), channel_id=1, source_target_pairs={{0,8},{1,9},{2,10},{3,11},{4,12},{5,13},{6,14},{7,15},{8,0},{9,1},... | collective-permute-start | bytes 663560 | tf_op jit(solution)/shard_map/ppermute | solution.py:838
  33.9 11.6 %collective-permute-start.15 = (bf16[48,768]{1,0:T(8,128)(2,1)S(1)}, bf16[48,768]{1,0:T(8,128)(2,1)S(1)}, u32[]{:S(2)}, u32[]{:S(2)}) collective-permute-start(bf16[48,768]{1,0:T(8,128)(2,1)S(1)} %shard_map.227), channel_id=1, source_target_pairs={{0,4},{1,3},{2,6},{3,1},{4,0},{5,7},{6,2},{7,5},{8,12},{9,11},{10,... | collective-permute-start | bytes 221192 | tf_op jit(solution)/shard_map/ppermute | solution.py:838
  43.5 16.3 %collective-permute-start.12 = (bf16[192,1664]{1,0:T(8,128)(2,1)S(1)}, bf16[192,1664]{1,0:T(8,128)(2,1)S(1)}, u32[]{:S(2)}, u32[]{:S(2)}) collective-permute-start(bf16[192,1664]{1,0:T(8,128)(2,1)S(1)} %shard_map.225.refs_2_.refs_8_.refs_4_), channel_id=1, source_target_pairs={{0,4},{1,3},{2,6},{3,1},{4,0},{5,7},{6,2},{7,5},{8,12},{9,11},{10,... | collective-permute-start | bytes 1916936 | tf_op jit(solution)/shard_map/ppermute | solution.py:838
  45.9 16.3 %collective-permute-start.20 = (bf16[192,1536]{1,0:T(8,128)(2,1)S(1)}, bf16[192,1536]{1,0:T(8,128)(2,1)S(1)}, u32[]{:S(2)}, u32[]{:S(2)}) collective-permute-start(bf16[192,1536]{1,0:T(8,128)(2,1)S(1)} %get-tuple-element.131.refs_1_), channel_id=1, source_target_pairs={{0,2},{1,5},{2,0},{3,7},{4,6},{5,1},{6,4},{7,3},{8,10},{9,13},{10,... | collective-permute-start | bytes 1769480 | tf_op jit(solution)/shard_map/ppermute | solution.py:838
  47.2 19.4 %collective-permute-start.21 = (bf16[192,1536]{1,0:T(8,128)(2,1)S(1)}, bf16[192,1536]{1,0:T(8,128)(2,1)S(1)}, u32[]{:S(2)}, u32[]{:S(2)}) collective-permute-start(bf16[192,1536]{1,0:T(8,128)(2,1)S(1)} %get-tuple-element.131.refs_1_), channel_id=1, source_target_pairs={{0,4},{1,3},{2,6},{3,1},{4,0},{5,7},{6,2},{7,5},{8,12},{9,11},{10,... | collective-permute-start | bytes 1769480 | tf_op jit(solution)/shard_map/ppermute | solution.py:838
  47.5 22.0 %collective-permute-start.18 = (bf16[96,2304]{1,0:T(8,128)(2,1)S(1)}, bf16[96,2304]{1,0:T(8,128)(2,1)S(1)}, u32[]{:S(2)}, u32[]{:S(2)}) collective-permute-start(bf16[96,2304]{1,0:T(8,128)(2,1)S(1)} %get-tuple-element.129.refs_0_.refs_2_), channel_id=1, source_target_pairs={{0,16},{1,17},{2,18},{3,19},{4,20},{5,21},{6,22},{7,23},{8,24},{9,... | collective-permute-start | bytes 1327112 | tf_op jit(solution)/shard_map/ppermute | solution.py:838
  49.0 17.5 %collective-permute-start.19 = (bf16[192,768]{1,0:T(8,128)(2,1)S(1)}, bf16[192,768]{1,0:T(8,128)(2,1)S(1)}, u32[]{:S(2)}, u32[]{:S(2)}) collective-permute-start(bf16[192,768]{1,0:T(8,128)(2,1)S(1)} %get-tuple-element.130.refs_4_.refs_6_.refs_8_), channel_id=1, source_target_pairs={{0,8},{1,9},{2,10},{3,11},{4,12},{5,13},{6,14},{7,15},{8,0},{9,1},... | collective-permute-start | bytes 884744 | tf_op jit(solution)/shard_map/ppermute | solution.py:838
  60.4 9.2 %collective-permute-start.13 = (bf16[768,384]{1,0:T(8,128)(2,1)S(1)}, bf16[768,384]{1,0:T(8,128)(2,1)S(1)}, u32[]{:S(2)}, u32[]{:S(2)}) collective-permute-start(bf16[768,384]{1,0:T(8,128)(2,1)S(1)} %shard_map.226.refs_8_.refs_7_), channel_id=1, source_target_pairs={{0,1},{1,0},{2,3},{3,2},{4,5},{5,4},{6,7},{7,6},{8,9},{9,8},{10,11... | collective-permute-start | bytes 1769480 | tf_op jit(solution)/shard_map/ppermute | solution.py:838
  69.7 22.0 %collective-permute-start.23 = (bf16[192,1536]{1,0:T(8,128)(2,1)S(1)}, bf16[192,1536]{1,0:T(8,128)(2,1)S(1)}, u32[]{:S(2)}, u32[]{:S(2)}) collective-permute-start(bf16[192,1536]{1,0:T(8,128)(2,1)S(1)} %shard_map.233.refs_10_.refs_1_), channel_id=1, source_target_pairs={{0,2},{1,5},{2,0},{3,7},{4,6},{5,1},{6,4},{7,3},{8,10},{9,13},{10,... | collective-permute-start | bytes 1769480 | tf_op jit(solution)/shard_map/ppermute | solution.py:838
  70.7 21.0 %collective-permute-start.24 = (bf16[192,1536]{1,0:T(8,128)(2,1)S(1)}, bf16[192,1536]{1,0:T(8,128)(2,1)S(1)}, u32[]{:S(2)}, u32[]{:S(2)}) collective-permute-start(bf16[192,1536]{1,0:T(8,128)(2,1)S(1)} %shard_map.233.refs_10_.refs_1_), channel_id=1, source_target_pairs={{0,4},{1,3},{2,6},{3,1},{4,0},{5,7},{6,2},{7,5},{8,12},{9,11},{10,... | collective-permute-start | bytes 1769480 | tf_op jit(solution)/shard_map/ppermute | solution.py:838
  71.7 20.0 %collective-permute-start.22 = (bf16[192,1536]{1,0:T(8,128)(2,1)S(1)}, bf16[192,1536]{1,0:T(8,128)(2,1)S(1)}, u32[]{:S(2)}, u32[]{:S(2)}) collective-permute-start(bf16[192,1536]{1,0:T(8,128)(2,1)S(1)} %shard_map.235.refs_2_), channel_id=1, source_target_pairs={{0,4},{1,3},{2,6},{3,1},{4,0},{5,7},{6,2},{7,5},{8,12},{9,11},{10,... | collective-permute-start | bytes 1769480 | tf_op jit(solution)/shard_map/ppermute | solution.py:838
  72.7 18.9 %collective-permute-start.25 = (bf16[384,512]{1,0:T(8,128)(2,1)S(1)}, bf16[384,512]{1,0:T(8,128)(2,1)S(1)}, u32[]{:S(2)}, u32[]{:S(2)}) collective-permute-start(bf16[384,512]{1,0:T(8,128)(2,1)S(1)} %shard_map.236), channel_id=1, source_target_pairs={{0,16},{1,17},{2,18},{3,19},{4,20},{5,21},{6,22},{7,23},{8,24},{9,... | collective-permute-start | bytes 1179656 | tf_op jit(solution)/shard_map/ppermute | solution.py:838
  93.6 15.7 %collective-permute-start.28 = (bf16[192,1536]{1,0:T(8,128)(2,1)S(1)}, bf16[192,1536]{1,0:T(8,128)(2,1)S(1)}, u32[]{:S(2)}, u32[]{:S(2)}) collective-permute-start(bf16[192,1536]{1,0:T(8,128)(2,1)S(1)} %shard_map.237.refs_1_.refs_2_), channel_id=1, source_target_pairs={{0,4},{1,3},{2,6},{3,1},{4,0},{5,7},{6,2},{7,5},{8,12},{9,11},{10,... | collective-permute-start | bytes 1769480 | tf_op jit(solution)/shard_map/ppermute | solution.py:838
  94.4 12.8 %collective-permute-start.29 = (bf16[192,768]{1,0:T(8,128)(2,1)S(1)}, bf16[192,768]{1,0:T(8,128)(2,1)S(1)}, u32[]{:S(2)}, u32[]{:S(2)}) collective-permute-start(bf16[192,768]{1,0:T(8,128)(2,1)S(1)} %shard_map.238.refs_1_), channel_id=1, source_target_pairs={{0,2},{1,5},{2,0},{3,7},{4,6},{5,1},{6,4},{7,3},{8,10},{9,13},{10,... | collective-permute-start | bytes 884744 | tf_op jit(solution)/shard_map/ppermute | solution.py:838
  95.3 14.0 %collective-permute-start.30 = (bf16[192,768]{1,0:T(8,128)(2,1)S(1)}, bf16[192,768]{1,0:T(8,128)(2,1)S(1)}, u32[]{:S(2)}, u32[]{:S(2)}) collective-permute-start(bf16[192,768]{1,0:T(8,128)(2,1)S(1)} %shard_map.238.refs_1_), channel_id=1, source_target_pairs={{0,4},{1,3},{2,6},{3,1},{4,0},{5,7},{6,2},{7,5},{8,12},{9,11},{10,... | collective-permute-start | bytes 884744 | tf_op jit(solution)/shard_map/ppermute | solution.py:838
  96.3 10.8 %collective-permute-start.31 = (bf16[384,256]{1,0:T(8,128)(2,1)S(1)}, bf16[384,256]{1,0:T(8,128)(2,1)S(1)}, u32[]{:S(2)}, u32[]{:S(2)}) collective-permute-start(bf16[384,256]{1,0:T(8,128)(2,1)S(1)} %shard_map.242), channel_id=1, source_target_pairs={{0,16},{1,17},{2,18},{3,19},{4,20},{5,21},{6,22},{7,23},{8,24},{9,... | collective-permute-start | bytes 589832 | tf_op jit(solution)/shard_map/ppermute | solution.py:838
  109.3 10.1 %collective-permute-start.33 = (bf16[192,768]{1,0:T(8,128)(2,1)S(1)}, bf16[192,768]{1,0:T(8,128)(2,1)S(1)}, u32[]{:S(2)}, u32[]{:S(2)}) collective-permute-start(bf16[192,768]{1,0:T(8,128)(2,1)S(1)} %shard_map.246), channel_id=1, source_target_pairs={{0,4},{1,3},{2,6},{3,1},{4,0},{5,7},{6,2},{7,5},{8,12},{9,11},{10,... | collective-permute-start | bytes 884744 | tf_op jit(solution)/shard_map/ppermute | solution.py:838
  117.7 8.6 %collective-permute-start.34 = (bf16[192,896]{1,0:T(8,128)(2,1)S(1)}, bf16[192,896]{1,0:T(8,128)(2,1)S(1)}, u32[]{:S(2)}, u32[]{:S(2)}) collective-permute-start(bf16[192,896]{1,0:T(8,128)(2,1)S(1)} %get-tuple-element.156), channel_id=1, source_target_pairs={{0,2},{1,5},{2,0},{3,7},{4,6},{5,1},{6,4},{7,3},{8,10},{9,13},{10,... | collective-permute-start | bytes 1032200 | tf_op jit(solution)/shard_map/ppermute | solution.py:838
  126.5 20.7 %collective-permute-start.39 = (bf16[192,896]{1,0:T(8,128)(2,1)S(1)}, bf16[192,896]{1,0:T(8,128)(2,1)S(1)}, u32[]{:S(2)}, u32[]{:S(2)}) collective-permute-start(bf16[192,896]{1,0:T(8,128)(2,1)S(1)} %shard_map.249.refs_1_.refs_18_), channel_id=1, source_target_pairs={{0,4},{1,3},{2,6},{3,1},{4,0},{5,7},{6,2},{7,5},{8,12},{9,11},{10,... | collective-permute-start | bytes 1032200 | tf_op jit(solution)/shard_map/ppermute | solution.py:838
  127.3 21.2 %collective-permute-start.41 = (bf16[192,1536]{1,0:T(8,128)(2,1)S(1)}, bf16[192,1536]{1,0:T(8,128)(2,1)S(1)}, u32[]{:S(2)}, u32[]{:S(2)}) collective-permute-start(bf16[192,1536]{1,0:T(8,128)(2,1)S(1)} %shard_map.255), channel_id=1, source_target_pairs={{0,2},{1,5},{2,0},{3,7},{4,6},{5,1},{6,4},{7,3},{8,10},{9,13},{10,... | collective-permute-start | bytes 1769480 | tf_op jit(solution)/shard_map/ppermute | solution.py:838
  128.3 20.2 %collective-permute-start.40 = (bf16[384,512]{1,0:T(8,128)(2,1)S(1)}, bf16[384,512]{1,0:T(8,128)(2,1)S(1)}, u32[]{:S(2)}, u32[]{:S(2)}) collective-permute-start(bf16[384,512]{1,0:T(8,128)(2,1)S(1)} %shard_map.254), channel_id=1, source_target_pairs={{0,16},{1,17},{2,18},{3,19},{4,20},{5,21},{6,22},{7,23},{8,24},{9,... | collective-permute-start | bytes 1179656 | tf_op jit(solution)/shard_map/ppermute | solution.py:838
  130.8 16.4 %collective-permute-start.38 = (bf16[192,896]{1,0:T(8,128)(2,1)S(1)}, bf16[192,896]{1,0:T(8,128)(2,1)S(1)}, u32[]{:S(2)}, u32[]{:S(2)}) collective-permute-start(bf16[192,896]{1,0:T(8,128)(2,1)S(1)} %shard_map.253), channel_id=1, source_target_pairs={{0,2},{1,5},{2,0},{3,7},{4,6},{5,1},{6,4},{7,3},{8,10},{9,13},{10,... | collective-permute-start | bytes 1032200 | tf_op jit(solution)/shard_map/ppermute | solution.py:838
  131.9 17.7 %collective-permute-start.37 = (bf16[192,1536]{1,0:T(8,128)(2,1)S(1)}, bf16[192,1536]{1,0:T(8,128)(2,1)S(1)}, u32[]{:S(2)}, u32[]{:S(2)}) collective-permute-start(bf16[192,1536]{1,0:T(8,128)(2,1)S(1)} %shard_map.252), channel_id=1, source_target_pairs={{0,2},{1,5},{2,0},{3,7},{4,6},{5,1},{6,4},{7,3},{8,10},{9,13},{10,... | collective-permute-start | bytes 1769480 | tf_op jit(solution)/shard_map/ppermute | solution.py:838
  150.3 21.9 %collective-permute-start.44 = (bf16[192,1536]{1,0:T(8,128)(2,1)S(1)}, bf16[192,1536]{1,0:T(8,128)(2,1)S(1)}, u32[]{:S(2)}, u32[]{:S(2)}) collective-permute-start(bf16[192,1536]{1,0:T(8,128)(2,1)S(1)} %get-tuple-element.168.refs_1_.refs_17_), channel_id=1, source_target_pairs={{0,4},{1,3},{2,6},{3,1},{4,0},{5,7},{6,2},{7,5},{8,12},{9,11},{10,... | collective-permute-start | bytes 1769480 | tf_op jit(solution)/shard_map/ppermute | solution.py:838
  151.2 16.4 %collective-permute-start.47 = (bf16[192,1536]{1,0:T(8,128)(2,1)S(1)}, bf16[192,1536]{1,0:T(8,128)(2,1)S(1)}, u32[]{:S(2)}, u32[]{:S(2)}) collective-permute-start(bf16[192,1536]{1,0:T(8,128)(2,1)S(1)} %shard_map.260), channel_id=1, source_target_pairs={{0,2},{1,5},{2,0},{3,7},{4,6},{5,1},{6,4},{7,3},{8,10},{9,13},{10,... | collective-permute-start | bytes 1769480 | tf_op jit(solution)/shard_map/ppermute | solution.py:838
  152.2 19.9 %collective-permute-start.43 = (bf16[192,1536]{1,0:T(8,128)(2,1)S(1)}, bf16[192,1536]{1,0:T(8,128)(2,1)S(1)}, u32[]{:S(2)}, u32[]{:S(2)}) collective-permute-start(bf16[192,1536]{1,0:T(8,128)(2,1)S(1)} %shard_map.259), channel_id=1, source_target_pairs={{0,2},{1,5},{2,0},{3,7},{4,6},{5,1},{6,4},{7,3},{8,10},{9,13},{10,... | collective-permute-start | bytes 1769480 | tf_op jit(solution)/shard_map/ppermute | solution.py:838
  153.3 14.3 %collective-permute-start.46 = (bf16[192,640]{1,0:T(8,128)(2,1)S(1)}, bf16[192,640]{1,0:T(8,128)(2,1)S(1)}, u32[]{:S(2)}, u32[]{:S(2)}) collective-permute-start(bf16[192,640]{1,0:T(8,128)(2,1)S(1)} %get-tuple-element.184), channel_id=1, source_target_pairs={{0,8},{1,9},{2,10},{3,11},{4,12},{5,13},{6,14},{7,15},{8,0},{9,1},... | collective-permute-start | bytes 737288 | tf_op jit(solution)/shard_map/ppermute | solution.py:838
  155.4 12.1 %collective-permute-start.45 = (bf16[96,896]{1,0:T(8,128)(2,1)S(1)}, bf16[96,896]{1,0:T(8,128)(2,1)S(1)}, u32[]{:S(2)}, u32[]{:S(2)}) collective-permute-start(bf16[96,896]{1,0:T(8,128)(2,1)S(1)} %get-tuple-element.182), channel_id=1, source_target_pairs={{0,16},{1,17},{2,18},{3,19},{4,20},{5,21},{6,22},{7,23},{8,24},{9,... | collective-permute-start | bytes 516104 | tf_op jit(solution)/shard_map/ppermute | solution.py:838
  172.5 18.0 %collective-permute-start.49 = (bf16[192,1536]{1,0:T(8,128)(2,1)S(1)}, bf16[192,1536]{1,0:T(8,128)(2,1)S(1)}, u32[]{:S(2)}, u32[]{:S(2)}) collective-permute-start(bf16[192,1536]{1,0:T(8,128)(2,1)S(1)} %get-tuple-element.186.refs_1_.refs_2_), channel_id=1, source_target_pairs={{0,4},{1,3},{2,6},{3,1},{4,0},{5,7},{6,2},{7,5},{8,12},{9,11},{10,... | collective-permute-start | bytes 1769480 | tf_op jit(solution)/shard_map/ppermute | solution.py:838
  173.4 17.2 %collective-permute-start.48 = (bf16[192,1664]{1,0:T(8,128)(2,1)S(1)}, bf16[192,1664]{1,0:T(8,128)(2,1)S(1)}, u32[]{:S(2)}, u32[]{:S(2)}) collective-permute-start(bf16[192,1664]{1,0:T(8,128)(2,1)S(1)} %shard_map.262), channel_id=1, source_target_pairs={{0,2},{1,5},{2,0},{3,7},{4,6},{5,1},{6,4},{7,3},{8,10},{9,13},{10,... | collective-permute-start | bytes 1916936 | tf_op jit(solution)/shard_map/ppermute | solution.py:838
  174.3 16.2 %collective-permute-start.50 = (bf16[96,1536]{1,0:T(8,128)(2,1)S(1)}, bf16[96,1536]{1,0:T(8,128)(2,1)S(1)}, u32[]{:S(2)}, u32[]{:S(2)}) collective-permute-start(bf16[96,1536]{1,0:T(8,128)(2,1)S(1)} %get-tuple-element.189), channel_id=1, source_target_pairs={{0,16},{1,17},{2,18},{3,19},{4,20},{5,21},{6,22},{7,23},{8,24},{9,... | collective-permute-start | bytes 884744 | tf_op jit(solution)/shard_map/ppermute | solution.py:838
  176.9 13.1 %collective-permute-start.52 = (bf16[96,640]{1,0:T(8,128)(2,1)S(1)}, bf16[96,640]{1,0:T(8,128)(2,1)S(1)}, u32[]{:S(2)}, u32[]{:S(2)}) collective-permute-start(bf16[96,640]{1,0:T(8,128)(2,1)S(1)} %get-tuple-element.194), channel_id=1, source_target_pairs={{0,2},{1,5},{2,0},{3,7},{4,6},{5,1},{6,4},{7,3},{8,10},{9,13},{10,... | collective-permute-start | bytes 368648 | tf_op jit(solution)/shard_map/ppermute | solution.py:838
  191.6 17.8 %collective-permute-start.56 = (bf16[192,1664]{1,0:T(8,128)(2,1)S(1)}, bf16[192,1664]{1,0:T(8,128)(2,1)S(1)}, u32[]{:S(2)}, u32[]{:S(2)}) collective-permute-start(bf16[192,1664]{1,0:T(8,128)(2,1)S(1)} %get-tuple-element.197.refs_1_), channel_id=1, source_target_pairs={{0,4},{1,3},{2,6},{3,1},{4,0},{5,7},{6,2},{7,5},{8,12},{9,11},{10,... | collective-permute-start | bytes 1916936 | tf_op jit(solution)/shard_map/ppermute | solution.py:838
  192.6 16.8 %collective-permute-start.55 = (bf16[192,1664]{1,0:T(8,128)(2,1)S(1)}, bf16[192,1664]{1,0:T(8,128)(2,1)S(1)}, u32[]{:S(2)}, u32[]{:S(2)}) collective-permute-start(bf16[192,1664]{1,0:T(8,128)(2,1)S(1)} %shard_map.268), channel_id=1, source_target_pairs={{0,2},{1,5},{2,0},{3,7},{4,6},{5,1},{6,4},{7,3},{8,10},{9,13},{10,... | collective-permute-start | bytes 1916936 | tf_op jit(solution)/shard_map/ppermute | solution.py:838
  193.6 15.8 %collective-permute-start.57 = (bf16[96,1536]{1,0:T(8,128)(2,1)S(1)}, bf16[96,1536]{1,0:T(8,128)(2,1)S(1)}, u32[]{:S(2)}, u32[]{:S(2)}) collective-permute-start(bf16[96,1536]{1,0:T(8,128)(2,1)S(1)} %get-tuple-element.205), channel_id=1, source_target_pairs={{0,16},{1,17},{2,18},{3,19},{4,20},{5,21},{6,22},{7,23},{8,24},{9,... | collective-permute-start | bytes 884744 | tf_op jit(solution)/shard_map/ppermute | solution.py:838
  195.7 13.7 %collective-permute-start.59 = (bf16[48,1536]{1,0:T(8,128)(2,1)S(1)}, bf16[48,1536]{1,0:T(8,128)(2,1)S(1)}, u32[]{:S(2)}, u32[]{:S(2)}) collective-permute-start(bf16[48,1536]{1,0:T(8,128)(2,1)S(1)} %get-tuple-element.209), channel_id=1, source_target_pairs={{0,8},{1,9},{2,10},{3,11},{4,12},{5,13},{6,14},{7,15},{8,0},{9,1},... | collective-permute-start | bytes 442376 | tf_op jit(solution)/shard_map/ppermute | solution.py:838
  196.6 12.8 %collective-permute-start.58 = (bf16[48,640]{1,0:T(8,128)(2,1)S(1)}, bf16[48,640]{1,0:T(8,128)(2,1)S(1)}, u32[]{:S(2)}, u32[]{:S(2)}) collective-permute-start(bf16[48,640]{1,0:T(8,128)(2,1)S(1)} %get-tuple-element.207), channel_id=1, source_target_pairs={{0,4},{1,3},{2,6},{3,1},{4,0},{5,7},{6,2},{7,5},{8,12},{9,11},{10,... | collective-permute-start | bytes 184328 | tf_op jit(solution)/shard_map/ppermute | solution.py:838
  211.0 12.0 %collective-permute-start.60 = (bf16[48,3200]{1,0:T(8,128)(2,1)S(1)}, bf16[48,3200]{1,0:T(8,128)(2,1)S(1)}, u32[]{:S(2)}, u32[]{:S(2)}) collective-permute-start(bf16[48,3200]{1,0:T(8,128)(2,1)S(1)} %get-tuple-element.211), channel_id=1, source_target_pairs={{0,8},{1,9},{2,10},{3,11},{4,12},{5,13},{6,14},{7,15},{8,0},{9,1},... | collective-permute-start | bytes 921608 | tf_op jit(solution)/shard_map/ppermute | solution.py:838
  212.7 11.2 %collective-permute-start.61 = (bf16[48,1664]{1,0:T(8,128)(2,1)}, bf16[48,1664]{1,0:T(8,128)(2,1)S(1)}, u32[]{:S(2)}, u32[]{:S(2)}) collective-permute-start(bf16[48,1664]{1,0:T(8,128)(2,1)} %copy-done.17), channel_id=1, source_target_pairs={{0,16},{1,17},{2,18},{3,19},{4,20},{5,21},{6,22},{7,23},{8,24},{9,... | collective-permute-start | bytes 479240 | tf_op jit(solution)/shard_map/ppermute | solution.py:838
  213.6 14.3 %collective-permute-start.62 = (bf16[48,1664]{1,0:T(8,128)(2,1)S(1)}, bf16[48,1664]{1,0:T(8,128)(2,1)S(1)}, u32[]{:S(2)}, u32[]{:S(2)}) collective-permute-start(bf16[48,1664]{1,0:T(8,128)(2,1)S(1)} %get-tuple-element.213), channel_id=1, source_target_pairs={{0,24},{1,25},{2,26},{3,27},{4,28},{5,29},{6,30},{7,31},{8,16},{9,... | collective-permute-start | bytes 479240 | tf_op jit(solution)/shard_map/ppermute | solution.py:838
  (57 other events, 341.2 us)

commit v8 on v7

--- a/solution.py
+++ b/solution.py
@@ -222,17 +222,19 @@
                 targets[o][pl.ds(row, blk), :] = pieces[q][r * blk : (r + 1) * blk, lo:hi]
 
 
-def place_levels(near, far, offs_ref, step, shift, target):
-    blk = near.shape[0] // 8
-    lo = 0
-    for level, src in ((0, near), *((2, part) for part in far)):
-        at = 0 if level == 0 else lo
-        for q in range(4):
-            for r in range(2):
-                row = pl.multiple_of(offs_ref[0, q * 4 + level + r] * step + shift, 16)
-                rows = slice((r * 4 + q) * blk, (r * 4 + q + 1) * blk)
-                target[pl.ds(row, blk), at : at + src.shape[1]] = src[rows, :]
-        lo += src.shape[1] if level else 0
+def place_last(own, far, near, offs_ref, target):
+    blk = own.shape[0] // 4
+    for q in range(4):
+        for r in range(4):
+            at = q * blk + (own.shape[0] if r == 3 else 0)
+            for (lo, width), part in zip(CUTS, near):
+                src, base = ((own, lo), (part, 0), (far, lo), (part, 0))[r]
+                for first, end, shift, col in ((0, D, blk, 0), (D, LAST, 0, FIRST - D)):
+                    a, b = max(lo, first), min(lo + width, end)
+                    if a < b:
+                        row = pl.multiple_of(offs_ref[0, q * 4 + r] * (2 * blk) + shift, 16)
+                        values = src[at if r % 2 else q * blk : (at if r % 2 else q * blk) + blk, base + a - lo : base + b - lo]
+                        target[pl.ds(row, blk), a + col : b + col] = values
 
 
 def place_rows(pieces, offs, which, cols, shape, hold=()):
@@ -293,7 +295,8 @@
         for dst in outs:
             width = dst.shape[1]
             dst[b * rows : (b + 1) * rows, :] = jnp.where(c == 0, top[:, :width], under[:, :width])
-    last[...] = wout[2 * rows :, :]
+    last[:, :D] = wout[2 * rows :, :]
+    last[:, D:] = wout[0 : 2 * rows, FIRST:]
 
 
 def order_mlp_kernel(core, keep, got, wout, three):
@@ -301,7 +304,7 @@
     rows, width = keep.shape
     for b, (top, under) in enumerate(((keep, got), (got, keep))):
         three[b * rows : (b + 1) * rows, :width] = jnp.where(c == 0, top[...], under[...])
-    three[:, width:] = wout[0 : 2 * rows, :]
+    three[:, width:] = wout[0 : 2 * rows, :FIRST]
 
 
 def cats(jobs, after=()):
@@ -478,11 +481,11 @@
     loop(4, step)
 
 
-def mlp_kernel(offs, pieces, near, far, g, slope, win, hidden, own, comb, ginner, wout):
+def mlp_kernel(offs, pieces, plane, far, near, g, slope, win, hidden, own, comb, ginner, wout):
     half = own.shape[0]
     blk = D // 16
-    place(pieces, offs, 0, [(0, D, 0, 2 * blk, 0)], (wout,))
-    place_levels(near, far, offs, 2 * blk, blk, wout)
+    place(pieces, offs, 0, [(0, FIRST, 0, 2 * blk, 0)], (wout.at[:, :FIRST],))
+    place_last(plane, far, near, offs, wout)
     g, slope, win = ready(g, slope, win)
 
     def back(b):
@@ -507,15 +510,16 @@
             row, rows = (4 * i + k // 2) * blk, slice(k * blk, (k + 1) * blk)
             if k % 2:
                 dz[row : row + blk, :] = part[rows, :LEVELS]
-                dw[row : row + blk, D:] = part[rows, LEVELS:]
+                if LEVELS < D:
+                    dw[row : row + blk, D:] = part[rows, LEVELS:]
             else:
                 dw[row : row + blk, :D] = part[rows]
     send_out(dw, offs, (own, a, b, ab))
     for q in range(4):
         for r in range(4):
             rows = pl.ds(pl.multiple_of(offs[0, q * 4 + r] * blk, 16), blk)
-            at = ((r % 2) * 4 + q) * blk
-            if r < 2:
+            at = ((r // 2) * 4 + q) * blk
+            if r % 2 == 0:
                 near[at : at + blk, :] = dz[rows, :]
                 continue
             for dst, (lo, width) in zip(far, FAR_CUTS):
@@ -523,9 +527,9 @@
 
 
 def mlp_and_grad_kernel(
-    offs, pown, pa, pb, pab, near, far_a, far_b, g, slope, win, hidden, third, own, comb, d_own, d_a, d_b, d_ab, ginner, wout, dw
+    offs, pown, pa, pb, pab, plane, far, near_a, near_b, g, slope, win, hidden, third, own, comb, d_own, d_a, d_b, d_ab, ginner, wout, dw
 ):
-    mlp_kernel(offs, (pown, pa, pb, pab), near, (far_a, far_b), g, slope, win, hidden, own, comb, ginner, wout)
+    mlp_kernel(offs, (pown, pa, pb, pab), plane, far, (near_a, near_b), g, slope, win, hidden, own, comb, ginner, wout)
     dmlpin_kernel(offs, third, ginner, d_own, d_a, d_b, d_ab, dw)
 
 
@@ -822,8 +826,10 @@
         out[:, (2 * k + 1) * hr : (2 * k + 2) * hr] = jnp.where(c == 0, b, a)
 
 
-CUTS = ((0, 512), (512, 256))
-FAR_CUTS = ((0, 128), (128, 512))
+FIRST = 512
+LAST = 2 * D - FIRST
+CUTS = ((0, 512), (512, 512))
+FAR_CUTS = ((0, 256), (256, 384))
 LEVELS = 640
 
 
@@ -953,7 +959,7 @@
         return kernel_call(
             mlp_and_grad_kernel,
             [offs, *pieces, g, slope, w_in, hidden, third],
-            [SM] + [VM] * 12,
+            [SM] + [VM] * 13,
             [sds((rows, D), BF), sds((3 * rows, D), BF)] + [sds((4 * wb, fh), BF)] * 4,
             scratch=[pltpu.VMEM((r2, fh), BF), pltpu.VMEM((fh, D), BF), pltpu.VMEM((D, fh), BF)],
             cost=11,
@@ -1054,7 +1060,7 @@
             order_kernel,
             [core, keep, sib(send), mlp_out],
             [SM] + [VM] * 3,
-            [sds((2 * wr, D), BF), sds((2 * wr, width), BF), sds((2 * wr, widths[0]), BF)],
+            [sds((2 * wr, LAST), BF), sds((2 * wr, width), BF), sds((2 * wr, widths[0]), BF)],
             cost=1,
             after=[pairs[1], pairs[3]],
         )
@@ -1074,7 +1080,7 @@
             pack_inner_kernel, [core, mlp_in], [SM, VM], [sds((wr, fh), BF)] * 2, cost=1, after=(one,)
         )
         (three,) = kernel_call(
-            order_mlp_kernel, [core, keep, sib(send), mlp_out], [SM] + [VM] * 3, [sds((2 * wr, 6 * DH), BF)], cost=1
+            order_mlp_kernel, [core, keep, sib(send), mlp_out], [SM] + [VM] * 3, [sds((2 * wr, 4 * DH + FIRST), BF)], cost=1
         )
         ab_last = tie(a_last, one)
         a1, b1, far_two, near_three, ab_last = side_a(one), side_b(one), far(two), near(three), side_b(ab_last)
@@ -1082,38 +1088,38 @@
         two, last, three = cats(
             [whole(two, far_two), whole(last, a_last, b_last, ab_last), whole(three, near_three)], after=(a1,)
         )
-        ab1, a2, b2, far_three, near_last = side_b(a1), side_a(two), side_b(two), far(three), near(last)
+        ab1, a2, b2, far_three = side_b(a1), side_a(two), side_b(two), far(three)
         a2 = tie(a2, b2, ab1)
-        three, four, last, *parts = cats(
+        three, four = cats(
             [
                 [(three, 0, 4 * DH), (far_three, 0, 4 * DH)],
-                [(three, 4 * DH, D), (far_three, 4 * DH, D)],
-                whole(last, near_last),
-                *([(last, lo, width), (near_last, lo, width)] for lo, width in CUTS),
+                [(three, 4 * DH, FIRST), (far_three, 4 * DH, FIRST)],
             ],
             after=(a2,),
         )
         out = out_rows([one, a1, b1, ab1], offs, 3 * DH)
         out = (out, sib(out))
         three, a2 = tie(three, out[1]), tie(a2, out[1])
-        ab2, a3, b3, far_a = side_b(a2), side_a(three), side_b(three), far(tie(parts[0], out[1]))
+        last = tie(last, out[1])
+        ab2, a3, b3, far_last = side_b(a2), side_a(three), side_b(three), far(last)
         first, packed, probs, comb, vec, w_qkv = self_attention([one, a1, b1, ab1], lens, xhat, *out, after=(three,))
-        a3 = tie(a3, b3, ab2, comb, far_a)
+        cout = out_rows([two, a2, b2, ab2], offs, 0)
+        a3 = tie(a3, b3, comb, far_last, cout)
         four = tie(four, a3)
+        parts = cats([[(last, lo, width), (far_last, lo, width)] for lo, width in CUTS], after=(four,))
         comb = tie(comb, four)
-        cout = out_rows([two, a2, b2, ab2], offs, 0)
         cout = (cout, sib(cout))
         self_mixed = (comb, sib(comb))
-        ab3, a4, b4, far_b = side_b(a3), side_a(four), side_b(four), far(tie(parts[1], four))
+        ab3, a4, b4, near_a = side_b(a3), side_a(four), side_b(four), near(parts[0])
         kv, w_ckv, w_cq, resid_one, second, cq, cprobs, comb = cross_attention(
             [two, a2, b2, ab2], mem, vec, tok, *self_mixed, *cout
         )
-        comb = tie(comb, ab3, a4, b4, far_b)
-        cross_mixed, ab4 = (comb, sib(comb)), side_b(tie(a4, comb))
+        comb = tie(comb, ab3, a4, b4, near_a)
+        cross_mixed, ab4, near_b = (comb, sib(comb)), side_b(tie(a4, comb)), near(tie(parts[1], comb))
         hold = [kv, cprobs, cq, w_cq, *cout, w_ckv, second]
         w_in = inner_weight([three, a3, b3, ab3], hold)
         resid_two, third, hidden, slope = inner_part(resid_one, *cross_mixed, vec, w_in, hold)
-        last = [four, a4, b4, ab4, last, far_a, far_b]
+        last = [four, a4, b4, ab4, last, far_last, near_a, near_b]
     else:
         tok, g, mem, xhat = prepare(lens, pairs)
         everywhere = lambda w: lax.all_gather(w, AXES, axis=0, tiled=True)
@@ -1133,9 +1139,11 @@
         rowed = everywhere(mlp_out).reshape(moves.n // 2, 2, hr, D)
         rowed = lax.dynamic_index_in_dim(rowed, c, 1, keepdims=False).reshape(16, 2, fh // 32, D)
         rowed = rowed.transpose(1, 0, 2, 3)
-        levels = rowed[1].reshape(4, 4, wb, D).transpose(1, 0, 2, 3).reshape(D, D)
-        last = split(rowed[0].reshape(D, D)) + [levels[: D // 2]]
-        last += [levels[D // 2 :, lo : lo + width] for lo, width in CUTS]
+        levels = jnp.concatenate([rowed[1].reshape(D, D), rowed[0].reshape(D, D)[:, FIRST:]], 1)
+        levels = levels.reshape(4, 4, wb, LAST).transpose(1, 0, 2, 3).reshape(4, 4 * wb, LAST)
+        odd = levels[1::2].reshape(8 * wb, LAST)
+        last = split(rowed[0].reshape(D, D)[:, :FIRST]) + [levels[0], levels[2]]
+        last += [odd[:, lo : lo + width] for lo, width in CUTS]
         hold = ()
         first, packed, probs, comb, vec, w_qkv = self_attention(one, lens, xhat, *out)
         self_mixed = (comb, sib(comb))
@@ -1163,12 +1171,12 @@
         hold=[*hold, *held, third],
     )
     if fast:
-        got_ab1, got_z1 = side_a(d_mlpout[3]), far(d_mlpout[5])
+        got_ab1, got_z1 = side_a(d_mlpout[3]), near(d_mlpout[5])
     part, comb, *d_mlpin = mlp_part(last, g, slope, w_in, hidden, third, after=d_mlpout[:1], hold=[*hold, *held])
     if fast:
         (on,) = merge([("pass", d_mlpout[2], got_ab1)], after=(part, got_z1))
         comb = tie(comb, on)
-        got_b1, got_a1, got_z2 = side_b(on), side_a(tie(d_mlpout[1], on)), far(tie(d_mlpout[6], on))
+        got_b1, got_a1, got_z2 = side_b(on), side_a(tie(d_mlpout[1], on)), near(tie(d_mlpout[6], on))
         got_ab2, got_a2 = side_a(tie(d_mlpin[3], on)), side_a(tie(d_mlpin[1], on))
         after = (on,)
     recv = sib(comb)
@@ -1183,7 +1191,7 @@
             after=(dvec_two, got_a2),
         )
         gsecond = tie(gsecond, on)
-        got_b2, got_far1, got_near_z = side_b(on), far(on_far), near(on_z)
+        got_b2, got_far1, got_far_z = side_b(on), far(on_far), far(on_z)
         got_ab3, got_a3 = side_a(tie(d_cross[3], on)), side_a(tie(d_cross[1], on))
         after = (on,)
     recv = sib(gsecond)
@@ -1194,7 +1202,7 @@
                 ("pass", d_cross[2], got_ab3),
                 ("half", d_mlpin[0], got_a2, got_b2),
                 ("near", kept1, got_far1),
-                ("columns", kept_z, got_near_z),
+                ("columns", kept_z, got_far_z),
             ],
             after=(gfirst, got_a3),
         )
@@ -1285,7 +1293,8 @@
         own_gains, own_biases = vectors[:3], vectors[3:]
         grad_in = joined(placed(d_mlpin), 0, fh, ff // (2 * hr))
         first_rows = jnp.concatenate(d_mlpout[:4], 0)
-        levels = jnp.concatenate([d_mlpout[4], jnp.concatenate(d_mlpout[5:], 1)], 0).reshape(4, 4, wb, LEVELS)
+        levels = jnp.stack([d_mlpout[4], jnp.concatenate(d_mlpout[5:], 1)], 0).reshape(2, 2, 4, wb, LEVELS)
+        levels = levels.transpose(1, 0, 2, 3, 4).reshape(4, 4, wb, LEVELS)
         levels = jnp.concatenate([levels.transpose(1, 0, 2, 3).reshape(D, LEVELS), first_rows[:, D:]], 1)
         term = jnp.stack([first_rows[:, :D].reshape(16, wb, D), levels.reshape(16, wb, D)], 1).astype(F32)
         term = term.reshape(moves.n // 2, 1, hr, D)

time: 231 us -> 229 us (level)
  waiting for transfers between devices: 83.9 us -> 80.7 us
    ppermute x66, waiting for transfers between devices: 83.9 us -> 80.7 us  [permute(): lax.ppermute(x, AXES, [(a, z * self.nf + 2 * yx + c) for a, (z, yx, c) in...]
    unnamed x82 -> x80, local copies, waits for them, and re-layouts: 6.95 us -> 6.23 us
    pallas_call x30 -> x31, Pallas kernels: 71.2 us -> 71.2 us  [kernel_call(): pl.pallas_call(run, out_shape=list(outs), in_specs=[space(spec) for spec...]
where the time goes in v8:
time: 229 us
  waiting for transfers between devices  80.7 us (35%)
  Pallas kernels  71.2 us (31%)
  starting transfers between devices  66.2 us (29%)
  local copies, waits for them, and re-layouts  8.06 us (4%)
    ppermute x66, waiting for transfers between devices, permute(): lax.ppermute(x, AXES, [(a, z * self.nf + 2 * yx + c) for a, (z, yx, c) in...  80.7 us
    pallas_call x31, Pallas kernels, kernel_call(): pl.pallas_call(run, out_shape=list(outs), in_specs=[space(spec) for spec...  71.2 us
    ppermute x66, starting transfers between devices, permute(): lax.ppermute(x, AXES, [(a, z * self.nf + 2 * yx + c) for a, (z, yx, c) in...  66.2 us
    unnamed x80, local copies, waits for them, and re-layouts  6.23 us
  transfers between devices with their start and end apart: 66, of which 23 were waited for; matrix products, arithmetic and copies ran while one was open for 3% of the time, Pallas kernels for 30%

profile of v8, /device:TPU:0, one launch (start us, length us, event | category | flops | bytes accessed | tf_op | source)
XLA Modules:
  0.0 228.6 jit_solution(13397111150427604567)
XLA Ops:
  1.7 1.9 shard_map.220
  4.1 1.5 copy.54.refs_5_
  5.9 3.7 %collective-permute-start.5 = (bf16[48,1664]{1,0:T(8,128)(2,1)S(1)}, bf16[48,1664]{1,0:T(8,128)(2,1)S(1)}, u32[]{:S(2)}, u32[]{:S(2)}) collective-permute-start(bf16[48,1664]{1,0:T(8,128)(2,1)S(1)} %get-tuple-element.119.refs_7_.refs_0_), channel_id=1, source_target_pairs={{0,16},{1,17},{2,18},{3,19},{4,20},{5,21},{6,22},{7,23},{8,24},{9,... | collective-permute-start | bytes 479240 | tf_op jit(solution)/shard_map/ppermute | solution.py:844
  9.6 1.3 collective-permute-start.6
  11.2 1.5 copy.55.refs_6_
  12.8 1.8 shard_map.222
  14.6 1.6 copy-done.27
  16.2 1.5 collective-permute-start.8
  17.7 1.5 collective-permute-start.9
  19.3 2.2 collective-permute-done.5.refs_2_
  21.5 4.2 %collective-permute-done.4.refs_1_.refs_5_ = bf16[48,3200]{1,0:T(8,128)(2,1)S(1)} collective-permute-done((bf16[48,3200]{1,0:T(8,128)(2,1)S(1)}, bf16[48,3200]{1,0:T(8,128)(2,1)S(1)}, u32[]{:S(2)}, u32[]{:S(2)}) %collective-permute-start.4) | collective-permute-done | bytes 307232 | tf_op jit(solution)/shard_map/ppermute | solution.py:844
  26.7 1.6 collective-permute-start.10
  28.2 1.5 collective-permute-start.11
  29.8 1.6 collective-permute-start.14
  31.4 2.5 %collective-permute-start.17 = (bf16[48,2048]{1,0:T(8,128)(2,1)S(1)}, bf16[48,2048]{1,0:T(8,128)(2,1)S(1)}, u32[]{:S(2)}, u32[]{:S(2)}) collective-permute-start(bf16[48,2048]{1,0:T(8,128)(2,1)S(1)} %shard_map.229.refs_6_), channel_id=1, source_target_pairs={{0,8},{1,9},{2,10},{3,11},{4,12},{5,13},{6,14},{7,15},{8,0},{9,1},... | collective-permute-start | bytes 589832 | tf_op jit(solution)/shard_map/ppermute | solution.py:844
  34.5 8.6 %collective-permute-done.10.refs_0_ = bf16[192,1664]{1,0:T(8,128)(2,1)S(1)} collective-permute-done((bf16[192,1664]{1,0:T(8,128)(2,1)S(1)}, bf16[192,1664]{1,0:T(8,128)(2,1)S(1)}, u32[]{:S(2)}, u32[]{:S(2)}) %collective-permute-start.10) | collective-permute-done | bytes 639008 | tf_op jit(solution)/shard_map/ppermute | solution.py:844
  43.5 2.1 collective-permute-start.12
  45.9 1.3 collective-permute-start.19
  47.8 1.6 collective-permute-start.18
  49.3 10.5 %collective-permute-done.12.refs_4_.refs_2_.refs_6_ = bf16[192,1664]{1,0:T(8,128)(2,1)S(1)} collective-permute-done((bf16[192,1664]{1,0:T(8,128)(2,1)S(1)}, bf16[192,1664]{1,0:T(8,128)(2,1)S(1)}, u32[]{:S(2)}, u32[]{:S(2)}) %collective-permute-start.12) | collective-permute-done | bytes 639008 | tf_op jit(solution)/shard_map/ppermute | solution.py:844
  60.5 1.8 collective-permute-done.19.refs_0_
  62.2 4.3 %collective-permute-done.20.refs_1_.refs_3_ = bf16[192,1536]{1,0:T(8,128)(2,1)S(1)} collective-permute-done((bf16[192,1536]{1,0:T(8,128)(2,1)S(1)}, bf16[192,1536]{1,0:T(8,128)(2,1)S(1)}, u32[]{:S(2)}, u32[]{:S(2)}) %collective-permute-start.20) | collective-permute-done | bytes 589856 | tf_op jit(solution)/shard_map/ppermute | solution.py:844
  68.5 1.6 collective-permute-start.23
  70.5 1.3 collective-permute-start.24
  71.8 7.4 %shard_map.234 = (bf16[512,768]{1,0:T(8,128)(2,1)S(1)}, bf16[512,1152]{1,0:T(8,128)(2,1)S(1)}, bf16[8,64,384]{2,1,0:T(8,128)(2,1)S(1)}, bf16[512,1152]{1,0:T(8,1...) custom-call(s32[8]{0:T(128)S(1)} %pad_add_fusion.1.refs_0_, s32[1]{0:T(128)} %bitcast.2.refs_0_.refs_1_.refs_6_, ...), custom_call_target="tpu_custom_call" | custom-call | flops 41999998976 | tf_op jit(solution)/shard_map/pallas_call | solution.py:97
  79.3 9.3 %collective-permute-done.21.refs_4_ = bf16[192,1536]{1,0:T(8,128)(2,1)S(1)} collective-permute-done((bf16[192,1536]{1,0:T(8,128)(2,1)S(1)}, bf16[192,1536]{1,0:T(8,128)(2,1)S(1)}, u32[]{:S(2)}, u32[]{:S(2)}) %collective-permute-start.21) | collective-permute-done | bytes 589856 | tf_op jit(solution)/shard_map/ppermute | solution.py:844
  93.5 10.3 %shard_map.241 = (bf16[1920,768]{1,0:T(8,128)(2,1)S(1)}, bf16[768,768]{1,0:T(8,128)(2,1)S(1)}, bf16[768,384]{1,0:T(8,128)(2,1)S(1)}, f32[512,768]{1,0:T(8,128)S(...) custom-call(s32[2,16]{1,0:T(2,128)S(1)} %pad_add_fusion.refs_0_.refs, ...), custom_call_target="tpu_custom_call" | custom-call | flops 83999997952 | tf_op jit(solution)/shard_map/pallas_call | solution.py:97
  107.9 3.4 %shard_map.245 = (f32[512,768]{1,0:T(8,128)S(1)}, bf16[512,768]{1,0:T(8,128)(2,1)S(1)}, bf16[512,1536]{1,0:T(8,128)(2,1)S(1)}, bf16[512,1536]{1,0:T(8,128)(2,1)S(1)}) custom-call(f32[512,768]{1,0:T(8,128)S(1)} %get-tuple-element.136.refs_0_.refs_3_, bf16[512,1152]{1,0:T(8,128)(2,1)S(1)} %shard_map.243.refs_1_.refs_14_, ...), custom_call_target="tpu_custom_call" | custom-call | flops 35000000512 | tf_op jit(solution)/shard_map/pallas_call | solution.py:97
  111.3 2.2 shard_map.248
  116.3 6.8 %shard_map.249 = (bf16[256,768]{1,0:T(8,128)(2,1)S(1)}, bf16[768,768]{1,0:T(8,128)(2,1)S(1)}, bf16[192,1536]{1,0:T(8,128)(2,1)S(1)}, bf16[192,1536]{1,0:T(8,128)...) custom-call(s32[2,16]{1,0:T(2,128)S(1)} %pad_add_fusion.refs_0_.refs_2_, ...), custom_call_target="tpu_custom_call" | custom-call | flops 76999999488 | tf_op jit(solution)/shard_map/pallas_call | solution.py:97
  128.7 14.4 %shard_map.252 = (bf16[256,768]{1,0:T(8,128)(2,1)}, f32[512,768]{1,0:T(8,128)S(1)}, bf16[512,768]{1,0:T(8,128)(2,1)S(1)}, f32[8,768]{1,0:T(8,128)S(1)}, bf16[192...) custom-call(s32[2,16]{1,0:T(2,128)S(1)} %pad_add_fusion.refs_0_.refs, ...), custom_call_target="tpu_custom_call" | custom-call | flops 98000003072 | tf_op jit(solution)/shard_map/pallas_call | solution.py:97
  143.1 3.3 %collective-permute-done.37.refs_1_ = bf16[192,1536]{1,0:T(8,128)(2,1)S(1)} collective-permute-done((bf16[192,1536]{1,0:T(8,128)(2,1)S(1)}, bf16[192,1536]{1,0:T(8,128)(2,1)S(1)}, u32[]{:S(2)}, u32[]{:S(2)}) %collective-permute-start.37) | collective-permute-done | bytes 589856 | tf_op jit(solution)/shard_map/ppermute | solution.py:844
  150.5 2.8 %collective-permute-start.46 = (bf16[192,640]{1,0:T(8,128)(2,1)S(1)}, bf16[192,640]{1,0:T(8,128)(2,1)S(1)}, u32[]{:S(2)}, u32[]{:S(2)}) collective-permute-start(bf16[192,640]{1,0:T(8,128)(2,1)S(1)} %get-tuple-element.182), channel_id=1, source_target_pairs={{0,16},{1,17},{2,18},{3,19},{4,20},{5,21},{6,22},{7,23},{8,24},{9,... | collective-permute-start | bytes 737288 | tf_op jit(solution)/shard_map/ppermute | solution.py:844
  153.5 11.6 %shard_map.259 = (f32[256,768]{1,0:T(8,128)S(1)}, bf16[256,768]{1,0:T(8,128)(2,1)S(1)}, bf16[256,768]{1,0:T(8,128)(2,1)S(1)}, bf16[192,1664]{1,0:T(8,128)(2,1)S(...) custom-call(s32[2,16]{1,0:T(2,128)S(1)} %pad_add_fusion.refs_0_.refs_2_, ...), custom_call_target="tpu_custom_call" | custom-call | flops 76999999488 | tf_op jit(solution)/shard_map/pallas_call | solution.py:97
  165.0 6.4 %collective-permute-done.45.refs_6_ = bf16[96,896]{1,0:T(8,128)(2,1)S(1)} collective-permute-done((bf16[96,896]{1,0:T(8,128)(2,1)S(1)}, bf16[96,896]{1,0:T(8,128)(2,1)S(1)}, u32[]{:S(2)}, u32[]{:S(2)}) %collective-permute-start.45) | collective-permute-done | bytes 172064 | tf_op jit(solution)/shard_map/ppermute | solution.py:844
  175.3 3.1 %collective-permute-start.51 = (bf16[48,896]{1,0:T(8,128)(2,1)S(1)}, bf16[48,896]{1,0:T(8,128)(2,1)S(1)}, u32[]{:S(2)}, u32[]{:S(2)}) collective-permute-start(bf16[48,896]{1,0:T(8,128)(2,1)S(1)} %get-tuple-element.189), channel_id=1, source_target_pairs={{0,8},{1,9},{2,10},{3,11},{4,12},{5,13},{6,14},{7,15},{8,0},{9,1},... | collective-permute-start | bytes 258056 | tf_op jit(solution)/shard_map/ppermute | solution.py:844
  178.5 2.5 %shard_map.264 = (bf16[960,768]{1,0:T(8,128)(2,1)S(1)}, bf16[960,768]{1,0:T(8,128)(2,1)S(1)}) custom-call(bf16[1920,768]{1,0:T(8,128)(2,1)S(1)} %get-tuple-element.193.refs_0_, bf16[768,768]{1,0:T(8,128)(2,1)S(1)} %get-tuple-element.143.refs_11_.refs_9_.refs_21_.refs_1_, bf16[192,1536]{1,0:T(8,128)(2,1)S(1)} %get-tuple-element.184.refs_1_.refs_2_), custom_call_target="tpu_custom_call" | custom-call | flops 20999999488 | tf_op jit(solution)/shard_map/pallas_call | solution.py:97
  181.0 1.8 collective-permute-done.51.refs_8_
  182.7 5.9 %collective-permute-done.52.refs_11_ = bf16[96,640]{1,0:T(8,128)(2,1)S(1)} collective-permute-done((bf16[96,640]{1,0:T(8,128)(2,1)S(1)}, bf16[96,640]{1,0:T(8,128)(2,1)S(1)}, u32[]{:S(2)}, u32[]{:S(2)}) %collective-permute-start.52) | collective-permute-done | bytes 122912 | tf_op jit(solution)/shard_map/ppermute | solution.py:844
  190.7 1.5 collective-permute-start.55
  193.3 1.9 collective-permute-start.59
  196.2 2.2 shard_map.268
  198.3 9.5 %collective-permute-done.58.refs_6_ = bf16[48,640]{1,0:T(8,128)(2,1)S(1)} collective-permute-done((bf16[48,640]{1,0:T(8,128)(2,1)S(1)}, bf16[48,640]{1,0:T(8,128)(2,1)S(1)}, u32[]{:S(2)}, u32[]{:S(2)}) %collective-permute-start.58) | collective-permute-done | bytes 61472 | tf_op jit(solution)/shard_map/ppermute | solution.py:844
  209.5 3.1 %collective-permute-start.61 = (bf16[48,1664]{1,0:T(8,128)(2,1)}, bf16[48,1664]{1,0:T(8,128)(2,1)S(1)}, u32[]{:S(2)}, u32[]{:S(2)}) collective-permute-start(bf16[48,1664]{1,0:T(8,128)(2,1)} %copy-done.19), channel_id=1, source_target_pairs={{0,16},{1,17},{2,18},{3,19},{4,20},{5,21},{6,22},{7,23},{8,24},{9,... | collective-permute-start | bytes 479240 | tf_op jit(solution)/shard_map/ppermute | solution.py:844
  212.7 1.3 collective-permute-start.62
  214.1 1.6 copy.57
  216.5 6.3 %collective-permute-done.60.refs_1_ = bf16[48,3200]{1,0:T(8,128)(2,1)S(1)} collective-permute-done((bf16[48,3200]{1,0:T(8,128)(2,1)S(1)}, bf16[48,3200]{1,0:T(8,128)(2,1)S(1)}, u32[]{:S(2)}, u32[]{:S(2)}) %collective-permute-start.60) | collective-permute-done | bytes 307232 | tf_op jit(solution)/shard_map/ppermute | solution.py:844
  223.6 2.4 %collective-permute-done.62.refs_5_ = bf16[48,1664]{1,0:T(8,128)(2,1)S(1)} collective-permute-done((bf16[48,1664]{1,0:T(8,128)(2,1)S(1)}, bf16[48,1664]{1,0:T(8,128)(2,1)S(1)}, u32[]{:S(2)}, u32[]{:S(2)}) %collective-permute-start.62) | collective-permute-done | bytes 159776 | tf_op jit(solution)/shard_map/ppermute | solution.py:844
  (237 shorter events, 43.4 us)
Async XLA Ops:
  1.2 10.0 %collective-permute-start.7 = (bf16[4,228,768]{2,0,1:T(4,128)(2,1)}, bf16[4,228,768]{2,0,1:T(4,128)(2,1)}, u32[]{:S(2)}, u32[]{:S(2)}) collective-permute-start(bf16[4,228,768]{2,0,1:T(4,128)(2,1)} %param.14), channel_id=1, source_target_pairs={{0,1},{1,0},{2,3},{3,2},{4,5},{5,4},{6,7},{7,6},{8,9},{9,8},{10,11... | collective-permute-start | bytes 4202504 | tf_op jit(solution)/shard_map/ppermute | solution.py:844
  5.9 15.6 %collective-permute-start.5 = (bf16[48,1664]{1,0:T(8,128)(2,1)S(1)}, bf16[48,1664]{1,0:T(8,128)(2,1)S(1)}, u32[]{:S(2)}, u32[]{:S(2)}) collective-permute-start(bf16[48,1664]{1,0:T(8,128)(2,1)S(1)} %get-tuple-element.119.refs_7_.refs_0_), channel_id=1, source_target_pairs={{0,16},{1,17},{2,18},{3,19},{4,20},{5,21},{6,22},{7,23},{8,24},{9,... | collective-permute-start | bytes 479240 | tf_op jit(solution)/shard_map/ppermute | solution.py:844
  9.6 11.9 %collective-permute-start.6 = (bf16[48,1664]{1,0:T(8,128)(2,1)S(1)}, bf16[48,1664]{1,0:T(8,128)(2,1)S(1)}, u32[]{:S(2)}, u32[]{:S(2)}) collective-permute-start(bf16[48,1664]{1,0:T(8,128)(2,1)S(1)} %get-tuple-element.119.refs_7_.refs_0_), channel_id=1, source_target_pairs={{0,24},{1,25},{2,26},{3,27},{4,28},{5,29},{6,30},{7,31},{8,16},{9,... | collective-permute-start | bytes 479240 | tf_op jit(solution)/shard_map/ppermute | solution.py:844
  11.0 14.7 %collective-permute-start.4 = (bf16[48,3200]{1,0:T(8,128)(2,1)S(1)}, bf16[48,3200]{1,0:T(8,128)(2,1)S(1)}, u32[]{:S(2)}, u32[]{:S(2)}) collective-permute-start(bf16[48,3200]{1,0:T(8,128)(2,1)S(1)} %get-tuple-element.120.refs_8_.refs_4_), channel_id=1, source_target_pairs={{0,8},{1,9},{2,10},{3,11},{4,12},{5,13},{6,14},{7,15},{8,0},{9,1},... | collective-permute-start | bytes 921608 | tf_op jit(solution)/shard_map/ppermute | solution.py:844
  16.2 9.5 %collective-permute-start.8 = (bf16[48,1024]{1,0:T(8,128)(2,1)S(1)}, bf16[48,1024]{1,0:T(8,128)(2,1)S(1)}, u32[]{:S(2)}, u32[]{:S(2)}) collective-permute-start(bf16[48,1024]{1,0:T(8,128)(2,1)S(1)} %shard_map.223.refs_2_), channel_id=1, source_target_pairs={{0,2},{1,5},{2,0},{3,7},{4,6},{5,1},{6,4},{7,3},{8,10},{9,13},{10,... | collective-permute-start | bytes 294920 | tf_op jit(solution)/shard_map/ppermute | solution.py:844
  26.7 16.5 %collective-permute-start.10 = (bf16[192,1664]{1,0:T(8,128)(2,1)S(1)}, bf16[192,1664]{1,0:T(8,128)(2,1)S(1)}, u32[]{:S(2)}, u32[]{:S(2)}) collective-permute-start(bf16[192,1664]{1,0:T(8,128)(2,1)S(1)} %get-tuple-element.123.refs_1_.refs_2_.refs_3_), channel_id=1, source_target_pairs={{0,2},{1,5},{2,0},{3,7},{4,6},{5,1},{6,4},{7,3},{8,10},{9,13},{10,... | collective-permute-start | bytes 1916936 | tf_op jit(solution)/shard_map/ppermute | solution.py:844
  28.2 15.2 %collective-permute-start.11 = (bf16[192,1664]{1,0:T(8,128)(2,1)S(1)}, bf16[192,1664]{1,0:T(8,128)(2,1)S(1)}, u32[]{:S(2)}, u32[]{:S(2)}) collective-permute-start(bf16[192,1664]{1,0:T(8,128)(2,1)S(1)} %get-tuple-element.123.refs_1_.refs_2_.refs_3_), channel_id=1, source_target_pairs={{0,4},{1,3},{2,6},{3,1},{4,0},{5,7},{6,2},{7,5},{8,12},{9,11},{10,... | collective-permute-start | bytes 1916936 | tf_op jit(solution)/shard_map/ppermute | solution.py:844
  29.8 16.1 %collective-permute-start.14 = (bf16[96,1536]{1,0:T(8,128)(2,1)S(1)}, bf16[96,1536]{1,0:T(8,128)(2,1)S(1)}, u32[]{:S(2)}, u32[]{:S(2)}) collective-permute-start(bf16[96,1536]{1,0:T(8,128)(2,1)S(1)} %get-tuple-element.125.refs_0_), channel_id=1, source_target_pairs={{0,16},{1,17},{2,18},{3,19},{4,20},{5,21},{6,22},{7,23},{8,24},{9,... | collective-permute-start | bytes 884744 | tf_op jit(solution)/shard_map/ppermute | solution.py:844
  31.4 14.2 %collective-permute-start.17 = (bf16[48,2048]{1,0:T(8,128)(2,1)S(1)}, bf16[48,2048]{1,0:T(8,128)(2,1)S(1)}, u32[]{:S(2)}, u32[]{:S(2)}) collective-permute-start(bf16[48,2048]{1,0:T(8,128)(2,1)S(1)} %shard_map.229.refs_6_), channel_id=1, source_target_pairs={{0,8},{1,9},{2,10},{3,11},{4,12},{5,13},{6,14},{7,15},{8,0},{9,1},... | collective-permute-start | bytes 589832 | tf_op jit(solution)/shard_map/ppermute | solution.py:844
  33.9 11.6 %collective-permute-start.15 = (bf16[48,1024]{1,0:T(8,128)(2,1)S(1)}, bf16[48,1024]{1,0:T(8,128)(2,1)S(1)}, u32[]{:S(2)}, u32[]{:S(2)}) collective-permute-start(bf16[48,1024]{1,0:T(8,128)(2,1)S(1)} %shard_map.227), channel_id=1, source_target_pairs={{0,4},{1,3},{2,6},{3,1},{4,0},{5,7},{6,2},{7,5},{8,12},{9,11},{10,... | collective-permute-start | bytes 294920 | tf_op jit(solution)/shard_map/ppermute | solution.py:844
  43.5 16.3 %collective-permute-start.12 = (bf16[192,1664]{1,0:T(8,128)(2,1)S(1)}, bf16[192,1664]{1,0:T(8,128)(2,1)S(1)}, u32[]{:S(2)}, u32[]{:S(2)}) collective-permute-start(bf16[192,1664]{1,0:T(8,128)(2,1)S(1)} %shard_map.225.refs_2_.refs_8_.refs_4_), channel_id=1, source_target_pairs={{0,4},{1,3},{2,6},{3,1},{4,0},{5,7},{6,2},{7,5},{8,12},{9,11},{10,... | collective-permute-start | bytes 1916936 | tf_op jit(solution)/shard_map/ppermute | solution.py:844
  45.9 16.3 %collective-permute-start.19 = (bf16[192,1536]{1,0:T(8,128)(2,1)S(1)}, bf16[192,1536]{1,0:T(8,128)(2,1)S(1)}, u32[]{:S(2)}, u32[]{:S(2)}) collective-permute-start(bf16[192,1536]{1,0:T(8,128)(2,1)S(1)} %get-tuple-element.129.refs_1_), channel_id=1, source_target_pairs={{0,2},{1,5},{2,0},{3,7},{4,6},{5,1},{6,4},{7,3},{8,10},{9,13},{10,... | collective-permute-start | bytes 1769480 | tf_op jit(solution)/shard_map/ppermute | solution.py:844
  47.2 19.4 %collective-permute-start.20 = (bf16[192,1536]{1,0:T(8,128)(2,1)S(1)}, bf16[192,1536]{1,0:T(8,128)(2,1)S(1)}, u32[]{:S(2)}, u32[]{:S(2)}) collective-permute-start(bf16[192,1536]{1,0:T(8,128)(2,1)S(1)} %get-tuple-element.129.refs_1_), channel_id=1, source_target_pairs={{0,4},{1,3},{2,6},{3,1},{4,0},{5,7},{6,2},{7,5},{8,12},{9,11},{10,... | collective-permute-start | bytes 1769480 | tf_op jit(solution)/shard_map/ppermute | solution.py:844
  47.8 19.9 %collective-permute-start.18 = (bf16[96,2048]{1,0:T(8,128)(2,1)S(1)}, bf16[96,2048]{1,0:T(8,128)(2,1)S(1)}, u32[]{:S(2)}, u32[]{:S(2)}) collective-permute-start(bf16[96,2048]{1,0:T(8,128)(2,1)S(1)} %get-tuple-element.128.refs_0_.refs_2_), channel_id=1, source_target_pairs={{0,16},{1,17},{2,18},{3,19},{4,20},{5,21},{6,22},{7,23},{8,24},{9,... | collective-permute-start | bytes 1179656 | tf_op jit(solution)/shard_map/ppermute | solution.py:844
  67.8 21.6 %collective-permute-start.22 = (bf16[192,1536]{1,0:T(8,128)(2,1)S(1)}, bf16[192,1536]{1,0:T(8,128)(2,1)S(1)}, u32[]{:S(2)}, u32[]{:S(2)}) collective-permute-start(bf16[192,1536]{1,0:T(8,128)(2,1)S(1)} %shard_map.233.refs_10_.refs_1_), channel_id=1, source_target_pairs={{0,2},{1,5},{2,0},{3,7},{4,6},{5,1},{6,4},{7,3},{8,10},{9,13},{10,... | collective-permute-start | bytes 1769480 | tf_op jit(solution)/shard_map/ppermute | solution.py:844
  68.5 20.9 %collective-permute-start.23 = (bf16[192,1536]{1,0:T(8,128)(2,1)S(1)}, bf16[192,1536]{1,0:T(8,128)(2,1)S(1)}, u32[]{:S(2)}, u32[]{:S(2)}) collective-permute-start(bf16[192,1536]{1,0:T(8,128)(2,1)S(1)} %shard_map.233.refs_10_.refs_1_), channel_id=1, source_target_pairs={{0,4},{1,3},{2,6},{3,1},{4,0},{5,7},{6,2},{7,5},{8,12},{9,11},{10,... | collective-permute-start | bytes 1769480 | tf_op jit(solution)/shard_map/ppermute | solution.py:844
  70.1 18.4 %collective-permute-start.21 = (bf16[192,1536]{1,0:T(8,128)(2,1)S(1)}, bf16[192,1536]{1,0:T(8,128)(2,1)S(1)}, u32[]{:S(2)}, u32[]{:S(2)}) collective-permute-start(bf16[192,1536]{1,0:T(8,128)(2,1)S(1)} %shard_map.235.refs_2_), channel_id=1, source_target_pairs={{0,4},{1,3},{2,6},{3,1},{4,0},{5,7},{6,2},{7,5},{8,12},{9,11},{10,... | collective-permute-start | bytes 1769480 | tf_op jit(solution)/shard_map/ppermute | solution.py:844
  70.5 18.8 %collective-permute-start.24 = (bf16[192,1024]{1,0:T(8,128)(2,1)S(1)}, bf16[192,1024]{1,0:T(8,128)(2,1)S(1)}, u32[]{:S(2)}, u32[]{:S(2)}) collective-permute-start(bf16[192,1024]{1,0:T(8,128)(2,1)S(1)} %shard_map.236.refs_0_.refs_2_.refs_5_), channel_id=1, source_target_pairs={{0,16},{1,17},{2,18},{3,19},{4,20},{5,21},{6,22},{7,23},{8,24},{9,... | collective-permute-start | bytes 1179656 | tf_op jit(solution)/shard_map/ppermute | solution.py:844
  90.1 14.6 %collective-permute-start.27 = (bf16[192,1536]{1,0:T(8,128)(2,1)S(1)}, bf16[192,1536]{1,0:T(8,128)(2,1)S(1)}, u32[]{:S(2)}, u32[]{:S(2)}) collective-permute-start(bf16[192,1536]{1,0:T(8,128)(2,1)S(1)} %shard_map.238.refs_1_.refs_2_), channel_id=1, source_target_pairs={{0,4},{1,3},{2,6},{3,1},{4,0},{5,7},{6,2},{7,5},{8,12},{9,11},{10,... | collective-permute-start | bytes 1769480 | tf_op jit(solution)/shard_map/ppermute | solution.py:844
  91.2 12.6 %collective-permute-start.28 = (bf16[192,512]{1,0:T(8,128)(2,1)S(1)}, bf16[192,512]{1,0:T(8,128)(2,1)S(1)}, u32[]{:S(2)}, u32[]{:S(2)}) collective-permute-start(bf16[192,512]{1,0:T(8,128)(2,1)S(1)} %shard_map.239.refs_1_.refs_4_), channel_id=1, source_target_pairs={{0,2},{1,5},{2,0},{3,7},{4,6},{5,1},{6,4},{7,3},{8,10},{9,13},{10,... | collective-permute-start | bytes 589832 | tf_op jit(solution)/shard_map/ppermute | solution.py:844
  92.2 11.9 %collective-permute-start.29 = (bf16[192,512]{1,0:T(8,128)(2,1)S(1)}, bf16[192,512]{1,0:T(8,128)(2,1)S(1)}, u32[]{:S(2)}, u32[]{:S(2)}) collective-permute-start(bf16[192,512]{1,0:T(8,128)(2,1)S(1)} %shard_map.239.refs_1_.refs_4_), channel_id=1, source_target_pairs={{0,4},{1,3},{2,6},{3,1},{4,0},{5,7},{6,2},{7,5},{8,12},{9,11},{10,... | collective-permute-start | bytes 589832 | tf_op jit(solution)/shard_map/ppermute | solution.py:844
  93.3 11.4 %collective-permute-start.30 = (bf16[384,512]{1,0:T(8,128)(2,1)S(1)}, bf16[384,512]{1,0:T(8,128)(2,1)S(1)}, u32[]{:S(2)}, u32[]{:S(2)}) collective-permute-start(bf16[384,512]{1,0:T(8,128)(2,1)S(1)} %get-tuple-element.138), channel_id=1, source_target_pairs={{0,8},{1,9},{2,10},{3,11},{4,12},{5,13},{6,14},{7,15},{8,0},{9,1},... | collective-permute-start | bytes 1179656 | tf_op jit(solution)/shard_map/ppermute | solution.py:844
  104.7 11.6 %collective-permute-start.33 = (bf16[384,512]{1,0:T(8,128)(2,1)S(1)}, bf16[384,512]{1,0:T(8,128)(2,1)S(1)}, u32[]{:S(2)}, u32[]{:S(2)}) collective-permute-start(bf16[384,512]{1,0:T(8,128)(2,1)S(1)} %shard_map.247), channel_id=1, source_target_pairs={{0,8},{1,9},{2,10},{3,11},{4,12},{5,13},{6,14},{7,15},{8,0},{9,1},... | collective-permute-start | bytes 1179656 | tf_op jit(solution)/shard_map/ppermute | solution.py:844
  106.0 9.5 %collective-permute-start.32 = (bf16[192,512]{1,0:T(8,128)(2,1)S(1)}, bf16[192,512]{1,0:T(8,128)(2,1)S(1)}, u32[]{:S(2)}, u32[]{:S(2)}) collective-permute-start(bf16[192,512]{1,0:T(8,128)(2,1)S(1)} %shard_map.246), channel_id=1, source_target_pairs={{0,4},{1,3},{2,6},{3,1},{4,0},{5,7},{6,2},{7,5},{8,12},{9,11},{10,... | collective-permute-start | bytes 589832 | tf_op jit(solution)/shard_map/ppermute | solution.py:844
  113.5 9.6 %collective-permute-start.34 = (bf16[192,896]{1,0:T(8,128)(2,1)S(1)}, bf16[192,896]{1,0:T(8,128)(2,1)S(1)}, u32[]{:S(2)}, u32[]{:S(2)}) collective-permute-start(bf16[192,896]{1,0:T(8,128)(2,1)S(1)} %get-tuple-element.154), channel_id=1, source_target_pairs={{0,2},{1,5},{2,0},{3,7},{4,6},{5,1},{6,4},{7,3},{8,10},{9,13},{10,... | collective-permute-start | bytes 1032200 | tf_op jit(solution)/shard_map/ppermute | solution.py:844
  114.5 8.6 %collective-permute-start.35 = (bf16[384,256]{1,0:T(8,128)(2,1)S(1)}, bf16[384,256]{1,0:T(8,128)(2,1)S(1)}, u32[]{:S(2)}, u32[]{:S(2)}) collective-permute-start(bf16[384,256]{1,0:T(8,128)(2,1)S(1)} %get-tuple-element.156), channel_id=1, source_target_pairs={{0,8},{1,9},{2,10},{3,11},{4,12},{5,13},{6,14},{7,15},{8,0},{9,1},... | collective-permute-start | bytes 589832 | tf_op jit(solution)/shard_map/ppermute | solution.py:844
  123.3 19.8 %collective-permute-start.39 = (bf16[192,896]{1,0:T(8,128)(2,1)S(1)}, bf16[192,896]{1,0:T(8,128)(2,1)S(1)}, u32[]{:S(2)}, u32[]{:S(2)}) collective-permute-start(bf16[192,896]{1,0:T(8,128)(2,1)S(1)} %shard_map.250.refs_1_.refs_18_), channel_id=1, source_target_pairs={{0,4},{1,3},{2,6},{3,1},{4,0},{5,7},{6,2},{7,5},{8,12},{9,11},{10,... | collective-permute-start | bytes 1032200 | tf_op jit(solution)/shard_map/ppermute | solution.py:844
  124.5 18.6 %collective-permute-start.41 = (bf16[192,1536]{1,0:T(8,128)(2,1)S(1)}, bf16[192,1536]{1,0:T(8,128)(2,1)S(1)}, u32[]{:S(2)}, u32[]{:S(2)}) collective-permute-start(bf16[192,1536]{1,0:T(8,128)(2,1)S(1)} %shard_map.256), channel_id=1, source_target_pairs={{0,2},{1,5},{2,0},{3,7},{4,6},{5,1},{6,4},{7,3},{8,10},{9,13},{10,... | collective-permute-start | bytes 1769480 | tf_op jit(solution)/shard_map/ppermute | solution.py:844
  125.5 17.5 %collective-permute-start.40 = (bf16[384,384]{1,0:T(8,128)(2,1)S(1)}, bf16[384,384]{1,0:T(8,128)(2,1)S(1)}, u32[]{:S(2)}, u32[]{:S(2)}) collective-permute-start(bf16[384,384]{1,0:T(8,128)(2,1)S(1)} %shard_map.255), channel_id=1, source_target_pairs={{0,8},{1,9},{2,10},{3,11},{4,12},{5,13},{6,14},{7,15},{8,0},{9,1},... | collective-permute-start | bytes 884744 | tf_op jit(solution)/shard_map/ppermute | solution.py:844
  126.7 16.4 %collective-permute-start.38 = (bf16[192,896]{1,0:T(8,128)(2,1)S(1)}, bf16[192,896]{1,0:T(8,128)(2,1)S(1)}, u32[]{:S(2)}, u32[]{:S(2)}) collective-permute-start(bf16[192,896]{1,0:T(8,128)(2,1)S(1)} %shard_map.254), channel_id=1, source_target_pairs={{0,2},{1,5},{2,0},{3,7},{4,6},{5,1},{6,4},{7,3},{8,10},{9,13},{10,... | collective-permute-start | bytes 1032200 | tf_op jit(solution)/shard_map/ppermute | solution.py:844
  127.7 18.7 %collective-permute-start.37 = (bf16[192,1536]{1,0:T(8,128)(2,1)S(1)}, bf16[192,1536]{1,0:T(8,128)(2,1)S(1)}, u32[]{:S(2)}, u32[]{:S(2)}) collective-permute-start(bf16[192,1536]{1,0:T(8,128)(2,1)S(1)} %shard_map.253), channel_id=1, source_target_pairs={{0,2},{1,5},{2,0},{3,7},{4,6},{5,1},{6,4},{7,3},{8,10},{9,13},{10,... | collective-permute-start | bytes 1769480 | tf_op jit(solution)/shard_map/ppermute | solution.py:844
  147.2 24.2 %collective-permute-start.44 = (bf16[192,1536]{1,0:T(8,128)(2,1)S(1)}, bf16[192,1536]{1,0:T(8,128)(2,1)S(1)}, u32[]{:S(2)}, u32[]{:S(2)}) collective-permute-start(bf16[192,1536]{1,0:T(8,128)(2,1)S(1)} %get-tuple-element.166.refs_1_.refs_17_), channel_id=1, source_target_pairs={{0,4},{1,3},{2,6},{3,1},{4,0},{5,7},{6,2},{7,5},{8,12},{9,11},{10,... | collective-permute-start | bytes 1769480 | tf_op jit(solution)/shard_map/ppermute | solution.py:844
  148.4 23.0 %collective-permute-start.47 = (bf16[192,1536]{1,0:T(8,128)(2,1)S(1)}, bf16[192,1536]{1,0:T(8,128)(2,1)S(1)}, u32[]{:S(2)}, u32[]{:S(2)}) collective-permute-start(bf16[192,1536]{1,0:T(8,128)(2,1)S(1)} %shard_map.261), channel_id=1, source_target_pairs={{0,2},{1,5},{2,0},{3,7},{4,6},{5,1},{6,4},{7,3},{8,10},{9,13},{10,... | collective-permute-start | bytes 1769480 | tf_op jit(solution)/shard_map/ppermute | solution.py:844
  149.5 22.0 %collective-permute-start.43 = (bf16[192,1536]{1,0:T(8,128)(2,1)S(1)}, bf16[192,1536]{1,0:T(8,128)(2,1)S(1)}, u32[]{:S(2)}, u32[]{:S(2)}) collective-permute-start(bf16[192,1536]{1,0:T(8,128)(2,1)S(1)} %shard_map.260), channel_id=1, source_target_pairs={{0,2},{1,5},{2,0},{3,7},{4,6},{5,1},{6,4},{7,3},{8,10},{9,13},{10,... | collective-permute-start | bytes 1769480 | tf_op jit(solution)/shard_map/ppermute | solution.py:844
  150.5 20.9 %collective-permute-start.46 = (bf16[192,640]{1,0:T(8,128)(2,1)S(1)}, bf16[192,640]{1,0:T(8,128)(2,1)S(1)}, u32[]{:S(2)}, u32[]{:S(2)}) collective-permute-start(bf16[192,640]{1,0:T(8,128)(2,1)S(1)} %get-tuple-element.182), channel_id=1, source_target_pairs={{0,16},{1,17},{2,18},{3,19},{4,20},{5,21},{6,22},{7,23},{8,24},{9,... | collective-permute-start | bytes 737288 | tf_op jit(solution)/shard_map/ppermute | solution.py:844
  153.3 18.2 %collective-permute-start.45 = (bf16[96,896]{1,0:T(8,128)(2,1)S(1)}, bf16[96,896]{1,0:T(8,128)(2,1)S(1)}, u32[]{:S(2)}, u32[]{:S(2)}) collective-permute-start(bf16[96,896]{1,0:T(8,128)(2,1)S(1)} %get-tuple-element.180), channel_id=1, source_target_pairs={{0,16},{1,17},{2,18},{3,19},{4,20},{5,21},{6,22},{7,23},{8,24},{9,... | collective-permute-start | bytes 516104 | tf_op jit(solution)/shard_map/ppermute | solution.py:844
  171.8 17.1 %collective-permute-start.49 = (bf16[192,1536]{1,0:T(8,128)(2,1)S(1)}, bf16[192,1536]{1,0:T(8,128)(2,1)S(1)}, u32[]{:S(2)}, u32[]{:S(2)}) collective-permute-start(bf16[192,1536]{1,0:T(8,128)(2,1)S(1)} %get-tuple-element.184.refs_1_.refs_2_), channel_id=1, source_target_pairs={{0,4},{1,3},{2,6},{3,1},{4,0},{5,7},{6,2},{7,5},{8,12},{9,11},{10,... | collective-permute-start | bytes 1769480 | tf_op jit(solution)/shard_map/ppermute | solution.py:844
  172.9 16.0 %collective-permute-start.48 = (bf16[192,1664]{1,0:T(8,128)(2,1)S(1)}, bf16[192,1664]{1,0:T(8,128)(2,1)S(1)}, u32[]{:S(2)}, u32[]{:S(2)}) collective-permute-start(bf16[192,1664]{1,0:T(8,128)(2,1)S(1)} %shard_map.263), channel_id=1, source_target_pairs={{0,2},{1,5},{2,0},{3,7},{4,6},{5,1},{6,4},{7,3},{8,10},{9,13},{10,... | collective-permute-start | bytes 1916936 | tf_op jit(solution)/shard_map/ppermute | solution.py:844
  173.8 15.1 %collective-permute-start.50 = (bf16[96,1536]{1,0:T(8,128)(2,1)S(1)}, bf16[96,1536]{1,0:T(8,128)(2,1)S(1)}, u32[]{:S(2)}, u32[]{:S(2)}) collective-permute-start(bf16[96,1536]{1,0:T(8,128)(2,1)S(1)} %get-tuple-element.187), channel_id=1, source_target_pairs={{0,16},{1,17},{2,18},{3,19},{4,20},{5,21},{6,22},{7,23},{8,24},{9,... | collective-permute-start | bytes 884744 | tf_op jit(solution)/shard_map/ppermute | solution.py:844
  174.4 14.2 %collective-permute-start.52 = (bf16[96,640]{1,0:T(8,128)(2,1)S(1)}, bf16[96,640]{1,0:T(8,128)(2,1)S(1)}, u32[]{:S(2)}, u32[]{:S(2)}) collective-permute-start(bf16[96,640]{1,0:T(8,128)(2,1)S(1)} %get-tuple-element.192), channel_id=1, source_target_pairs={{0,2},{1,5},{2,0},{3,7},{4,6},{5,1},{6,4},{7,3},{8,10},{9,13},{10,... | collective-permute-start | bytes 368648 | tf_op jit(solution)/shard_map/ppermute | solution.py:844
  190.0 17.9 %collective-permute-start.56 = (bf16[192,1664]{1,0:T(8,128)(2,1)S(1)}, bf16[192,1664]{1,0:T(8,128)(2,1)S(1)}, u32[]{:S(2)}, u32[]{:S(2)}) collective-permute-start(bf16[192,1664]{1,0:T(8,128)(2,1)S(1)} %get-tuple-element.195.refs_1_), channel_id=1, source_target_pairs={{0,4},{1,3},{2,6},{3,1},{4,0},{5,7},{6,2},{7,5},{8,12},{9,11},{10,... | collective-permute-start | bytes 1916936 | tf_op jit(solution)/shard_map/ppermute | solution.py:844
  190.7 17.2 %collective-permute-start.55 = (bf16[192,1664]{1,0:T(8,128)(2,1)S(1)}, bf16[192,1664]{1,0:T(8,128)(2,1)S(1)}, u32[]{:S(2)}, u32[]{:S(2)}) collective-permute-start(bf16[192,1664]{1,0:T(8,128)(2,1)S(1)} %shard_map.269), channel_id=1, source_target_pairs={{0,2},{1,5},{2,0},{3,7},{4,6},{5,1},{6,4},{7,3},{8,10},{9,13},{10,... | collective-permute-start | bytes 1916936 | tf_op jit(solution)/shard_map/ppermute | solution.py:844
  192.2 15.7 %collective-permute-start.57 = (bf16[96,1536]{1,0:T(8,128)(2,1)S(1)}, bf16[96,1536]{1,0:T(8,128)(2,1)S(1)}, u32[]{:S(2)}, u32[]{:S(2)}) collective-permute-start(bf16[96,1536]{1,0:T(8,128)(2,1)S(1)} %get-tuple-element.203), channel_id=1, source_target_pairs={{0,16},{1,17},{2,18},{3,19},{4,20},{5,21},{6,22},{7,23},{8,24},{9,... | collective-permute-start | bytes 884744 | tf_op jit(solution)/shard_map/ppermute | solution.py:844
  193.3 14.6 %collective-permute-start.59 = (bf16[48,1536]{1,0:T(8,128)(2,1)S(1)}, bf16[48,1536]{1,0:T(8,128)(2,1)S(1)}, u32[]{:S(2)}, u32[]{:S(2)}) collective-permute-start(bf16[48,1536]{1,0:T(8,128)(2,1)S(1)} %get-tuple-element.207), channel_id=1, source_target_pairs={{0,8},{1,9},{2,10},{3,11},{4,12},{5,13},{6,14},{7,15},{8,0},{9,1},... | collective-permute-start | bytes 442376 | tf_op jit(solution)/shard_map/ppermute | solution.py:844
  195.2 12.7 %collective-permute-start.58 = (bf16[48,640]{1,0:T(8,128)(2,1)S(1)}, bf16[48,640]{1,0:T(8,128)(2,1)S(1)}, u32[]{:S(2)}, u32[]{:S(2)}) collective-permute-start(bf16[48,640]{1,0:T(8,128)(2,1)S(1)} %get-tuple-element.205), channel_id=1, source_target_pairs={{0,4},{1,3},{2,6},{3,1},{4,0},{5,7},{6,2},{7,5},{8,12},{9,11},{10,... | collective-permute-start | bytes 184328 | tf_op jit(solution)/shard_map/ppermute | solution.py:844
  209.5 13.3 %collective-permute-start.60 = (bf16[48,3200]{1,0:T(8,128)(2,1)S(1)}, bf16[48,3200]{1,0:T(8,128)(2,1)S(1)}, u32[]{:S(2)}, u32[]{:S(2)}) collective-permute-start(bf16[48,3200]{1,0:T(8,128)(2,1)S(1)} %get-tuple-element.209), channel_id=1, source_target_pairs={{0,8},{1,9},{2,10},{3,11},{4,12},{5,13},{6,14},{7,15},{8,0},{9,1},... | collective-permute-start | bytes 921608 | tf_op jit(solution)/shard_map/ppermute | solution.py:844
  209.5 14.1 %collective-permute-start.61 = (bf16[48,1664]{1,0:T(8,128)(2,1)}, bf16[48,1664]{1,0:T(8,128)(2,1)S(1)}, u32[]{:S(2)}, u32[]{:S(2)}) collective-permute-start(bf16[48,1664]{1,0:T(8,128)(2,1)} %copy-done.19), channel_id=1, source_target_pairs={{0,16},{1,17},{2,18},{3,19},{4,20},{5,21},{6,22},{7,23},{8,24},{9,... | collective-permute-start | bytes 479240 | tf_op jit(solution)/shard_map/ppermute | solution.py:844
  212.7 13.3 %collective-permute-start.62 = (bf16[48,1664]{1,0:T(8,128)(2,1)S(1)}, bf16[48,1664]{1,0:T(8,128)(2,1)S(1)}, u32[]{:S(2)}, u32[]{:S(2)}) collective-permute-start(bf16[48,1664]{1,0:T(8,128)(2,1)S(1)} %get-tuple-element.211), channel_id=1, source_target_pairs={{0,24},{1,25},{2,26},{3,27},{4,28},{5,29},{6,30},{7,31},{8,16},{9,... | collective-permute-start | bytes 479240 | tf_op jit(solution)/shard_map/ppermute | solution.py:844
  (56 other events, 340.1 us)

commit v9 on v8

--- a/solution.py
+++ b/solution.py
@@ -518,8 +518,8 @@
     for q in range(4):
         for r in range(4):
             rows = pl.ds(pl.multiple_of(offs[0, q * 4 + r] * blk, 16), blk)
-            at = ((r // 2) * 4 + q) * blk
-            if r % 2 == 0:
+            at = ((r % 2) * 4 + q) * blk
+            if r < 2:
                 near[at : at + blk, :] = dz[rows, :]
                 continue
             for dst, (lo, width) in zip(far, FAR_CUTS):
@@ -829,7 +829,7 @@
 FIRST = 512
 LAST = 2 * D - FIRST
 CUTS = ((0, 512), (512, 512))
-FAR_CUTS = ((0, 256), (256, 384))
+FAR_CUTS = ((0, 128), (128, 512))
 LEVELS = 640
 
 
@@ -1171,12 +1171,12 @@
         hold=[*hold, *held, third],
     )
     if fast:
-        got_ab1, got_z1 = side_a(d_mlpout[3]), near(d_mlpout[5])
+        got_ab1, got_z1 = side_a(d_mlpout[3]), far(d_mlpout[5])
     part, comb, *d_mlpin = mlp_part(last, g, slope, w_in, hidden, third, after=d_mlpout[:1], hold=[*hold, *held])
     if fast:
         (on,) = merge([("pass", d_mlpout[2], got_ab1)], after=(part, got_z1))
         comb = tie(comb, on)
-        got_b1, got_a1, got_z2 = side_b(on), side_a(tie(d_mlpout[1], on)), near(tie(d_mlpout[6], on))
+        got_b1, got_a1, got_z2 = side_b(on), side_a(tie(d_mlpout[1], on)), far(tie(d_mlpout[6], on))
         got_ab2, got_a2 = side_a(tie(d_mlpin[3], on)), side_a(tie(d_mlpin[1], on))
         after = (on,)
     recv = sib(comb)
@@ -1191,7 +1191,7 @@
             after=(dvec_two, got_a2),
         )
         gsecond = tie(gsecond, on)
-        got_b2, got_far1, got_far_z = side_b(on), far(on_far), far(on_z)
+        got_b2, got_far1, got_far_z = side_b(on), far(on_far), near(on_z)
         got_ab3, got_a3 = side_a(tie(d_cross[3], on)), side_a(tie(d_cross[1], on))
         after = (on,)
     recv = sib(gsecond)
@@ -1293,8 +1293,7 @@
         own_gains, own_biases = vectors[:3], vectors[3:]
         grad_in = joined(placed(d_mlpin), 0, fh, ff // (2 * hr))
         first_rows = jnp.concatenate(d_mlpout[:4], 0)
-        levels = jnp.stack([d_mlpout[4], jnp.concatenate(d_mlpout[5:], 1)], 0).reshape(2, 2, 4, wb, LEVELS)
-        levels = levels.transpose(1, 0, 2, 3, 4).reshape(4, 4, wb, LEVELS)
+        levels = jnp.concatenate([d_mlpout[4], jnp.concatenate(d_mlpout[5:], 1)], 0).reshape(4, 4, wb, LEVELS)
         levels = jnp.concatenate([levels.transpose(1, 0, 2, 3).reshape(D, LEVELS), first_rows[:, D:]], 1)
         term = jnp.stack([first_rows[:, :D].reshape(16, wb, D), levels.reshape(16, wb, D)], 1).astype(F32)
         term = term.reshape(moves.n // 2, 1, hr, D)

time: 229 us -> 229 us (level)
  transfers between devices with their start and end apart: 66 -> 66, of which waited for: 23 -> 22; matrix products, arithmetic and copies ran while one was open for 3% -> 3% of each run, Pallas kernels for 30% -> 30%
where the time goes in v9:
time: 229 us
  waiting for transfers between devices  78.5 us (34%)
  Pallas kernels  71.3 us (31%)
  starting transfers between devices  68.2 us (30%)
  local copies, waits for them, and re-layouts  8.06 us (4%)
    ppermute x66, waiting for transfers between devices, permute(): lax.ppermute(x, AXES, [(a, z * self.nf + 2 * yx + c) for a, (z, yx, c) in...  78.5 us
    pallas_call x31, Pallas kernels, kernel_call(): pl.pallas_call(run, out_shape=list(outs), in_specs=[space(spec) for spec...  71.3 us
    ppermute x66, starting transfers between devices, permute(): lax.ppermute(x, AXES, [(a, z * self.nf + 2 * yx + c) for a, (z, yx, c) in...  68.2 us
    unnamed x80, local copies, waits for them, and re-layouts  6.22 us
  transfers between devices with their start and end apart: 66, of which 22 were waited for; matrix products, arithmetic and copies ran while one was open for 3% of the time, Pallas kernels for 30%

profile of v9, /device:TPU:0, one launch (start us, length us, event | category | flops | bytes accessed | tf_op | source)
XLA Modules:
  0.0 228.6 jit_solution(17274342579246303222)
XLA Ops:
  1.7 1.9 shard_map.220
  4.1 1.5 copy.54.refs_5_
  5.9 3.7 %collective-permute-start.5 = (bf16[48,1664]{1,0:T(8,128)(2,1)S(1)}, bf16[48,1664]{1,0:T(8,128)(2,1)S(1)}, u32[]{:S(2)}, u32[]{:S(2)}) collective-permute-start(bf16[48,1664]{1,0:T(8,128)(2,1)S(1)} %get-tuple-element.119.refs_7_.refs_0_), channel_id=1, source_target_pairs={{0,16},{1,17},{2,18},{3,19},{4,20},{5,21},{6,22},{7,23},{8,24},{9,... | collective-permute-start | bytes 479240 | tf_op jit(solution)/shard_map/ppermute | solution.py:844
  9.6 1.3 collective-permute-start.6
  11.2 1.5 copy.55.refs_6_
  12.8 1.8 shard_map.222
  14.6 1.6 copy-done.27
  16.2 1.5 collective-permute-start.8
  17.7 1.5 collective-permute-start.9
  19.3 2.2 collective-permute-done.5.refs_2_
  21.5 4.2 %collective-permute-done.4.refs_1_.refs_5_ = bf16[48,3200]{1,0:T(8,128)(2,1)S(1)} collective-permute-done((bf16[48,3200]{1,0:T(8,128)(2,1)S(1)}, bf16[48,3200]{1,0:T(8,128)(2,1)S(1)}, u32[]{:S(2)}, u32[]{:S(2)}) %collective-permute-start.4) | collective-permute-done | bytes 307232 | tf_op jit(solution)/shard_map/ppermute | solution.py:844
  26.7 1.6 collective-permute-start.10
  28.2 1.5 collective-permute-start.11
  29.8 1.6 collective-permute-start.14
  31.4 2.5 %collective-permute-start.17 = (bf16[48,2048]{1,0:T(8,128)(2,1)S(1)}, bf16[48,2048]{1,0:T(8,128)(2,1)S(1)}, u32[]{:S(2)}, u32[]{:S(2)}) collective-permute-start(bf16[48,2048]{1,0:T(8,128)(2,1)S(1)} %shard_map.229.refs_6_), channel_id=1, source_target_pairs={{0,8},{1,9},{2,10},{3,11},{4,12},{5,13},{6,14},{7,15},{8,0},{9,1},... | collective-permute-start | bytes 589832 | tf_op jit(solution)/shard_map/ppermute | solution.py:844
  34.5 8.6 %collective-permute-done.10.refs_0_ = bf16[192,1664]{1,0:T(8,128)(2,1)S(1)} collective-permute-done((bf16[192,1664]{1,0:T(8,128)(2,1)S(1)}, bf16[192,1664]{1,0:T(8,128)(2,1)S(1)}, u32[]{:S(2)}, u32[]{:S(2)}) %collective-permute-start.10) | collective-permute-done | bytes 639008 | tf_op jit(solution)/shard_map/ppermute | solution.py:844
  43.5 2.1 collective-permute-start.12
  47.8 1.6 collective-permute-start.18
  49.3 10.5 %collective-permute-done.12.refs_4_.refs_2_.refs_6_ = bf16[192,1664]{1,0:T(8,128)(2,1)S(1)} collective-permute-done((bf16[192,1664]{1,0:T(8,128)(2,1)S(1)}, bf16[192,1664]{1,0:T(8,128)(2,1)S(1)}, u32[]{:S(2)}, u32[]{:S(2)}) %collective-permute-start.12) | collective-permute-done | bytes 639008 | tf_op jit(solution)/shard_map/ppermute | solution.py:844
  60.5 1.8 collective-permute-done.19.refs_0_
  62.2 4.3 %collective-permute-done.20.refs_1_.refs_3_ = bf16[192,1536]{1,0:T(8,128)(2,1)S(1)} collective-permute-done((bf16[192,1536]{1,0:T(8,128)(2,1)S(1)}, bf16[192,1536]{1,0:T(8,128)(2,1)S(1)}, u32[]{:S(2)}, u32[]{:S(2)}) %collective-permute-start.20) | collective-permute-done | bytes 589856 | tf_op jit(solution)/shard_map/ppermute | solution.py:844
  68.5 1.6 collective-permute-start.23
  70.5 1.3 collective-permute-start.24
  71.8 7.4 %shard_map.234 = (bf16[512,768]{1,0:T(8,128)(2,1)S(1)}, bf16[512,1152]{1,0:T(8,128)(2,1)S(1)}, bf16[8,64,384]{2,1,0:T(8,128)(2,1)S(1)}, bf16[512,1152]{1,0:T(8,1...) custom-call(s32[8]{0:T(128)S(1)} %pad_add_fusion.1.refs_0_, s32[1]{0:T(128)} %bitcast.2.refs_0_.refs_1_.refs_6_, ...), custom_call_target="tpu_custom_call" | custom-call | flops 41999998976 | tf_op jit(solution)/shard_map/pallas_call | solution.py:97
  79.3 9.3 %collective-permute-done.21.refs_4_ = bf16[192,1536]{1,0:T(8,128)(2,1)S(1)} collective-permute-done((bf16[192,1536]{1,0:T(8,128)(2,1)S(1)}, bf16[192,1536]{1,0:T(8,128)(2,1)S(1)}, u32[]{:S(2)}, u32[]{:S(2)}) %collective-permute-start.21) | collective-permute-done | bytes 589856 | tf_op jit(solution)/shard_map/ppermute | solution.py:844
  93.5 10.3 %shard_map.241 = (bf16[1920,768]{1,0:T(8,128)(2,1)S(1)}, bf16[768,768]{1,0:T(8,128)(2,1)S(1)}, bf16[768,384]{1,0:T(8,128)(2,1)S(1)}, f32[512,768]{1,0:T(8,128)S(...) custom-call(s32[2,16]{1,0:T(2,128)S(1)} %pad_add_fusion.refs_0_.refs, ...), custom_call_target="tpu_custom_call" | custom-call | flops 83999997952 | tf_op jit(solution)/shard_map/pallas_call | solution.py:97
  107.9 3.4 %shard_map.245 = (f32[512,768]{1,0:T(8,128)S(1)}, bf16[512,768]{1,0:T(8,128)(2,1)S(1)}, bf16[512,1536]{1,0:T(8,128)(2,1)S(1)}, bf16[512,1536]{1,0:T(8,128)(2,1)S(1)}) custom-call(f32[512,768]{1,0:T(8,128)S(1)} %get-tuple-element.136.refs_0_.refs_3_, bf16[512,1152]{1,0:T(8,128)(2,1)S(1)} %shard_map.243.refs_1_.refs_14_, ...), custom_call_target="tpu_custom_call" | custom-call | flops 35000000512 | tf_op jit(solution)/shard_map/pallas_call | solution.py:97
  111.3 2.2 shard_map.248
  114.5 2.6 %collective-permute-start.35 = (bf16[384,128]{1,0:T(8,128)(2,1)S(1)}, bf16[384,128]{1,0:T(8,128)(2,1)S(1)}, u32[]{:S(2)}, u32[]{:S(2)}) collective-permute-start(bf16[384,128]{1,0:T(8,128)(2,1)S(1)} %get-tuple-element.156), channel_id=1, source_target_pairs={{0,16},{1,17},{2,18},{3,19},{4,20},{5,21},{6,22},{7,23},{8,24},{9,... | collective-permute-start | bytes 294920 | tf_op jit(solution)/shard_map/ppermute | solution.py:844
  117.2 6.8 %shard_map.249 = (bf16[256,768]{1,0:T(8,128)(2,1)S(1)}, bf16[768,768]{1,0:T(8,128)(2,1)S(1)}, bf16[192,1536]{1,0:T(8,128)(2,1)S(1)}, bf16[192,1536]{1,0:T(8,128)...) custom-call(s32[2,16]{1,0:T(2,128)S(1)} %pad_add_fusion.refs_0_.refs_2_, ...), custom_call_target="tpu_custom_call" | custom-call | flops 76999999488 | tf_op jit(solution)/shard_map/pallas_call | solution.py:97
  126.2 2.6 %collective-permute-start.40 = (bf16[384,512]{1,0:T(8,128)(2,1)S(1)}, bf16[384,512]{1,0:T(8,128)(2,1)S(1)}, u32[]{:S(2)}, u32[]{:S(2)}) collective-permute-start(bf16[384,512]{1,0:T(8,128)(2,1)S(1)} %shard_map.255), channel_id=1, source_target_pairs={{0,16},{1,17},{2,18},{3,19},{4,20},{5,21},{6,22},{7,23},{8,24},{9,... | collective-permute-start | bytes 1179656 | tf_op jit(solution)/shard_map/ppermute | solution.py:844
  130.9 14.4 %shard_map.252 = (bf16[256,768]{1,0:T(8,128)(2,1)}, f32[512,768]{1,0:T(8,128)S(1)}, bf16[512,768]{1,0:T(8,128)(2,1)S(1)}, f32[8,768]{1,0:T(8,128)S(1)}, bf16[192...) custom-call(s32[2,16]{1,0:T(2,128)S(1)} %pad_add_fusion.refs_0_.refs, ...), custom_call_target="tpu_custom_call" | custom-call | flops 98000003072 | tf_op jit(solution)/shard_map/pallas_call | solution.py:97
  152.4 1.7 collective-permute-start.45
  154.1 11.6 %shard_map.259 = (f32[256,768]{1,0:T(8,128)S(1)}, bf16[256,768]{1,0:T(8,128)(2,1)S(1)}, bf16[256,768]{1,0:T(8,128)(2,1)S(1)}, bf16[192,1664]{1,0:T(8,128)(2,1)S(...) custom-call(s32[2,16]{1,0:T(2,128)S(1)} %pad_add_fusion.refs_0_.refs_2_, ...), custom_call_target="tpu_custom_call" | custom-call | flops 76999999488 | tf_op jit(solution)/shard_map/pallas_call | solution.py:97
  165.7 4.1 %collective-permute-done.43.refs_1_ = bf16[192,1536]{1,0:T(8,128)(2,1)S(1)} collective-permute-done((bf16[192,1536]{1,0:T(8,128)(2,1)S(1)}, bf16[192,1536]{1,0:T(8,128)(2,1)S(1)}, u32[]{:S(2)}, u32[]{:S(2)}) %collective-permute-start.43) | collective-permute-done | bytes 589856 | tf_op jit(solution)/shard_map/ppermute | solution.py:844
  172.2 2.6 %collective-permute-start.50 = (bf16[96,1536]{1,0:T(8,128)(2,1)S(1)}, bf16[96,1536]{1,0:T(8,128)(2,1)S(1)}, u32[]{:S(2)}, u32[]{:S(2)}) collective-permute-start(bf16[96,1536]{1,0:T(8,128)(2,1)S(1)} %get-tuple-element.187), channel_id=1, source_target_pairs={{0,16},{1,17},{2,18},{3,19},{4,20},{5,21},{6,22},{7,23},{8,24},{9,... | collective-permute-start | bytes 884744 | tf_op jit(solution)/shard_map/ppermute | solution.py:844
  176.2 2.5 %shard_map.264 = (bf16[960,768]{1,0:T(8,128)(2,1)S(1)}, bf16[960,768]{1,0:T(8,128)(2,1)S(1)}) custom-call(bf16[1920,768]{1,0:T(8,128)(2,1)S(1)} %get-tuple-element.193.refs_0_, bf16[768,768]{1,0:T(8,128)(2,1)S(1)} %get-tuple-element.143.refs_11_.refs_9_.refs_21_.refs_1_, bf16[192,1536]{1,0:T(8,128)(2,1)S(1)} %get-tuple-element.184.refs_1_.refs_2_), custom_call_target="tpu_custom_call" | custom-call | flops 20999999488 | tf_op jit(solution)/shard_map/pallas_call | solution.py:97
  178.7 4.5 %collective-permute-done.51.refs_8_ = bf16[48,896]{1,0:T(8,128)(2,1)S(1)} collective-permute-done((bf16[48,896]{1,0:T(8,128)(2,1)S(1)}, bf16[48,896]{1,0:T(8,128)(2,1)S(1)}, u32[]{:S(2)}, u32[]{:S(2)}) %collective-permute-start.51) | collective-permute-done | bytes 86048 | tf_op jit(solution)/shard_map/ppermute | solution.py:844
  183.1 4.8 %collective-permute-done.52.refs_11_ = bf16[96,640]{1,0:T(8,128)(2,1)S(1)} collective-permute-done((bf16[96,640]{1,0:T(8,128)(2,1)S(1)}, bf16[96,640]{1,0:T(8,128)(2,1)S(1)}, u32[]{:S(2)}, u32[]{:S(2)}) %collective-permute-start.52) | collective-permute-done | bytes 122912 | tf_op jit(solution)/shard_map/ppermute | solution.py:844
  191.5 2.0 collective-permute-start.57
  194.2 1.3 collective-permute-start.58
  195.5 2.2 shard_map.268
  197.7 9.6 %collective-permute-done.58.refs_6_ = bf16[48,640]{1,0:T(8,128)(2,1)S(1)} collective-permute-done((bf16[48,640]{1,0:T(8,128)(2,1)S(1)}, bf16[48,640]{1,0:T(8,128)(2,1)S(1)}, u32[]{:S(2)}, u32[]{:S(2)}) %collective-permute-start.58) | collective-permute-done | bytes 61472 | tf_op jit(solution)/shard_map/ppermute | solution.py:844
  209.5 2.4 %collective-permute-start.61 = (bf16[48,1664]{1,0:T(8,128)(2,1)}, bf16[48,1664]{1,0:T(8,128)(2,1)S(1)}, u32[]{:S(2)}, u32[]{:S(2)}) collective-permute-start(bf16[48,1664]{1,0:T(8,128)(2,1)} %copy-done.19), channel_id=1, source_target_pairs={{0,16},{1,17},{2,18},{3,19},{4,20},{5,21},{6,22},{7,23},{8,24},{9,... | collective-permute-start | bytes 479240 | tf_op jit(solution)/shard_map/ppermute | solution.py:844
  211.9 1.5 collective-permute-start.62
  213.5 1.6 copy.57
  215.8 6.0 %collective-permute-done.60.refs_1_ = bf16[48,3200]{1,0:T(8,128)(2,1)S(1)} collective-permute-done((bf16[48,3200]{1,0:T(8,128)(2,1)S(1)}, bf16[48,3200]{1,0:T(8,128)(2,1)S(1)}, u32[]{:S(2)}, u32[]{:S(2)}) %collective-permute-start.60) | collective-permute-done | bytes 307232 | tf_op jit(solution)/shard_map/ppermute | solution.py:844
  222.7 3.3 %collective-permute-done.62.refs_5_ = bf16[48,1664]{1,0:T(8,128)(2,1)S(1)} collective-permute-done((bf16[48,1664]{1,0:T(8,128)(2,1)S(1)}, bf16[48,1664]{1,0:T(8,128)(2,1)S(1)}, u32[]{:S(2)}, u32[]{:S(2)}) %collective-permute-start.62) | collective-permute-done | bytes 159776 | tf_op jit(solution)/shard_map/ppermute | solution.py:844
  (237 shorter events, 44.9 us)
Async XLA Ops:
  1.2 10.0 %collective-permute-start.7 = (bf16[4,228,768]{2,0,1:T(4,128)(2,1)}, bf16[4,228,768]{2,0,1:T(4,128)(2,1)}, u32[]{:S(2)}, u32[]{:S(2)}) collective-permute-start(bf16[4,228,768]{2,0,1:T(4,128)(2,1)} %param.14), channel_id=1, source_target_pairs={{0,1},{1,0},{2,3},{3,2},{4,5},{5,4},{6,7},{7,6},{8,9},{9,8},{10,11... | collective-permute-start | bytes 4202504 | tf_op jit(solution)/shard_map/ppermute | solution.py:844
  5.9 15.6 %collective-permute-start.5 = (bf16[48,1664]{1,0:T(8,128)(2,1)S(1)}, bf16[48,1664]{1,0:T(8,128)(2,1)S(1)}, u32[]{:S(2)}, u32[]{:S(2)}) collective-permute-start(bf16[48,1664]{1,0:T(8,128)(2,1)S(1)} %get-tuple-element.119.refs_7_.refs_0_), channel_id=1, source_target_pairs={{0,16},{1,17},{2,18},{3,19},{4,20},{5,21},{6,22},{7,23},{8,24},{9,... | collective-permute-start | bytes 479240 | tf_op jit(solution)/shard_map/ppermute | solution.py:844
  9.6 11.9 %collective-permute-start.6 = (bf16[48,1664]{1,0:T(8,128)(2,1)S(1)}, bf16[48,1664]{1,0:T(8,128)(2,1)S(1)}, u32[]{:S(2)}, u32[]{:S(2)}) collective-permute-start(bf16[48,1664]{1,0:T(8,128)(2,1)S(1)} %get-tuple-element.119.refs_7_.refs_0_), channel_id=1, source_target_pairs={{0,24},{1,25},{2,26},{3,27},{4,28},{5,29},{6,30},{7,31},{8,16},{9,... | collective-permute-start | bytes 479240 | tf_op jit(solution)/shard_map/ppermute | solution.py:844
  11.0 14.7 %collective-permute-start.4 = (bf16[48,3200]{1,0:T(8,128)(2,1)S(1)}, bf16[48,3200]{1,0:T(8,128)(2,1)S(1)}, u32[]{:S(2)}, u32[]{:S(2)}) collective-permute-start(bf16[48,3200]{1,0:T(8,128)(2,1)S(1)} %get-tuple-element.120.refs_8_.refs_4_), channel_id=1, source_target_pairs={{0,8},{1,9},{2,10},{3,11},{4,12},{5,13},{6,14},{7,15},{8,0},{9,1},... | collective-permute-start | bytes 921608 | tf_op jit(solution)/shard_map/ppermute | solution.py:844
  16.2 9.5 %collective-permute-start.8 = (bf16[48,1024]{1,0:T(8,128)(2,1)S(1)}, bf16[48,1024]{1,0:T(8,128)(2,1)S(1)}, u32[]{:S(2)}, u32[]{:S(2)}) collective-permute-start(bf16[48,1024]{1,0:T(8,128)(2,1)S(1)} %shard_map.223.refs_2_), channel_id=1, source_target_pairs={{0,2},{1,5},{2,0},{3,7},{4,6},{5,1},{6,4},{7,3},{8,10},{9,13},{10,... | collective-permute-start | bytes 294920 | tf_op jit(solution)/shard_map/ppermute | solution.py:844
  26.7 16.5 %collective-permute-start.10 = (bf16[192,1664]{1,0:T(8,128)(2,1)S(1)}, bf16[192,1664]{1,0:T(8,128)(2,1)S(1)}, u32[]{:S(2)}, u32[]{:S(2)}) collective-permute-start(bf16[192,1664]{1,0:T(8,128)(2,1)S(1)} %get-tuple-element.123.refs_1_.refs_2_.refs_3_), channel_id=1, source_target_pairs={{0,2},{1,5},{2,0},{3,7},{4,6},{5,1},{6,4},{7,3},{8,10},{9,13},{10,... | collective-permute-start | bytes 1916936 | tf_op jit(solution)/shard_map/ppermute | solution.py:844
  28.2 15.2 %collective-permute-start.11 = (bf16[192,1664]{1,0:T(8,128)(2,1)S(1)}, bf16[192,1664]{1,0:T(8,128)(2,1)S(1)}, u32[]{:S(2)}, u32[]{:S(2)}) collective-permute-start(bf16[192,1664]{1,0:T(8,128)(2,1)S(1)} %get-tuple-element.123.refs_1_.refs_2_.refs_3_), channel_id=1, source_target_pairs={{0,4},{1,3},{2,6},{3,1},{4,0},{5,7},{6,2},{7,5},{8,12},{9,11},{10,... | collective-permute-start | bytes 1916936 | tf_op jit(solution)/shard_map/ppermute | solution.py:844
  29.8 16.1 %collective-permute-start.14 = (bf16[96,1536]{1,0:T(8,128)(2,1)S(1)}, bf16[96,1536]{1,0:T(8,128)(2,1)S(1)}, u32[]{:S(2)}, u32[]{:S(2)}) collective-permute-start(bf16[96,1536]{1,0:T(8,128)(2,1)S(1)} %get-tuple-element.125.refs_0_), channel_id=1, source_target_pairs={{0,16},{1,17},{2,18},{3,19},{4,20},{5,21},{6,22},{7,23},{8,24},{9,... | collective-permute-start | bytes 884744 | tf_op jit(solution)/shard_map/ppermute | solution.py:844
  31.4 14.2 %collective-permute-start.17 = (bf16[48,2048]{1,0:T(8,128)(2,1)S(1)}, bf16[48,2048]{1,0:T(8,128)(2,1)S(1)}, u32[]{:S(2)}, u32[]{:S(2)}) collective-permute-start(bf16[48,2048]{1,0:T(8,128)(2,1)S(1)} %shard_map.229.refs_6_), channel_id=1, source_target_pairs={{0,8},{1,9},{2,10},{3,11},{4,12},{5,13},{6,14},{7,15},{8,0},{9,1},... | collective-permute-start | bytes 589832 | tf_op jit(solution)/shard_map/ppermute | solution.py:844
  33.9 11.6 %collective-permute-start.15 = (bf16[48,1024]{1,0:T(8,128)(2,1)S(1)}, bf16[48,1024]{1,0:T(8,128)(2,1)S(1)}, u32[]{:S(2)}, u32[]{:S(2)}) collective-permute-start(bf16[48,1024]{1,0:T(8,128)(2,1)S(1)} %shard_map.227), channel_id=1, source_target_pairs={{0,4},{1,3},{2,6},{3,1},{4,0},{5,7},{6,2},{7,5},{8,12},{9,11},{10,... | collective-permute-start | bytes 294920 | tf_op jit(solution)/shard_map/ppermute | solution.py:844
  43.5 16.3 %collective-permute-start.12 = (bf16[192,1664]{1,0:T(8,128)(2,1)S(1)}, bf16[192,1664]{1,0:T(8,128)(2,1)S(1)}, u32[]{:S(2)}, u32[]{:S(2)}) collective-permute-start(bf16[192,1664]{1,0:T(8,128)(2,1)S(1)} %shard_map.225.refs_2_.refs_8_.refs_4_), channel_id=1, source_target_pairs={{0,4},{1,3},{2,6},{3,1},{4,0},{5,7},{6,2},{7,5},{8,12},{9,11},{10,... | collective-permute-start | bytes 1916936 | tf_op jit(solution)/shard_map/ppermute | solution.py:844
  45.9 16.3 %collective-permute-start.19 = (bf16[192,1536]{1,0:T(8,128)(2,1)S(1)}, bf16[192,1536]{1,0:T(8,128)(2,1)S(1)}, u32[]{:S(2)}, u32[]{:S(2)}) collective-permute-start(bf16[192,1536]{1,0:T(8,128)(2,1)S(1)} %get-tuple-element.129.refs_1_), channel_id=1, source_target_pairs={{0,2},{1,5},{2,0},{3,7},{4,6},{5,1},{6,4},{7,3},{8,10},{9,13},{10,... | collective-permute-start | bytes 1769480 | tf_op jit(solution)/shard_map/ppermute | solution.py:844
  47.2 19.4 %collective-permute-start.20 = (bf16[192,1536]{1,0:T(8,128)(2,1)S(1)}, bf16[192,1536]{1,0:T(8,128)(2,1)S(1)}, u32[]{:S(2)}, u32[]{:S(2)}) collective-permute-start(bf16[192,1536]{1,0:T(8,128)(2,1)S(1)} %get-tuple-element.129.refs_1_), channel_id=1, source_target_pairs={{0,4},{1,3},{2,6},{3,1},{4,0},{5,7},{6,2},{7,5},{8,12},{9,11},{10,... | collective-permute-start | bytes 1769480 | tf_op jit(solution)/shard_map/ppermute | solution.py:844
  47.8 19.9 %collective-permute-start.18 = (bf16[96,2048]{1,0:T(8,128)(2,1)S(1)}, bf16[96,2048]{1,0:T(8,128)(2,1)S(1)}, u32[]{:S(2)}, u32[]{:S(2)}) collective-permute-start(bf16[96,2048]{1,0:T(8,128)(2,1)S(1)} %get-tuple-element.128.refs_0_.refs_2_), channel_id=1, source_target_pairs={{0,16},{1,17},{2,18},{3,19},{4,20},{5,21},{6,22},{7,23},{8,24},{9,... | collective-permute-start | bytes 1179656 | tf_op jit(solution)/shard_map/ppermute | solution.py:844
  67.8 21.6 %collective-permute-start.22 = (bf16[192,1536]{1,0:T(8,128)(2,1)S(1)}, bf16[192,1536]{1,0:T(8,128)(2,1)S(1)}, u32[]{:S(2)}, u32[]{:S(2)}) collective-permute-start(bf16[192,1536]{1,0:T(8,128)(2,1)S(1)} %shard_map.233.refs_10_.refs_1_), channel_id=1, source_target_pairs={{0,2},{1,5},{2,0},{3,7},{4,6},{5,1},{6,4},{7,3},{8,10},{9,13},{10,... | collective-permute-start | bytes 1769480 | tf_op jit(solution)/shard_map/ppermute | solution.py:844
  68.5 20.9 %collective-permute-start.23 = (bf16[192,1536]{1,0:T(8,128)(2,1)S(1)}, bf16[192,1536]{1,0:T(8,128)(2,1)S(1)}, u32[]{:S(2)}, u32[]{:S(2)}) collective-permute-start(bf16[192,1536]{1,0:T(8,128)(2,1)S(1)} %shard_map.233.refs_10_.refs_1_), channel_id=1, source_target_pairs={{0,4},{1,3},{2,6},{3,1},{4,0},{5,7},{6,2},{7,5},{8,12},{9,11},{10,... | collective-permute-start | bytes 1769480 | tf_op jit(solution)/shard_map/ppermute | solution.py:844
  70.1 18.4 %collective-permute-start.21 = (bf16[192,1536]{1,0:T(8,128)(2,1)S(1)}, bf16[192,1536]{1,0:T(8,128)(2,1)S(1)}, u32[]{:S(2)}, u32[]{:S(2)}) collective-permute-start(bf16[192,1536]{1,0:T(8,128)(2,1)S(1)} %shard_map.235.refs_2_), channel_id=1, source_target_pairs={{0,4},{1,3},{2,6},{3,1},{4,0},{5,7},{6,2},{7,5},{8,12},{9,11},{10,... | collective-permute-start | bytes 1769480 | tf_op jit(solution)/shard_map/ppermute | solution.py:844
  70.5 18.8 %collective-permute-start.24 = (bf16[192,1024]{1,0:T(8,128)(2,1)S(1)}, bf16[192,1024]{1,0:T(8,128)(2,1)S(1)}, u32[]{:S(2)}, u32[]{:S(2)}) collective-permute-start(bf16[192,1024]{1,0:T(8,128)(2,1)S(1)} %shard_map.236.refs_0_.refs_2_.refs_5_), channel_id=1, source_target_pairs={{0,16},{1,17},{2,18},{3,19},{4,20},{5,21},{6,22},{7,23},{8,24},{9,... | collective-permute-start | bytes 1179656 | tf_op jit(solution)/shard_map/ppermute | solution.py:844
  90.1 14.6 %collective-permute-start.27 = (bf16[192,1536]{1,0:T(8,128)(2,1)S(1)}, bf16[192,1536]{1,0:T(8,128)(2,1)S(1)}, u32[]{:S(2)}, u32[]{:S(2)}) collective-permute-start(bf16[192,1536]{1,0:T(8,128)(2,1)S(1)} %shard_map.238.refs_1_.refs_2_), channel_id=1, source_target_pairs={{0,4},{1,3},{2,6},{3,1},{4,0},{5,7},{6,2},{7,5},{8,12},{9,11},{10,... | collective-permute-start | bytes 1769480 | tf_op jit(solution)/shard_map/ppermute | solution.py:844
  91.2 12.6 %collective-permute-start.28 = (bf16[192,512]{1,0:T(8,128)(2,1)S(1)}, bf16[192,512]{1,0:T(8,128)(2,1)S(1)}, u32[]{:S(2)}, u32[]{:S(2)}) collective-permute-start(bf16[192,512]{1,0:T(8,128)(2,1)S(1)} %shard_map.239.refs_1_.refs_4_), channel_id=1, source_target_pairs={{0,2},{1,5},{2,0},{3,7},{4,6},{5,1},{6,4},{7,3},{8,10},{9,13},{10,... | collective-permute-start | bytes 589832 | tf_op jit(solution)/shard_map/ppermute | solution.py:844
  92.2 11.9 %collective-permute-start.29 = (bf16[192,512]{1,0:T(8,128)(2,1)S(1)}, bf16[192,512]{1,0:T(8,128)(2,1)S(1)}, u32[]{:S(2)}, u32[]{:S(2)}) collective-permute-start(bf16[192,512]{1,0:T(8,128)(2,1)S(1)} %shard_map.239.refs_1_.refs_4_), channel_id=1, source_target_pairs={{0,4},{1,3},{2,6},{3,1},{4,0},{5,7},{6,2},{7,5},{8,12},{9,11},{10,... | collective-permute-start | bytes 589832 | tf_op jit(solution)/shard_map/ppermute | solution.py:844
  93.3 11.4 %collective-permute-start.30 = (bf16[384,512]{1,0:T(8,128)(2,1)S(1)}, bf16[384,512]{1,0:T(8,128)(2,1)S(1)}, u32[]{:S(2)}, u32[]{:S(2)}) collective-permute-start(bf16[384,512]{1,0:T(8,128)(2,1)S(1)} %get-tuple-element.138), channel_id=1, source_target_pairs={{0,8},{1,9},{2,10},{3,11},{4,12},{5,13},{6,14},{7,15},{8,0},{9,1},... | collective-permute-start | bytes 1179656 | tf_op jit(solution)/shard_map/ppermute | solution.py:844
  104.7 12.4 %collective-permute-start.33 = (bf16[384,512]{1,0:T(8,128)(2,1)S(1)}, bf16[384,512]{1,0:T(8,128)(2,1)S(1)}, u32[]{:S(2)}, u32[]{:S(2)}) collective-permute-start(bf16[384,512]{1,0:T(8,128)(2,1)S(1)} %shard_map.247), channel_id=1, source_target_pairs={{0,8},{1,9},{2,10},{3,11},{4,12},{5,13},{6,14},{7,15},{8,0},{9,1},... | collective-permute-start | bytes 1179656 | tf_op jit(solution)/shard_map/ppermute | solution.py:844
  106.0 11.2 %collective-permute-start.32 = (bf16[192,512]{1,0:T(8,128)(2,1)S(1)}, bf16[192,512]{1,0:T(8,128)(2,1)S(1)}, u32[]{:S(2)}, u32[]{:S(2)}) collective-permute-start(bf16[192,512]{1,0:T(8,128)(2,1)S(1)} %shard_map.246), channel_id=1, source_target_pairs={{0,4},{1,3},{2,6},{3,1},{4,0},{5,7},{6,2},{7,5},{8,12},{9,11},{10,... | collective-permute-start | bytes 589832 | tf_op jit(solution)/shard_map/ppermute | solution.py:844
  113.5 10.5 %collective-permute-start.34 = (bf16[192,896]{1,0:T(8,128)(2,1)S(1)}, bf16[192,896]{1,0:T(8,128)(2,1)S(1)}, u32[]{:S(2)}, u32[]{:S(2)}) collective-permute-start(bf16[192,896]{1,0:T(8,128)(2,1)S(1)} %get-tuple-element.154), channel_id=1, source_target_pairs={{0,2},{1,5},{2,0},{3,7},{4,6},{5,1},{6,4},{7,3},{8,10},{9,13},{10,... | collective-permute-start | bytes 1032200 | tf_op jit(solution)/shard_map/ppermute | solution.py:844
  114.5 9.4 %collective-permute-start.35 = (bf16[384,128]{1,0:T(8,128)(2,1)S(1)}, bf16[384,128]{1,0:T(8,128)(2,1)S(1)}, u32[]{:S(2)}, u32[]{:S(2)}) collective-permute-start(bf16[384,128]{1,0:T(8,128)(2,1)S(1)} %get-tuple-element.156), channel_id=1, source_target_pairs={{0,16},{1,17},{2,18},{3,19},{4,20},{5,21},{6,22},{7,23},{8,24},{9,... | collective-permute-start | bytes 294920 | tf_op jit(solution)/shard_map/ppermute | solution.py:844
  124.2 21.1 %collective-permute-start.39 = (bf16[192,896]{1,0:T(8,128)(2,1)S(1)}, bf16[192,896]{1,0:T(8,128)(2,1)S(1)}, u32[]{:S(2)}, u32[]{:S(2)}) collective-permute-start(bf16[192,896]{1,0:T(8,128)(2,1)S(1)} %shard_map.250.refs_1_.refs_18_), channel_id=1, source_target_pairs={{0,4},{1,3},{2,6},{3,1},{4,0},{5,7},{6,2},{7,5},{8,12},{9,11},{10,... | collective-permute-start | bytes 1032200 | tf_op jit(solution)/shard_map/ppermute | solution.py:844
  125.3 21.2 %collective-permute-start.41 = (bf16[192,1536]{1,0:T(8,128)(2,1)S(1)}, bf16[192,1536]{1,0:T(8,128)(2,1)S(1)}, u32[]{:S(2)}, u32[]{:S(2)}) collective-permute-start(bf16[192,1536]{1,0:T(8,128)(2,1)S(1)} %shard_map.256), channel_id=1, source_target_pairs={{0,2},{1,5},{2,0},{3,7},{4,6},{5,1},{6,4},{7,3},{8,10},{9,13},{10,... | collective-permute-start | bytes 1769480 | tf_op jit(solution)/shard_map/ppermute | solution.py:844
  126.2 20.2 %collective-permute-start.40 = (bf16[384,512]{1,0:T(8,128)(2,1)S(1)}, bf16[384,512]{1,0:T(8,128)(2,1)S(1)}, u32[]{:S(2)}, u32[]{:S(2)}) collective-permute-start(bf16[384,512]{1,0:T(8,128)(2,1)S(1)} %shard_map.255), channel_id=1, source_target_pairs={{0,16},{1,17},{2,18},{3,19},{4,20},{5,21},{6,22},{7,23},{8,24},{9,... | collective-permute-start | bytes 1179656 | tf_op jit(solution)/shard_map/ppermute | solution.py:844
  128.8 16.4 %collective-permute-start.38 = (bf16[192,896]{1,0:T(8,128)(2,1)S(1)}, bf16[192,896]{1,0:T(8,128)(2,1)S(1)}, u32[]{:S(2)}, u32[]{:S(2)}) collective-permute-start(bf16[192,896]{1,0:T(8,128)(2,1)S(1)} %shard_map.254), channel_id=1, source_target_pairs={{0,2},{1,5},{2,0},{3,7},{4,6},{5,1},{6,4},{7,3},{8,10},{9,13},{10,... | collective-permute-start | bytes 1032200 | tf_op jit(solution)/shard_map/ppermute | solution.py:844
  129.7 17.6 %collective-permute-start.37 = (bf16[192,1536]{1,0:T(8,128)(2,1)S(1)}, bf16[192,1536]{1,0:T(8,128)(2,1)S(1)}, u32[]{:S(2)}, u32[]{:S(2)}) collective-permute-start(bf16[192,1536]{1,0:T(8,128)(2,1)S(1)} %shard_map.253), channel_id=1, source_target_pairs={{0,2},{1,5},{2,0},{3,7},{4,6},{5,1},{6,4},{7,3},{8,10},{9,13},{10,... | collective-permute-start | bytes 1769480 | tf_op jit(solution)/shard_map/ppermute | solution.py:844
  148.1 21.7 %collective-permute-start.44 = (bf16[192,1536]{1,0:T(8,128)(2,1)S(1)}, bf16[192,1536]{1,0:T(8,128)(2,1)S(1)}, u32[]{:S(2)}, u32[]{:S(2)}) collective-permute-start(bf16[192,1536]{1,0:T(8,128)(2,1)S(1)} %get-tuple-element.166.refs_1_.refs_17_), channel_id=1, source_target_pairs={{0,4},{1,3},{2,6},{3,1},{4,0},{5,7},{6,2},{7,5},{8,12},{9,11},{10,... | collective-permute-start | bytes 1769480 | tf_op jit(solution)/shard_map/ppermute | solution.py:844
  149.1 16.6 %collective-permute-start.47 = (bf16[192,1536]{1,0:T(8,128)(2,1)S(1)}, bf16[192,1536]{1,0:T(8,128)(2,1)S(1)}, u32[]{:S(2)}, u32[]{:S(2)}) collective-permute-start(bf16[192,1536]{1,0:T(8,128)(2,1)S(1)} %shard_map.261), channel_id=1, source_target_pairs={{0,2},{1,5},{2,0},{3,7},{4,6},{5,1},{6,4},{7,3},{8,10},{9,13},{10,... | collective-permute-start | bytes 1769480 | tf_op jit(solution)/shard_map/ppermute | solution.py:844
  150.1 19.7 %collective-permute-start.43 = (bf16[192,1536]{1,0:T(8,128)(2,1)S(1)}, bf16[192,1536]{1,0:T(8,128)(2,1)S(1)}, u32[]{:S(2)}, u32[]{:S(2)}) collective-permute-start(bf16[192,1536]{1,0:T(8,128)(2,1)S(1)} %shard_map.260), channel_id=1, source_target_pairs={{0,2},{1,5},{2,0},{3,7},{4,6},{5,1},{6,4},{7,3},{8,10},{9,13},{10,... | collective-permute-start | bytes 1769480 | tf_op jit(solution)/shard_map/ppermute | solution.py:844
  151.2 14.5 %collective-permute-start.46 = (bf16[192,640]{1,0:T(8,128)(2,1)S(1)}, bf16[192,640]{1,0:T(8,128)(2,1)S(1)}, u32[]{:S(2)}, u32[]{:S(2)}) collective-permute-start(bf16[192,640]{1,0:T(8,128)(2,1)S(1)} %get-tuple-element.182), channel_id=1, source_target_pairs={{0,8},{1,9},{2,10},{3,11},{4,12},{5,13},{6,14},{7,15},{8,0},{9,1},... | collective-permute-start | bytes 737288 | tf_op jit(solution)/shard_map/ppermute | solution.py:844
  152.4 13.3 %collective-permute-start.45 = (bf16[96,896]{1,0:T(8,128)(2,1)S(1)}, bf16[96,896]{1,0:T(8,128)(2,1)S(1)}, u32[]{:S(2)}, u32[]{:S(2)}) collective-permute-start(bf16[96,896]{1,0:T(8,128)(2,1)S(1)} %get-tuple-element.180), channel_id=1, source_target_pairs={{0,16},{1,17},{2,18},{3,19},{4,20},{5,21},{6,22},{7,23},{8,24},{9,... | collective-permute-start | bytes 516104 | tf_op jit(solution)/shard_map/ppermute | solution.py:844
  170.2 18.2 %collective-permute-start.49 = (bf16[192,1536]{1,0:T(8,128)(2,1)S(1)}, bf16[192,1536]{1,0:T(8,128)(2,1)S(1)}, u32[]{:S(2)}, u32[]{:S(2)}) collective-permute-start(bf16[192,1536]{1,0:T(8,128)(2,1)S(1)} %get-tuple-element.184.refs_1_.refs_2_), channel_id=1, source_target_pairs={{0,4},{1,3},{2,6},{3,1},{4,0},{5,7},{6,2},{7,5},{8,12},{9,11},{10,... | collective-permute-start | bytes 1769480 | tf_op jit(solution)/shard_map/ppermute | solution.py:844
  171.3 17.2 %collective-permute-start.48 = (bf16[192,1664]{1,0:T(8,128)(2,1)S(1)}, bf16[192,1664]{1,0:T(8,128)(2,1)S(1)}, u32[]{:S(2)}, u32[]{:S(2)}) collective-permute-start(bf16[192,1664]{1,0:T(8,128)(2,1)S(1)} %shard_map.263), channel_id=1, source_target_pairs={{0,2},{1,5},{2,0},{3,7},{4,6},{5,1},{6,4},{7,3},{8,10},{9,13},{10,... | collective-permute-start | bytes 1916936 | tf_op jit(solution)/shard_map/ppermute | solution.py:844
  172.2 16.2 %collective-permute-start.50 = (bf16[96,1536]{1,0:T(8,128)(2,1)S(1)}, bf16[96,1536]{1,0:T(8,128)(2,1)S(1)}, u32[]{:S(2)}, u32[]{:S(2)}) collective-permute-start(bf16[96,1536]{1,0:T(8,128)(2,1)S(1)} %get-tuple-element.187), channel_id=1, source_target_pairs={{0,16},{1,17},{2,18},{3,19},{4,20},{5,21},{6,22},{7,23},{8,24},{9,... | collective-permute-start | bytes 884744 | tf_op jit(solution)/shard_map/ppermute | solution.py:844
  174.9 13.1 %collective-permute-start.52 = (bf16[96,640]{1,0:T(8,128)(2,1)S(1)}, bf16[96,640]{1,0:T(8,128)(2,1)S(1)}, u32[]{:S(2)}, u32[]{:S(2)}) collective-permute-start(bf16[96,640]{1,0:T(8,128)(2,1)S(1)} %get-tuple-element.192), channel_id=1, source_target_pairs={{0,2},{1,5},{2,0},{3,7},{4,6},{5,1},{6,4},{7,3},{8,10},{9,13},{10,... | collective-permute-start | bytes 368648 | tf_op jit(solution)/shard_map/ppermute | solution.py:844
  189.5 17.8 %collective-permute-start.56 = (bf16[192,1664]{1,0:T(8,128)(2,1)S(1)}, bf16[192,1664]{1,0:T(8,128)(2,1)S(1)}, u32[]{:S(2)}, u32[]{:S(2)}) collective-permute-start(bf16[192,1664]{1,0:T(8,128)(2,1)S(1)} %get-tuple-element.195.refs_1_), channel_id=1, source_target_pairs={{0,4},{1,3},{2,6},{3,1},{4,0},{5,7},{6,2},{7,5},{8,12},{9,11},{10,... | collective-permute-start | bytes 1916936 | tf_op jit(solution)/shard_map/ppermute | solution.py:844
  190.5 16.8 %collective-permute-start.55 = (bf16[192,1664]{1,0:T(8,128)(2,1)S(1)}, bf16[192,1664]{1,0:T(8,128)(2,1)S(1)}, u32[]{:S(2)}, u32[]{:S(2)}) collective-permute-start(bf16[192,1664]{1,0:T(8,128)(2,1)S(1)} %shard_map.269), channel_id=1, source_target_pairs={{0,2},{1,5},{2,0},{3,7},{4,6},{5,1},{6,4},{7,3},{8,10},{9,13},{10,... | collective-permute-start | bytes 1916936 | tf_op jit(solution)/shard_map/ppermute | solution.py:844
  191.5 15.7 %collective-permute-start.57 = (bf16[96,1536]{1,0:T(8,128)(2,1)S(1)}, bf16[96,1536]{1,0:T(8,128)(2,1)S(1)}, u32[]{:S(2)}, u32[]{:S(2)}) collective-permute-start(bf16[96,1536]{1,0:T(8,128)(2,1)S(1)} %get-tuple-element.203), channel_id=1, source_target_pairs={{0,16},{1,17},{2,18},{3,19},{4,20},{5,21},{6,22},{7,23},{8,24},{9,... | collective-permute-start | bytes 884744 | tf_op jit(solution)/shard_map/ppermute | solution.py:844
  193.5 13.8 %collective-permute-start.59 = (bf16[48,1536]{1,0:T(8,128)(2,1)S(1)}, bf16[48,1536]{1,0:T(8,128)(2,1)S(1)}, u32[]{:S(2)}, u32[]{:S(2)}) collective-permute-start(bf16[48,1536]{1,0:T(8,128)(2,1)S(1)} %get-tuple-element.207), channel_id=1, source_target_pairs={{0,8},{1,9},{2,10},{3,11},{4,12},{5,13},{6,14},{7,15},{8,0},{9,1},... | collective-permute-start | bytes 442376 | tf_op jit(solution)/shard_map/ppermute | solution.py:844
  194.2 13.1 %collective-permute-start.58 = (bf16[48,640]{1,0:T(8,128)(2,1)S(1)}, bf16[48,640]{1,0:T(8,128)(2,1)S(1)}, u32[]{:S(2)}, u32[]{:S(2)}) collective-permute-start(bf16[48,640]{1,0:T(8,128)(2,1)S(1)} %get-tuple-element.205), channel_id=1, source_target_pairs={{0,4},{1,3},{2,6},{3,1},{4,0},{5,7},{6,2},{7,5},{8,12},{9,11},{10,... | collective-permute-start | bytes 184328 | tf_op jit(solution)/shard_map/ppermute | solution.py:844
  208.9 13.0 %collective-permute-start.60 = (bf16[48,3200]{1,0:T(8,128)(2,1)S(1)}, bf16[48,3200]{1,0:T(8,128)(2,1)S(1)}, u32[]{:S(2)}, u32[]{:S(2)}) collective-permute-start(bf16[48,3200]{1,0:T(8,128)(2,1)S(1)} %get-tuple-element.209), channel_id=1, source_target_pairs={{0,8},{1,9},{2,10},{3,11},{4,12},{5,13},{6,14},{7,15},{8,0},{9,1},... | collective-permute-start | bytes 921608 | tf_op jit(solution)/shard_map/ppermute | solution.py:844
  209.5 13.2 %collective-permute-start.61 = (bf16[48,1664]{1,0:T(8,128)(2,1)}, bf16[48,1664]{1,0:T(8,128)(2,1)S(1)}, u32[]{:S(2)}, u32[]{:S(2)}) collective-permute-start(bf16[48,1664]{1,0:T(8,128)(2,1)} %copy-done.19), channel_id=1, source_target_pairs={{0,16},{1,17},{2,18},{3,19},{4,20},{5,21},{6,22},{7,23},{8,24},{9,... | collective-permute-start | bytes 479240 | tf_op jit(solution)/shard_map/ppermute | solution.py:844
  211.9 14.1 %collective-permute-start.62 = (bf16[48,1664]{1,0:T(8,128)(2,1)S(1)}, bf16[48,1664]{1,0:T(8,128)(2,1)S(1)}, u32[]{:S(2)}, u32[]{:S(2)}) collective-permute-start(bf16[48,1664]{1,0:T(8,128)(2,1)S(1)} %get-tuple-element.211), channel_id=1, source_target_pairs={{0,24},{1,25},{2,26},{3,27},{4,28},{5,29},{6,30},{7,31},{8,16},{9,... | collective-permute-start | bytes 479240 | tf_op jit(solution)/shard_map/ppermute | solution.py:844
  (56 other events, 343.9 us)
